TPU v7x, 128 devices: a whole 4x4x4 slice. The times are simulated.
128 devices in a mesh: rep: 16 (over x, z_lo, core), grp: 8 (over y, z_hi).
Axes of the slice: x: 4, y: 4, z: 4 (z_hi: 2, z_lo: 2; z = z_hi * 2 + z_lo), core: 2. Of those that a mesh axis runs over, the one named last changes fastest.
Arguments:
- tokens: bfloat16 [16, 1024, 1600], P('rep', 'grp'), may hold values from -6 to 6
- ln1_gain: bfloat16 [1600], P('grp'), may hold values from 0.25 to 1.75
- ln1_bias: bfloat16 [1600], P('grp'), may hold values from -1.5 to 1.5
- w_qkv: bfloat16 [1600, 4800], P('grp'), may hold values from -0.15625 to 0.15625
- bias_q: bfloat16 [1600], P('grp'), may hold values from -1.5 to 1.5
- bias_v: bfloat16 [1600], P('grp'), may hold values from -1.5 to 1.5
- w_out: bfloat16 [1600, 1600], P('grp'), may hold values from -1.25 to 1.25
- bias_out: bfloat16 [1600], P('grp'), may hold values from -1.5 to 1.5
- ln2_gain: bfloat16 [1600], P('grp'), may hold values from 0.25 to 1.75
- ln2_bias: bfloat16 [1600], P('grp'), may hold values from -1.5 to 1.5
- w_fc: bfloat16 [1600, 6400], P('grp'), may hold values from -0.15625 to 0.15625
- bias_fc: bfloat16 [6400], P('grp'), may hold values from -2.5 to 2.5
- w_proj: bfloat16 [6400, 1600], P('grp'), may hold values from -0.078125 to 0.078125
- bias_proj: bfloat16 [1600], P('grp'), may hold values from -1.5 to 1.5
- cotangent: bfloat16 [16, 1024, 1600], P('rep', 'grp'), may hold values from -6 to 6
Outputs:
- output: bfloat16 [16, 1024, 1600], P('rep', 'grp')
- grad_tokens: float32 [16, 1024, 1600], P('rep', 'grp')
- grad_ln1_gain: float32 [1600], P('grp')
- grad_ln1_bias: float32 [1600], P('grp')
- grad_w_qkv: float32 [1600, 4800], P('grp')
- grad_bias_q: float32 [1600], P('grp')
- grad_bias_v: float32 [1600], P('grp')
- grad_w_out: float32 [1600, 1600], P('grp')
- grad_bias_out: float32 [1600], P('grp')
- grad_ln2_gain: float32 [1600], P('grp')
- grad_ln2_bias: float32 [1600], P('grp')
- grad_w_fc: float32 [1600, 6400], P('grp')
- grad_bias_fc: float32 [6400], P('grp')
- grad_w_proj: float32 [6400, 1600], P('grp')
- grad_bias_proj: float32 [1600], P('grp')
All inputs are finite; a program needn't handle non-finite values.
Results may differ from a plain program's by a relative error of at most 0.02.
Values may be sent and summed in bfloat16 or wider, within the bound.
No kernel may reach another device: no remote copies, remote signals or barrier semaphores. Data moves between devices by JAX's collectives and lax.ppermute only.
A program may use at most 256 MiB of HBM per device.

v0:
```python
import math

import jax
import jax.numpy as jnp
from jax import lax
from jax.sharding import PartitionSpec as P

HEADS = 25


def norm_parts(value, gain, shift):
    center = value - jnp.mean(value, axis=-1, keepdims=True)
    spread = jnp.mean(center * center, axis=-1, keepdims=True)
    factor = lax.rsqrt(spread + 1e-05)
    normed = center * factor
    return (normed * gain + shift, normed, factor)


def norm_back(grad_value, normed, factor, gain):
    grad_normed = grad_value * gain
    mean_first = jnp.mean(grad_normed, axis=-1, keepdims=True)
    mean_second = jnp.mean(grad_normed * normed, axis=-1, keepdims=True)
    return factor * (grad_normed - mean_first - normed * mean_second)


def gelu_tanh(value):
    return (
        0.5
        * value
        * (1.0 + jnp.tanh(0.7978845608028654 * (value + 0.044715 * value * value * value)))
    )


def project(inputs, weight):
    return jnp.dot(
        inputs,
        lax.all_gather(weight, "grp", axis=0, tiled=True),
        preferred_element_type=jnp.float32,
    )


def project_back(grads, weight):
    return lax.dot_general(
        grads,
        lax.all_gather(weight, "grp", axis=0, tiled=True),
        (((1,), (1,)), ((), ())),
        preferred_element_type=jnp.float32,
    )


def weight_grad(inputs, grads):
    return lax.psum_scatter(
        lax.dot_general(
            inputs, grads, (((0,), (0,)), ((), ())), preferred_element_type=jnp.float32
        ).astype(jnp.bfloat16),
        "grp",
        scatter_dimension=0,
        tiled=True,
    ).astype(jnp.float32)


def per_device(
    tokens,
    ln1_gain,
    ln1_bias,
    w_qkv,
    bias_q,
    bias_v,
    w_out,
    bias_out,
    ln2_gain,
    ln2_bias,
    w_fc,
    bias_fc,
    w_proj,
    bias_proj,
    cotangent,
):
    seq_count, span_len, model_width = tokens.shape
    group_size = lax.axis_size("grp")
    group_rank = lax.axis_index("grp")
    full_length = span_len * group_size
    head_count = HEADS
    head_dim = model_width // head_count
    score_scale = 1.0 / math.sqrt(head_dim)
    row_count = seq_count * span_len
    bf16 = jnp.bfloat16
    f32 = jnp.float32
    gathered_small = (
        lax.all_gather(ln1_gain, "grp", axis=0, tiled=True),
        lax.all_gather(ln1_bias, "grp", axis=0, tiled=True),
        lax.all_gather(bias_q, "grp", axis=0, tiled=True),
        lax.all_gather(bias_v, "grp", axis=0, tiled=True),
        lax.all_gather(bias_out, "grp", axis=0, tiled=True),
        lax.all_gather(ln2_gain, "grp", axis=0, tiled=True),
        lax.all_gather(ln2_bias, "grp", axis=0, tiled=True),
        lax.all_gather(bias_fc, "grp", axis=0, tiled=True),
        lax.all_gather(bias_proj, "grp", axis=0, tiled=True),
    )
    (
        gain_first,
        shift_first,
        query_bias,
        value_bias,
        output_bias,
        gain_second,
        shift_second,
        hidden_bias,
        down_bias,
    ) = [p.astype(f32) for p in gathered_small]
    inputs = tokens.astype(f32).reshape(row_count, model_width)
    first, normed_first, factor_first = norm_parts(inputs, gain_first, shift_first)
    first_low = first.astype(bf16)
    mixed = project(first_low, w_qkv)
    query = (mixed[:, :model_width] + query_bias).astype(bf16)
    key_local = (
        mixed[:, model_width : 2 * model_width]
        .astype(bf16)
        .reshape(seq_count, span_len, model_width)
    )
    value_local = (
        (mixed[:, 2 * model_width :] + value_bias)
        .astype(bf16)
        .reshape(seq_count, span_len, model_width)
    )
    query_heads = query.reshape(seq_count, span_len, head_count, head_dim)
    position = group_rank * span_len + lax.broadcasted_iota(jnp.int32, (span_len, 1), 0)
    key_position = lax.broadcasted_iota(jnp.int32, (1, full_length), 1)
    allowed = key_position <= position

    def masked_scores(key_whole):
        key_heads = key_whole.reshape(seq_count, full_length, head_count, head_dim)
        raw_scores = (
            jnp.einsum("sqhd,skhd->shqk", query_heads, key_heads, preferred_element_type=f32)
            * score_scale
        )
        return jnp.where(allowed, raw_scores, -1e30)

    gathered_kv = (
        lax.all_gather(key_local, "grp", axis=1, tiled=True),
        lax.all_gather(value_local, "grp", axis=1, tiled=True),
    )
    scores = masked_scores(gathered_kv[0])
    row_top = jnp.max(scores, axis=-1, keepdims=True)
    unscaled = jnp.exp(scores - row_top)
    row_total = jnp.sum(unscaled, axis=-1, keepdims=True)
    probs = unscaled / row_total
    value_heads = gathered_kv[1].reshape(seq_count, full_length, head_count, head_dim)
    attended = jnp.einsum(
        "shqk,skhd->sqhd", probs.astype(bf16), value_heads, preferred_element_type=f32
    )
    attended_low = attended.reshape(row_count, model_width).astype(bf16)
    middle = inputs + (project(attended_low, w_out) + output_bias)
    second, normed_second, factor_second = norm_parts(middle, gain_second, shift_second)
    second_low = second.astype(bf16)
    hidden_pre = project(second_low, w_fc) + hidden_bias
    active, gelu_pull = jax.vjp(gelu_tanh, hidden_pre)
    active_low = active.astype(bf16)
    down_value = project(active_low, w_proj)
    output = middle + (down_value + down_bias)
    grad_low = cotangent.reshape(row_count, model_width)
    grad_full = grad_low.astype(f32)
    grad_active = project_back(grad_low, w_proj)
    proj_grad = weight_grad(active_low, grad_low)
    grad_hidden = gelu_pull(grad_active)[0].astype(bf16)
    hidden_grad = weight_grad(second_low, grad_hidden)
    grad_second = project_back(grad_hidden, w_fc)
    grad_middle = grad_full + norm_back(grad_second, normed_second, factor_second, gain_second)
    grad_branch = grad_middle.astype(bf16)
    outproj_grad = weight_grad(attended_low, grad_branch)
    grad_attended = project_back(grad_branch, w_out).astype(bf16)
    kept_kv = (
        lax.all_gather(key_local, "grp", axis=1, tiled=True),
        lax.all_gather(value_local, "grp", axis=1, tiled=True),
    )
    scores_again = masked_scores(kept_kv[0])
    probs_again = jnp.exp(scores_again - row_top) / row_total
    probs_low = probs_again.astype(bf16)
    key_heads_again = kept_kv[0].reshape(seq_count, full_length, head_count, head_dim)
    value_heads_again = kept_kv[1].reshape(seq_count, full_length, head_count, head_dim)
    grad_heads = grad_attended.reshape(seq_count, span_len, head_count, head_dim)
    grad_probs = jnp.einsum(
        "sqhd,skhd->shqk", grad_heads, value_heads_again, preferred_element_type=f32
    )
    row_delta = jnp.sum(probs_again * grad_probs, axis=-1, keepdims=True)
    grad_scores = (probs_again * (grad_probs - row_delta)).astype(bf16)
    grad_query = (
        jnp.einsum("shqk,skhd->sqhd", grad_scores, key_heads_again, preferred_element_type=f32)
        * score_scale
    )
    key_terms = (
        jnp.einsum("shqk,sqhd->skhd", grad_scores, query_heads, preferred_element_type=f32)
        * score_scale
    )
    value_terms = jnp.einsum("shqk,sqhd->skhd", probs_low, grad_heads, preferred_element_type=f32)
    key_terms = key_terms.reshape(seq_count, full_length, model_width)
    value_terms = value_terms.reshape(seq_count, full_length, model_width)
    grad_keys, grad_values = (
        lax.psum_scatter(
            key_terms.astype(jnp.bfloat16), "grp", scatter_dimension=1, tiled=True
        ).astype(jnp.float32),
        lax.psum_scatter(
            value_terms.astype(jnp.bfloat16), "grp", scatter_dimension=1, tiled=True
        ).astype(jnp.float32),
    )
    query_low = grad_query.reshape(row_count, model_width).astype(bf16)
    keys_low = grad_keys.reshape(row_count, model_width).astype(bf16)
    values_low = grad_values.reshape(row_count, model_width).astype(bf16)
    grad_mixed = jnp.concatenate([query_low, keys_low, values_low], axis=1)
    qkv_grad = weight_grad(first_low, grad_mixed)
    grad_first = project_back(grad_mixed, w_qkv)
    grad_inputs = grad_middle + norm_back(grad_first, normed_first, factor_first, gain_first)
    small_terms = (
        jnp.sum(grad_first * normed_first, axis=0),
        jnp.sum(grad_first, axis=0),
        jnp.sum(query_low.astype(f32), axis=0),
        jnp.sum(values_low.astype(f32), axis=0),
        jnp.sum(grad_branch.astype(f32), axis=0),
        jnp.sum(grad_second * normed_second, axis=0),
        jnp.sum(grad_second, axis=0),
        jnp.sum(grad_hidden.astype(f32), axis=0),
        jnp.sum(grad_full, axis=0),
    )
    small_totals = lax.psum(
        (
            small_terms[0],
            small_terms[1],
            small_terms[2],
            small_terms[3],
            small_terms[4],
            small_terms[5],
            small_terms[6],
            small_terms[7],
            small_terms[8],
        ),
        ("rep", "grp"),
    )
    owned_small = [
        lax.dynamic_slice_in_dim(
            vector, group_rank * (vector.shape[0] // group_size), vector.shape[0] // group_size
        )
        for vector in small_totals
    ]
    qkv_total, outproj_total, hidden_total, proj_total = (
        lax.psum(qkv_grad.astype(jnp.bfloat16), "rep").astype(jnp.float32),
        lax.psum(outproj_grad.astype(jnp.bfloat16), "rep").astype(jnp.float32),
        lax.psum(hidden_grad.astype(jnp.bfloat16), "rep").astype(jnp.float32),
        lax.psum(proj_grad.astype(jnp.bfloat16), "rep").astype(jnp.float32),
    )
    return (
        output.reshape(seq_count, span_len, model_width).astype(bf16),
        grad_inputs.reshape(seq_count, span_len, model_width),
        owned_small[0],
        owned_small[1],
        qkv_total,
        owned_small[2],
        owned_small[3],
        outproj_total,
        owned_small[4],
        owned_small[5],
        owned_small[6],
        hidden_total,
        owned_small[7],
        proj_total,
        owned_small[8],
    )


def solution(mesh):
    in_specs = (
        P("rep", "grp", None),
        P("grp"),
        P("grp"),
        P("grp", None),
        P("grp"),
        P("grp"),
        P("grp", None),
        P("grp"),
        P("grp"),
        P("grp"),
        P("grp", None),
        P("grp"),
        P("grp", None),
        P("grp"),
        P("rep", "grp", None),
    )
    out_specs = (
        P("rep", "grp", None),
        P("rep", "grp", None),
        P("grp"),
        P("grp"),
        P("grp", None),
        P("grp"),
        P("grp"),
        P("grp", None),
        P("grp"),
        P("grp"),
        P("grp"),
        P("grp", None),
        P("grp"),
        P("grp", None),
        P("grp"),
    )
    return jax.shard_map(
        per_device, mesh=mesh, in_specs=in_specs, out_specs=out_specs, check_vma=False
    )
```

profile of v0, /device:TPU:17, one launch (start us, length us, event | category | flops | bytes accessed | tf_op | source)
XLA Modules:
  0.0 2297.0 jit_solution(374040371909755784)
XLA Ops:
  18.2 33.9 %all-reduce.13 = (bf16[1600]{0:T(1024)(128)(2,1)S(1)}, bf16[1600]{0:T(1024)(128)(2,1)S(1)}, bf16[1600]{0:T(1024)(128)(2,1)S(1)}, bf16[1600]{0:T(1024)(128)(2,1)S...) all-reduce(bf16[1600]{0:T(1024)(128)(2,1)S(1)} %dynamic-update-slic, ...), channel_id=1, replica_groups=mesh['rep'=16,'grp'=8] {'grp'}, use_global_device_ids=true, to_apply=%add.1 | all-reduce | flops 19200 | bytes 76800
  54.6 132.8 %all-gather.9.cloned.1.call-done = bf16[1600,4800]{1,0:T(8,128)(2,1)} async-done(((bf16[200,4800]{1,0:T(8,128)(2,1)}), bf16[1600,4800]{1,0:T(8,128)(2,1)}) %all-gather.9.cloned.1.call-update) | async-done | bytes 15360016 | tf_op jit(solution)/shard_map/all_gather | solution.py:37
  202.3 63.0 %all-gather.19.cloned.1.call-done = bf16[1024,1600]{0,1:T(8,128)(2,1)} async-done(((bf16[128,1600]{0,1:T(8,128)(2,1)}), bf16[1024,1600]{0,1:T(8,128)(2,1)}) %all-gather.19.cloned.1.call-update) | async-done | bytes 3276816 | tf_op jit(solution)/shard_map/all_gather | solution.py:140
  265.3 11.5 fusion.61
  276.7 59.1 %all-gather.17.cloned.1.call-done = bf16[1024,1600]{0,1:T(8,128)(2,1)} async-done(((bf16[128,1600]{0,1:T(8,128)(2,1)}), bf16[1024,1600]{0,1:T(8,128)(2,1)}) %all-gather.17.cloned.1.call-update) | async-done | bytes 3276816 | tf_op jit(solution)/shard_map/all_gather | solution.py:141
  344.0 74.0 %all-gather.11.cloned.1.call-done = bf16[1600,1600]{1,0:T(8,128)(2,1)} async-done(((bf16[200,1600]{1,0:T(8,128)(2,1)}), bf16[1600,1600]{1,0:T(8,128)(2,1)}) %all-gather.11.cloned.1.call-update) | async-done | bytes 5120016 | tf_op jit(solution)/shard_map/all_gather | solution.py:37
  423.0 214.9 %all-gather.13.cloned.1.call-done = bf16[1600,6400]{1,0:T(8,128)(2,1)} async-done(((bf16[200,6400]{1,0:T(8,128)(2,1)}), bf16[1600,6400]{1,0:T(8,128)(2,1)}) %all-gather.13.cloned.1.call-update) | async-done | bytes 20480016 | tf_op jit(solution)/shard_map/all_gather | solution.py:37
  638.0 12.4 convolution_add_fusion
  650.4 215.1 %all-gather.15.cloned.1.call-done = bf16[6400,1600]{1,0:T(8,128)(2,1)} async-done(((bf16[800,1600]{1,0:T(8,128)(2,1)}), bf16[6400,1600]{1,0:T(8,128)(2,1)}) %all-gather.15.cloned.1.call-update) | async-done | bytes 20480016 | tf_op jit(solution)/shard_map/all_gather | solution.py:37
  865.5 12.1 convert_reduce_fusion
  877.6 12.7 multiply_reduce_fusion.1
  903.2 16.2 copy.32
  943.3 16.2 copy.30
  976.0 27.0 %reduce-scatter.21.cloned.1.call-done = bf16[128,1600]{1,0:T(8,128)(2,1)} async-done(((bf16[1024,1600]{1,0:T(8,128)(2,1)}), bf16[128,1600]{1,0:T(8,128)(2,1)}) %reduce-scatter.21.cloned.1.call-update) | async-done | bytes 409616
  1005.7 82.6 %reduce-scatter.19.cloned.1.call-done = bf16[128,1600]{1,0:T(8,128)(2,1)} async-done(((bf16[1024,1600]{1,0:T(8,128)(2,1)}), bf16[128,1600]{1,0:T(8,128)(2,1)}) %reduce-scatter.19.cloned.1.call-update) | async-done | bytes 409616
  1101.1 11.6 convolution_convert_fusion.1
  1113.7 11.6 convolution_convert_fusion
  1138.6 61.2 %reduce-scatter.23.cloned.1.call-done = bf16[200,1600]{1,0:T(8,128)(2,1)} async-done(((bf16[1600,1600]{1,0:T(8,128)(2,1)}), bf16[200,1600]{1,0:T(8,128)(2,1)}) %reduce-scatter.23.cloned.1.call-update) | async-done | bytes 640016
  1199.8 189.6 %reduce-scatter.15.cloned.1.call-done = bf16[200,4800]{1,0:T(8,128)(2,1)} async-done(((bf16[1600,4800]{1,0:T(8,128)(2,1)}), bf16[200,4800]{1,0:T(8,128)(2,1)}) %reduce-scatter.15.cloned.1.call-update) | async-done | bytes 1920016 | tf_op jit(solution)/shard_map/reduce_scatter | solution.py:52
  1389.4 296.6 %reduce-scatter.25.cloned.1.call-done = bf16[200,6400]{1,0:T(8,128)(2,1)} async-done(((bf16[1600,6400]{1,0:T(8,128)(2,1)}), bf16[200,6400]{1,0:T(8,128)(2,1)}) %reduce-scatter.25.cloned.1.call-update) | async-done | bytes 2560016
  1686.0 250.6 %reduce-scatter.17.cloned.1.call-done = bf16[800,1600]{1,0:T(8,128)(2,1)} async-done(((bf16[6400,1600]{1,0:T(8,128)(2,1)}), bf16[800,1600]{1,0:T(8,128)(2,1)}) %reduce-scatter.17.cloned.1.call-update) | async-done | bytes 2560016 | tf_op jit(solution)/shard_map/reduce_scatter | solution.py:52
  1937.2 14.8 fusion.18
  1953.2 138.8 %all-reduce.17.cloned.1.call-done = (f32[1600]{0:T(1024)}, f32[1600]{0:T(1024)}, f32[1600]{0:T(1024)}, f32[1600]{0:T(1024)}, f32[1600]{0:T(1024)}, /*index=5*/f3...) async-done(((f32[1600]{0:T(1024)}, f32[1600]{0:T(1024)}, f32[1600]{0:T(1024)}, f32[1600]{0:T(1024)}, f32[1600]{0:T(1024)}, /*index=5*/f32[1600]{0:T(1024)}, ...) | async-done | bytes 76816 | tf_op jit(solution)/shard_map/psum | solution.py:224
  2104.1 175.5 %all-reduce.19.cloned.1.call-done = (bf16[200,4800]{1,0:T(8,128)(2,1)}, bf16[200,1600]{1,0:T(8,128)(2,1)}, bf16[200,6400]{1,0:T(8,128)(2,1)}, bf16[800,1600]{1,0:T(8,128)(2,1)}) async-done(((bf16[200,4800]{1,0:T(8,128)(2,1)}, bf16[200,1600]{1,0:T(8,128)(2,1)}, bf16[200,6400]{1,0:T(8,128)(2,1)}, bf16[800,1600]{1,0:T(8,128)(2,1)}), (bf16[200,4800]{1,0:T(8,128)(2,1)}, bf16[200,1600]{1,0:T(8,128)(2,1)}, ...) | async-done | bytes 7680016 | tf_op jit(solution)/shard_map/psum | solution.py:245
  (133 shorter events, 147.5 us)
Async XLA Ops:
  7.2 180.3 %all-gather.9.cloned.1.call-start = ((), (), s32[]{:S(2)}) async-start(), calls=%async_computation.6 | async-start | bytes 17510400 | tf_op jit(solution)/shard_map/all_gather | solution.py:37
  7.9 257.3 %all-gather.19.cloned.1.call-start = ((), (), s32[]{:S(2)}) async-start(), calls=%async_computation.13 | async-start | bytes 3686400 | tf_op jit(solution)/shard_map/all_gather | solution.py:140
  198.8 137.0 %all-gather.17.cloned.1.call-start = ((), (), s32[]{:S(2)}) async-start(), calls=%async_computation.12 | async-start | bytes 3686400 | tf_op jit(solution)/shard_map/all_gather | solution.py:141
  200.1 76.7 %copy-start.5 = (bf16[128,1600]{0,1:T(8,128)(2,1)}, bf16[128,1600]{0,1:T(8,128)(2,1)S(1)}, u32[]{:S(2)}) copy-start(bf16[128,1600]{0,1:T(8,128)(2,1)S(1)} %get-tuple-element.47) | copy-start | bytes 1228804
  200.1 217.9 %all-gather.11.cloned.1.call-start = ((), (), s32[]{:S(2)}) async-start(), calls=%async_computation.7 | async-start | bytes 5990400 | tf_op jit(solution)/shard_map/all_gather | solution.py:37
  200.7 437.3 %all-gather.13.cloned.1.call-start = ((), (), s32[]{:S(2)}) async-start(), calls=%async_computation.8 | async-start | bytes 23040000 | tf_op jit(solution)/shard_map/all_gather | solution.py:37
  201.3 664.2 %all-gather.15.cloned.1.call-start = ((), (), s32[]{:S(2)}) async-start(), calls=%async_computation.9 | async-start | bytes 23961600 | tf_op jit(solution)/shard_map/all_gather | solution.py:37
  201.8 801.2 %reduce-scatter.21.cloned.1.call-start = ((), (), s32[]{:S(2)}) async-start(), calls=%async_computation.15 | async-start | bytes 3833856
  335.8 82.2 %copy-start.1 = (bf16[1,128,1600]{1,2,0:T(8,128)(2,1)S(1)}, bf16[1,128,1600]{1,2,0:T(8,128)(2,1)}, u32[]{:S(2)}) copy-start(bf16[1,128,1600]{1,2,0:T(8,128)(2,1)} %param.15) | copy-start | bytes 1228804
  423.0 442.4 %copy-start.9 = (bf16[1,128,1600]{1,2,0:T(8,128)(2,1)S(1)}, bf16[1,128,1600]{1,2,0:T(8,128)(2,1)}, u32[]{:S(2)}) copy-start(bf16[1,128,1600]{1,2,0:T(8,128)(2,1)} %param.29) | copy-start | bytes 1228804
  877.6 12.7 copy-start.2
  924.6 163.7 %reduce-scatter.19.cloned.1.call-start = ((), (), s32[]{:S(2)}) async-start(), calls=%async_computation.14 | async-start | bytes 3833856
  932.9 6.6 copy-start.6
  939.6 3.7 copy-start
  964.7 235.0 %reduce-scatter.23.cloned.1.call-start = ((), (), s32[]{:S(2)}) async-start(), calls=%async_computation.16 | async-start | bytes 5990400
  968.8 420.6 %reduce-scatter.15.cloned.1.call-start = ((), (), s32[]{:S(2)}) async-start(), calls=%async_computation.10 | async-start | bytes 17510400 | tf_op jit(solution)/shard_map/reduce_scatter | solution.py:52
  1101.0 585.0 %reduce-scatter.25.cloned.1.call-start = ((), (), s32[]{:S(2)}) async-start(), calls=%async_computation.17 | async-start | bytes 23040000
  1112.7 823.8 %reduce-scatter.17.cloned.1.call-start = ((), (), s32[]{:S(2)}) async-start(), calls=%async_computation.11 | async-start | bytes 23961600 | tf_op jit(solution)/shard_map/reduce_scatter | solution.py:52
  1125.3 966.7 %all-reduce.17.cloned.1.call-start = ((), (), s32[]{:S(2)}) async-start(), calls=%async_computation.18 | async-start | bytes 188416 | tf_op jit(solution)/shard_map/psum | solution.py:224
  1138.3 1141.2 %all-reduce.19.cloned.1.call-start = ((), (), s32[]{:S(2)}) async-start(), calls=%async_computation.19 | async-start | bytes 15667200 | tf_op jit(solution)/shard_map/psum | solution.py:245
  1937.2 14.8 copy-start.11
  2279.6 3.9 copy-start.12
  2279.6 5.0 copy-start.4
  2284.6 2.9 copy-start.3
  (4 other events, 4.8 us)
Sparse Core Ops, SparseCore 0:
  10.4 177.0 all-gather.8
  198.9 66.3 all-gather.18
  268.0 67.7 all-gather.16
  337.9 80.0 all-gather.10
  420.3 217.6 all-gather.12
  640.2 225.2 all-gather.14
  924.7 78.2 reduce-scatter.20
  1008.1 80.2 reduce-scatter.18
  1092.6 107.1 reduce-scatter.22
  1203.9 185.4 reduce-scatter.14
  1393.6 292.3 reduce-scatter.24
  1689.7 246.7 reduce-scatter.16
  1945.2 146.7 all-reduce.16
  2094.7 184.8 all-reduce.18
where the time goes:
time: 2310 us; the launch traced here: 2300 us
  waiting for transfers between devices  1980 us (86%)
  matrix products  165 us (7%)
  local copies, waits for them, and re-layouts  73.1 us (3%)
  blocking collectives  33.9 us (1%)
  other arithmetic  24.4 us (1%)
    all_gather x4, waiting for transfers between devices, project(): lax.all_gather(weight, 'grp', axis=0, tiled=True)  637 us
    unnamed x18, waiting for transfers between devices  470 us
    reduce_scatter x2, waiting for transfers between devices, weight_grad(): lax.psum_scatter(lax.dot_general(inputs, grads, (((0,), (0,)), ((), ())),...  440 us
    psum x1, waiting for transfers between devices, per_device(): lax.psum(qkv_grad.astype(jnp.bfloat16), 'rep').astype(jnp.float32)  176 us
    psum x1, waiting for transfers between devices, per_device(): lax.psum((small_terms[0], small_terms[1], small_terms[2], small_terms[3],...  139 us
    all_gather x1, waiting for transfers between devices, per_device(): lax.all_gather(key_local, 'grp', axis=1, tiled=True)  63 us
    unnamed x55, local copies, waits for them, and re-layouts  59.7 us
    all_gather x1, waiting for transfers between devices, per_device(): lax.all_gather(value_local, 'grp', axis=1, tiled=True)  59.1 us
  transfers between devices with their start and end apart: 14, of which 14 were waited for; matrix products, arithmetic and copies ran while one was open for 8% of the time, Pallas kernels for 0%

commit v1 on v0

v1 whole, which is shorter than its diff:
```python
import math

import jax
import jax.numpy as jnp
from jax import lax
from jax.experimental import pallas as pl
from jax.experimental.pallas import tpu as pltpu
from jax.sharding import PartitionSpec as P

HEADS = 25
HEAD_DIM = 64
SLOTS = 4
SLOT_WIDTH = SLOTS * HEAD_DIM
STRIDE = 3 * HEAD_DIM
AXES = ("rep", "grp")
BLOCK = 256

bf16 = jnp.bfloat16
f32 = jnp.float32


def linear(x, zl, c, y, zh):
    return ((x * 2 + zl) * 2 + c) * 8 + y * 2 + zh


PLACES = [
    (x, zl, c, y, zh)
    for x in range(4)
    for zl in range(2)
    for c in range(2)
    for y in range(4)
    for zh in range(2)
]


def pairs(where):
    return [(linear(*place), linear(*where(*place))) for place in PLACES]


def z_moved(x, zl, c, y, zh, step):
    z = (zh * 2 + zl - step) % 4
    return (x, z % 2, c, y, z // 2)


X_RING = [pairs(lambda x, zl, c, y, zh, k=k: ((x - k) % 4, zl, c, y, zh)) for k in range(4)]
Y_RING = [pairs(lambda x, zl, c, y, zh, k=k: (x, zl, c, (y - k) % 4, zh)) for k in range(4)]
Z_RING = [pairs(lambda x, zl, c, y, zh, k=k: z_moved(x, zl, c, y, zh, k)) for k in range(4)]
CORE = pairs(lambda x, zl, c, y, zh: (x, zl, 1 - c, y, zh))
Z_LOW = pairs(lambda x, zl, c, y, zh: (x, 1 - zl, c, y, zh))
Z_HIGH = pairs(lambda x, zl, c, y, zh: (x, zl, c, y, 1 - zh))
ROLES = pairs(lambda x, zl, c, y, zh: (x, zl, zh, y, c))
OWNERS = [pairs(lambda x, zl, c, y, zh, i=i: (x, zh ^ i, zl, y, c)) for i in range(2)]


def send(value, perm):
    return lax.ppermute(value, AXES, perm)


def pick(stack, index, axis=0):
    return lax.dynamic_index_in_dim(stack, index, axis, keepdims=False)


def placed(parts, me):
    whole = jnp.zeros((4,) + parts[0].shape, parts[0].dtype)
    for k, part in enumerate(parts):
        whole = lax.dynamic_update_index_in_dim(whole, part, (me + k) % 4, 0)
    return whole


def ring_gather(block, ring, me):
    return placed([block] + [send(block, ring[k]) for k in range(1, 4)], me)


def ring_exchange(stack, ring, me):
    return placed(
        [pick(stack, me)] + [send(pick(stack, (me - k) % 4), ring[k]) for k in range(1, 4)], me
    )


def ring_scatter(stack, ring, me):
    total = pick(stack, me).astype(f32)
    for k in range(1, 4):
        total = total + send(pick(stack, (me - k) % 4), ring[k]).astype(f32)
    return total


def paired(own, other, bit, axis=1):
    return jnp.where(
        bit == 0, jnp.stack([own, other], axis), jnp.stack([other, own], axis)
    )


def norm_parts(value, gain, shift):
    center = value - jnp.mean(value, axis=-1, keepdims=True)
    spread = jnp.mean(center * center, axis=-1, keepdims=True)
    factor = lax.rsqrt(spread + 1e-05)
    normed = center * factor
    return (normed * gain + shift, normed, factor)


def norm_back(grad_value, normed, factor, gain):
    grad_normed = grad_value * gain
    mean_first = jnp.mean(grad_normed, axis=-1, keepdims=True)
    mean_second = jnp.mean(grad_normed * normed, axis=-1, keepdims=True)
    return factor * (grad_normed - mean_first - normed * mean_second)


def gelu_tanh(value):
    return (
        0.5
        * value
        * (1.0 + jnp.tanh(0.7978845608028654 * (value + 0.044715 * value * value * value)))
    )


def dot(left, right):
    return jnp.dot(left, right, preferred_element_type=f32)


def dot_rows(left, right):
    return lax.dot_general(left, right, (((0,), (0,)), ((), ())), preferred_element_type=f32)


def dot_cols(left, right):
    return lax.dot_general(left, right, (((1,), (1,)), ((), ())), preferred_element_type=f32)


def attention_kernel(qkv_ref, out_ref, top_ref):
    length = qkv_ref.shape[0]
    for head in range(SLOTS):
        lanes = slice(head * HEAD_DIM, (head + 1) * HEAD_DIM)
        keys = qkv_ref[:, SLOT_WIDTH + head * HEAD_DIM : SLOT_WIDTH + (head + 1) * HEAD_DIM]
        values = qkv_ref[
            :, 2 * SLOT_WIDTH + head * HEAD_DIM : 2 * SLOT_WIDTH + (head + 1) * HEAD_DIM
        ]
        for block in range(length // BLOCK):
            rows = slice(block * BLOCK, (block + 1) * BLOCK)
            width = (block + 1) * BLOCK
            query = qkv_ref[rows, lanes] * bf16(1.0 / math.sqrt(HEAD_DIM))
            scores = dot_cols(query, keys[:width])
            row = lax.broadcasted_iota(jnp.int32, (BLOCK, width), 0) + block * BLOCK
            col = lax.broadcasted_iota(jnp.int32, (BLOCK, width), 1)
            scores = jnp.where(col <= row, scores, -1e30)
            top = jnp.max(scores, axis=-1, keepdims=True)
            probs = jnp.exp(scores - top)
            total = jnp.sum(probs, axis=-1, keepdims=True)
            mixed = dot(probs.astype(bf16), values[:width])
            out_ref[rows, lanes] = (mixed / total).astype(bf16)
            top_ref[rows, head : head + 1] = top + jnp.log(total)


def attention(qkv):
    length = qkv.shape[0]
    return pl.pallas_call(
        attention_kernel,
        out_shape=(
            jax.ShapeDtypeStruct((length, SLOT_WIDTH), bf16),
            jax.ShapeDtypeStruct((length, SLOTS), f32),
        ),
        in_specs=[pl.BlockSpec(memory_space=pltpu.VMEM)],
        out_specs=(
            pl.BlockSpec(memory_space=pltpu.VMEM),
            pl.BlockSpec(memory_space=pltpu.VMEM),
        ),
        compiler_params=pltpu.CompilerParams(vmem_limit_bytes=48 * 2**20),
        name="attention",
    )(qkv)


def attention_back_kernel(qkv_ref, grad_ref, top_ref, delta_ref, out_ref, query_ref):
    length = qkv_ref.shape[0]
    scale = 1.0 / math.sqrt(HEAD_DIM)
    for head in range(SLOTS):
        base = head * HEAD_DIM
        lanes = slice(base, base + HEAD_DIM)
        key_lanes = slice(SLOT_WIDTH + base, SLOT_WIDTH + base + HEAD_DIM)
        value_lanes = slice(2 * SLOT_WIDTH + base, 2 * SLOT_WIDTH + base + HEAD_DIM)
        query = qkv_ref[:, lanes] * bf16(scale)
        grad = grad_ref[:, lanes]
        top = top_ref[head : head + 1, :]
        delta = delta_ref[head : head + 1, :]
        for block in range(length // BLOCK):
            start = block * BLOCK
            rows = slice(start, start + BLOCK)
            width = length - start
            keys = qkv_ref[rows, key_lanes]
            values = qkv_ref[rows, value_lanes]
            scores = dot_cols(keys, query[start:])
            row = lax.broadcasted_iota(jnp.int32, (BLOCK, width), 0)
            col = lax.broadcasted_iota(jnp.int32, (BLOCK, width), 1)
            probs = jnp.where(row <= col, jnp.exp(scores - top[:, start:]), 0.0)
            grad_probs = dot_cols(values, grad[start:])
            grad_scores = (probs * (grad_probs - delta[:, start:])).astype(bf16)
            out_ref[rows, value_lanes] = dot(probs.astype(bf16), grad[start:]).astype(bf16)
            out_ref[rows, key_lanes] = dot(grad_scores, query[start:]).astype(bf16)
            term = dot_rows(grad_scores, keys)
            if block == 0:
                query_ref[...] = term
            else:
                query_ref[start:, :] += term
        out_ref[:, lanes] = (query_ref[...] * scale).astype(bf16)


def attention_back(qkv, grad, top, delta):
    return pl.pallas_call(
        attention_back_kernel,
        out_shape=jax.ShapeDtypeStruct(qkv.shape, bf16),
        in_specs=[pl.BlockSpec(memory_space=pltpu.VMEM)] * 4,
        out_specs=pl.BlockSpec(memory_space=pltpu.VMEM),
        scratch_shapes=[pltpu.VMEM((qkv.shape[0], HEAD_DIM), f32)],
        compiler_params=pltpu.CompilerParams(vmem_limit_bytes=48 * 2**20),
        name="attention_back",
    )(qkv, grad, top, delta)


def per_device(
    tokens,
    ln1_gain,
    ln1_bias,
    w_qkv,
    bias_q,
    bias_v,
    w_out,
    bias_out,
    ln2_gain,
    ln2_bias,
    w_fc,
    bias_fc,
    w_proj,
    bias_proj,
    cotangent,
):
    _, span, width = tokens.shape
    shard = width // 8
    hidden = w_fc.shape[1] // 8
    length = span * 8
    rep = lax.axis_index("rep")
    grp = lax.axis_index("grp")
    x, zl, c = rep // 4, (rep // 2) % 2, rep % 2
    y, zh = grp // 2, grp % 2
    z = zh * 2 + zl
    rank = y * 2 + c

    def group_gather(block):
        own = ring_gather(block, Y_RING, y)
        return paired(own, send(own, CORE), c)

    def group_scatter(parts):
        parts = parts.astype(bf16).reshape((4, 2, span) + parts.shape[1:])
        got = send(pick(parts, 1 - c, 1), CORE)
        both = pick(parts, c, 1).astype(f32) + got.astype(f32)
        low = both.astype(bf16)
        total = pick(both, y)
        for k in range(1, 4):
            total = total + send(pick(low, (y - k) % 4), Y_RING[k]).astype(f32)
        return total

    def to_tokens(parts):
        parts = parts.reshape(4, 2 * span, -1)
        own = ring_exchange(parts, Y_RING, y).reshape(4, 2, span, -1)
        got = send(pick(own, 1 - c, 1), CORE)
        return paired(pick(own, c, 1), got, c)

    def from_tokens(parts):
        got = send(pick(parts, 1 - c, 1), CORE)
        both = paired(pick(parts, c, 1), got, c)
        return ring_exchange(both, Y_RING, y).reshape(length, -1)

    def columns(parts):
        own = ring_exchange(pick(parts, c, 1), Y_RING, y)
        other = send(own, Z_HIGH)
        return paired(own, other, zh).reshape(8 * shard, -1)

    own_tokens = send(tokens.reshape(span, width), ROLES)
    small = jnp.concatenate(
        [ln1_gain, ln1_bias, bias_q, bias_v, bias_out, ln2_gain, ln2_bias, bias_proj]
    ).reshape(2, 4 * shard)
    small = jnp.concatenate([small, bias_fc.reshape(1, hidden)], axis=0)
    small = send(small, ROLES)
    hidden_bias = small[2].astype(f32)
    small_all = group_gather(small).reshape(8, 3, 4 * shard)
    vectors = small_all[:, :2].reshape(8, 8, shard).transpose(1, 0, 2).reshape(8, width)
    vectors = vectors.astype(f32)
    gain_first, shift_first, query_bias, value_bias = [vectors[i] for i in range(4)]
    output_bias, gain_second, shift_second, down_bias = [vectors[i] for i in range(4, 8)]

    all_tokens = group_gather(own_tokens).reshape(length, width)
    slots = [
        [w_qkv[:, p * width + STRIDE * r : p * width + STRIDE * r + SLOT_WIDTH] for p in range(3)]
        for r in range(8)
    ]
    slots = jnp.stack([jnp.concatenate(s, axis=1) for s in slots])
    qkv_cols = columns(slots.reshape(4, 2, shard, 3 * SLOT_WIDTH))
    own_cot = send(cotangent.reshape(span, width), ROLES)
    all_cot = group_gather(own_cot).reshape(length, width)
    out_rows = send(w_out, ROLES)
    out_all = group_gather(out_rows).reshape(width, width)
    fc_cols = columns(w_fc.reshape(shard, 4, 2, hidden).transpose(1, 2, 0, 3))
    proj_rows = send(w_proj, ROLES)

    inputs = own_tokens.astype(f32)
    _, normed_first, factor_first = norm_parts(inputs, gain_first, shift_first)
    first = norm_parts(all_tokens.astype(f32), gain_first, shift_first)[0].astype(bf16)
    zeros = jnp.zeros((SLOT_WIDTH,), f32)
    bias_slots = jnp.concatenate(
        [
            lax.dynamic_slice_in_dim(query_bias, STRIDE * rank, SLOT_WIDTH),
            zeros,
            lax.dynamic_slice_in_dim(value_bias, STRIDE * rank, SLOT_WIDTH),
        ]
    )
    qkv = (dot(first, qkv_cols) + bias_slots).astype(bf16)
    attended_slots, top = attention(qkv)
    attended = to_tokens(attended_slots).reshape(8, span, SLOT_WIDTH)
    attended = jnp.concatenate(
        [attended[r, :, : STRIDE if r < 7 else SLOT_WIDTH] for r in range(8)], axis=1
    )

    middle = inputs + (dot(attended, out_all) + output_bias)
    second, normed_second, factor_second = norm_parts(middle, gain_second, shift_second)
    second_all = group_gather(second.astype(bf16)).reshape(length, width)
    grad_active = dot_cols(all_cot, proj_rows)
    hidden_pre = dot(second_all, fc_cols) + hidden_bias
    active, gelu_pull = jax.vjp(gelu_tanh, hidden_pre)
    active_low = active.astype(bf16)
    grad_hidden = gelu_pull(grad_active)[0].astype(bf16)
    grad_second = group_scatter(dot_cols(grad_hidden, fc_cols))
    output = middle + (group_scatter(dot(active_low, proj_rows)) + down_bias)
    proj_grad = dot_rows(active_low, all_cot).astype(bf16)
    fc_grad = dot_rows(second_all, grad_hidden).astype(bf16)

    grad_middle = own_cot.astype(f32) + norm_back(
        grad_second, normed_second, factor_second, gain_second
    )
    grad_branch = grad_middle.astype(bf16)

    grad_attended = dot_cols(grad_branch, out_all).astype(bf16)
    grad_slots = jnp.stack(
        [grad_attended[:, STRIDE * r : STRIDE * r + SLOT_WIDTH] for r in range(8)]
    ).reshape(4, 2, span, SLOT_WIDTH)
    grad_heads = from_tokens(grad_slots)
    lane = lax.broadcasted_iota(jnp.int32, (1, SLOT_WIDTH), 1)
    grad_heads = jnp.where((lane < STRIDE) | (rank == 7), grad_heads, jnp.zeros_like(grad_heads))
    delta = jnp.sum(
        (grad_heads.astype(f32) * attended_slots.astype(f32)).reshape(length, SLOTS, HEAD_DIM),
        axis=-1,
    )
    grad_mixed = attention_back(qkv, grad_heads, top.T, delta.T)
    grad_first = group_scatter(dot_cols(grad_mixed, qkv_cols))
    qkv_grad = dot_rows(first, grad_mixed).astype(bf16)
    grad_inputs = grad_middle + norm_back(grad_first, normed_first, factor_first, gain_first)

    branch_all = group_gather(grad_branch).reshape(length, width)
    attended_own = from_tokens(
        attended.reshape(span, 4, 2, shard).transpose(1, 2, 0, 3)
    )
    out_grad = dot_rows(attended_own, branch_all).astype(bf16)

    def row_total(parts):
        total = ring_scatter(parts, X_RING, x).astype(bf16)
        total = ring_scatter(total, Z_RING, z).astype(bf16)
        two = paired(send(total, OWNERS[0]), send(total, OWNERS[1]), zl, 0)
        whole = ring_gather(two, X_RING, x)
        return paired(whole, send(whole, CORE), c, 2)

    def column_total(grad):
        count = grad.shape[1]
        total = ring_scatter(grad.reshape(4, 2 * shard, count), X_RING, x).astype(bf16)
        total = ring_scatter(total.reshape(4, shard // 2, count), Z_RING, z).astype(bf16)
        spread = ring_gather(total, X_RING, x)
        spread = ring_exchange(spread, Y_RING, y)
        spread = paired(spread, send(spread, Z_LOW), zl)
        spread = paired(spread, send(spread, CORE), c)
        return spread.reshape(8, shard, count).transpose(1, 0, 2)

    proj_total = row_total(proj_grad.reshape(4, 4, hidden // 16, width))
    proj_total = proj_total.reshape(hidden, width).astype(f32)
    fc_total = column_total(fc_grad).reshape(shard, 8 * hidden).astype(f32)
    out_parts = out_grad.reshape(4, shard // 4, 4, width // 4).transpose(0, 2, 1, 3)
    out_total = row_total(out_parts).reshape(4, 4, shard // 4, width // 4)
    out_total = out_total.transpose(0, 2, 1, 3).reshape(shard, width).astype(f32)
    qkv_parts = column_total(qkv_grad)
    qkv_total = jnp.concatenate(
        [
            qkv_parts[:, r, p * SLOT_WIDTH : p * SLOT_WIDTH + (STRIDE if r < 7 else SLOT_WIDTH)]
            for p in range(3)
            for r in range(8)
        ],
        axis=1,
    ).astype(f32)

    bias_sums = jnp.sum(grad_mixed.astype(f32), axis=0)
    blank = jnp.zeros((width,), f32)
    small_terms = [
        jnp.sum(grad_first * normed_first, axis=0),
        jnp.sum(grad_first, axis=0),
        lax.dynamic_update_slice_in_dim(blank, bias_sums[:SLOT_WIDTH], STRIDE * rank, 0),
        lax.dynamic_update_slice_in_dim(blank, bias_sums[2 * SLOT_WIDTH :], STRIDE * rank, 0),
        jnp.sum(grad_branch.astype(f32), axis=0),
        jnp.sum(grad_second * normed_second, axis=0),
        jnp.sum(grad_second, axis=0),
        jnp.sum(own_cot.astype(f32), axis=0),
        lax.dynamic_update_slice_in_dim(
            jnp.zeros((8 * hidden,), f32),
            jnp.sum(grad_hidden.astype(f32), axis=0),
            hidden * rank,
            0,
        ),
    ]
    small_sum = jnp.concatenate(small_terms).reshape(24, 4 * shard)
    small_sum = small_sum + send(small_sum, CORE)
    for ring, me in ((Y_RING, y), (X_RING, x), (Z_RING, z)):
        small_sum = jnp.sum(ring_gather(small_sum, ring, me), axis=0)
    small_sum = small_sum.reshape(-1)
    owned = [
        lax.dynamic_slice_in_dim(small_sum, width * i + shard * grp, shard) for i in range(8)
    ]
    owned_hidden = lax.dynamic_slice_in_dim(small_sum, width * 8 + hidden * grp, hidden)

    output_home = send(output.astype(bf16), ROLES).reshape(1, span, width)
    inputs_home = send(grad_inputs.astype(bf16), ROLES).astype(f32).reshape(1, span, width)
    return (
        output_home,
        inputs_home,
        owned[0],
        owned[1],
        qkv_total,
        owned[2],
        owned[3],
        out_total,
        owned[4],
        owned[5],
        owned[6],
        fc_total,
        owned_hidden,
        proj_total,
        owned[7],
    )


def solution(mesh):
    in_specs = (
        P("rep", "grp", None),
        P("grp"),
        P("grp"),
        P("grp", None),
        P("grp"),
        P("grp"),
        P("grp", None),
        P("grp"),
        P("grp"),
        P("grp"),
        P("grp", None),
        P("grp"),
        P("grp", None),
        P("grp"),
        P("rep", "grp", None),
    )
    out_specs = (
        P("rep", "grp", None),
        P("rep", "grp", None),
        P("grp"),
        P("grp"),
        P("grp", None),
        P("grp"),
        P("grp"),
        P("grp", None),
        P("grp"),
        P("grp"),
        P("grp"),
        P("grp", None),
        P("grp"),
        P("grp", None),
        P("grp"),
    )
    return jax.shard_map(
        per_device, mesh=mesh, in_specs=in_specs, out_specs=out_specs, check_vma=False
    )
```

time: 2310 us -> 894 us (0.39)
  the two profiles are of different devices: /device:TPU:17 before, /device:TPU:0 now
where the time goes in v1:
time: 894 us; the launch traced here: 877 us
  local copies, waits for them, and re-layouts  305 us (34%)
  waiting for transfers between devices  216 us (24%)
  starting transfers between devices  195 us (22%)
  other arithmetic  85.9 us (10%)
  matrix products  57.5 us (6%)
  Pallas kernels  14.5 us (2%)
    ppermute x125, waiting for transfers between devices, send(): return lax.ppermute(value, AXES, perm)  216 us
    ppermute x125, starting transfers between devices, send(): return lax.ppermute(value, AXES, perm)  195 us
    dynamic_update_slice x73, local copies, waits for them, and re-layouts, placed(): whole = lax.dynamic_update_index_in_dim(whole, part, (me + k) % 4, 0)  97.5 us
    dynamic_slice x13, local copies, waits for them, and re-layouts, pick(): return lax.dynamic_index_in_dim(stack, index, axis, keepdims=False)  35.9 us
    select_n x19, other arithmetic, paired(): jnp.where(bit == 0, jnp.stack([own, other], axis), jnp.stack([other, own]...  28.8 us
    reshape x3, local copies, waits for them, and re-layouts, group_scatter(): parts = parts.astype(bf16).reshape((4, 2, span) + parts.shape[1:])  24.4 us
    dot_general x4, matrix products, dot(): return jnp.dot(left, right, preferred_element_type=f32)  23 us
    convert_element_type x4, local copies, waits for them, and re-layouts, per_device(): fc_total = column_total(fc_grad).reshape(shard, 8 * hidden).astype(f32)  22.3 us
  transfers between devices with their start and end apart: 125, of which 57 were waited for; matrix products, arithmetic and copies ran while one was open for 46% of the time, Pallas kernels for 2%

profile of v1, /device:TPU:0, one launch (start us, length us, event | category | flops | bytes accessed | tf_op | source)
XLA Modules:
  0.0 877.5 jit_solution(8325789695372643260)
XLA Ops:
  68.3 21.4 %collective-permute-start.31 = (bf16[800,1600]{1,0:T(8,128)(2,1)}, bf16[800,1600]{1,0:T(8,128)(2,1)}, u32[]{:S(2)}, u32[]{:S(2)}) collective-permute-start(bf16[800,1600]{1,0:T(8,128)(2,1)} %param.27), channel_id=1, source_target_pairs={{0,0},{1,8},{2,2},{3,10},{4,4},{5,12},{6,6},{7,14},{8,1},{9,9},{10... | collective-permute-start | bytes 7680008 | tf_op jit(solution)/shard_map/ppermute | solution.py:56
  121.2 11.4 %collective-permute-done.38 = bf16[128,1600]{0,1:T(8,128)(2,1)S(1)} collective-permute-done((bf16[128,1600]{0,1:T(8,128)(2,1)S(1)}, bf16[128,1600]{0,1:T(8,128)(2,1)S(1)}, u32[]{:S(2)}, u32[]{:S(2)}) %collective-permute-start.38) | collective-permute-done | bytes 409632 | tf_op jit(solution)/shard_map/ppermute | solution.py:56
  140.7 24.4 %collective-permute-done.19 = bf16[200,1600]{1,0:T(8,128)(2,1)S(1)} collective-permute-done((bf16[200,1600]{1,0:T(8,128)(2,1)}, bf16[200,1600]{1,0:T(8,128)(2,1)S(1)}, u32[]{:S(2)}, u32[]{:S(2)}) %collective-permute-start.19) | collective-permute-done | bytes 640032 | tf_op jit(solution)/shard_map/ppermute | solution.py:56
  165.1 8.8 collective-permute-start.30
  246.5 7.4 copy.671
  257.4 10.7 %collective-permute-done.24 = bf16[128,1600]{0,1:T(8,128)(2,1)S(1)} collective-permute-done((bf16[128,1600]{0,1:T(8,128)(2,1)}, bf16[128,1600]{0,1:T(8,128)(2,1)S(1)}, u32[]{:S(2)}, u32[]{:S(2)}) %collective-permute-start.24) | collective-permute-done | bytes 409632 | tf_op jit(solution)/shard_map/ppermute | solution.py:56
  268.8 7.2 collective-permute-done.25
  324.8 6.8 convert_reduce_fusion.1
  366.6 8.5 reshape.701
  375.1 8.7 convolution_convert_fusion.2
  383.9 8.5 reshape.698
  392.4 9.5 %collective-permute-done.100 = bf16[400,800]{1,0:T(8,128)(2,1)} collective-permute-done((bf16[400,800]{1,0:T(8,128)(2,1)}, bf16[400,800]{1,0:T(8,128)(2,1)}, u32[]{:S(2)}, u32[]{:S(2)}) %collective-permute-start.100) | collective-permute-done | bytes 640032 | tf_op jit(solution)/shard_map/ppermute | solution.py:56
  401.9 17.1 %constant_dynamic-slice_fusion.11 = (bf16[4,1,128,1600]{2,1,0,3:T(2,128)(2,1)}, bf16[4,1,128,1600]{2,1,0,3:T(2,128)(2,1)S(1)}, bf16[4,1,128,1600]{2,1,0,3:T(2,128)(2,1)S(1)}, bf16[4,1,128,1600]{2,1,0,3:T(2,128)(2,1)}) fusion(bf16[4,2,128,1600]{2,1,0,3:T(2,128)(2,1)} %reshape.701, s32[]{:T(128)S(6)} %select_n.906, s32[]{:T(128)S(6)} %select_n.920, ...), kind=kLoop, calls=%fused_computation.358 | loop fusion | bytes 13107208 | tf_op jit(solution)/shard_map/jit(dynamic_index_in_dim)/dynamic_slice | solution.py:60
  482.4 7.8 collective-permute-done.110
  521.4 12.2 %dynamic_update_slice.341 = bf16[4,2,50,1600]{3,0,2,1:T(4,128)(2,1)} dynamic-update-slice(bf16[4,2,50,1600]{3,0,2,1:T(4,128)(2,1)} %broadcast_in_dim.375, bf16[1,2,50,1600]{3,0,2,1:T(2,128)(2,1)} %copy.713, s32[]{:T(128)S(6)} %select_n.938, s32[]{:T(128)} %constant.996.clone.1, s32[]{:T(128)} %constant.996.clone.1, s32[]{:T(128)} %constant.996.clone.1) | dynamic-update-slice | bytes 640004 | tf_op jit(solution)/shard_map/jit(dynamic_update_index_in_dim)/dynamic_update_slice | solution.py:66
  539.7 12.2 %dynamic_update_slice.342 = bf16[4,2,50,1600]{3,0,2,1:T(4,128)(2,1)} dynamic-update-slice(bf16[4,2,50,1600]{3,0,2,1:T(4,128)(2,1)} %dynamic_update_slice.341, bf16[1,2,50,1600]{3,0,2,1:T(2,128)(2,1)} %copy.714, s32[]{:T(128)S(6)} %select_n.940, s32[]{:T(128)} %constant.996.clone.1, s32[]{:T(128)} %constant.996.clone.1, s32[]{:T(128)} %constant.996.clone.1) | dynamic-update-slice | bytes 640004 | tf_op jit(solution)/shard_map/jit(dynamic_update_index_in_dim)/dynamic_update_slice | solution.py:66
  551.9 12.2 %dynamic_update_slice.343 = bf16[4,2,50,1600]{3,0,2,1:T(4,128)(2,1)} dynamic-update-slice(bf16[4,2,50,1600]{3,0,2,1:T(4,128)(2,1)} %dynamic_update_slice.342, bf16[1,2,50,1600]{3,0,2,1:T(2,128)(2,1)} %copy.715, s32[]{:T(128)S(6)} %select_n.942, s32[]{:T(128)} %constant.996.clone.1, s32[]{:T(128)} %constant.996.clone.1, s32[]{:T(128)} %constant.996.clone.1) | dynamic-update-slice | bytes 640004 | tf_op jit(solution)/shard_map/jit(dynamic_update_index_in_dim)/dynamic_update_slice | solution.py:66
  564.1 12.2 %dynamic_update_slice.344 = bf16[4,2,50,1600]{3,0,2,1:T(4,128)(2,1)} dynamic-update-slice(bf16[4,2,50,1600]{3,0,2,1:T(4,128)(2,1)} %dynamic_update_slice.343, bf16[1,2,50,1600]{3,0,2,1:T(2,128)(2,1)} %copy.716, s32[]{:T(128)S(6)} %select_n.944, s32[]{:T(128)} %constant.996.clone.1, s32[]{:T(128)} %constant.996.clone.1, s32[]{:T(128)} %constant.996.clone.1) | dynamic-update-slice | bytes 640004 | tf_op jit(solution)/shard_map/jit(dynamic_update_index_in_dim)/dynamic_update_slice | solution.py:66
  602.4 18.3 %collective-permute-done.47 = bf16[2,128,256]{2,1,0:T(8,128)(2,1)S(1)} collective-permute-done((bf16[2,128,256]{2,1,0:T(8,128)(2,1)S(1)}, bf16[2,128,256]{2,1,0:T(8,128)(2,1)S(1)}, u32[]{:S(2)}, u32[]{:S(2)}) %collective-permute-start.47) | collective-permute-done | bytes 131104 | tf_op jit(solution)/shard_map/ppermute | solution.py:56
  632.5 7.8 attention_back.1
  653.2 7.4 reshape.705
  660.6 7.7 constant_dynamic-slice_fusion.7
  674.3 10.4 %collective-permute-done.67 = bf16[400,768]{1,0:T(8,128)(2,1)S(1)} collective-permute-done((bf16[400,768]{1,0:T(8,128)(2,1)S(1)}, bf16[400,768]{1,0:T(8,128)(2,1)S(1)}, u32[]{:S(2)}, u32[]{:S(2)}) %collective-permute-start.67) | collective-permute-done | bytes 614432 | tf_op jit(solution)/shard_map/ppermute | solution.py:56
  742.3 7.4 reshape.731
  (674 shorter events, 608.0 us)
Async XLA Ops:
  10.3 80.9 %collective-permute-start = (bf16[128,1600]{0,1:T(8,128)(2,1)}, bf16[128,1600]{0,1:T(8,128)(2,1)S(1)}, u32[]{:S(2)}, u32[]{:S(2)}) collective-permute-start(bf16[128,1600]{0,1:T(8,128)(2,1)} %bitcast), channel_id=1, source_target_pairs={{0,0},{1,8},{2,2},{3,10},{4,4},{5,12},{6,6},{7,14},{8,1},{9,9},{10... | collective-permute-start | bytes 1228808 | tf_op jit(solution)/shard_map/ppermute | solution.py:56
  45.6 55.8 %collective-permute-start.18 = (bf16[200,1600]{1,0:T(8,128)(2,1)}, bf16[200,1600]{1,0:T(8,128)(2,1)}, u32[]{:S(2)}, u32[]{:S(2)}) collective-permute-start(bf16[200,1600]{1,0:T(8,128)(2,1)} %param.21), channel_id=1, source_target_pairs={{0,0},{1,8},{2,2},{3,10},{4,4},{5,12},{6,6},{7,14},{8,1},{9,9},{10... | collective-permute-start | bytes 1920008 | tf_op jit(solution)/shard_map/ppermute | solution.py:56
  68.3 256.5 %collective-permute-start.31 = (bf16[800,1600]{1,0:T(8,128)(2,1)}, bf16[800,1600]{1,0:T(8,128)(2,1)}, u32[]{:S(2)}, u32[]{:S(2)}) collective-permute-start(bf16[800,1600]{1,0:T(8,128)(2,1)} %param.27), channel_id=1, source_target_pairs={{0,0},{1,8},{2,2},{3,10},{4,4},{5,12},{6,6},{7,14},{8,1},{9,9},{10... | collective-permute-start | bytes 7680008 | tf_op jit(solution)/shard_map/ppermute | solution.py:56
  90.5 85.1 %collective-permute-start.13 = (bf16[4,200,768]{2,1,0:T(8,128)(2,1)S(1)}, bf16[4,200,768]{2,1,0:T(8,128)(2,1)S(1)}, u32[]{:S(2)}, u32[]{:S(2)}) collective-permute-start(bf16[4,200,768]{2,1,0:T(8,128)(2,1)S(1)} %bitcast_dynamic-update-slice_fusion.24), channel_id=1, source_target_pairs={{0,1},{1,0},{2,3},{3,2},{4,5},{5,4},{6,7},{7,6},{8,9},{9,8},{10,11... | collective-permute-start | bytes 3686408 | tf_op jit(solution)/shard_map/ppermute | solution.py:56
  165.1 53.6 %collective-permute-start.30 = (bf16[4,200,800]{2,1,0:T(8,128)(2,1)}, bf16[4,200,800]{2,1,0:T(8,128)(2,1)}, u32[]{:S(2)}, u32[]{:S(2)}) collective-permute-start(bf16[4,200,800]{2,1,0:T(8,128)(2,1)} %bitcast_dynamic-update-slice_fusion.21), channel_id=1, source_target_pairs={{0,1},{1,0},{2,3},{3,2},{4,5},{5,4},{6,7},{7,6},{8,9},{9,8},{10,11... | collective-permute-start | bytes 3840008 | tf_op jit(solution)/shard_map/ppermute | solution.py:56
  175.6 107.4 %collective-permute-start.41 = (bf16[4,128,1600]{1,2,0:T(8,128)(2,1)}, bf16[4,128,1600]{1,2,0:T(8,128)(2,1)}, u32[]{:S(2)}, u32[]{:S(2)}) collective-permute-start(bf16[4,128,1600]{1,2,0:T(8,128)(2,1)} %bitcast_dynamic-update-slice_fusion.8), channel_id=1, source_target_pairs={{0,8},{1,9},{2,10},{3,11},{4,12},{5,13},{6,14},{7,15},{8,0},{9,1},... | collective-permute-start | bytes 4915208 | tf_op jit(solution)/shard_map/ppermute | solution.py:56
  348.5 80.8 %collective-permute-start.113 = (bf16[4,50,1600]{2,0,1:T(4,128)(2,1)}, bf16[4,50,1600]{2,0,1:T(4,128)(2,1)}, u32[]{:S(2)}, u32[]{:S(2)}) collective-permute-start(bf16[4,50,1600]{2,0,1:T(4,128)(2,1)} %bitcast.639), channel_id=1, source_target_pairs={{0,96},{1,97},{2,98},{3,99},{4,100},{5,101},{6,102},{7,103},{8,104... | collective-permute-start | bytes 1920008 | tf_op jit(solution)/shard_map/ppermute | solution.py:56
  352.5 77.1 %collective-permute-start.114 = (bf16[4,50,1600]{2,0,1:T(4,128)(2,1)}, bf16[4,50,1600]{2,0,1:T(4,128)(2,1)}, u32[]{:S(2)}, u32[]{:S(2)}) collective-permute-start(bf16[4,50,1600]{2,0,1:T(4,128)(2,1)} %bitcast.638), channel_id=1, source_target_pairs={{0,64},{1,65},{2,66},{3,67},{4,68},{5,69},{6,70},{7,71},{8,72},{9,... | collective-permute-start | bytes 1920008 | tf_op jit(solution)/shard_map/ppermute | solution.py:56
  354.4 78.0 %collective-permute-start.115 = (bf16[4,50,1600]{2,0,1:T(4,128)(2,1)}, bf16[4,50,1600]{2,0,1:T(4,128)(2,1)}, u32[]{:S(2)}, u32[]{:S(2)}) collective-permute-start(bf16[4,50,1600]{2,0,1:T(4,128)(2,1)} %bitcast.637), channel_id=1, source_target_pairs={{0,32},{1,33},{2,34},{3,35},{4,36},{5,37},{6,38},{7,39},{8,40},{9,... | collective-permute-start | bytes 1920008 | tf_op jit(solution)/shard_map/ppermute | solution.py:56
  365.3 56.6 %collective-permute-start.101 = (bf16[400,800]{1,0:T(8,128)(2,1)}, bf16[400,800]{1,0:T(8,128)(2,1)}, u32[]{:S(2)}, u32[]{:S(2)}) collective-permute-start(bf16[400,800]{1,0:T(8,128)(2,1)} %get-tuple-element.67), channel_id=1, source_target_pairs={{0,32},{1,33},{2,34},{3,35},{4,36},{5,37},{6,38},{7,39},{8,40},{9,... | collective-permute-start | bytes 1920008 | tf_op jit(solution)/shard_map/ppermute | solution.py:56
  421.9 76.1 %collective-permute-start.82 = (bf16[2,128,200]{1,2,0:T(8,128)(2,1)}, bf16[2,128,200]{1,2,0:T(8,128)(2,1)S(1)}, u32[]{:S(2)}, u32[]{:S(2)}) collective-permute-start(bf16[2,128,200]{1,2,0:T(8,128)(2,1)} %get-tuple-element.173), channel_id=1, source_target_pairs={{0,2},{1,3},{2,4},{3,5},{4,6},{5,7},{6,0},{7,1},{8,10},{9,11},{10,... | collective-permute-start | bytes 307208 | tf_op jit(solution)/shard_map/ppermute | solution.py:56
  423.3 69.4 %collective-permute-start.32 = (bf16[4,128,1600]{1,2,0:T(8,128)(2,1)}, bf16[4,128,1600]{1,2,0:T(8,128)(2,1)}, u32[]{:S(2)}, u32[]{:S(2)}) collective-permute-start(bf16[4,128,1600]{1,2,0:T(8,128)(2,1)} %bitcast.634), channel_id=1, source_target_pairs={{0,8},{1,9},{2,10},{3,11},{4,12},{5,13},{6,14},{7,15},{8,0},{9,1},... | collective-permute-start | bytes 4915208 | tf_op jit(solution)/shard_map/ppermute | solution.py:56
  446.9 54.5 %collective-permute-start.42 = (bf16[4,128,1600]{1,2,0:T(8,128)(2,1)S(1)}, bf16[4,128,1600]{1,2,0:T(8,128)(2,1)S(1)}, u32[]{:S(2)}, u32[]{:S(2)}) collective-permute-start(bf16[4,128,1600]{1,2,0:T(8,128)(2,1)S(1)} %bitcast.701), channel_id=1, source_target_pairs={{0,8},{1,9},{2,10},{3,11},{4,12},{5,13},{6,14},{7,15},{8,0},{9,1},... | collective-permute-start | bytes 4915208 | tf_op jit(solution)/shard_map/ppermute | solution.py:56
  506.4 71.9 %collective-permute-start.34 = (bf16[128,1600]{0,1:T(8,128)(2,1)}, bf16[128,1600]{0,1:T(8,128)(2,1)}, u32[]{:S(2)}, u32[]{:S(2)}) collective-permute-start(bf16[128,1600]{0,1:T(8,128)(2,1)} %get-tuple-element.135), channel_id=1, source_target_pairs={{0,4},{1,5},{2,6},{3,7},{4,0},{5,1},{6,2},{7,3},{8,12},{9,13},{10,... | collective-permute-start | bytes 1228808 | tf_op jit(solution)/shard_map/ppermute | solution.py:56
  506.8 71.6 %collective-permute-start.35 = (bf16[128,1600]{0,1:T(8,128)(2,1)}, bf16[128,1600]{0,1:T(8,128)(2,1)}, u32[]{:S(2)}, u32[]{:S(2)}) collective-permute-start(bf16[128,1600]{0,1:T(8,128)(2,1)} %get-tuple-element.134), channel_id=1, source_target_pairs={{0,2},{1,3},{2,4},{3,5},{4,6},{5,7},{6,0},{7,1},{8,10},{9,11},{10,... | collective-permute-start | bytes 1228808 | tf_op jit(solution)/shard_map/ppermute | solution.py:56
  510.5 67.9 %collective-permute-start.43 = (bf16[128,1600]{0,1:T(8,128)(2,1)}, bf16[128,1600]{0,1:T(8,128)(2,1)}, u32[]{:S(2)}, u32[]{:S(2)}) collective-permute-start(bf16[128,1600]{0,1:T(8,128)(2,1)} %get-tuple-element.130), channel_id=1, source_target_pairs={{0,6},{1,7},{2,0},{3,1},{4,2},{5,3},{6,4},{7,5},{8,14},{9,15},{10,... | collective-permute-start | bytes 1228808 | tf_op jit(solution)/shard_map/ppermute | solution.py:56
  515.4 63.0 %collective-permute-start.44 = (bf16[128,1600]{0,1:T(8,128)(2,1)}, bf16[128,1600]{0,1:T(8,128)(2,1)}, u32[]{:S(2)}, u32[]{:S(2)}) collective-permute-start(bf16[128,1600]{0,1:T(8,128)(2,1)} %get-tuple-element.132), channel_id=1, source_target_pairs={{0,4},{1,5},{2,6},{3,7},{4,0},{5,1},{6,2},{7,3},{8,12},{9,13},{10,... | collective-permute-start | bytes 1228808 | tf_op jit(solution)/shard_map/ppermute | solution.py:56
  517.1 61.3 %collective-permute-start.45 = (bf16[128,1600]{0,1:T(8,128)(2,1)}, bf16[128,1600]{0,1:T(8,128)(2,1)}, u32[]{:S(2)}, u32[]{:S(2)}) collective-permute-start(bf16[128,1600]{0,1:T(8,128)(2,1)} %get-tuple-element.131), channel_id=1, source_target_pairs={{0,2},{1,3},{2,4},{3,5},{4,6},{5,7},{6,0},{7,1},{8,10},{9,11},{10,... | collective-permute-start | bytes 1228808 | tf_op jit(solution)/shard_map/ppermute | solution.py:56
  578.4 122.5 %collective-permute-start.124 = (bf16[4,2,50,1600]{3,0,2,1:T(4,128)(2,1)}, bf16[4,2,50,1600]{3,0,2,1:T(4,128)(2,1)}, u32[]{:S(2)}, u32[]{:S(2)}) collective-permute-start(bf16[4,2,50,1600]{3,0,2,1:T(4,128)(2,1)} %dynamic_update_slice.344), channel_id=1, source_target_pairs={{0,8},{1,9},{2,10},{3,11},{4,12},{5,13},{6,14},{7,15},{8,0},{9,1},... | collective-permute-start | bytes 3840008 | tf_op jit(solution)/shard_map/ppermute | solution.py:56
  594.5 75.5 %collective-permute-start.83 = (bf16[128,1600]{0,1:T(8,128)(2,1)}, bf16[128,1600]{0,1:T(8,128)(2,1)}, u32[]{:S(2)}, u32[]{:S(2)}) collective-permute-start(bf16[128,1600]{0,1:T(8,128)(2,1)} %get-tuple-element.38), channel_id=1, source_target_pairs={{0,6},{1,7},{2,0},{3,1},{4,2},{5,3},{6,4},{7,5},{8,14},{9,15},{10,... | collective-permute-start | bytes 1228808 | tf_op jit(solution)/shard_map/ppermute | solution.py:56
  597.2 74.6 %collective-permute-start.84 = (bf16[128,1600]{0,1:T(8,128)(2,1)}, bf16[128,1600]{0,1:T(8,128)(2,1)}, u32[]{:S(2)}, u32[]{:S(2)}) collective-permute-start(bf16[128,1600]{0,1:T(8,128)(2,1)} %get-tuple-element.38), channel_id=1, source_target_pairs={{0,4},{1,5},{2,6},{3,7},{4,0},{5,1},{6,2},{7,3},{8,12},{9,13},{10,... | collective-permute-start | bytes 1228808 | tf_op jit(solution)/shard_map/ppermute | solution.py:56
  695.7 68.5 %collective-permute-start.50 = (bf16[4,128,1600]{1,2,0:T(8,128)(2,1)}, bf16[4,128,1600]{1,2,0:T(8,128)(2,1)}, u32[]{:S(2)}, u32[]{:S(2)}) collective-permute-start(bf16[4,128,1600]{1,2,0:T(8,128)(2,1)} %bitcast.702), channel_id=1, source_target_pairs={{0,8},{1,9},{2,10},{3,11},{4,12},{5,13},{6,14},{7,15},{8,0},{9,1},... | collective-permute-start | bytes 4915208 | tf_op jit(solution)/shard_map/ppermute | solution.py:56
  697.2 71.2 %collective-permute-start.86 = (bf16[4,128,1600]{1,2,0:T(8,128)(2,1)}, bf16[4,128,1600]{1,2,0:T(8,128)(2,1)}, u32[]{:S(2)}, u32[]{:S(2)}) collective-permute-start(bf16[4,128,1600]{1,2,0:T(8,128)(2,1)} %bitcast_dynamic-update-slice_fusion.4), channel_id=1, source_target_pairs={{0,8},{1,9},{2,10},{3,11},{4,12},{5,13},{6,14},{7,15},{8,0},{9,1},... | collective-permute-start | bytes 4915208 | tf_op jit(solution)/shard_map/ppermute | solution.py:56
  795.0 67.5 %collective-permute-start.78 = (bf16[4,2,100,768]{3,0,2,1:T(4,128)(2,1)}, bf16[4,2,100,768]{3,0,2,1:T(4,128)(2,1)}, u32[]{:S(2)}, u32[]{:S(2)}) collective-permute-start(bf16[4,2,100,768]{3,0,2,1:T(4,128)(2,1)} %copy.677), channel_id=1, source_target_pairs={{0,8},{1,9},{2,10},{3,11},{4,12},{5,13},{6,14},{7,15},{8,0},{9,1},... | collective-permute-start | bytes 3686408 | tf_op jit(solution)/shard_map/ppermute | solution.py:56
  (166 other events, 2642.2 us)

commit v2 on v1

v2 whole, which is shorter than its diff:
```python
import math

import jax
import jax.numpy as jnp
from jax import lax
from jax.experimental import pallas as pl
from jax.experimental.pallas import tpu as pltpu
from jax.sharding import PartitionSpec as P

HEADS = 25
HEAD_DIM = 64
SLOTS = 4
SLOT_WIDTH = SLOTS * HEAD_DIM
STRIDE = 3 * HEAD_DIM
BLOCK = 256

bf16 = jnp.bfloat16
f32 = jnp.float32


LAYOUT = (("x", 4), ("zl", 2), ("c", 2), ("y", 4), ("zh", 2))
REP = ("x", "zl", "c")
GRP = ("y", "zh")
TEAM = ("y", "c")
REPLICAS = ("zl", "x", "zh")
ROLES = [(0, 0), (1, 2), (2, 1), (3, 3)]


def swap_roles(value):
    return lax.ppermute(value, ("c", "zh"), ROLES)


def other_core(value):
    return lax.ppermute(value, "c", [(0, 1), (1, 0)])


def exchange(parts, axes):
    return lax.all_to_all(parts, axes, 0, 0)


def gather(block, axes):
    return lax.all_gather(block, axes, axis=0)


def team_sum(parts):
    return lax.psum_scatter(parts.astype(bf16), TEAM, scatter_dimension=0, tiled=True).astype(f32)


def windows(rows, count):
    tiles = rows // 8
    starts = [tiles * i // count for i in range(count)]
    size = max(b - a for a, b in zip(starts, starts[1:] + [tiles]))
    return size * 8, [8 * s for s in starts]


def joined(parts, starts, rows, axis):
    ends = starts[1:] + [rows]
    return jnp.concatenate(
        [lax.slice_in_dim(p, 0, e - s, axis=axis) for p, s, e in zip(parts, starts, ends)], axis
    )


def norm_parts(value, gain, shift):
    center = value - jnp.mean(value, axis=-1, keepdims=True)
    spread = jnp.mean(center * center, axis=-1, keepdims=True)
    factor = lax.rsqrt(spread + 1e-05)
    normed = center * factor
    return (normed * gain + shift, normed, factor)


def norm_back(grad_value, normed, factor, gain):
    grad_normed = grad_value * gain
    mean_first = jnp.mean(grad_normed, axis=-1, keepdims=True)
    mean_second = jnp.mean(grad_normed * normed, axis=-1, keepdims=True)
    return factor * (grad_normed - mean_first - normed * mean_second)


def dot(left, right):
    return jnp.dot(left, right, preferred_element_type=f32)


def dot_rows(left, right):
    return lax.dot_general(left, right, (((0,), (0,)), ((), ())), preferred_element_type=f32)


def dot_cols(left, right):
    return lax.dot_general(left, right, (((1,), (1,)), ((), ())), preferred_element_type=f32)


def call(kernel, name, out_shape, *operands, scratch=(), flops=0):
    specs = [
        pl.BlockSpec(memory_space=pltpu.SMEM if op.dtype == jnp.int32 else pltpu.VMEM)
        for op in operands
    ]
    out_specs = jax.tree.map(lambda _: pl.BlockSpec(memory_space=pltpu.VMEM), out_shape)
    moved = sum(op.size * op.dtype.itemsize for op in operands)
    moved += sum(o.size * o.dtype.itemsize for o in jax.tree.leaves(out_shape))
    return pl.pallas_call(
        kernel,
        out_shape=out_shape,
        in_specs=specs,
        out_specs=out_specs,
        scratch_shapes=list(scratch),
        compiler_params=pltpu.CompilerParams(vmem_limit_bytes=56 * 2**20),
        cost_estimate=pl.CostEstimate(
            flops=int(flops), bytes_accessed=int(moved), transcendentals=0
        ),
        name=name,
    )(*operands)


def struct(shape, dtype):
    return jax.ShapeDtypeStruct(shape, dtype)


def qkv_columns_kernel(place_ref, weight_ref, out_ref):
    c = place_ref[0]
    width = weight_ref.shape[1] // 3
    for part in range(3):
        for y in range(4):
            start = part * width + 2 * STRIDE * y
            even = weight_ref[:, start : start + SLOT_WIDTH]
            odd = weight_ref[:, start + STRIDE : start + STRIDE + SLOT_WIDTH]
            block = jnp.where(c == 0, even, odd)
            for zh in range(2):
                out_ref[2 * y + zh, :, part * SLOT_WIDTH : (part + 1) * SLOT_WIDTH] = block


def fc_columns_kernel(place_ref, weight_ref, out_ref):
    c = place_ref[0]
    hidden = weight_ref.shape[1] // 8
    for y in range(4):
        start = 2 * hidden * y
        even = weight_ref[:, start : start + hidden]
        odd = weight_ref[:, start + hidden : start + 2 * hidden]
        out_ref[y] = jnp.where(c == 0, even, odd)


def attend_kernel(tokens_ref, cols_ref, norm_ref, bias_ref, first_ref, qkv_ref, out_ref, top_ref):
    length = tokens_ref.shape[0]
    gain = norm_ref[0:1, :]
    shift = norm_ref[1:2, :]
    for block in range(length // BLOCK):
        rows = slice(block * BLOCK, (block + 1) * BLOCK)
        first = norm_parts(tokens_ref[rows, :].astype(f32), gain, shift)[0].astype(bf16)
        first_ref[rows, :] = first
        qkv_ref[rows, :] = (dot(first, cols_ref[...]) + bias_ref[...]).astype(bf16)
    for head in range(SLOTS):
        lanes = slice(head * HEAD_DIM, (head + 1) * HEAD_DIM)
        keys = qkv_ref[:, SLOT_WIDTH + head * HEAD_DIM : SLOT_WIDTH + (head + 1) * HEAD_DIM]
        values = qkv_ref[
            :, 2 * SLOT_WIDTH + head * HEAD_DIM : 2 * SLOT_WIDTH + (head + 1) * HEAD_DIM
        ]
        for block in range(length // BLOCK):
            rows = slice(block * BLOCK, (block + 1) * BLOCK)
            width = (block + 1) * BLOCK
            query = qkv_ref[rows, lanes] * bf16(1.0 / math.sqrt(HEAD_DIM))
            scores = dot_cols(query, keys[:width])
            row = lax.broadcasted_iota(jnp.int32, (BLOCK, width), 0) + block * BLOCK
            col = lax.broadcasted_iota(jnp.int32, (BLOCK, width), 1)
            scores = jnp.where(col <= row, scores, -1e30)
            top = jnp.max(scores, axis=-1, keepdims=True)
            probs = jnp.exp(scores - top)
            total = jnp.sum(probs, axis=-1, keepdims=True)
            mixed = dot(probs.astype(bf16), values[:width])
            out_ref[rows, lanes] = (mixed / total).astype(bf16)
            top_ref[rows, head : head + 1] = top + jnp.log(total)


def branch_kernel(
    place_ref, slots_ref, own_ref, other_ref, tokens_ref, norm_ref, middle_ref, second_ref, parts_ref, flat_ref
):
    c = place_ref[0]
    shard = own_ref.shape[1]
    for rank in range(8):
        wide = STRIDE if rank < 7 else SLOT_WIDTH
        flat_ref[:, STRIDE * rank : STRIDE * rank + wide] = slots_ref[rank, :, :wide]
    for rank in range(8):
        parts_ref[rank] = flat_ref[:, shard * rank : shard * (rank + 1)]
    total = tokens_ref[...].astype(f32) + norm_ref[4:5, :]
    for y in range(4):
        total = total + dot(parts_ref[2 * y + c], own_ref[y])
        total = total + dot(parts_ref[2 * y + 1 - c], other_ref[y])
    middle_ref[...] = total
    second_ref[...] = norm_parts(total, norm_ref[5:6, :], norm_ref[6:7, :])[0].astype(bf16)


def branch_back_kernel(
    place_ref,
    grad_ref,
    middle_ref,
    cot_ref,
    norm_ref,
    own_ref,
    other_ref,
    grad_middle_ref,
    branch_ref,
    slots_ref,
    sums_ref,
    parts_ref,
    flat_ref,
):
    c = place_ref[0]
    shard = own_ref.shape[1]
    gain = norm_ref[5:6, :]
    _, normed, factor = norm_parts(middle_ref[...], gain, gain)
    grad = grad_ref[...].astype(f32)
    cot = cot_ref[...].astype(f32)
    grad_middle = cot + norm_back(grad, normed, factor, gain)
    branch = grad_middle.astype(bf16)
    grad_middle_ref[...] = grad_middle
    branch_ref[...] = branch
    for y in range(4):
        parts_ref[2 * y + c] = dot_cols(branch, own_ref[y]).astype(bf16)
        parts_ref[2 * y + 1 - c] = dot_cols(branch, other_ref[y]).astype(bf16)
    for rank in range(8):
        flat_ref[:, shard * rank : shard * (rank + 1)] = parts_ref[rank]
    for rank in range(8):
        slots_ref[rank] = flat_ref[:, STRIDE * rank : STRIDE * rank + SLOT_WIDTH]
    sums_ref[0:1, :] = jnp.sum(branch.astype(f32), axis=0, keepdims=True)
    sums_ref[1:2, :] = jnp.sum(grad * normed, axis=0, keepdims=True)
    sums_ref[2:3, :] = jnp.sum(grad, axis=0, keepdims=True)
    sums_ref[3:4, :] = jnp.sum(cot, axis=0, keepdims=True)


def hidden_kernel(
    second_ref, cols_ref, bias_ref, grad_ref, active_ref, hidden_ref, sums_ref, out_ref
):
    length = second_ref.shape[0]
    sums = jnp.zeros(sums_ref.shape, f32)
    for block in range(length // BLOCK):
        rows = slice(block * BLOCK, (block + 1) * BLOCK)
        pre = dot(second_ref[rows, :], cols_ref[...]) + bias_ref[...]
        square = pre * pre
        bent = jnp.tanh(0.7978845608028654 * (pre + 0.044715 * square * pre))
        half = 0.5 * (1.0 + bent)
        active_ref[rows, :] = (pre * half).astype(bf16)
        slope = half + 0.5 * pre * (1.0 - bent * bent) * (
            0.7978845608028654 + (3.0 * 0.044715 * 0.7978845608028654) * square
        )
        grad = (grad_ref[rows, :] * slope).astype(bf16)
        hidden_ref[rows, :] = grad
        sums = sums + jnp.sum(grad.astype(f32), axis=0, keepdims=True)
        out_ref[rows, :] = dot_cols(grad, cols_ref[...]).astype(bf16)
    sums_ref[...] = sums


def attend_back_kernel(
    place_ref, qkv_ref, grad_ref, out_ref, top_ref, cols_ref, mixed_ref, first_ref, sums_ref, query_ref
):
    length = qkv_ref.shape[0]
    scale = 1.0 / math.sqrt(HEAD_DIM)
    ones = jnp.ones((8, HEAD_DIM), bf16)
    for head in range(SLOTS):
        base = head * HEAD_DIM
        lanes = slice(base, base + HEAD_DIM)
        key_lanes = slice(SLOT_WIDTH + base, SLOT_WIDTH + base + HEAD_DIM)
        value_lanes = slice(2 * SLOT_WIDTH + base, 2 * SLOT_WIDTH + base + HEAD_DIM)
        query = qkv_ref[:, lanes] * bf16(scale)
        grad = grad_ref[:, lanes]
        if head == SLOTS - 1:
            grad = jnp.where(place_ref[1] == 7, grad, jnp.zeros_like(grad))
        top = top_ref[head : head + 1, :]
        delta = dot_cols(ones, grad * out_ref[:, lanes])[0:1, :]
        for block in range(length // BLOCK):
            start = block * BLOCK
            rows = slice(start, start + BLOCK)
            width = length - start
            keys = qkv_ref[rows, key_lanes]
            values = qkv_ref[rows, value_lanes]
            scores = dot_cols(keys, query[start:])
            row = lax.broadcasted_iota(jnp.int32, (BLOCK, width), 0)
            col = lax.broadcasted_iota(jnp.int32, (BLOCK, width), 1)
            probs = jnp.where(row <= col, jnp.exp(scores - top[:, start:]), 0.0)
            grad_probs = dot_cols(values, grad[start:])
            grad_scores = (probs * (grad_probs - delta[:, start:])).astype(bf16)
            mixed_ref[rows, value_lanes] = dot(probs.astype(bf16), grad[start:]).astype(bf16)
            mixed_ref[rows, key_lanes] = dot(grad_scores, query[start:]).astype(bf16)
            term = dot_rows(grad_scores, keys)
            if block == 0:
                query_ref[...] = term
            else:
                query_ref[start:, :] += term
        mixed_ref[:, lanes] = (query_ref[...] * scale).astype(bf16)
    sums = jnp.zeros(sums_ref.shape, f32)
    for block in range(length // BLOCK):
        rows = slice(block * BLOCK, (block + 1) * BLOCK)
        mixed = mixed_ref[rows, :]
        sums = sums + jnp.sum(mixed.astype(f32), axis=0, keepdims=True)
        first_ref[rows, :] = dot_cols(mixed, cols_ref[...]).astype(bf16)
    sums_ref[...] = sums


def input_back_kernel(grad_ref, tokens_ref, middle_ref, norm_ref, out_ref, sums_ref):
    gain = norm_ref[0:1, :]
    _, normed, factor = norm_parts(tokens_ref[...].astype(f32), gain, gain)
    grad = grad_ref[...].astype(f32)
    out_ref[...] = (middle_ref[...] + norm_back(grad, normed, factor, gain)).astype(bf16)
    sums_ref[0:1, :] = jnp.sum(grad * normed, axis=0, keepdims=True)
    sums_ref[1:2, :] = jnp.sum(grad, axis=0, keepdims=True)


def column_grad_kernel(left_ref, right_ref, out_ref):
    shard = left_ref.shape[1] // 8
    size, starts = windows(shard, 8)
    grad = dot_rows(left_ref[...], right_ref[...])
    for y in range(4):
        for zh in range(2):
            base = (2 * y + zh) * shard
            for i, start in enumerate(starts):
                out_ref[2 * i + zh, y] = grad[base + start : base + start + size].astype(bf16)


def row_grad_kernel(left_ref, right_ref, out_ref):
    size, starts = windows(left_ref.shape[1], 16)
    grad = dot_rows(left_ref[...], right_ref[...])
    for i, start in enumerate(starts):
        out_ref[i] = grad[start : start + size].astype(bf16)


def qkv_total_kernel(place_ref, own_ref, other_ref, out_ref):
    c = place_ref[0]
    width = out_ref.shape[1] // 3
    _, starts = windows(out_ref.shape[0], 8)
    ends = starts[1:] + [out_ref.shape[0]]
    for i, (start, end) in enumerate(zip(starts, ends)):
        for rank in range(8):
            own, other = own_ref[i, rank // 2], other_ref[i, rank // 2]
            block = jnp.where(c == rank % 2, own, other)[: end - start].astype(f32)
            wide = STRIDE if rank < 7 else SLOT_WIDTH
            for part in range(3):
                lanes = slice(part * width + STRIDE * rank, part * width + STRIDE * rank + wide)
                out_ref[start:end, lanes] = block[
                    :, part * SLOT_WIDTH : part * SLOT_WIDTH + wide
                ]


def fc_total_kernel(place_ref, own_ref, other_ref, out_ref):
    c = place_ref[0]
    hidden = out_ref.shape[1] // 8
    _, starts = windows(out_ref.shape[0], 8)
    ends = starts[1:] + [out_ref.shape[0]]
    for i, (start, end) in enumerate(zip(starts, ends)):
        for rank in range(8):
            own, other = own_ref[i, rank // 2], other_ref[i, rank // 2]
            block = jnp.where(c == rank % 2, own, other)[: end - start].astype(f32)
            out_ref[start:end, rank * hidden : (rank + 1) * hidden] = block


def row_total_kernel(place_ref, own_ref, other_ref, out_ref):
    mine = place_ref[2]
    _, starts = windows(out_ref.shape[0], 16)
    ends = starts[1:] + [out_ref.shape[0]]
    for i, (start, end) in enumerate(zip(starts, ends)):
        block = jnp.where(mine == 1, own_ref[i], other_ref[i])
        out_ref[start:end, :] = block[: end - start].astype(f32)


def after(value, *others):
    return lax.optimization_barrier((value,) + others)[0]


def per_device(
    tokens,
    ln1_gain,
    ln1_bias,
    w_qkv,
    bias_q,
    bias_v,
    w_out,
    bias_out,
    ln2_gain,
    ln2_bias,
    w_fc,
    bias_fc,
    w_proj,
    bias_proj,
    cotangent,
):
    _, span, width = tokens.shape
    shard = width // 8
    hidden = w_fc.shape[1] // 8
    length = span * 8
    slots = 3 * SLOT_WIDTH
    c = lax.axis_index("c")
    zh = lax.axis_index("zh")
    rank = lax.axis_index("y") * 2 + c
    place = jnp.stack([c, rank, (c == zh).astype(jnp.int32)]).astype(jnp.int32)

    own_tokens = swap_roles(tokens.reshape(span, width))
    small = jnp.concatenate(
        [ln1_gain, ln1_bias, bias_q, bias_v, bias_out, ln2_gain, ln2_bias, bias_proj, bias_fc]
    ).reshape(3, hidden)
    qkv_parts = call(
        qkv_columns_kernel, "qkv_columns", struct((8, shard, slots), bf16), place, w_qkv
    )
    small_all = exchange(jnp.broadcast_to(small, (8, 3, hidden)), GRP).astype(f32)
    hidden_bias = lax.dynamic_index_in_dim(small_all, rank, 0, keepdims=False)[2:3]
    vectors = small_all[:, :2].reshape(8, 8, shard).transpose(1, 0, 2).reshape(8, width)
    all_tokens = gather(own_tokens, TEAM).reshape(length, width)
    qkv_cols = exchange(qkv_parts, GRP).reshape(width, slots)
    out_rows = swap_roles(w_out)
    own_cot = swap_roles(cotangent.reshape(span, width))
    fc_parts = call(fc_columns_kernel, "fc_columns", struct((4, shard, hidden), bf16), place, w_fc)

    bias_slots = jnp.concatenate(
        [
            lax.dynamic_slice_in_dim(vectors[2], STRIDE * rank, SLOT_WIDTH),
            jnp.zeros((SLOT_WIDTH,), f32),
            lax.dynamic_slice_in_dim(vectors[3], STRIDE * rank, SLOT_WIDTH),
        ]
    ).reshape(1, slots)
    out_rows, own_cot, fc_parts, qkv_cols, all_tokens = lax.optimization_barrier(
        (out_rows, own_cot, fc_parts, qkv_cols, all_tokens)
    )
    out_own = exchange(jnp.broadcast_to(out_rows, (4, shard, width)), "y")
    all_cot = gather(own_cot, TEAM).reshape(length, width)
    fc_own = exchange(fc_parts, "y")

    first, qkv, attended_slots, top = call(
        attend_kernel,
        "attend",
        (
            struct((length, width), bf16),
            struct((length, slots), bf16),
            struct((length, SLOT_WIDTH), bf16),
            struct((length, SLOTS), f32),
        ),
        all_tokens,
        qkv_cols,
        vectors,
        bias_slots,
        flops=2 * length * width * slots,
    )
    out_other = other_core(out_own)
    attended = exchange(attended_slots.reshape(8, span, SLOT_WIDTH), TEAM)
    middle, second, attended_parts = call(
        branch_kernel,
        "branch",
        (
            struct((span, width), f32),
            struct((span, width), bf16),
            struct((8, span, shard), bf16),
        ),
        place,
        attended,
        out_own,
        out_other,
        own_tokens,
        vectors,
        scratch=[pltpu.VMEM((span, width), bf16)],
        flops=2 * span * width * width,
    )

    second_all = gather(second, TEAM).reshape(length, width)
    proj_rows = swap_roles(after(w_proj, fc_own))
    fc_other = lax.ppermute(fc_own, "zh", [(0, 1), (1, 0)])
    fc_cols = jnp.where(
        zh == 0, jnp.stack([fc_own, fc_other], 1), jnp.stack([fc_other, fc_own], 1)
    ).reshape(width, hidden)
    grad_active = dot_cols(all_cot, proj_rows)
    active, grad_hidden, hidden_sums, second_parts = call(
        hidden_kernel,
        "hidden",
        (
            struct((length, hidden), bf16),
            struct((length, hidden), bf16),
            struct((1, hidden), f32),
            struct((length, width), bf16),
        ),
        second_all,
        fc_cols,
        hidden_bias,
        grad_active,
        flops=4 * length * width * hidden,
    )
    grad_second = team_sum(second_parts)
    proj_parts = call(
        row_grad_kernel,
        "proj_grad",
        struct((16, windows(hidden, 16)[0], width), bf16),
        active,
        all_cot,
        flops=2 * length * width * hidden,
    )
    proj_parts = exchange(proj_parts, REPLICAS)
    fc_grad = call(
        column_grad_kernel,
        "fc_grad",
        struct((16, 4, windows(shard, 8)[0], hidden), bf16),
        second_all,
        grad_hidden,
        flops=2 * length * width * hidden,
    )
    down_parts = dot(active, proj_rows).astype(bf16)
    fc_grad = exchange(fc_grad, REPLICAS)

    grad_middle, grad_branch, grad_slots, branch_sums = call(
        branch_back_kernel,
        "branch_back",
        (
            struct((span, width), f32),
            struct((span, width), bf16),
            struct((8, span, SLOT_WIDTH), bf16),
            struct((4, width), f32),
        ),
        place,
        grad_second,
        middle,
        own_cot,
        vectors,
        out_own,
        out_other,
        scratch=[pltpu.VMEM((8, span, shard), bf16), pltpu.VMEM((span, width), bf16)],
        flops=2 * span * width * width,
    )
    grad_heads = exchange(grad_slots, TEAM).reshape(length, SLOT_WIDTH)
    branch_all = gather(after(grad_branch, grad_heads), TEAM).reshape(length, width)
    grad_mixed, first_parts, mixed_sums = call(
        attend_back_kernel,
        "attend_back",
        (
            struct((length, slots), bf16),
            struct((length, width), bf16),
            struct((1, slots), f32),
        ),
        place,
        qkv,
        grad_heads,
        attended_slots,
        top.T,
        qkv_cols,
        scratch=[pltpu.VMEM((length, HEAD_DIM), f32)],
        flops=2 * length * width * slots,
    )
    grad_first = team_sum(first_parts)
    qkv_grad = call(
        column_grad_kernel,
        "qkv_grad",
        struct((16, 4, windows(shard, 8)[0], slots), bf16),
        first,
        grad_mixed,
        flops=2 * length * width * slots,
    )
    qkv_grad = exchange(qkv_grad, REPLICAS)

    def replica_sum(parts):
        return jnp.sum(parts.astype(f32), axis=0).astype(bf16)

    proj_parts = replica_sum(after(proj_parts, grad_mixed))
    fc_grad = exchange(replica_sum(after(fc_grad, grad_mixed)), "y")
    attended_own = exchange(after(attended_parts, grad_mixed), TEAM).reshape(length, shard)
    out_grad = call(
        row_grad_kernel,
        "out_grad",
        struct((16, windows(shard, 16)[0], width), bf16),
        attended_own,
        branch_all,
        flops=2 * length * width * shard,
    )
    out_grad = exchange(out_grad, REPLICAS)
    output = middle + (team_sum(after(down_parts, first_parts)) + vectors[7])

    grad_inputs, first_sums = call(
        input_back_kernel,
        "input_back",
        (struct((span, width), bf16), struct((2, width), f32)),
        grad_first,
        own_tokens,
        grad_middle,
        vectors,
    )
    inputs_home = swap_roles(grad_inputs).astype(f32).reshape(1, span, width)

    blank = jnp.zeros((1, width), f32)
    at = (0, STRIDE * rank)
    small_terms = jnp.concatenate(
        [
            first_sums,
            lax.dynamic_update_slice(blank, mixed_sums[:, :SLOT_WIDTH], at),
            lax.dynamic_update_slice(blank, mixed_sums[:, 2 * SLOT_WIDTH :], at),
            branch_sums,
        ]
    )
    hidden_term = lax.dynamic_update_slice(
        jnp.zeros((8, hidden), f32), hidden_sums, (rank, 0)
    )
    small_terms = small_terms.reshape(8, 8, shard).transpose(1, 0, 2).reshape(8, 2, hidden)
    small_terms = jnp.concatenate([small_terms, hidden_term[:, None]], axis=1)
    small_sum = jnp.sum(exchange(small_terms, GRP), axis=0)
    small_sum = jnp.sum(exchange(jnp.broadcast_to(small_sum, (16, 3, hidden)), REP), axis=0)
    owned = small_sum[:2].reshape(8, shard)

    def row_total(parts, rows, name):
        whole = gather(parts, REPLICAS)
        return call(
            row_total_kernel, name, struct((rows, width), f32), place, whole, other_core(whole)
        )

    proj_total = row_total(proj_parts, hidden, "proj_total")
    fc_whole = gather(fc_grad, ("zl", "x"))
    fc_total = call(
        fc_total_kernel,
        "fc_total",
        struct((shard, 8 * hidden), f32),
        place,
        fc_whole,
        other_core(fc_whole),
    )
    qkv_grad = exchange(replica_sum(qkv_grad), "y")
    qkv_whole = exchange(jnp.broadcast_to(qkv_grad, (8,) + qkv_grad.shape), ("zl", "x"))
    out_total = row_total(replica_sum(out_grad), shard, "out_total")
    qkv_total = call(
        qkv_total_kernel,
        "qkv_total",
        struct((shard, 3 * width), f32),
        place,
        qkv_whole,
        other_core(qkv_whole),
    )

    output_home = swap_roles(output.astype(bf16)).reshape(1, span, width)
    return (
        output_home,
        inputs_home,
        owned[0],
        owned[1],
        qkv_total,
        owned[2],
        owned[3],
        out_total,
        owned[4],
        owned[5],
        owned[6],
        fc_total,
        small_sum[2],
        proj_total,
        owned[7],
    )


def solution(mesh):
    names = tuple(name for name, _ in LAYOUT)
    fine = jax.sharding.Mesh(mesh.devices.reshape([size for _, size in LAYOUT]), names)
    in_specs = (
        P(REP, GRP, None),
        P(GRP),
        P(GRP),
        P(GRP, None),
        P(GRP),
        P(GRP),
        P(GRP, None),
        P(GRP),
        P(GRP),
        P(GRP),
        P(GRP, None),
        P(GRP),
        P(GRP, None),
        P(GRP),
        P(REP, GRP, None),
    )
    out_specs = (
        P(REP, GRP, None),
        P(REP, GRP, None),
        P(GRP),
        P(GRP),
        P(GRP, None),
        P(GRP),
        P(GRP),
        P(GRP, None),
        P(GRP),
        P(GRP),
        P(GRP),
        P(GRP, None),
        P(GRP),
        P(GRP, None),
        P(GRP),
    )
    return jax.shard_map(
        per_device, mesh=fine, in_specs=in_specs, out_specs=out_specs, check_vma=False
    )
```

time: 894 us -> 806 us (0.902)
  the two profiles are of different devices: /device:TPU:0 before, /device:TPU:17 now
where the time goes in v2:
time: 806 us; the launch traced here: 797 us
  waiting for transfers between devices  277 us (34%)
  blocking collectives  212 us (26%)
  starting transfers between devices  131 us (16%)
  Pallas kernels  112 us (14%)
  local copies, waits for them, and re-layouts  20.6 us (3%)
  matrix products  16.5 us (2%)
  between operations  14.8 us (2%)
  other arithmetic  13.8 us (2%)
    all_to_all x7, blocking collectives, exchange(): return lax.all_to_all(parts, axes, 0, 0)  174 us
    all_to_all x9, waiting for transfers between devices, exchange(): return lax.all_to_all(parts, axes, 0, 0)  118 us
    pallas_call x16, Pallas kernels, call(): pl.pallas_call(kernel, out_shape=out_shape, in_specs=specs, out_specs=out...  112 us
    all_to_all x9, starting transfers between devices, exchange(): return lax.all_to_all(parts, axes, 0, 0)  64 us
    reduce_scatter x3, waiting for transfers between devices, team_sum(): lax.psum_scatter(parts.astype(bf16), TEAM, scatter_dimension=0, tiled=True)  46.7 us
    ppermute x1, waiting for transfers between devices, per_device(): fc_other = lax.ppermute(fc_own, 'zh', [(0, 1), (1, 0)])  44.1 us
    all_gather x1, blocking collectives, gather(): return lax.all_gather(block, axes, axis=0)  38.2 us
    ppermute x6, waiting for transfers between devices, swap_roles(): return lax.ppermute(value, ('c', 'zh'), ROLES)  37 us
  transfers between devices with their start and end apart: 30, of which 13 were waited for; matrix products, arithmetic and copies ran while one was open for 5% of the time, Pallas kernels for 11%

profile of v2, /device:TPU:17, one launch (start us, length us, event | category | flops | bytes accessed | tf_op | source)
XLA Modules:
  0.0 797.2 jit_solution(15686664333430302212)
XLA Ops:
  30.1 8.1 %collective-permute-start = (bf16[200,1600]{1,0:T(8,128)(2,1)}, bf16[200,1600]{1,0:T(8,128)(2,1)}, u32[]{:S(2)}, u32[]{:S(2)}) collective-permute-start(bf16[200,1600]{1,0:T(8,128)(2,1)} %param.21), channel_id=1, source_target_pairs={{0,0},{1,8},{8,1},{9,9},{2,2},{3,10},{10,3},{11,11},{4,4},{5,12},{... | collective-permute-start | bytes 1920008 | tf_op jit(solution)/shard_map/ppermute | solution.py:30
  44.6 27.3 %collective-permute-done.1.cot_ref = bf16[128,1600]{1,0:T(8,128)(2,1)S(1)} collective-permute-done((bf16[128,1600]{1,0:T(8,128)(2,1)}, bf16[128,1600]{1,0:T(8,128)(2,1)S(1)}, u32[]{:S(2)}, u32[]{:S(2)}) %collective-permute-start.1) | collective-permute-done | bytes 409632 | tf_op jit(solution)/shard_map/ppermute | solution.py:30
  75.4 46.0 %all_to_all.80.own_ref = bf16[4,200,1600]{2,1,0:T(8,128)(2,1)S(1)} all-to-all(bf16[4,200,1600]{2,1,0:T(8,128)(2,1)S(1)} %broadcast_in_dim.26), channel_id=1, replica_groups=mesh['x'=4,'zl'=2,'c'=2,'y'=4,'zh'=2] {'y'}, dimensions={0} | all-to-all | bytes 5120000 | tf_op jit(solution)/shard_map/all_to_all | solution.py:38
  137.6 14.2 %attend.1 = (bf16[1024,1600]{1,0:T(8,128)(2,1)}, bf16[1024,768]{1,0:T(8,128)(2,1)}, bf16[1024,256]{1,0:T(8,128)(2,1)}, f32[1024,4]{1,0:T(8,128)}) custom-call(bf16[1024,1600]{1,0:T(8,128)(2,1)} %all-gather.14.cloned.1.call-done.tokens_ref, bf16[1600,768]{1,0:T(8,128)(2,1)} %bitcast.46, f32[8,1600]{1,0:T(8,128)} %reshape.110.norm_ref, f32[1,768]{1,0:T(1,128)} %reshape.111.bias_ref), custom_call_target="tpu_custom_call" | custom-call | flops 2516582400 | bytes 11179008 | tf_op jit(solution)/shard_map/attend/pallas_call | solution.py:98
  151.8 14.1 %all_to_all.81.slots_ref = bf16[8,128,256]{2,1,0:T(8,128)(2,1)} all-to-all(bf16[8,128,256]{2,1,0:T(8,128)(2,1)} %bitcast.52), channel_id=1, replica_groups=mesh['x'=4,'zl'=2,'c'=2,'y'=4,'zh'=2] {'y','c'}, dimensions={0} | all-to-all | bytes 1048576 | tf_op jit(solution)/shard_map/all_to_all | solution.py:38
  171.6 28.6 %all_to_all.82 = bf16[4,200,800]{2,1,0:T(8,128)(2,1)S(1)} all-to-all(bf16[4,200,800]{2,1,0:T(8,128)(2,1)S(1)} %copy-done.2), channel_id=1, replica_groups=mesh['x'=4,'zl'=2,'c'=2,'y'=4,'zh'=2] {'y'}, dimensions={0} | all-to-all | bytes 2560000 | tf_op jit(solution)/shard_map/all_to_all | solution.py:38
  204.8 15.2 %collective-permute-start.4 = (bf16[4,200,800]{2,1,0:T(8,128)(2,1)S(1)}, bf16[4,200,800]{2,1,0:T(8,128)(2,1)S(1)}, u32[]{:S(2)}, u32[]{:S(2)}) collective-permute-start(bf16[4,200,800]{2,1,0:T(8,128)(2,1)S(1)} %all_to_all.82), channel_id=1, source_target_pairs={{0,1},{1,0},{2,3},{3,2},{4,5},{5,4},{6,7},{7,6},{8,9},{9,8},{10,11... | collective-permute-start | bytes 3840008 | tf_op jit(solution)/shard_map/ppermute | solution.py:457
  220.6 44.1 %collective-permute-done.4 = bf16[4,200,800]{2,1,0:T(8,128)(2,1)S(1)} collective-permute-done((bf16[4,200,800]{2,1,0:T(8,128)(2,1)S(1)}, bf16[4,200,800]{2,1,0:T(8,128)(2,1)S(1)}, u32[]{:S(2)}, u32[]{:S(2)}) %collective-permute-start.4) | collective-permute-done | bytes 1280032 | tf_op jit(solution)/shard_map/ppermute | solution.py:457
  267.8 8.5 %fusion.2.grad_ref = f32[1024,800]{1,0:T(8,128)} fusion(bf16[1024,1600]{1,0:T(8,128)(2,1)} %all-gather.18.cloned.1.call-done.right_ref, bf16[800,1600]{1,0:T(8,128)(2,1)} %collective-permute-done.5), kind=kOutput, calls=%fused_computation.17 | convolution fusion | flops 2621440000 | bytes 9113600 | tf_op jit(solution)/shard_map/dot_general | solution.py:87
  276.3 14.8 %hidden.1 = (bf16[1024,800]{1,0:T(8,128)(2,1)}, bf16[1024,800]{1,0:T(8,128)(2,1)}, f32[1,800]{1,0:T(1,128)}, bf16[1024,1600]{1,0:T(8,128)(2,1)}) custom-call(bf16[1024,1600]{1,0:T(8,128)(2,1)} %all-gather.16.cloned.1.call-done.second_ref.left_ref, bf16[1600,800]{1,0:T(8,128)(2,1)} %bitcast.45, f32[1,800]{1,0:T(1,128)} %dynamic-slice_bitcast_fusion.bias_ref, ...), custom_call_target="tpu_custom_call" | custom-call | flops 5242880000 | bytes 15673600 | tf_op jit(solution)/shard_map/hidden/pallas_call | solution.py:98
  291.1 36.1 %reduce-scatter.4.cloned.1.call-done = bf16[128,1600]{1,0:T(8,128)(2,1)} async-done(((bf16[1024,1600]{1,0:T(8,128)(2,1)}), bf16[128,1600]{1,0:T(8,128)(2,1)}) %reduce-scatter.4.cloned.1.call-update) | async-done | bytes 409616 | tf_op jit(solution)/shard_map/reduce_scatter | solution.py:46
  336.5 8.2 %all-to-all-start.5 = ((bf16[8,128,256]{2,1,0:T(8,128)(2,1)}), bf16[8,128,256]{2,1,0:T(8,128)(2,1)S(1)}, u32[]{:S(2)}, u32[]{:S(2)}) async-start(bf16[8,128,256]{2,1,0:T(8,128)(2,1)} %get-tuple-element.58), calls=%async_computation.6 | async-start | bytes 1048576 | tf_op jit(solution)/shard_map/all_to_all | solution.py:38
  361.1 15.4 %attend_back.1 = (bf16[1024,768]{1,0:T(8,128)(2,1)}, bf16[1024,1600]{1,0:T(8,128)(2,1)}, f32[1,768]{1,0:T(1,128)}) custom-call(s32[3]{0:T(128)} %pad_add_fusion.place_ref, bf16[1024,768]{1,0:T(8,128)(2,1)} %get-tuple-element.56.qkv_ref, bf16[1024,256]{1,0:T(8,128)(2,1)} %bitcast.53, bf16[1024,256]{1,0:T(8,128)(2,1)} %get-tuple-element.48.out_ref, ...), custom_call_target="tpu_custom_call" | custom-call | flops 2516582400 | bytes 9948172 | tf_op jit(solution)/shard_map/attend_back/pallas_call | solution.py:98
  376.4 39.4 %all-to-all-done.13 = bf16[16,4,32,800]{3,2,1,0:T(8,128)(2,1)} async-done(((bf16[16,4,32,800]{3,2,1,0:T(8,128)(2,1)}), bf16[16,4,32,800]{3,2,1,0:T(8,128)(2,1)}, u32[]{:S(2)}, u32[]{:S(2)}) %all-to-all-start.13) | async-done | bytes 3276832 | tf_op jit(solution)/shard_map/all_to_all | solution.py:38
  433.3 59.9 %all_to_all.84 = bf16[16,56,1600]{2,1,0:T(8,128)(2,1)S(1)} all-to-all(bf16[16,56,1600]{2,1,0:T(8,128)(2,1)} %proj_grad.1), channel_id=1, replica_groups=mesh['x'=4,'zl'=2,'c'=2,'y'=4,'zh'=2] {'zl','x','zh'}, dimensions={0} | all-to-all | bytes 5734400 | tf_op jit(solution)/shard_map/all_to_all | solution.py:38
  506.6 8.0 %convolution_convert_fusion = bf16[1024,1600]{1,0:T(8,128)(2,1)} fusion(bf16[1024,800]{1,0:T(8,128)(2,1)} %get-tuple-element.55.left_ref, bf16[800,1600]{1,0:T(8,128)(2,1)} %collective-permute-done.5), kind=kOutput, calls=%fused_computation | convolution fusion | flops 2623078400 | bytes 7475200 | tf_op jit(solution)/shard_map/dot_general | solution.py:79
  514.6 46.4 %all-to-all-done.8 = bf16[16,4,32,768]{3,2,1,0:T(8,128)(2,1)S(1)} async-done(((bf16[16,4,32,768]{3,2,1,0:T(8,128)(2,1)}), bf16[16,4,32,768]{3,2,1,0:T(8,128)(2,1)S(1)}, u32[]{:S(2)}, u32[]{:S(2)}) %all-to-all-start.8) | async-done | bytes 3145760 | tf_op jit(solution)/shard_map/all_to_all | solution.py:38
  570.5 16.4 %all-to-all-start.10 = ((bf16[8,4,32,768]{3,2,1,0:T(8,128)(2,1)}), bf16[8,4,32,768]{3,2,1,0:T(8,128)(2,1)S(1)}, u32[]{:S(2)}, u32[]{:S(2)}) async-start(bf16[8,4,32,768]{3,2,1,0:T(8,128)(2,1)} %broadcast_in_dim.31), calls=%async_computation.13 | async-start | bytes 3145728 | tf_op jit(solution)/shard_map/all_to_all | solution.py:38
  589.9 23.4 %all-to-all-done.10.own_ref = bf16[8,4,32,768]{3,2,1,0:T(8,128)(2,1)S(1)} async-done(((bf16[8,4,32,768]{3,2,1,0:T(8,128)(2,1)}), bf16[8,4,32,768]{3,2,1,0:T(8,128)(2,1)S(1)}, u32[]{:S(2)}, u32[]{:S(2)}) %all-to-all-start.10) | async-done | bytes 1572896 | tf_op jit(solution)/shard_map/all_to_all | solution.py:38
  617.5 10.5 %all_to_all.86 = bf16[8,128,200]{1,2,0:T(8,128)(2,1)S(1)} all-to-all(bf16[8,128,200]{1,2,0:T(8,128)(2,1)S(1)} %copy.81), channel_id=1, replica_groups=mesh['x'=4,'zl'=2,'c'=2,'y'=4,'zh'=2] {'y','c'}, dimensions={0} | all-to-all | bytes 819200 | tf_op jit(solution)/shard_map/all_to_all | solution.py:38
  635.8 27.5 %all-gather.20.cloned.1.call-done.right_ref = bf16[1024,1600]{1,0:T(8,128)(2,1)} async-done(((bf16[128,1600]{1,0:T(8,128)(2,1)}), bf16[1024,1600]{1,0:T(8,128)(2,1)}) %all-gather.20.cloned.1.call-update) | async-done | bytes 3276816 | tf_op jit(solution)/shard_map/all_gather | solution.py:42
  688.4 10.5 %reduce-scatter.8.cloned.1.call-done = bf16[128,1600]{1,0:T(8,128)(2,1)} async-done(((bf16[1024,1600]{1,0:T(8,128)(2,1)}), bf16[128,1600]{1,0:T(8,128)(2,1)}) %reduce-scatter.8.cloned.1.call-update) | async-done | bytes 409616 | tf_op jit(solution)/shard_map/reduce_scatter | solution.py:46
  705.6 9.0 %all-to-all-start.6 = ((f32[8,3,800]{2,1,0:T(4,128)}), f32[8,3,800]{2,1,0:T(4,128)S(1)}, u32[]{:S(2)}, u32[]{:S(2)}) async-start(f32[8,3,800]{2,1,0:T(4,128)} %pad_maximum_fusion), calls=%async_computation.9 | async-start | bytes 229376 | tf_op jit(solution)/shard_map/all_to_all | solution.py:38
  714.6 38.2 %all-gather.4 = bf16[256,1600]{1,0:T(8,128)(2,1)S(1)} all-gather(bf16[16,1600]{1,0:T(8,128)(2,1)S(1)} %reduce_sum.69), channel_id=6, replica_groups=mesh['x'=4,'zl'=2,'c'=2,'y'=4,'zh'=2] {'zl','x','zh'}, dimensions={0}, use_global_device_ids=true | all-gather | bytes 870400 | tf_op jit(solution)/shard_map/all_gather | solution.py:42
  (178 shorter events, 212.7 us)
Async XLA Ops:
  7.2 66.8 %all-gather.14.cloned.1.call-start = ((), (), s32[]{:S(2)}) async-start(), calls=%async_computation.22 | async-start | bytes 3833856 | tf_op jit(solution)/shard_map/all_gather | solution.py:42
  25.7 46.3 %all-to-all-start = ((bf16[8,200,768]{2,1,0:T(8,128)(2,1)}), bf16[8,200,768]{2,1,0:T(8,128)(2,1)S(1)}, u32[]{:S(2)}, u32[]{:S(2)}) async-start(bf16[8,200,768]{2,1,0:T(8,128)(2,1)} %qkv_columns.1), calls=%async_computation | async-start | bytes 4915200 | tf_op jit(solution)/shard_map/all_to_all | solution.py:38
  30.1 237.7 %all-gather.18.cloned.1.call-start = ((), (), s32[]{:S(2)}) async-start(), calls=%async_computation.24 | async-start | bytes 3833856 | tf_op jit(solution)/shard_map/all_gather | solution.py:42
  30.1 41.9 %collective-permute-start = (bf16[200,1600]{1,0:T(8,128)(2,1)}, bf16[200,1600]{1,0:T(8,128)(2,1)}, u32[]{:S(2)}, u32[]{:S(2)}) collective-permute-start(bf16[200,1600]{1,0:T(8,128)(2,1)} %param.21), channel_id=1, source_target_pairs={{0,0},{1,8},{8,1},{9,9},{2,2},{3,10},{10,3},{11,11},{4,4},{5,12},{... | collective-permute-start | bytes 1920008 | tf_op jit(solution)/shard_map/ppermute | solution.py:30
  39.2 32.8 %collective-permute-start.1 = (bf16[128,1600]{1,0:T(8,128)(2,1)}, bf16[128,1600]{1,0:T(8,128)(2,1)S(1)}, u32[]{:S(2)}, u32[]{:S(2)}) collective-permute-start(bf16[128,1600]{1,0:T(8,128)(2,1)} %bitcast.54), channel_id=1, source_target_pairs={{0,0},{1,8},{8,1},{9,9},{2,2},{3,10},{10,3},{11,11},{4,4},{5,12},{... | collective-permute-start | bytes 1228808 | tf_op jit(solution)/shard_map/ppermute | solution.py:30
  121.4 44.5 %collective-permute-start.3 = (bf16[4,200,1600]{2,1,0:T(8,128)(2,1)S(1)}, bf16[4,200,1600]{2,1,0:T(8,128)(2,1)}, u32[]{:S(2)}, u32[]{:S(2)}) collective-permute-start(bf16[4,200,1600]{2,1,0:T(8,128)(2,1)S(1)} %all_to_all.80.own_ref), channel_id=1, source_target_pairs={{0,8},{8,0},{1,9},{9,1},{2,10},{10,2},{3,11},{11,3},{4,12},{12,4},... | collective-permute-start | bytes 7680008 | tf_op jit(solution)/shard_map/ppermute | solution.py:34
  130.8 145.5 %all-gather.16.cloned.1.call-start = ((), (), s32[]{:S(2)}) async-start(), calls=%async_computation.23 | async-start | bytes 3833856 | tf_op jit(solution)/shard_map/all_gather | solution.py:42
  171.5 155.7 %reduce-scatter.4.cloned.1.call-start = ((), (), s32[]{:S(2)}) async-start(), calls=%async_computation.19 | async-start | bytes 3833856 | tf_op jit(solution)/shard_map/reduce_scatter | solution.py:46
  200.2 67.6 %collective-permute-start.5 = (bf16[800,1600]{1,0:T(8,128)(2,1)}, bf16[800,1600]{1,0:T(8,128)(2,1)}, u32[]{:S(2)}, u32[]{:S(2)}) collective-permute-start(bf16[800,1600]{1,0:T(8,128)(2,1)} %param.27), channel_id=1, source_target_pairs={{0,0},{1,8},{8,1},{9,9},{2,2},{3,10},{10,3},{11,11},{4,4},{5,12},{... | collective-permute-start | bytes 7680008 | tf_op jit(solution)/shard_map/ppermute | solution.py:30
  204.8 59.9 %collective-permute-start.4 = (bf16[4,200,800]{2,1,0:T(8,128)(2,1)S(1)}, bf16[4,200,800]{2,1,0:T(8,128)(2,1)S(1)}, u32[]{:S(2)}, u32[]{:S(2)}) collective-permute-start(bf16[4,200,800]{2,1,0:T(8,128)(2,1)S(1)} %all_to_all.82), channel_id=1, source_target_pairs={{0,1},{1,0},{2,3},{3,2},{4,5},{5,4},{6,7},{7,6},{8,9},{9,8},{10,11... | collective-permute-start | bytes 3840008 | tf_op jit(solution)/shard_map/ppermute | solution.py:457
  353.4 62.4 %all-to-all-start.13 = ((bf16[16,4,32,800]{3,2,1,0:T(8,128)(2,1)}), bf16[16,4,32,800]{3,2,1,0:T(8,128)(2,1)}, u32[]{:S(2)}, u32[]{:S(2)}) async-start(bf16[16,4,32,800]{3,2,1,0:T(8,128)(2,1)} %fc_grad.1), calls=%async_computation.16 | async-start | bytes 7340032 | tf_op jit(solution)/shard_map/all_to_all | solution.py:38
  360.2 226.7 %all-gather.22.cloned.1.call-start = ((), (), s32[]{:S(2)}) async-start(), calls=%async_computation.26 | async-start | bytes 2064384 | tf_op jit(solution)/shard_map/all_gather | solution.py:42
  425.7 203.3 %all-gather.24.cloned.1.call-start = ((), (), s32[]{:S(2)}) async-start(), calls=%async_computation.27 | async-start | bytes 3168256 | tf_op jit(solution)/shard_map/all_gather | solution.py:42
  494.4 168.9 %all-gather.20.cloned.1.call-start = ((), (), s32[]{:S(2)}) async-start(), calls=%async_computation.25 | async-start | bytes 3833856 | tf_op jit(solution)/shard_map/all_gather | solution.py:42
  495.1 203.8 %reduce-scatter.8.cloned.1.call-start = ((), (), s32[]{:S(2)}) async-start(), calls=%async_computation.21 | async-start | bytes 3833856 | tf_op jit(solution)/shard_map/reduce_scatter | solution.py:46
  502.8 58.2 %all-to-all-start.8 = ((bf16[16,4,32,768]{3,2,1,0:T(8,128)(2,1)}), bf16[16,4,32,768]{3,2,1,0:T(8,128)(2,1)S(1)}, u32[]{:S(2)}, u32[]{:S(2)}) async-start(bf16[16,4,32,768]{3,2,1,0:T(8,128)(2,1)} %qkv_grad.1), calls=%async_computation.11 | async-start | bytes 6291456 | tf_op jit(solution)/shard_map/all_to_all | solution.py:38
  506.5 259.1 %reduce-scatter.6.cloned.1.call-start = ((), (), s32[]{:S(2)}) async-start(), calls=%async_computation.20 | async-start | bytes 3833856 | tf_op jit(solution)/shard_map/reduce_scatter | solution.py:46
  570.5 42.8 %all-to-all-start.10 = ((bf16[8,4,32,768]{3,2,1,0:T(8,128)(2,1)}), bf16[8,4,32,768]{3,2,1,0:T(8,128)(2,1)S(1)}, u32[]{:S(2)}, u32[]{:S(2)}) async-start(bf16[8,4,32,768]{3,2,1,0:T(8,128)(2,1)} %broadcast_in_dim.31), calls=%async_computation.13 | async-start | bytes 3145728 | tf_op jit(solution)/shard_map/all_to_all | solution.py:38
  586.9 87.8 %collective-permute-start.10 = (bf16[8,4,32,800]{3,2,1,0:T(8,128)(2,1)}, bf16[8,4,32,800]{3,2,1,0:T(8,128)(2,1)}, u32[]{:S(2)}, u32[]{:S(2)}) collective-permute-start(bf16[8,4,32,800]{3,2,1,0:T(8,128)(2,1)} %bitcast.49), channel_id=1, source_target_pairs={{0,8},{8,0},{1,9},{9,1},{2,10},{10,2},{3,11},{11,3},{4,12},{12,4},... | collective-permute-start | bytes 4915208 | tf_op jit(solution)/shard_map/ppermute | solution.py:34
  613.3 66.8 %collective-permute-start.8 = (bf16[8,4,32,768]{3,2,1,0:T(8,128)(2,1)S(1)}, bf16[8,4,32,768]{3,2,1,0:T(8,128)(2,1)}, u32[]{:S(2)}, u32[]{:S(2)}) collective-permute-start(bf16[8,4,32,768]{3,2,1,0:T(8,128)(2,1)S(1)} %all-to-all-done.10.own_ref), channel_id=1, source_target_pairs={{0,8},{8,0},{1,9},{9,1},{2,10},{10,2},{3,11},{11,3},{4,12},{12,4},... | collective-permute-start | bytes 4718600 | tf_op jit(solution)/shard_map/ppermute | solution.py:34
  629.0 155.7 %collective-permute-start.11 = (bf16[16,56,1600]{2,1,0:T(8,128)(2,1)}, bf16[16,56,1600]{2,1,0:T(8,128)(2,1)}, u32[]{:S(2)}, u32[]{:S(2)}) collective-permute-start(bf16[16,56,1600]{2,1,0:T(8,128)(2,1)} %bitcast.43), channel_id=1, source_target_pairs={{0,8},{8,0},{1,9},{9,1},{2,10},{10,2},{3,11},{11,3},{4,12},{12,4},... | collective-permute-start | bytes 8601608 | tf_op jit(solution)/shard_map/ppermute | solution.py:34
  667.3 20.9 %all-to-all-start.12 = ((bf16[16,16,1600]{2,1,0:T(8,128)(2,1)}), bf16[16,16,1600]{2,1,0:T(8,128)(2,1)S(1)}, u32[]{:S(2)}, u32[]{:S(2)}) async-start(bf16[16,16,1600]{2,1,0:T(8,128)(2,1)} %out_grad.1), calls=%async_computation.15 | async-start | bytes 1703936 | tf_op jit(solution)/shard_map/all_to_all | solution.py:38
  705.6 55.8 %all-to-all-start.6 = ((f32[8,3,800]{2,1,0:T(4,128)}), f32[8,3,800]{2,1,0:T(4,128)S(1)}, u32[]{:S(2)}, u32[]{:S(2)}) async-start(f32[8,3,800]{2,1,0:T(4,128)} %pad_maximum_fusion), calls=%async_computation.9 | async-start | bytes 229376 | tf_op jit(solution)/shard_map/all_to_all | solution.py:38
  752.8 28.5 %collective-permute-start.9 = (bf16[16,16,1600]{2,1,0:T(8,128)(2,1)S(1)}, bf16[16,16,1600]{2,1,0:T(8,128)(2,1)S(1)}, u32[]{:S(2)}, u32[]{:S(2)}) collective-permute-start(bf16[16,16,1600]{2,1,0:T(8,128)(2,1)S(1)} %bitcast.41), channel_id=1, source_target_pairs={{0,8},{8,0},{1,9},{9,1},{2,10},{10,2},{3,11},{11,3},{4,12},{12,4},... | collective-permute-start | bytes 2457608 | tf_op jit(solution)/shard_map/ppermute | solution.py:34
  (31 other events, 830.9 us)
Sparse Core Ops, SparseCore 0:
  21.2 52.7 all-gather.13
  75.7 49.6 all-gather.17
  171.7 37.9 all-gather.15
  291.2 35.9 reduce-scatter.3
  425.8 61.9 all-gather.21
  494.5 134.1 all-gather.23
  630.3 32.8 all-gather.19
  665.7 33.1 reduce-scatter.7
  701.9 36.7 reduce-scatter.5

commit v3 on v2

--- a/solution.py
+++ b/solution.py
@@ -1,3 +1,4 @@
+import functools
 import math
 
 import jax
@@ -23,7 +24,22 @@
 GRP = ("y", "zh")
 TEAM = ("y", "c")
 REPLICAS = ("zl", "x", "zh")
+Z_RING = ("zl", "zh")
+Z_PLACES = (0, 2, 1, 3)
 ROLES = [(0, 0), (1, 2), (2, 1), (3, 3)]
+
+
+def ring(value, axis, step):
+    index = Z_PLACES if axis == Z_RING else range(4)
+    return lax.ppermute(value, axis, [(index[(i + step) % 4], index[i]) for i in range(4)])
+
+
+def ring_all(values, axis):
+    return [values[0]] + [ring(values[k], axis, k) for k in range(1, 4)]
+
+
+def flipped(value, axis):
+    return lax.ppermute(value, axis, [(0, 1), (1, 0)])
 
 
 def swap_roles(value):
@@ -113,38 +129,219 @@
     return jax.ShapeDtypeStruct(shape, dtype)
 
 
-def qkv_columns_kernel(place_ref, weight_ref, out_ref):
-    c = place_ref[0]
+Y, C, RANK, ZH, Z, X, ZL, MINE = range(8)
+
+
+def qkv_columns_kernel(place_ref, weight_ref, *refs):
+    out_refs, held_ref = refs[:4], refs[4]
+    c = place_ref[C]
     width = weight_ref.shape[1] // 3
     for part in range(3):
+        lanes = slice(part * SLOT_WIDTH, (part + 1) * SLOT_WIDTH)
         for y in range(4):
             start = part * width + 2 * STRIDE * y
             even = weight_ref[:, start : start + SLOT_WIDTH]
             odd = weight_ref[:, start + STRIDE : start + STRIDE + SLOT_WIDTH]
-            block = jnp.where(c == 0, even, odd)
-            for zh in range(2):
-                out_ref[2 * y + zh, :, part * SLOT_WIDTH : (part + 1) * SLOT_WIDTH] = block
-
-
-def fc_columns_kernel(place_ref, weight_ref, out_ref):
-    c = place_ref[0]
+            held_ref[y, :, lanes] = jnp.where(c == 0, even, odd)
+    for k in range(4):
+        out_refs[k][...] = held_ref[lax.rem(place_ref[Y] + 4 - k, 4)]
+
+
+def fc_columns_kernel(place_ref, weight_ref, *refs):
+    out_refs, held_ref = refs[:4], refs[4]
+    c = place_ref[C]
     hidden = weight_ref.shape[1] // 8
     for y in range(4):
         start = 2 * hidden * y
         even = weight_ref[:, start : start + hidden]
         odd = weight_ref[:, start + hidden : start + 2 * hidden]
-        out_ref[y] = jnp.where(c == 0, even, odd)
-
-
-def attend_kernel(tokens_ref, cols_ref, norm_ref, bias_ref, first_ref, qkv_ref, out_ref, top_ref):
+        held_ref[y] = jnp.where(c == 0, even, odd)
+    for k in range(4):
+        out_refs[k][...] = held_ref[lax.rem(place_ref[Y] + 4 - k, 4)]
+
+
+def fc_whole_kernel(place_ref, *refs):
+    out_ref = refs[8]
+    zh = place_ref[ZH]
+    for k in range(4):
+        y = lax.rem(place_ref[Y] + k, 4)
+        out_ref[2 * y + zh] = refs[k][...]
+        out_ref[2 * y + 1 - zh] = refs[4 + k][...]
+
+
+def branch_kernel(place_ref, slots_ref, tokens_ref, norm_ref, *refs):
+    rows_refs, (middle_ref, second_ref, parts_ref, flat_ref) = refs[:8], refs[8:]
+    c = place_ref[C]
+    shard = rows_refs[0].shape[0]
+    for rank in range(8):
+        wide = STRIDE if rank < 7 else SLOT_WIDTH
+        flat_ref[:, STRIDE * rank : STRIDE * rank + wide] = slots_ref[rank, :, :wide]
+    for rank in range(8):
+        parts_ref[rank] = flat_ref[:, shard * rank : shard * (rank + 1)]
+    total = tokens_ref[...].astype(f32) + norm_ref[4:5, :]
+    for k in range(4):
+        y = lax.rem(place_ref[Y] + k, 4)
+        total = total + dot(parts_ref[2 * y + c], rows_refs[k][...])
+        total = total + dot(parts_ref[2 * y + 1 - c], rows_refs[4 + k][...])
+    middle_ref[...] = total
+    second_ref[...] = norm_parts(total, norm_ref[5:6, :], norm_ref[6:7, :])[0].astype(bf16)
+
+
+def branch_back_kernel(place_ref, grad_ref, middle_ref, cot_ref, norm_ref, *refs):
+    rows_refs = refs[:8]
+    grad_middle_ref, branch_ref, slots_ref, sums_ref, parts_ref, flat_ref = refs[8:]
+    c = place_ref[C]
+    shard = rows_refs[0].shape[0]
+    gain = norm_ref[5:6, :]
+    _, normed, factor = norm_parts(middle_ref[...], gain, gain)
+    grad = grad_ref[...].astype(f32)
+    cot = cot_ref[...].astype(f32)
+    grad_middle = cot + norm_back(grad, normed, factor, gain)
+    branch = grad_middle.astype(bf16)
+    grad_middle_ref[...] = grad_middle
+    branch_ref[...] = branch
+    for k in range(4):
+        y = lax.rem(place_ref[Y] + k, 4)
+        parts_ref[2 * y + c] = dot_cols(branch, rows_refs[k][...]).astype(bf16)
+        parts_ref[2 * y + 1 - c] = dot_cols(branch, rows_refs[4 + k][...]).astype(bf16)
+    for rank in range(8):
+        flat_ref[:, shard * rank : shard * (rank + 1)] = parts_ref[rank]
+    for rank in range(8):
+        slots_ref[rank] = flat_ref[:, STRIDE * rank : STRIDE * rank + SLOT_WIDTH]
+    sums_ref[0:1, :] = jnp.sum(branch.astype(f32), axis=0, keepdims=True)
+    sums_ref[1:2, :] = jnp.sum(grad * normed, axis=0, keepdims=True)
+    sums_ref[2:3, :] = jnp.sum(grad, axis=0, keepdims=True)
+    sums_ref[3:4, :] = jnp.sum(cot, axis=0, keepdims=True)
+
+
+def column_grad_kernel(left_ref, right_ref, out_ref):
+    shard = left_ref.shape[1] // 8
+    size, starts = windows(shard, 8)
+    grad = dot_rows(left_ref[...], right_ref[...])
+    for y in range(4):
+        for zh in range(2):
+            base = (2 * y + zh) * shard
+            for i, start in enumerate(starts):
+                out_ref[2 * i + zh, y] = grad[base + start : base + start + size].astype(bf16)
+
+
+def column_ring_kernel(place_ref, left_ref, right_ref, *refs):
+    out_refs, held_ref = refs[:4], refs[4]
+    shard = left_ref.shape[1] // 8
+    size, starts = windows(shard, 8)
+    held_ref[...] = dot_rows(left_ref[...], right_ref[...])
+    for k in range(4):
+        x = lax.rem(place_ref[X] + 4 - k, 4)
+        for z in range(4):
+            for y in range(4):
+                base = (2 * y + z // 2) * shard + starts[4 * (z % 2)]
+                at = pl.multiple_of(base + starts[1] * x, 8)
+                out_refs[k][z, y] = held_ref[pl.ds(at, size), :].astype(bf16)
+
+
+def row_start(rows, index):
+    return pl.multiple_of(lax.div(rows // 8 * index, 16) * 8, 8)
+
+
+def row_ring_kernel(place_ref, left_ref, right_ref, *refs):
+    out_refs, held_ref = refs[:4], refs[4]
+    rows = left_ref.shape[1]
+    size = windows(rows, 16)[0]
+    held_ref[...] = dot_rows(left_ref[...], right_ref[...])
+    for k in range(4):
+        z = lax.rem(place_ref[Z] + 4 - k, 4)
+        for x in range(4):
+            at = row_start(rows, (lax.rem(z, 2) * 4 + x) * 2 + lax.div(z, 2))
+            out_refs[k][x] = held_ref[pl.ds(at, size), :].astype(bf16)
+
+
+def out_grad_kernel(place_ref, left_ref, *refs):
+    blocks, out_ref, held_ref = refs[:8], refs[8], refs[9]
+    c = place_ref[C]
+    rows = left_ref.shape[2]
+    size, starts = windows(rows, 16)
+    for k in range(4):
+        y = lax.rem(place_ref[Y] + k, 4)
+        term = dot_rows(left_ref[2 * y + c], blocks[k][...])
+        term = term + dot_rows(left_ref[2 * y + 1 - c], blocks[4 + k][...])
+        if k == 0:
+            held_ref[...] = term
+        else:
+            held_ref[...] += term
+    for i, start in enumerate(starts):
+        out_ref[i] = held_ref[start : start + size, :].astype(bf16)
+
+
+def fold_kernel(which, place_ref, *refs):
+    for k in range(4):
+        at = lax.rem(place_ref[which] + 4 - k, 4)
+        total = refs[0][at].astype(f32)
+        for j in range(1, 4):
+            total = total + refs[j][at].astype(f32)
+        refs[4 + k][...] = total.astype(bf16)
+
+
+def stack_kernel(*refs):
+    for k, ref in enumerate(refs[:-1]):
+        refs[-1][k] = ref[...]
+
+
+def column_total_kernel(spans, ringed, place_ref, *refs):
+    out_ref = refs[8]
+    shard = out_ref.shape[0]
+    _, starts = windows(shard, 8)
+    step = starts[1]
+    for j in range(4):
+        x = lax.rem(place_ref[X] + j, 4)
+        for flip in range(2):
+            window = (place_ref[ZL] if flip == 0 else 1 - place_ref[ZL]) * 4 + x
+            at = pl.multiple_of(window * step, 8)
+            for rank in range(8):
+                k = lax.rem(rank // 2 + 4 - place_ref[Y], 4) if ringed else rank // 2
+                block = jnp.where(
+                    place_ref[C] == rank % 2, refs[j][flip, k], refs[4 + j][flip, k]
+                ).astype(f32)
+                for source, target, wide in spans[rank]:
+                    out_ref[pl.ds(at, step), target : target + wide] = block[
+                        :step, source : source + wide
+                    ]
+
+                @pl.when(window == 7)
+                def _(block=block, rank=rank):
+                    for source, target, wide in spans[rank]:
+                        out_ref[7 * step + step :, target : target + wide] = block[
+                            step:, source : source + wide
+                        ]
+
+
+def row_total_kernel(place_ref, own_ref, other_ref, out_ref):
+    mine = place_ref[MINE]
+    _, starts = windows(out_ref.shape[0], 16)
+    ends = starts[1:] + [out_ref.shape[0]]
+    for i, (start, end) in enumerate(zip(starts, ends)):
+        block = jnp.where(mine == 1, own_ref[i], other_ref[i])
+        out_ref[start:end, :] = block[: end - start].astype(f32)
+
+
+def attend_kernel(place_ref, tokens_ref, norm_ref, bias_ref, *refs):
+    pieces, (first_ref, qkv_ref, out_ref, top_ref, cols_ref) = refs[:8], refs[8:]
     length = tokens_ref.shape[0]
+    shard = cols_ref.shape[1]
+    zh = place_ref[ZH]
+    for k in range(4):
+        y = lax.rem(place_ref[Y] + k, 4)
+        cols_ref[2 * y + zh] = pieces[k][...]
+        cols_ref[2 * y + 1 - zh] = pieces[4 + k][...]
     gain = norm_ref[0:1, :]
     shift = norm_ref[1:2, :]
     for block in range(length // BLOCK):
         rows = slice(block * BLOCK, (block + 1) * BLOCK)
         first = norm_parts(tokens_ref[rows, :].astype(f32), gain, shift)[0].astype(bf16)
         first_ref[rows, :] = first
-        qkv_ref[rows, :] = (dot(first, cols_ref[...]) + bias_ref[...]).astype(bf16)
+        mixed = bias_ref[...]
+        for g in range(8):
+            mixed = mixed + dot(first[:, g * shard : (g + 1) * shard], cols_ref[g])
+        qkv_ref[rows, :] = mixed.astype(bf16)
     for head in range(SLOTS):
         lanes = slice(head * HEAD_DIM, (head + 1) * HEAD_DIM)
         keys = qkv_ref[:, SLOT_WIDTH + head * HEAD_DIM : SLOT_WIDTH + (head + 1) * HEAD_DIM]
@@ -167,64 +364,8 @@
             top_ref[rows, head : head + 1] = top + jnp.log(total)
 
 
-def branch_kernel(
-    place_ref, slots_ref, own_ref, other_ref, tokens_ref, norm_ref, middle_ref, second_ref, parts_ref, flat_ref
-):
-    c = place_ref[0]
-    shard = own_ref.shape[1]
-    for rank in range(8):
-        wide = STRIDE if rank < 7 else SLOT_WIDTH
-        flat_ref[:, STRIDE * rank : STRIDE * rank + wide] = slots_ref[rank, :, :wide]
-    for rank in range(8):
-        parts_ref[rank] = flat_ref[:, shard * rank : shard * (rank + 1)]
-    total = tokens_ref[...].astype(f32) + norm_ref[4:5, :]
-    for y in range(4):
-        total = total + dot(parts_ref[2 * y + c], own_ref[y])
-        total = total + dot(parts_ref[2 * y + 1 - c], other_ref[y])
-    middle_ref[...] = total
-    second_ref[...] = norm_parts(total, norm_ref[5:6, :], norm_ref[6:7, :])[0].astype(bf16)
-
-
-def branch_back_kernel(
-    place_ref,
-    grad_ref,
-    middle_ref,
-    cot_ref,
-    norm_ref,
-    own_ref,
-    other_ref,
-    grad_middle_ref,
-    branch_ref,
-    slots_ref,
-    sums_ref,
-    parts_ref,
-    flat_ref,
-):
-    c = place_ref[0]
-    shard = own_ref.shape[1]
-    gain = norm_ref[5:6, :]
-    _, normed, factor = norm_parts(middle_ref[...], gain, gain)
-    grad = grad_ref[...].astype(f32)
-    cot = cot_ref[...].astype(f32)
-    grad_middle = cot + norm_back(grad, normed, factor, gain)
-    branch = grad_middle.astype(bf16)
-    grad_middle_ref[...] = grad_middle
-    branch_ref[...] = branch
-    for y in range(4):
-        parts_ref[2 * y + c] = dot_cols(branch, own_ref[y]).astype(bf16)
-        parts_ref[2 * y + 1 - c] = dot_cols(branch, other_ref[y]).astype(bf16)
-    for rank in range(8):
-        flat_ref[:, shard * rank : shard * (rank + 1)] = parts_ref[rank]
-    for rank in range(8):
-        slots_ref[rank] = flat_ref[:, STRIDE * rank : STRIDE * rank + SLOT_WIDTH]
-    sums_ref[0:1, :] = jnp.sum(branch.astype(f32), axis=0, keepdims=True)
-    sums_ref[1:2, :] = jnp.sum(grad * normed, axis=0, keepdims=True)
-    sums_ref[2:3, :] = jnp.sum(grad, axis=0, keepdims=True)
-    sums_ref[3:4, :] = jnp.sum(cot, axis=0, keepdims=True)
-
-
 def hidden_kernel(
-    second_ref, cols_ref, bias_ref, grad_ref, active_ref, hidden_ref, sums_ref, out_ref
+    place_ref, second_ref, cols_ref, bias_ref, grad_ref, active_ref, hidden_ref, sums_ref, out_ref
 ):
     length = second_ref.shape[0]
     sums = jnp.zeros(sums_ref.shape, f32)
@@ -259,7 +400,7 @@
         query = qkv_ref[:, lanes] * bf16(scale)
         grad = grad_ref[:, lanes]
         if head == SLOTS - 1:
-            grad = jnp.where(place_ref[1] == 7, grad, jnp.zeros_like(grad))
+            grad = jnp.where(place_ref[RANK] == 7, grad, jnp.zeros_like(grad))
         top = top_ref[head : head + 1, :]
         delta = dot_cols(ones, grad * out_ref[:, lanes])[0:1, :]
         for block in range(length // BLOCK):
@@ -300,62 +441,6 @@
     sums_ref[1:2, :] = jnp.sum(grad, axis=0, keepdims=True)
 
 
-def column_grad_kernel(left_ref, right_ref, out_ref):
-    shard = left_ref.shape[1] // 8
-    size, starts = windows(shard, 8)
-    grad = dot_rows(left_ref[...], right_ref[...])
-    for y in range(4):
-        for zh in range(2):
-            base = (2 * y + zh) * shard
-            for i, start in enumerate(starts):
-                out_ref[2 * i + zh, y] = grad[base + start : base + start + size].astype(bf16)
-
-
-def row_grad_kernel(left_ref, right_ref, out_ref):
-    size, starts = windows(left_ref.shape[1], 16)
-    grad = dot_rows(left_ref[...], right_ref[...])
-    for i, start in enumerate(starts):
-        out_ref[i] = grad[start : start + size].astype(bf16)
-
-
-def qkv_total_kernel(place_ref, own_ref, other_ref, out_ref):
-    c = place_ref[0]
-    width = out_ref.shape[1] // 3
-    _, starts = windows(out_ref.shape[0], 8)
-    ends = starts[1:] + [out_ref.shape[0]]
-    for i, (start, end) in enumerate(zip(starts, ends)):
-        for rank in range(8):
-            own, other = own_ref[i, rank // 2], other_ref[i, rank // 2]
-            block = jnp.where(c == rank % 2, own, other)[: end - start].astype(f32)
-            wide = STRIDE if rank < 7 else SLOT_WIDTH
-            for part in range(3):
-                lanes = slice(part * width + STRIDE * rank, part * width + STRIDE * rank + wide)
-                out_ref[start:end, lanes] = block[
-                    :, part * SLOT_WIDTH : part * SLOT_WIDTH + wide
-                ]
-
-
-def fc_total_kernel(place_ref, own_ref, other_ref, out_ref):
-    c = place_ref[0]
-    hidden = out_ref.shape[1] // 8
-    _, starts = windows(out_ref.shape[0], 8)
-    ends = starts[1:] + [out_ref.shape[0]]
-    for i, (start, end) in enumerate(zip(starts, ends)):
-        for rank in range(8):
-            own, other = own_ref[i, rank // 2], other_ref[i, rank // 2]
-            block = jnp.where(c == rank % 2, own, other)[: end - start].astype(f32)
-            out_ref[start:end, rank * hidden : (rank + 1) * hidden] = block
-
-
-def row_total_kernel(place_ref, own_ref, other_ref, out_ref):
-    mine = place_ref[2]
-    _, starts = windows(out_ref.shape[0], 16)
-    ends = starts[1:] + [out_ref.shape[0]]
-    for i, (start, end) in enumerate(zip(starts, ends)):
-        block = jnp.where(mine == 1, own_ref[i], other_ref[i])
-        out_ref[start:end, :] = block[: end - start].astype(f32)
-
-
 def after(value, *others):
     return lax.optimization_barrier((value,) + others)[0]
 
@@ -382,27 +467,30 @@
     hidden = w_fc.shape[1] // 8
     length = span * 8
     slots = 3 * SLOT_WIDTH
-    c = lax.axis_index("c")
-    zh = lax.axis_index("zh")
-    rank = lax.axis_index("y") * 2 + c
-    place = jnp.stack([c, rank, (c == zh).astype(jnp.int32)]).astype(jnp.int32)
+    x, zl, c, y, zh = [lax.axis_index(name) for name, _ in LAYOUT]
+    rank = y * 2 + c
+    place = jnp.stack(
+        [y, c, rank, zh, zh * 2 + zl, x, zl, (c == zh).astype(jnp.int32)]
+    ).astype(jnp.int32)
 
     own_tokens = swap_roles(tokens.reshape(span, width))
     small = jnp.concatenate(
         [ln1_gain, ln1_bias, bias_q, bias_v, bias_out, ln2_gain, ln2_bias, bias_proj, bias_fc]
     ).reshape(3, hidden)
+    all_tokens = gather(own_tokens, TEAM).reshape(length, width)
     qkv_parts = call(
-        qkv_columns_kernel, "qkv_columns", struct((8, shard, slots), bf16), place, w_qkv
-    )
+        qkv_columns_kernel,
+        "qkv_columns",
+        [struct((shard, slots), bf16)] * 4,
+        place,
+        w_qkv,
+        scratch=[pltpu.VMEM((4, shard, slots), bf16)],
+    )
+    qkv_own = ring_all(qkv_parts, "y")
+    qkv_other = [flipped(part, "zh") for part in qkv_own]
     small_all = exchange(jnp.broadcast_to(small, (8, 3, hidden)), GRP).astype(f32)
     hidden_bias = lax.dynamic_index_in_dim(small_all, rank, 0, keepdims=False)[2:3]
     vectors = small_all[:, :2].reshape(8, 8, shard).transpose(1, 0, 2).reshape(8, width)
-    all_tokens = gather(own_tokens, TEAM).reshape(length, width)
-    qkv_cols = exchange(qkv_parts, GRP).reshape(width, slots)
-    out_rows = swap_roles(w_out)
-    own_cot = swap_roles(cotangent.reshape(span, width))
-    fc_parts = call(fc_columns_kernel, "fc_columns", struct((4, shard, hidden), bf16), place, w_fc)
-
     bias_slots = jnp.concatenate(
         [
             lax.dynamic_slice_in_dim(vectors[2], STRIDE * rank, SLOT_WIDTH),
@@ -410,14 +498,25 @@
             lax.dynamic_slice_in_dim(vectors[3], STRIDE * rank, SLOT_WIDTH),
         ]
     ).reshape(1, slots)
-    out_rows, own_cot, fc_parts, qkv_cols, all_tokens = lax.optimization_barrier(
-        (out_rows, own_cot, fc_parts, qkv_cols, all_tokens)
-    )
-    out_own = exchange(jnp.broadcast_to(out_rows, (4, shard, width)), "y")
-    all_cot = gather(own_cot, TEAM).reshape(length, width)
-    fc_own = exchange(fc_parts, "y")
-
-    first, qkv, attended_slots, top = call(
+    out_rows = swap_roles(w_out)
+    own_cot = swap_roles(cotangent.reshape(span, width))
+    fc_parts = call(
+        fc_columns_kernel,
+        "fc_columns",
+        [struct((shard, hidden), bf16)] * 4,
+        place,
+        w_fc,
+        scratch=[pltpu.VMEM((4, shard, hidden), bf16)],
+    )
+
+    out_own = ring_all([after(out_rows, *qkv_own)] * 4, "y")
+    out_other = [other_core(part) for part in out_own]
+    all_cot = gather(after(own_cot, all_tokens), TEAM).reshape(length, width)
+    fc_own = ring_all([after(part, *qkv_own) for part in fc_parts], "y")
+    fc_other = [flipped(after(part, *qkv_other), "zh") for part in fc_own]
+    proj_rows = swap_roles(after(w_proj, *fc_other))
+
+    first, qkv, attended_slots, top, qkv_cols = call(
         attend_kernel,
         "attend",
         (
@@ -425,14 +524,17 @@
             struct((length, slots), bf16),
             struct((length, SLOT_WIDTH), bf16),
             struct((length, SLOTS), f32),
+            struct((8, shard, slots), bf16),
         ),
+        after(place, bias_slots, out_rows, own_cot, *fc_own),
         all_tokens,
-        qkv_cols,
         vectors,
         bias_slots,
+        *qkv_own,
+        *qkv_other,
         flops=2 * length * width * slots,
     )
-    out_other = other_core(out_own)
+    qkv_cols = qkv_cols.reshape(width, slots)
     attended = exchange(attended_slots.reshape(8, span, SLOT_WIDTH), TEAM)
     middle, second, attended_parts = call(
         branch_kernel,
@@ -442,23 +544,28 @@
             struct((span, width), bf16),
             struct((8, span, shard), bf16),
         ),
-        place,
+        after(place, *fc_other),
         attended,
-        out_own,
-        out_other,
         own_tokens,
         vectors,
+        *out_own,
+        *out_other,
         scratch=[pltpu.VMEM((span, width), bf16)],
         flops=2 * span * width * width,
     )
 
     second_all = gather(second, TEAM).reshape(length, width)
-    proj_rows = swap_roles(after(w_proj, fc_own))
-    fc_other = lax.ppermute(fc_own, "zh", [(0, 1), (1, 0)])
-    fc_cols = jnp.where(
-        zh == 0, jnp.stack([fc_own, fc_other], 1), jnp.stack([fc_other, fc_own], 1)
+    attended_own = exchange(attended_parts, TEAM)
+    grad_active = dot_cols(after(all_cot, second), proj_rows)
+    fc_cols = call(
+        fc_whole_kernel,
+        "fc_whole",
+        struct((8, shard, hidden), bf16),
+        place,
+        after(fc_own[0], second),
+        *fc_own[1:],
+        *fc_other,
     ).reshape(width, hidden)
-    grad_active = dot_cols(all_cot, proj_rows)
     active, grad_hidden, hidden_sums, second_parts = call(
         hidden_kernel,
         "hidden",
@@ -468,6 +575,7 @@
             struct((1, hidden), f32),
             struct((length, width), bf16),
         ),
+        after(place, attended_own),
         second_all,
         fc_cols,
         hidden_bias,
@@ -475,25 +583,31 @@
         flops=4 * length * width * hidden,
     )
     grad_second = team_sum(second_parts)
-    proj_parts = call(
-        row_grad_kernel,
+    window = windows(shard, 8)[0]
+    fc_grad = call(
+        column_ring_kernel,
+        "fc_grad",
+        [struct((4, 4, window, hidden), bf16)] * 4,
+        place,
+        second_all,
+        grad_hidden,
+        scratch=[pltpu.VMEM((width, hidden), f32)],
+        flops=2 * length * width * hidden,
+    )
+    fc_grad = ring_all(fc_grad, "x")
+    row_window = windows(hidden, 16)[0]
+    proj_grad = call(
+        row_ring_kernel,
         "proj_grad",
-        struct((16, windows(hidden, 16)[0], width), bf16),
+        [struct((4, row_window, width), bf16)] * 4,
+        place,
         active,
         all_cot,
+        scratch=[pltpu.VMEM((hidden, width), f32)],
         flops=2 * length * width * hidden,
     )
-    proj_parts = exchange(proj_parts, REPLICAS)
-    fc_grad = call(
-        column_grad_kernel,
-        "fc_grad",
-        struct((16, 4, windows(shard, 8)[0], hidden), bf16),
-        second_all,
-        grad_hidden,
-        flops=2 * length * width * hidden,
-    )
+    proj_grad = ring_all(proj_grad, Z_RING)
     down_parts = dot(active, proj_rows).astype(bf16)
-    fc_grad = exchange(fc_grad, REPLICAS)
 
     grad_middle, grad_branch, grad_slots, branch_sums = call(
         branch_back_kernel,
@@ -504,18 +618,32 @@
             struct((8, span, SLOT_WIDTH), bf16),
             struct((4, width), f32),
         ),
-        place,
+        after(place, fc_grad[0], proj_grad[0], down_parts),
         grad_second,
         middle,
         own_cot,
         vectors,
-        out_own,
-        out_other,
+        *out_own,
+        *out_other,
         scratch=[pltpu.VMEM((8, span, shard), bf16), pltpu.VMEM((span, width), bf16)],
         flops=2 * span * width * width,
     )
     grad_heads = exchange(grad_slots, TEAM).reshape(length, SLOT_WIDTH)
-    branch_all = gather(after(grad_branch, grad_heads), TEAM).reshape(length, width)
+    down = team_sum(after(down_parts, grad_second))
+    branch_own = ring_all([after(grad_branch, grad_heads)] * 4, "y")
+
+    def fold(which, parts, name, *behind):
+        parts = [after(parts[0], *behind)] + parts[1:]
+        return call(
+            functools.partial(fold_kernel, which),
+            name,
+            [struct(parts[0].shape[1:], bf16)] * 4,
+            place,
+            *parts,
+        )
+
+    fc_grad = ring_all(fold(Z, fc_grad, "fc_fold", grad_slots), Z_RING)
+    proj_grad = ring_all(fold(X, proj_grad, "proj_fold", grad_slots), "x")
     grad_mixed, first_parts, mixed_sums = call(
         attend_back_kernel,
         "attend_back",
@@ -524,7 +652,7 @@
             struct((length, width), bf16),
             struct((1, slots), f32),
         ),
-        place,
+        after(place, fc_grad[0], proj_grad[0]),
         qkv,
         grad_heads,
         attended_slots,
@@ -533,33 +661,16 @@
         scratch=[pltpu.VMEM((length, HEAD_DIM), f32)],
         flops=2 * length * width * slots,
     )
-    grad_first = team_sum(first_parts)
+    grad_first = team_sum(after(first_parts, down))
     qkv_grad = call(
         column_grad_kernel,
         "qkv_grad",
-        struct((16, 4, windows(shard, 8)[0], slots), bf16),
+        struct((16, 4, window, slots), bf16),
         first,
         grad_mixed,
         flops=2 * length * width * slots,
     )
     qkv_grad = exchange(qkv_grad, REPLICAS)
-
-    def replica_sum(parts):
-        return jnp.sum(parts.astype(f32), axis=0).astype(bf16)
-
-    proj_parts = replica_sum(after(proj_parts, grad_mixed))
-    fc_grad = exchange(replica_sum(after(fc_grad, grad_mixed)), "y")
-    attended_own = exchange(after(attended_parts, grad_mixed), TEAM).reshape(length, shard)
-    out_grad = call(
-        row_grad_kernel,
-        "out_grad",
-        struct((16, windows(shard, 16)[0], width), bf16),
-        attended_own,
-        branch_all,
-        flops=2 * length * width * shard,
-    )
-    out_grad = exchange(out_grad, REPLICAS)
-    output = middle + (team_sum(after(down_parts, first_parts)) + vectors[7])
 
     grad_inputs, first_sums = call(
         input_back_kernel,
@@ -570,7 +681,6 @@
         grad_middle,
         vectors,
     )
-    inputs_home = swap_roles(grad_inputs).astype(f32).reshape(1, span, width)
 
     blank = jnp.zeros((1, width), f32)
     at = (0, STRIDE * rank)
@@ -591,35 +701,79 @@
     small_sum = jnp.sum(exchange(jnp.broadcast_to(small_sum, (16, 3, hidden)), REP), axis=0)
     owned = small_sum[:2].reshape(8, shard)
 
+    def replica_sum(parts):
+        return jnp.sum(parts.astype(f32), axis=0).astype(bf16)
+
+    def stacked(parts, name):
+        return call(
+            stack_kernel, name, struct((len(parts),) + parts[0].shape, bf16), *parts
+        )
+
+    def column_spread(parts, name):
+        near = stacked(parts, name + "_near")
+        both = stacked([near, flipped(near, "zl")], name + "_both")
+        own = ring_all([both] * 4, "x")
+        return own + [other_core(part) for part in own]
+
     def row_total(parts, rows, name):
         whole = gather(parts, REPLICAS)
         return call(
             row_total_kernel, name, struct((rows, width), f32), place, whole, other_core(whole)
         )
 
-    proj_total = row_total(proj_parts, hidden, "proj_total")
-    fc_whole = gather(fc_grad, ("zl", "x"))
+    fc_grad = ring_all(fold(Y, fc_grad, "fc_fold_last", grad_mixed), "y")
+    fc_pieces = column_spread(fc_grad, "fc")
+    proj_grad = [after(proj_grad[0], grad_mixed)] + proj_grad[1:]
+    proj_sum = sum(part.astype(f32) for part in proj_grad).astype(bf16)
+    proj_total = row_total(after(proj_sum, grad_first), hidden, "proj_total")
+    branch_own = [after(branch_own[0], grad_mixed)] + branch_own[1:]
+    branch_other = [other_core(part) for part in branch_own]
+    out_grad = call(
+        out_grad_kernel,
+        "out_grad",
+        struct((16, windows(shard, 16)[0], width), bf16),
+        place,
+        attended_own,
+        *branch_own,
+        *branch_other,
+        scratch=[pltpu.VMEM((shard, width), f32)],
+        flops=2 * length * width * shard,
+    )
+    out_grad = exchange(after(out_grad, qkv_grad), REPLICAS)
+    out_total = row_total(replica_sum(out_grad), shard, "out_total")
+
+    fc_spans = [[(0, rank * hidden, hidden)] for rank in range(8)]
     fc_total = call(
-        fc_total_kernel,
+        functools.partial(column_total_kernel, fc_spans, True),
         "fc_total",
         struct((shard, 8 * hidden), f32),
         place,
-        fc_whole,
-        other_core(fc_whole),
-    )
-    qkv_grad = exchange(replica_sum(qkv_grad), "y")
-    qkv_whole = exchange(jnp.broadcast_to(qkv_grad, (8,) + qkv_grad.shape), ("zl", "x"))
-    out_total = row_total(replica_sum(out_grad), shard, "out_total")
+        *fc_pieces,
+    )
+    qkv_sum = replica_sum(after(qkv_grad, grad_inputs))
+    qkv_sum = exchange(qkv_sum, "y")
+    both = stacked([qkv_sum, flipped(qkv_sum, "zl")], "qkv_both")
+    own = ring_all([both] * 4, "x")
+    qkv_pieces = own + [other_core(part) for part in own]
+    qkv_spans = [
+        [
+            (p * SLOT_WIDTH, p * width + STRIDE * r, STRIDE if r < 7 else SLOT_WIDTH)
+            for p in range(3)
+        ]
+        for r in range(8)
+    ]
     qkv_total = call(
-        qkv_total_kernel,
+        functools.partial(column_total_kernel, qkv_spans, False),
         "qkv_total",
         struct((shard, 3 * width), f32),
-        place,
-        qkv_whole,
-        other_core(qkv_whole),
-    )
-
+        after(place, small_sum, grad_inputs),
+        *qkv_pieces,
+    )
+
+    inputs_home = swap_roles(grad_inputs).astype(f32).reshape(1, span, width)
+    output = middle + (down + vectors[7])
     output_home = swap_roles(output.astype(bf16)).reshape(1, span, width)
+
     return (
         output_home,
         inputs_home,

time: 806 us -> 697 us (0.86)
  blocking collectives: 212 us -> 47.5 us
  starting transfers between devices: 131 us -> 171 us
  Pallas kernels: 112 us -> 140 us
  waiting for transfers between devices: 277 us -> 258 us
  local copies, waits for them, and re-layouts: 20.6 us -> 28.7 us
    all_to_all x7 -> x1, blocking collectives: 174 us -> 10.2 us  [exchange(): return lax.all_to_all(parts, axes, 0, 0)]
    ppermute x1 -> x43, waiting for transfers between devices: 44.1 us -> 120 us  [the longest x33 88.8 us: ring(): lax.ppermute(value, axis, [(index[(i + step) % 4], index[i]) for i in ran...]
    all_to_all x9 -> x8, waiting for transfers between devices: 118 us -> 49.5 us  [exchange(): return lax.all_to_all(parts, axes, 0, 0)]
    ppermute x1 -> x43, starting transfers between devices: 15.2 us -> 65.3 us  [the longest x33 49.4 us: ring(): lax.ppermute(value, axis, [(index[(i + step) % 4], index[i]) for i in ran...]
    reduce_scatter x3, waiting for transfers between devices: 46.7 us -> 18 us  [team_sum(): lax.psum_scatter(parts.astype(bf16), TEAM, scatter_dimension=0, tiled=True)]
    pallas_call x16 -> x23, Pallas kernels: 112 us -> 140 us  [call(): pl.pallas_call(kernel, out_shape=out_shape, in_specs=specs, out_specs=out...]
    all_gather x6 -> x4, waiting for transfers between devices: 29.5 us -> 44.1 us  [gather(): return lax.all_gather(block, axes, axis=0)]
    ppermute x6, waiting for transfers between devices: 37 us -> 24.7 us  [swap_roles(): return lax.ppermute(value, ('c', 'zh'), ROLES)]
  transfers between devices with their start and end apart: 30 -> 82, of which waited for: 13 -> 32; matrix products, arithmetic and copies ran while one was open for 5% -> 6% of each run, Pallas kernels for 11% -> 15%
where the time goes in v3:
time: 697 us; the launch traced here: 686 us
  waiting for transfers between devices  258 us (37%)
  starting transfers between devices  171 us (25%)
  Pallas kernels  140 us (20%)
  blocking collectives  47.5 us (7%)
  local copies, waits for them, and re-layouts  28.7 us (4%)
  matrix products  15.5 us (2%)
  between operations  15 us (2%)
  other arithmetic  10.5 us (2%)
    pallas_call x23, Pallas kernels, call(): pl.pallas_call(kernel, out_shape=out_shape, in_specs=specs, out_specs=out...  140 us
    ppermute x33, waiting for transfers between devices, ring(): lax.ppermute(value, axis, [(index[(i + step) % 4], index[i]) for i in ran...  88.8 us
    all_to_all x8, starting transfers between devices, exchange(): return lax.all_to_all(parts, axes, 0, 0)  55.8 us
    all_to_all x8, waiting for transfers between devices, exchange(): return lax.all_to_all(parts, axes, 0, 0)  49.5 us
    ppermute x33, starting transfers between devices, ring(): lax.ppermute(value, axis, [(index[(i + step) % 4], index[i]) for i in ran...  49.4 us
    all_gather x4, waiting for transfers between devices, gather(): return lax.all_gather(block, axes, axis=0)  44.1 us
    all_gather x1, blocking collectives, gather(): return lax.all_gather(block, axes, axis=0)  37.3 us
    ppermute x10, waiting for transfers between devices, flipped(): return lax.ppermute(value, axis, [(0, 1), (1, 0)])  31.4 us
  transfers between devices with their start and end apart: 82, of which 32 were waited for; matrix products, arithmetic and copies ran while one was open for 6% of the time, Pallas kernels for 15%

profile of v3, /device:TPU:17, one launch (start us, length us, event | category | flops | bytes accessed | tf_op | source)
XLA Modules:
  0.0 685.9 jit_solution(2018775689231009017)
XLA Ops:
  33.5 16.9 %all-gather.10.cloned.1.call-done.tokens_ref = bf16[1024,1600]{1,0:T(8,128)(2,1)} async-done(((bf16[128,1600]{1,0:T(8,128)(2,1)}), bf16[1024,1600]{1,0:T(8,128)(2,1)}) %all-gather.10.cloned.1.call-update) | async-done | bytes 3276816 | tf_op jit(solution)/shard_map/all_gather | solution.py:58
  76.8 10.4 %collective-permute-done.2.refs_3_ = bf16[200,768]{1,0:T(8,128)(2,1)S(1)} collective-permute-done((bf16[200,768]{1,0:T(8,128)(2,1)}, bf16[200,768]{1,0:T(8,128)(2,1)S(1)}, u32[]{:S(2)}, u32[]{:S(2)}) %collective-permute-start.2) | collective-permute-done | bytes 307232 | tf_op jit(solution)/shard_map/ppermute | solution.py:34
  128.4 20.3 %all-to-all-done = bf16[8,3,800]{2,1,0:T(4,128)(2,1)S(1)} async-done(((bf16[8,3,800]{2,1,0:T(4,128)(2,1)}), bf16[8,3,800]{2,1,0:T(4,128)(2,1)S(1)}, u32[]{:S(2)}, u32[]{:S(2)}) %all-to-all-start) | async-done | bytes 38432 | tf_op jit(solution)/shard_map/all_to_all | solution.py:54
  157.9 15.5 %attend.1 = (bf16[1024,1600]{1,0:T(8,128)(2,1)}, bf16[1024,768]{1,0:T(8,128)(2,1)}, bf16[1024,256]{1,0:T(8,128)(2,1)}, f32[1024,4]{1,0:T(8,128)}, bf16[8,200,768]{2,1,0:T(8,128)(2,1)}) custom-call(s32[8]{0:T(128)} %stack.39.place_ref, bf16[1024,1600]{1,0:T(8,128)(2,1)} %all-gather.10.cloned.1.call-done.tokens_ref, f32[8,1600]{1,0:T(8,128)} %reshape.102.norm_ref, ...), custom_call_target="tpu_custom_call" | custom-call | flops 2516582400 | bytes 13636640 | tf_op jit(solution)/shard_map/attend/pallas_call | solution.py:114
  182.0 8.9 %collective-permute-done.9.refs_5_ = bf16[200,800]{1,0:T(8,128)(2,1)S(1)} collective-permute-done((bf16[200,800]{1,0:T(8,128)(2,1)}, bf16[200,800]{1,0:T(8,128)(2,1)S(1)}, u32[]{:S(2)}, u32[]{:S(2)}) %collective-permute-start.9) | collective-permute-done | bytes 320032 | tf_op jit(solution)/shard_map/ppermute | solution.py:42
  219.7 13.1 %collective-permute-done.24 = bf16[800,1600]{1,0:T(8,128)(2,1)} collective-permute-done((bf16[800,1600]{1,0:T(8,128)(2,1)S(1)}, bf16[800,1600]{1,0:T(8,128)(2,1)}, u32[]{:S(2)}, u32[]{:S(2)}) %collective-permute-start.24) | collective-permute-done | bytes 2560032 | tf_op jit(solution)/shard_map/ppermute | solution.py:46
  232.7 8.5 %fusion.2.grad_ref = f32[1024,800]{1,0:T(8,128)} fusion(bf16[1024,1600]{1,0:T(8,128)(2,1)} %all-gather.14.cloned.1.call-done.right_ref, bf16[800,1600]{1,0:T(8,128)(2,1)} %collective-permute-done.24), kind=kOutput, calls=%fused_computation.16 | convolution fusion | flops 2621440000 | bytes 9113600 | tf_op jit(solution)/shard_map/dot_general | solution.py:103
  241.2 14.9 %hidden.1 = (bf16[1024,800]{1,0:T(8,128)(2,1)}, bf16[1024,800]{1,0:T(8,128)(2,1)}, f32[1,800]{1,0:T(1,128)}, bf16[1024,1600]{1,0:T(8,128)(2,1)}) custom-call(s32[8]{0:T(128)} %stack.39.place_ref, bf16[1024,1600]{1,0:T(8,128)(2,1)} %all-gather.12.cloned.1.call-done.second_ref.left_ref, bf16[1600,800]{1,0:T(8,128)(2,1)} %bitcast.43, ...), custom_call_target="tpu_custom_call" | custom-call | flops 5242880000 | bytes 15673632 | tf_op jit(solution)/shard_map/hidden/pallas_call | solution.py:114
  256.1 7.4 %proj_grad.1 = (bf16[4,56,1600]{2,1,0:T(8,128)(2,1)}, bf16[4,56,1600]{2,1,0:T(8,128)(2,1)}, bf16[4,56,1600]{2,1,0:T(8,128)(2,1)}, bf16[4,56,1600]{2,1,0:T(8,128)(2,1)}) custom-call(s32[8]{0:T(128)} %stack.39.place_ref, bf16[1024,800]{1,0:T(8,128)(2,1)} %get-tuple-element.122.left_ref, bf16[1024,1600]{1,0:T(8,128)(2,1)} %all-gather.14.cloned.1.call-done.right_ref), custom_call_target="tpu_custom_call" | custom-call | flops 2621440000 | bytes 7782432 | tf_op jit(solution)/shard_map/proj_grad/pallas_call | solution.py:114
  268.1 9.2 %fc_grad.1 = (bf16[4,4,32,800]{3,2,1,0:T(8,128)(2,1)}, bf16[4,4,32,800]{3,2,1,0:T(8,128)(2,1)}, bf16[4,4,32,800]{3,2,1,0:T(8,128)(2,1)}, bf16[4,4,32,800]{3,2,1,0:T(8,128)(2,1)}) custom-call(s32[8]{0:T(128)} %stack.39.place_ref, bf16[1024,1600]{1,0:T(8,128)(2,1)} %all-gather.12.cloned.1.call-done.second_ref.left_ref, ...), custom_call_target="tpu_custom_call" | custom-call | flops 2621440000 | bytes 8192032 | tf_op jit(solution)/shard_map/fc_grad/pallas_call | solution.py:114
  280.3 11.6 %collective-permute-done.29.refs_1_ = bf16[4,56,1600]{2,1,0:T(8,128)(2,1)S(1)} collective-permute-done((bf16[4,56,1600]{2,1,0:T(8,128)(2,1)}, bf16[4,56,1600]{2,1,0:T(8,128)(2,1)S(1)}, u32[]{:S(2)}, u32[]{:S(2)}) %collective-permute-start.29) | collective-permute-done | bytes 716832 | tf_op jit(solution)/shard_map/ppermute | solution.py:34
  309.9 9.6 %all-to-all-start.3 = ((bf16[8,128,256]{2,1,0:T(8,128)(2,1)}), bf16[8,128,256]{2,1,0:T(8,128)(2,1)}, u32[]{:S(2)}, u32[]{:S(2)}) async-start(bf16[8,128,256]{2,1,0:T(8,128)(2,1)} %get-tuple-element.129), calls=%async_computation.5 | async-start | bytes 1048576 | tf_op jit(solution)/shard_map/all_to_all | solution.py:54
  329.8 15.3 %attend_back.1 = (bf16[1024,768]{1,0:T(8,128)(2,1)}, bf16[1024,1600]{1,0:T(8,128)(2,1)}, f32[1,768]{1,0:T(1,128)}) custom-call(s32[8]{0:T(128)} %stack.39.place_ref, bf16[1024,768]{1,0:T(8,128)(2,1)} %get-tuple-element.141.qkv_ref, bf16[1024,256]{1,0:T(8,128)(2,1)} %bitcast.15.grad_ref, bf16[1024,256]{1,0:T(8,128)(2,1)} %get-tuple-element.112.out_ref, ...), custom_call_target="tpu_custom_call" | custom-call | flops 2516582400 | bytes 9948192 | tf_op jit(solution)/shard_map/attend_back/pallas_call | solution.py:114
  360.8 18.0 %reduce-scatter.8.cloned.1.call-done = bf16[128,1600]{1,0:T(8,128)(2,1)} async-done(((bf16[1024,1600]{1,0:T(8,128)(2,1)}), bf16[128,1600]{1,0:T(8,128)(2,1)}) %reduce-scatter.8.cloned.1.call-update) | async-done | bytes 409616 | tf_op jit(solution)/shard_map/reduce_scatter | solution.py:62
  429.1 24.1 %all-to-all-done.6 = bf16[16,4,32,768]{3,2,1,0:T(8,128)(2,1)S(1)} async-done(((bf16[16,4,32,768]{3,2,1,0:T(8,128)(2,1)}), bf16[16,4,32,768]{3,2,1,0:T(8,128)(2,1)S(1)}, u32[]{:S(2)}, u32[]{:S(2)}) %all-to-all-start.6) | async-done | bytes 3145760 | tf_op jit(solution)/shard_map/all_to_all | solution.py:54
  453.1 11.2 %all-to-all-start.8 = ((bf16[16,16,1600]{2,1,0:T(8,128)(2,1)}), bf16[16,16,1600]{2,1,0:T(8,128)(2,1)}, u32[]{:S(2)}, u32[]{:S(2)}) async-start(bf16[16,16,1600]{2,1,0:T(8,128)(2,1)} %out_grad.1), calls=%async_computation.11 | async-start | bytes 1703936 | tf_op jit(solution)/shard_map/all_to_all | solution.py:54
  464.4 11.0 %collective-permute-done.51.refs_3_ = bf16[4,32,800]{2,1,0:T(8,128)(2,1)} collective-permute-done((bf16[4,32,800]{2,1,0:T(8,128)(2,1)}, bf16[4,32,800]{2,1,0:T(8,128)(2,1)}, u32[]{:S(2)}, u32[]{:S(2)}) %collective-permute-start.51) | collective-permute-done | bytes 204832 | tf_op jit(solution)/shard_map/ppermute | solution.py:34
  496.3 27.2 %all-gather.16.cloned.1.call-done = bf16[896,1600]{1,0:T(8,128)(2,1)} async-done(((bf16[56,1600]{1,0:T(8,128)(2,1)}), bf16[896,1600]{1,0:T(8,128)(2,1)}) %all-gather.16.cloned.1.call-update) | async-done | bytes 2867216 | tf_op jit(solution)/shard_map/all_gather | solution.py:58
  538.3 7.6 %collective-permute-done.58.refs_3_ = bf16[2,4,32,800]{3,2,1,0:T(8,128)(2,1)} collective-permute-done((bf16[2,4,32,800]{3,2,1,0:T(8,128)(2,1)}, bf16[2,4,32,800]{3,2,1,0:T(8,128)(2,1)}, u32[]{:S(2)}, u32[]{:S(2)}) %collective-permute-start.58) | collective-permute-done | bytes 409632 | tf_op jit(solution)/shard_map/ppermute | solution.py:34
  546.5 10.2 %collective-permute-done.57.refs_2_ = bf16[2,4,32,800]{3,2,1,0:T(8,128)(2,1)} collective-permute-done((bf16[2,4,32,800]{3,2,1,0:T(8,128)(2,1)}, bf16[2,4,32,800]{3,2,1,0:T(8,128)(2,1)}, u32[]{:S(2)}, u32[]{:S(2)}) %collective-permute-start.57) | collective-permute-done | bytes 409632 | tf_op jit(solution)/shard_map/ppermute | solution.py:34
  558.8 37.3 %all-gather.3 = bf16[256,1600]{1,0:T(8,128)(2,1)} all-gather(bf16[16,1600]{1,0:T(8,128)(2,1)S(1)} %reduce_sum.45), channel_id=5, replica_groups=mesh['x'=4,'zl'=2,'c'=2,'y'=4,'zh'=2] {'zl','x','zh'}, dimensions={0}, use_global_device_ids=true | all-gather | bytes 870400 | tf_op jit(solution)/shard_map/all_gather | solution.py:58
  617.7 10.2 %all_to_all.45 = f32[8,3,800]{2,1,0:T(4,128)S(1)} all-to-all(f32[8,3,800]{2,1,0:T(4,128)S(1)} %pad_maximum_fusion), channel_id=1, replica_groups=mesh['x'=4,'zl'=2,'c'=2,'y'=4,'zh'=2] {'y','zh'}, dimensions={0} | all-to-all | bytes 153600 | tf_op jit(solution)/shard_map/all_to_all | solution.py:54
  644.6 8.9 %fc_total.1 = f32[200,6400]{1,0:T(8,128)} custom-call(s32[8]{0:T(128)} %stack.39.place_ref, bf16[2,4,32,800]{3,2,1,0:T(8,128)(2,1)} %fc_both.1.refs_0_, bf16[2,4,32,800]{3,2,1,0:T(8,128)(2,1)} %collective-permute-done.56.refs_1_, bf16[2,4,32,800]{3,2,1,0:T(8,128)(2,1)} %collective-permute-done.57.refs_2_, ...), custom_call_target="tpu_custom_call" | custom-call | bytes 8396832 | tf_op jit(solution)/shard_map/fc_total/pallas_call | solution.py:114
  664.2 9.1 %qkv_total.1 = f32[200,4800]{1,0:T(8,128)} custom-call(s32[8]{0:T(128)} %stack.39.place_ref, bf16[2,4,32,768]{3,2,1,0:T(8,128)(2,1)} %qkv_both.1.refs_0_, bf16[2,4,32,768]{3,2,1,0:T(8,128)(2,1)} %copy-done.20, bf16[2,4,32,768]{3,2,1,0:T(8,128)(2,1)} %copy-done.19, bf16[2,4,32,768]{3,2,1,0:T(8,128)(2,1)} %copy-done.18, bf16[2,4,32,768]{3,2,1,0:T(8,128)(2,1)} %copy-done.21, ...), custom_call_target="tpu_custom_call" | custom-call | bytes 6985760 | tf_op jit(solution)/shard_map/qkv_total/pallas_call | solution.py:114
  (340 shorter events, 334.4 us)
Async XLA Ops:
  7.2 43.2 %all-gather.10.cloned.1.call-start = ((), (), s32[]{:S(2)}) async-start(), calls=%async_computation.15 | async-start | bytes 3833856 | tf_op jit(solution)/shard_map/all_gather | solution.py:58
  21.2 198.4 %all-gather.14.cloned.1.call-start = ((), (), s32[]{:S(2)}) async-start(), calls=%async_computation.17 | async-start | bytes 3833856 | tf_op jit(solution)/shard_map/all_gather | solution.py:58
  50.4 42.0 %collective-permute-start.14 = (bf16[200,1600]{1,0:T(8,128)(2,1)}, bf16[200,1600]{1,0:T(8,128)(2,1)S(1)}, u32[]{:S(2)}, u32[]{:S(2)}) collective-permute-start(bf16[200,1600]{1,0:T(8,128)(2,1)} %param.21), channel_id=1, source_target_pairs={{0,0},{1,8},{8,1},{9,9},{2,2},{3,10},{10,3},{11,11},{4,4},{5,12},{... | collective-permute-start | bytes 1920008 | tf_op jit(solution)/shard_map/ppermute | solution.py:46
  113.7 42.8 %collective-permute-start.19 = (bf16[200,1600]{1,0:T(8,128)(2,1)S(1)}, bf16[200,1600]{1,0:T(8,128)(2,1)S(1)}, u32[]{:S(2)}, u32[]{:S(2)}) collective-permute-start(bf16[200,1600]{1,0:T(8,128)(2,1)S(1)} %collective-permute-done.14.refs_0_), channel_id=1, source_target_pairs={{6,0},{0,2},{2,4},{4,6},{7,1},{1,3},{3,5},{5,7},{14,8},{8,10},{10,... | collective-permute-start | bytes 1920008 | tf_op jit(solution)/shard_map/ppermute | solution.py:34
  179.4 61.8 %all-gather.12.cloned.1.call-start = ((), (), s32[]{:S(2)}) async-start(), calls=%async_computation.16 | async-start | bytes 3833856 | tf_op jit(solution)/shard_map/all_gather | solution.py:58
  209.4 91.5 %reduce-scatter.4.cloned.1.call-start = ((), (), s32[]{:S(2)}) async-start(), calls=%async_computation.12 | async-start | bytes 3833856 | tf_op jit(solution)/shard_map/reduce_scatter | solution.py:62
  263.5 58.0 %collective-permute-start.30 = (bf16[4,56,1600]{2,1,0:T(8,128)(2,1)}, bf16[4,56,1600]{2,1,0:T(8,128)(2,1)}, u32[]{:S(2)}, u32[]{:S(2)}) collective-permute-start(bf16[4,56,1600]{2,1,0:T(8,128)(2,1)} %get-tuple-element.137), channel_id=1, source_target_pairs={{1,0},{17,16},{0,1},{16,17},{3,2},{19,18},{2,3},{18,19},{5,4},{21,... | collective-permute-start | bytes 2150408 | tf_op jit(solution)/shard_map/ppermute | solution.py:34
  268.1 53.4 %collective-permute-start.31 = (bf16[4,56,1600]{2,1,0:T(8,128)(2,1)}, bf16[4,56,1600]{2,1,0:T(8,128)(2,1)}, u32[]{:S(2)}, u32[]{:S(2)}) collective-permute-start(bf16[4,56,1600]{2,1,0:T(8,128)(2,1)} %get-tuple-element.138), channel_id=1, source_target_pairs={{17,0},{0,16},{16,1},{1,17},{19,2},{2,18},{18,3},{3,19},{21,4},{4,... | collective-permute-start | bytes 2150408 | tf_op jit(solution)/shard_map/ppermute | solution.py:34
  277.3 47.1 %collective-permute-start.26 = (bf16[4,4,32,800]{3,2,1,0:T(8,128)(2,1)}, bf16[4,4,32,800]{3,2,1,0:T(8,128)(2,1)S(1)}, u32[]{:S(2)}, u32[]{:S(2)}) collective-permute-start(bf16[4,4,32,800]{3,2,1,0:T(8,128)(2,1)} %get-tuple-element.131), channel_id=1, source_target_pairs={{32,0},{64,32},{96,64},{0,96},{33,1},{65,33},{97,65},{1,97},{34,2}... | collective-permute-start | bytes 2457608 | tf_op jit(solution)/shard_map/ppermute | solution.py:34
  279.8 44.7 %collective-permute-start.27 = (bf16[4,4,32,800]{3,2,1,0:T(8,128)(2,1)}, bf16[4,4,32,800]{3,2,1,0:T(8,128)(2,1)S(1)}, u32[]{:S(2)}, u32[]{:S(2)}) collective-permute-start(bf16[4,4,32,800]{3,2,1,0:T(8,128)(2,1)} %get-tuple-element.132), channel_id=1, source_target_pairs={{64,0},{96,32},{0,64},{32,96},{65,1},{97,33},{1,65},{33,97},{66,2}... | collective-permute-start | bytes 2457608 | tf_op jit(solution)/shard_map/ppermute | solution.py:34
  319.5 59.3 %reduce-scatter.8.cloned.1.call-start = ((), (), s32[]{:S(2)}) async-start(), calls=%async_computation.14 | async-start | bytes 3833856 | tf_op jit(solution)/shard_map/reduce_scatter | solution.py:62
  345.2 178.3 %all-gather.16.cloned.1.call-start = ((), (), s32[]{:S(2)}) async-start(), calls=%async_computation.18 | async-start | bytes 3168256 | tf_op jit(solution)/shard_map/all_gather | solution.py:58
  380.8 221.2 %reduce-scatter.6.cloned.1.call-start = ((), (), s32[]{:S(2)}) async-start(), calls=%async_computation.13 | async-start | bytes 3833856 | tf_op jit(solution)/shard_map/reduce_scatter | solution.py:62
  388.5 64.6 %all-to-all-start.6 = ((bf16[16,4,32,768]{3,2,1,0:T(8,128)(2,1)}), bf16[16,4,32,768]{3,2,1,0:T(8,128)(2,1)S(1)}, u32[]{:S(2)}, u32[]{:S(2)}) async-start(bf16[16,4,32,768]{3,2,1,0:T(8,128)(2,1)} %qkv_grad.1), calls=%async_computation.9 | async-start | bytes 6291456 | tf_op jit(solution)/shard_map/all_to_all | solution.py:54
  418.8 45.5 %collective-permute-start.49 = (bf16[4,32,800]{2,1,0:T(8,128)(2,1)}, bf16[4,32,800]{2,1,0:T(8,128)(2,1)}, u32[]{:S(2)}, u32[]{:S(2)}) collective-permute-start(bf16[4,32,800]{2,1,0:T(8,128)(2,1)} %get-tuple-element.161), channel_id=1, source_target_pairs={{16,0},{1,16},{17,1},{0,17},{18,2},{3,18},{19,3},{2,19},{20,4},{5,... | collective-permute-start | bytes 614408 | tf_op jit(solution)/shard_map/ppermute | solution.py:34
  421.3 43.0 %collective-permute-start.50 = (bf16[4,32,800]{2,1,0:T(8,128)(2,1)}, bf16[4,32,800]{2,1,0:T(8,128)(2,1)}, u32[]{:S(2)}, u32[]{:S(2)}) collective-permute-start(bf16[4,32,800]{2,1,0:T(8,128)(2,1)} %get-tuple-element.162), channel_id=1, source_target_pairs={{1,0},{17,16},{0,1},{16,17},{3,2},{19,18},{2,3},{18,19},{5,4},{21,... | collective-permute-start | bytes 614408 | tf_op jit(solution)/shard_map/ppermute | solution.py:34
  422.9 52.5 %collective-permute-start.51 = (bf16[4,32,800]{2,1,0:T(8,128)(2,1)}, bf16[4,32,800]{2,1,0:T(8,128)(2,1)}, u32[]{:S(2)}, u32[]{:S(2)}) collective-permute-start(bf16[4,32,800]{2,1,0:T(8,128)(2,1)} %get-tuple-element.163), channel_id=1, source_target_pairs={{17,0},{0,16},{16,1},{1,17},{19,2},{2,18},{18,3},{3,19},{21,4},{4,... | collective-permute-start | bytes 614408 | tf_op jit(solution)/shard_map/ppermute | solution.py:34
  453.1 104.4 %all-to-all-start.8 = ((bf16[16,16,1600]{2,1,0:T(8,128)(2,1)}), bf16[16,16,1600]{2,1,0:T(8,128)(2,1)}, u32[]{:S(2)}, u32[]{:S(2)}) async-start(bf16[16,16,1600]{2,1,0:T(8,128)(2,1)} %out_grad.1), calls=%async_computation.11 | async-start | bytes 1703936 | tf_op jit(solution)/shard_map/all_to_all | solution.py:54
  523.5 149.9 %collective-permute-start.66 = (bf16[16,56,1600]{2,1,0:T(8,128)(2,1)}, bf16[16,56,1600]{2,1,0:T(8,128)(2,1)}, u32[]{:S(2)}, u32[]{:S(2)}) collective-permute-start(bf16[16,56,1600]{2,1,0:T(8,128)(2,1)} %bitcast.41), channel_id=1, source_target_pairs={{0,8},{8,0},{1,9},{9,1},{2,10},{10,2},{3,11},{11,3},{4,12},{12,4},... | collective-permute-start | bytes 8601608 | tf_op jit(solution)/shard_map/ppermute | solution.py:50
  536.0 60.2 %collective-permute-start.59 = (bf16[2,4,32,800]{3,2,1,0:T(8,128)(2,1)}, bf16[2,4,32,800]{3,2,1,0:T(8,128)(2,1)}, u32[]{:S(2)}, u32[]{:S(2)}) collective-permute-start(bf16[2,4,32,800]{3,2,1,0:T(8,128)(2,1)} %fc_both.1.refs_0_), channel_id=1, source_target_pairs={{0,8},{8,0},{1,9},{9,1},{2,10},{10,2},{3,11},{11,3},{4,12},{12,4},... | collective-permute-start | bytes 1228808 | tf_op jit(solution)/shard_map/ppermute | solution.py:50
  537.4 76.4 %collective-permute-start.56 = (bf16[2,4,32,800]{3,2,1,0:T(8,128)(2,1)}, bf16[2,4,32,800]{3,2,1,0:T(8,128)(2,1)}, u32[]{:S(2)}, u32[]{:S(2)}) collective-permute-start(bf16[2,4,32,800]{3,2,1,0:T(8,128)(2,1)} %fc_both.1.refs_0_), channel_id=1, source_target_pairs={{32,0},{64,32},{96,64},{0,96},{33,1},{65,33},{97,65},{1,97},{34,2}... | collective-permute-start | bytes 1228808 | tf_op jit(solution)/shard_map/ppermute | solution.py:34
  546.0 68.4 %collective-permute-start.62 = (bf16[2,4,32,800]{3,2,1,0:T(8,128)(2,1)}, bf16[2,4,32,800]{3,2,1,0:T(8,128)(2,1)}, u32[]{:S(2)}, u32[]{:S(2)}) collective-permute-start(bf16[2,4,32,800]{3,2,1,0:T(8,128)(2,1)} %collective-permute-done.58.refs_3_), channel_id=1, source_target_pairs={{0,8},{8,0},{1,9},{9,1},{2,10},{10,2},{3,11},{11,3},{4,12},{12,4},... | collective-permute-start | bytes 1228808 | tf_op jit(solution)/shard_map/ppermute | solution.py:50
  556.8 60.8 %collective-permute-start.61 = (bf16[2,4,32,800]{3,2,1,0:T(8,128)(2,1)}, bf16[2,4,32,800]{3,2,1,0:T(8,128)(2,1)}, u32[]{:S(2)}, u32[]{:S(2)}) collective-permute-start(bf16[2,4,32,800]{3,2,1,0:T(8,128)(2,1)} %collective-permute-done.57.refs_2_), channel_id=1, source_target_pairs={{0,8},{8,0},{1,9},{9,1},{2,10},{10,2},{3,11},{11,3},{4,12},{12,4},... | collective-permute-start | bytes 1228808 | tf_op jit(solution)/shard_map/ppermute | solution.py:50
  596.2 44.9 %collective-permute-start.48 = (bf16[16,16,1600]{2,1,0:T(8,128)(2,1)}, bf16[16,16,1600]{2,1,0:T(8,128)(2,1)}, u32[]{:S(2)}, u32[]{:S(2)}) collective-permute-start(bf16[16,16,1600]{2,1,0:T(8,128)(2,1)} %bitcast.25.own_ref), channel_id=1, source_target_pairs={{0,8},{8,0},{1,9},{9,1},{2,10},{10,2},{3,11},{11,3},{4,12},{12,4},... | collective-permute-start | bytes 2457608 | tf_op jit(solution)/shard_map/ppermute | solution.py:50
  (115 other events, 2810.1 us)
Sparse Core Ops, SparseCore 0:
  21.2 29.1 all-gather.9
  52.1 41.2 all-gather.13
  197.5 33.9 all-gather.11
  256.3 34.1 reduce-scatter.3
  345.3 33.4 reduce-scatter.7
  380.9 142.5 all-gather.15
  526.5 39.9 reduce-scatter.5

commit v4 on v3

--- a/solution.py
+++ b/solution.py
@@ -477,7 +477,9 @@
     small = jnp.concatenate(
         [ln1_gain, ln1_bias, bias_q, bias_v, bias_out, ln2_gain, ln2_bias, bias_proj, bias_fc]
     ).reshape(3, hidden)
+    small_all = exchange(jnp.broadcast_to(small, (8, 3, hidden)), GRP)
     all_tokens = gather(own_tokens, TEAM).reshape(length, width)
+    place = after(place, small_all)
     qkv_parts = call(
         qkv_columns_kernel,
         "qkv_columns",
@@ -488,7 +490,20 @@
     )
     qkv_own = ring_all(qkv_parts, "y")
     qkv_other = [flipped(part, "zh") for part in qkv_own]
-    small_all = exchange(jnp.broadcast_to(small, (8, 3, hidden)), GRP).astype(f32)
+    out_rows = swap_roles(after(w_out, small_all))
+    own_cot = swap_roles(after(cotangent, qkv_parts[0]).reshape(span, width))
+    place = after(place, qkv_parts[0])
+    fc_parts = call(
+        fc_columns_kernel,
+        "fc_columns",
+        [struct((shard, hidden), bf16)] * 4,
+        place,
+        w_fc,
+        scratch=[pltpu.VMEM((4, shard, hidden), bf16)],
+    )
+    place = after(place, fc_parts[0])
+
+    small_all = small_all.astype(f32)
     hidden_bias = lax.dynamic_index_in_dim(small_all, rank, 0, keepdims=False)[2:3]
     vectors = small_all[:, :2].reshape(8, 8, shard).transpose(1, 0, 2).reshape(8, width)
     bias_slots = jnp.concatenate(
@@ -498,23 +513,13 @@
             lax.dynamic_slice_in_dim(vectors[3], STRIDE * rank, SLOT_WIDTH),
         ]
     ).reshape(1, slots)
-    out_rows = swap_roles(w_out)
-    own_cot = swap_roles(cotangent.reshape(span, width))
-    fc_parts = call(
-        fc_columns_kernel,
-        "fc_columns",
-        [struct((shard, hidden), bf16)] * 4,
-        place,
-        w_fc,
-        scratch=[pltpu.VMEM((4, shard, hidden), bf16)],
-    )
 
     out_own = ring_all([after(out_rows, *qkv_own)] * 4, "y")
     out_other = [other_core(part) for part in out_own]
-    all_cot = gather(after(own_cot, all_tokens), TEAM).reshape(length, width)
-    fc_own = ring_all([after(part, *qkv_own) for part in fc_parts], "y")
-    fc_other = [flipped(after(part, *qkv_other), "zh") for part in fc_own]
-    proj_rows = swap_roles(after(w_proj, *fc_other))
+    all_cot = gather(after(own_cot, *qkv_own), TEAM).reshape(length, width)
+    proj_rows = swap_roles(after(w_proj, *qkv_other))
+    fc_own = ring_all([after(part, *out_own) for part in fc_parts], "y")
+    fc_other = [flipped(after(part, proj_rows), "zh") for part in fc_own]
 
     first, qkv, attended_slots, top, qkv_cols = call(
         attend_kernel,
@@ -526,7 +531,7 @@
             struct((length, SLOTS), f32),
             struct((8, shard, slots), bf16),
         ),
-        after(place, bias_slots, out_rows, own_cot, *fc_own),
+        after(place, bias_slots),
         all_tokens,
         vectors,
         bias_slots,
@@ -544,7 +549,7 @@
             struct((span, width), bf16),
             struct((8, span, shard), bf16),
         ),
-        after(place, *fc_other),
+        after(place, proj_rows, *fc_own),
         attended,
         own_tokens,
         vectors,
@@ -670,8 +675,30 @@
         grad_mixed,
         flops=2 * length * width * slots,
     )
+    place = after(place, qkv_grad)
     qkv_grad = exchange(qkv_grad, REPLICAS)
 
+    def replica_sum(parts):
+        return jnp.sum(parts.astype(f32), axis=0).astype(bf16)
+
+    def stacked(parts, name):
+        return call(
+            stack_kernel, name, struct((len(parts),) + parts[0].shape, bf16), *parts
+        )
+
+    def column_spread(near, name):
+        both = stacked([near, flipped(near, "zl")], name + "_both")
+        own = ring_all([both] * 4, "x")
+        return own + [other_core(part) for part in own]
+
+    def row_total(whole, rows, name):
+        return call(
+            row_total_kernel, name, struct((rows, width), f32), place, whole, other_core(whole)
+        )
+
+    fc_grad = ring_all(fold(Y, fc_grad, "fc_fold_last", place), "y")
+    proj_grad = [after(proj_grad[0], place)] + proj_grad[1:]
+    proj_sum = sum(part.astype(f32) for part in proj_grad).astype(bf16)
     grad_inputs, first_sums = call(
         input_back_kernel,
         "input_back",
@@ -679,54 +706,15 @@
         grad_first,
         own_tokens,
         grad_middle,
-        vectors,
-    )
-
-    blank = jnp.zeros((1, width), f32)
-    at = (0, STRIDE * rank)
-    small_terms = jnp.concatenate(
-        [
-            first_sums,
-            lax.dynamic_update_slice(blank, mixed_sums[:, :SLOT_WIDTH], at),
-            lax.dynamic_update_slice(blank, mixed_sums[:, 2 * SLOT_WIDTH :], at),
-            branch_sums,
-        ]
-    )
-    hidden_term = lax.dynamic_update_slice(
-        jnp.zeros((8, hidden), f32), hidden_sums, (rank, 0)
-    )
-    small_terms = small_terms.reshape(8, 8, shard).transpose(1, 0, 2).reshape(8, 2, hidden)
-    small_terms = jnp.concatenate([small_terms, hidden_term[:, None]], axis=1)
-    small_sum = jnp.sum(exchange(small_terms, GRP), axis=0)
-    small_sum = jnp.sum(exchange(jnp.broadcast_to(small_sum, (16, 3, hidden)), REP), axis=0)
-    owned = small_sum[:2].reshape(8, shard)
-
-    def replica_sum(parts):
-        return jnp.sum(parts.astype(f32), axis=0).astype(bf16)
-
-    def stacked(parts, name):
-        return call(
-            stack_kernel, name, struct((len(parts),) + parts[0].shape, bf16), *parts
-        )
-
-    def column_spread(parts, name):
-        near = stacked(parts, name + "_near")
-        both = stacked([near, flipped(near, "zl")], name + "_both")
-        own = ring_all([both] * 4, "x")
-        return own + [other_core(part) for part in own]
-
-    def row_total(parts, rows, name):
-        whole = gather(parts, REPLICAS)
-        return call(
-            row_total_kernel, name, struct((rows, width), f32), place, whole, other_core(whole)
-        )
-
-    fc_grad = ring_all(fold(Y, fc_grad, "fc_fold_last", grad_mixed), "y")
-    fc_pieces = column_spread(fc_grad, "fc")
-    proj_grad = [after(proj_grad[0], grad_mixed)] + proj_grad[1:]
-    proj_sum = sum(part.astype(f32) for part in proj_grad).astype(bf16)
-    proj_total = row_total(after(proj_sum, grad_first), hidden, "proj_total")
-    branch_own = [after(branch_own[0], grad_mixed)] + branch_own[1:]
+        after(vectors, fc_grad[0], proj_sum),
+    )
+    inputs_home = swap_roles(grad_inputs).astype(f32).reshape(1, span, width)
+    output = middle + (after(down, grad_inputs) + vectors[7])
+    output_home = swap_roles(output.astype(bf16)).reshape(1, span, width)
+    proj_whole = gather(after(proj_sum, grad_first), REPLICAS)
+    place = after(place, grad_inputs)
+    fc_pieces = column_spread(stacked([after(fc_grad[0], place)] + fc_grad[1:], "fc_near"), "fc")
+
     branch_other = [other_core(part) for part in branch_own]
     out_grad = call(
         out_grad_kernel,
@@ -739,22 +727,45 @@
         scratch=[pltpu.VMEM((shard, width), f32)],
         flops=2 * length * width * shard,
     )
-    out_grad = exchange(after(out_grad, qkv_grad), REPLICAS)
-    out_total = row_total(replica_sum(out_grad), shard, "out_total")
+    place = after(place, out_grad)
+    qkv_sum = exchange(replica_sum(after(qkv_grad, place)), "y")
+    out_grad = exchange(after(out_grad, qkv_sum), REPLICAS)
+    qkv_pieces = column_spread(qkv_sum, "qkv")
+
+    blank = jnp.zeros((1, width), f32)
+    at = (0, STRIDE * rank)
+    small_terms = jnp.concatenate(
+        [
+            first_sums,
+            lax.dynamic_update_slice(blank, mixed_sums[:, :SLOT_WIDTH], at),
+            lax.dynamic_update_slice(blank, mixed_sums[:, 2 * SLOT_WIDTH :], at),
+            branch_sums,
+        ]
+    )
+    hidden_term = lax.dynamic_update_slice(
+        jnp.zeros((8, hidden), f32), hidden_sums, (rank, 0)
+    )
+    small_terms = small_terms.reshape(8, 8, shard).transpose(1, 0, 2).reshape(8, 2, hidden)
+    small_terms = jnp.concatenate([small_terms, hidden_term[:, None]], axis=1)
+    small_sum = jnp.sum(exchange(after(small_terms, out_grad), GRP), axis=0)
+    out_sum = replica_sum(out_grad)
+    out_whole = exchange(
+        after(jnp.broadcast_to(out_sum, (16,) + out_sum.shape), small_sum), REPLICAS
+    )
+    small_sum = jnp.broadcast_to(after(small_sum, out_whole), (16, 3, hidden))
+    small_sum = jnp.sum(exchange(small_sum, REP), axis=0)
+    owned = small_sum[:2].reshape(8, shard)
 
     fc_spans = [[(0, rank * hidden, hidden)] for rank in range(8)]
     fc_total = call(
         functools.partial(column_total_kernel, fc_spans, True),
         "fc_total",
         struct((shard, 8 * hidden), f32),
-        place,
+        after(place, qkv_sum),
         *fc_pieces,
     )
-    qkv_sum = replica_sum(after(qkv_grad, grad_inputs))
-    qkv_sum = exchange(qkv_sum, "y")
-    both = stacked([qkv_sum, flipped(qkv_sum, "zl")], "qkv_both")
-    own = ring_all([both] * 4, "x")
-    qkv_pieces = own + [other_core(part) for part in own]
+    proj_total = row_total(proj_whole, hidden, "proj_total")
+    out_total = row_total(out_whole, shard, "out_total")
     qkv_spans = [
         [
             (p * SLOT_WIDTH, p * width + STRIDE * r, STRIDE if r < 7 else SLOT_WIDTH)
@@ -766,14 +777,9 @@
         functools.partial(column_total_kernel, qkv_spans, False),
         "qkv_total",
         struct((shard, 3 * width), f32),
-        after(place, small_sum, grad_inputs),
+        after(place, fc_total),
         *qkv_pieces,
     )
-
-    inputs_home = swap_roles(grad_inputs).astype(f32).reshape(1, span, width)
-    output = middle + (down + vectors[7])
-    output_home = swap_roles(output.astype(bf16)).reshape(1, span, width)
-
     return (
         output_home,
         inputs_home,

time: 697 us -> 720 us (1.033)
  waiting for transfers between devices: 258 us -> 323 us
  blocking collectives: 47.5 us -> 0 us
    ppermute x33, waiting for transfers between devices: 88.8 us -> 144 us  [ring(): lax.ppermute(value, axis, [(index[(i + step) % 4], index[i]) for i in ran...]
    all_gather x1 -> x0, blocking collectives: 37.3 us -> none  [gather(): return lax.all_gather(block, axes, axis=0)]
    all_to_all x8 -> x10, waiting for transfers between devices: 49.5 us -> 22.5 us  [exchange(): return lax.all_to_all(parts, axes, 0, 0)]
    reduce_scatter x3, waiting for transfers between devices: 18 us -> 44 us  [team_sum(): lax.psum_scatter(parts.astype(bf16), TEAM, scatter_dimension=0, tiled=True)]
    ppermute x6, waiting for transfers between devices: 24.7 us -> 41 us  [swap_roles(): return lax.ppermute(value, ('c', 'zh'), ROLES)]
    all_to_all x1 -> x0, blocking collectives: 10.2 us -> none  [exchange(): return lax.all_to_all(parts, axes, 0, 0)]
    ppermute x33, starting transfers between devices: 49.4 us -> 41.5 us  [ring(): lax.ppermute(value, axis, [(index[(i + step) % 4], index[i]) for i in ran...]
    all_gather x4, waiting for transfers between devices: 44.1 us -> 36.6 us  [gather(): return lax.all_gather(block, axes, axis=0)]
  transfers between devices with their start and end apart: 82 -> 84, of which waited for: 32 -> 35; matrix products, arithmetic and copies ran while one was open for 6% -> 7% of each run, Pallas kernels for 15% -> 17%
where the time goes in v4:
time: 720 us; the launch traced here: 706 us
  waiting for transfers between devices  323 us (45%)
  starting transfers between devices  165 us (23%)
  Pallas kernels  140 us (19%)
  local copies, waits for them, and re-layouts  34.3 us (5%)
  matrix products  15.6 us (2%)
  between operations  15.1 us (2%)
  other arithmetic  12.3 us (2%)
    ppermute x33, waiting for transfers between devices, ring(): lax.ppermute(value, axis, [(index[(i + step) % 4], index[i]) for i in ran...  144 us
    pallas_call x23, Pallas kernels, call(): pl.pallas_call(kernel, out_shape=out_shape, in_specs=specs, out_specs=out...  140 us
    all_to_all x10, starting transfers between devices, exchange(): return lax.all_to_all(parts, axes, 0, 0)  62.1 us
    reduce_scatter x3, waiting for transfers between devices, team_sum(): lax.psum_scatter(parts.astype(bf16), TEAM, scatter_dimension=0, tiled=True)  44 us
    ppermute x33, starting transfers between devices, ring(): lax.ppermute(value, axis, [(index[(i + step) % 4], index[i]) for i in ran...  41.5 us
    ppermute x6, waiting for transfers between devices, swap_roles(): return lax.ppermute(value, ('c', 'zh'), ROLES)  41 us
    all_gather x4, waiting for transfers between devices, gather(): return lax.all_gather(block, axes, axis=0)  36.6 us
    ppermute x10, waiting for transfers between devices, flipped(): return lax.ppermute(value, axis, [(0, 1), (1, 0)])  35.5 us
  transfers between devices with their start and end apart: 84, of which 35 were waited for; matrix products, arithmetic and copies ran while one was open for 7% of the time, Pallas kernels for 17%

profile of v4, /device:TPU:17, one launch (start us, length us, event | category | flops | bytes accessed | tf_op | source)
XLA Modules:
  0.0 706.2 jit_solution(12878612214024478240)
XLA Ops:
  103.6 35.2 %collective-permute-done.8.refs_0_ = bf16[200,1600]{1,0:T(8,128)(2,1)S(1)} collective-permute-done((bf16[200,1600]{1,0:T(8,128)(2,1)S(1)}, bf16[200,1600]{1,0:T(8,128)(2,1)S(1)}, u32[]{:S(2)}, u32[]{:S(2)}) %collective-permute-start.8) | collective-permute-done | bytes 640032 | tf_op jit(solution)/shard_map/ppermute | solution.py:46
  152.9 10.8 %collective-permute-done.10.refs_2_ = bf16[200,1600]{1,0:T(8,128)(2,1)S(1)} collective-permute-done((bf16[200,1600]{1,0:T(8,128)(2,1)S(1)}, bf16[200,1600]{1,0:T(8,128)(2,1)S(1)}, u32[]{:S(2)}, u32[]{:S(2)}) %collective-permute-start.10) | collective-permute-done | bytes 640032 | tf_op jit(solution)/shard_map/ppermute | solution.py:34
  177.4 15.5 %attend.1 = (bf16[1024,1600]{1,0:T(8,128)(2,1)}, bf16[1024,768]{1,0:T(8,128)(2,1)}, bf16[1024,256]{1,0:T(8,128)(2,1)}, f32[1024,4]{1,0:T(8,128)}, bf16[8,200,768]{2,1,0:T(8,128)(2,1)}) custom-call(s32[8]{0:T(128)} %stack.39.place_ref, bf16[1024,1600]{1,0:T(8,128)(2,1)} %all-gather.9.cloned.1.call-done.tokens_ref, f32[8,1600]{1,0:T(8,128)} %reshape.101.norm_ref, ...), custom_call_target="tpu_custom_call" | custom-call | flops 2516582400 | bytes 13636640 | tf_op jit(solution)/shard_map/attend/pallas_call | solution.py:114
  199.6 6.9 all-to-all-done.1.slots_ref
  220.5 8.0 %all-to-all-start.2 = ((bf16[8,128,200]{1,2,0:T(8,128)(2,1)}), bf16[8,128,200]{1,2,0:T(8,128)(2,1)S(1)}, u32[]{:S(2)}, u32[]{:S(2)}) async-start(bf16[8,128,200]{1,2,0:T(8,128)(2,1)} %copy.70), calls=%async_computation.2 | async-start | bytes 819200 | tf_op jit(solution)/shard_map/all_to_all | solution.py:54
  228.9 8.6 %fusion.2.grad_ref = f32[1024,800]{1,0:T(8,128)} fusion(bf16[1024,1600]{1,0:T(8,128)(2,1)} %all-gather.13.cloned.1.call-done.right_ref, bf16[800,1600]{1,0:T(8,128)(2,1)} %collective-permute-done.7), kind=kOutput, calls=%fused_computation.16 | convolution fusion | flops 2621440000 | bytes 9113600 | tf_op jit(solution)/shard_map/dot_general | solution.py:103
  238.7 7.7 %collective-permute-done.23.refs_7_ = bf16[200,800]{1,0:T(8,128)(2,1)S(1)} collective-permute-done((bf16[200,800]{1,0:T(8,128)(2,1)}, bf16[200,800]{1,0:T(8,128)(2,1)S(1)}, u32[]{:S(2)}, u32[]{:S(2)}) %collective-permute-start.23) | collective-permute-done | bytes 320032 | tf_op jit(solution)/shard_map/ppermute | solution.py:42
  250.7 14.8 %hidden.1 = (bf16[1024,800]{1,0:T(8,128)(2,1)}, bf16[1024,800]{1,0:T(8,128)(2,1)}, f32[1,800]{1,0:T(1,128)}, bf16[1024,1600]{1,0:T(8,128)(2,1)}) custom-call(s32[8]{0:T(128)} %stack.39.place_ref, bf16[1024,1600]{1,0:T(8,128)(2,1)} %all-gather.11.cloned.1.call-done.second_ref.left_ref, bf16[1600,800]{1,0:T(8,128)(2,1)} %bitcast.42, ...), custom_call_target="tpu_custom_call" | custom-call | flops 5242880000 | bytes 15673632 | tf_op jit(solution)/shard_map/hidden/pallas_call | solution.py:114
  266.9 7.0 convolution_convert_fusion
  274.0 25.2 %reduce-scatter.4.cloned.1.call-done = bf16[128,1600]{1,0:T(8,128)(2,1)} async-done(((bf16[1024,1600]{1,0:T(8,128)(2,1)}), bf16[128,1600]{1,0:T(8,128)(2,1)}) %reduce-scatter.4.cloned.1.call-update) | async-done | bytes 409616 | tf_op jit(solution)/shard_map/reduce_scatter | solution.py:62
  301.2 7.4 %proj_grad.1 = (bf16[4,56,1600]{2,1,0:T(8,128)(2,1)}, bf16[4,56,1600]{2,1,0:T(8,128)(2,1)}, bf16[4,56,1600]{2,1,0:T(8,128)(2,1)}, bf16[4,56,1600]{2,1,0:T(8,128)(2,1)}) custom-call(s32[8]{0:T(128)} %stack.39.place_ref, bf16[1024,800]{1,0:T(8,128)(2,1)} %get-tuple-element.141.left_ref, bf16[1024,1600]{1,0:T(8,128)(2,1)} %all-gather.13.cloned.1.call-done.right_ref), custom_call_target="tpu_custom_call" | custom-call | flops 2621440000 | bytes 7782432 | tf_op jit(solution)/shard_map/proj_grad/pallas_call | solution.py:114
  311.3 9.1 %fc_grad.1 = (bf16[4,4,32,800]{3,2,1,0:T(8,128)(2,1)}, bf16[4,4,32,800]{3,2,1,0:T(8,128)(2,1)}, bf16[4,4,32,800]{3,2,1,0:T(8,128)(2,1)}, bf16[4,4,32,800]{3,2,1,0:T(8,128)(2,1)}) custom-call(s32[8]{0:T(128)} %stack.39.place_ref, bf16[1024,1600]{1,0:T(8,128)(2,1)} %all-gather.11.cloned.1.call-done.second_ref.left_ref, ...), custom_call_target="tpu_custom_call" | custom-call | flops 2621440000 | bytes 8192032 | tf_op jit(solution)/shard_map/fc_grad/pallas_call | solution.py:114
  324.3 19.3 %collective-permute-done.28.refs_1_ = bf16[4,56,1600]{2,1,0:T(8,128)(2,1)S(1)} collective-permute-done((bf16[4,56,1600]{2,1,0:T(8,128)(2,1)}, bf16[4,56,1600]{2,1,0:T(8,128)(2,1)S(1)}, u32[]{:S(2)}, u32[]{:S(2)}) %collective-permute-start.28) | collective-permute-done | bytes 716832 | tf_op jit(solution)/shard_map/ppermute | solution.py:34
  343.6 7.3 %branch_back.1 = (f32[128,1600]{1,0:T(8,128)}, bf16[128,1600]{1,0:T(8,128)(2,1)}, bf16[8,128,256]{2,1,0:T(8,128)(2,1)}, f32[4,1600]{1,0:T(4,128)}) custom-call(s32[8]{0:T(128)} %stack.39.place_ref, f32[128,1600]{1,0:T(8,128)} %convert_element_type.41.grad_ref, f32[128,1600]{1,0:T(8,128)} %get-tuple-element.129.middle_ref, bf16[128,1600]{1,0:T(8,128)(2,1)} %copy-done.7, ...), custom_call_target="tpu_custom_call" | custom-call | flops 655360000 | bytes 8997920 | tf_op jit(solution)/shard_map/branch_back/pallas_call | solution.py:114
  351.0 6.9 all-to-all-start.3
  371.9 15.3 %attend_back.1 = (bf16[1024,768]{1,0:T(8,128)(2,1)}, bf16[1024,1600]{1,0:T(8,128)(2,1)}, f32[1,768]{1,0:T(1,128)}) custom-call(s32[8]{0:T(128)} %stack.39.place_ref, bf16[1024,768]{1,0:T(8,128)(2,1)} %get-tuple-element.160.qkv_ref, bf16[1024,256]{1,0:T(8,128)(2,1)} %bitcast.14.grad_ref, bf16[1024,256]{1,0:T(8,128)(2,1)} %get-tuple-element.128.out_ref, ...), custom_call_target="tpu_custom_call" | custom-call | flops 2516582400 | bytes 9948192 | tf_op jit(solution)/shard_map/attend_back/pallas_call | solution.py:114
  393.2 7.0 qkv_grad.1
  405.0 18.7 %reduce-scatter.8.cloned.1.call-done = bf16[128,1600]{1,0:T(8,128)(2,1)} async-done(((bf16[1024,1600]{1,0:T(8,128)(2,1)}), bf16[128,1600]{1,0:T(8,128)(2,1)}) %reduce-scatter.8.cloned.1.call-update) | async-done | bytes 409616 | tf_op jit(solution)/shard_map/reduce_scatter | solution.py:62
  439.8 52.3 %collective-permute-done.31.refs_1_ = bf16[4,32,800]{2,1,0:T(8,128)(2,1)} collective-permute-done((bf16[4,32,800]{2,1,0:T(8,128)(2,1)}, bf16[4,32,800]{2,1,0:T(8,128)(2,1)}, u32[]{:S(2)}, u32[]{:S(2)}) %collective-permute-start.31) | collective-permute-done | bytes 204832 | tf_op jit(solution)/shard_map/ppermute | solution.py:34
  497.0 14.0 %collective-permute-done.33.refs_3_ = bf16[4,32,800]{2,1,0:T(8,128)(2,1)} collective-permute-done((bf16[4,32,800]{2,1,0:T(8,128)(2,1)}, bf16[4,32,800]{2,1,0:T(8,128)(2,1)}, u32[]{:S(2)}, u32[]{:S(2)}) %collective-permute-start.33) | collective-permute-done | bytes 204832 | tf_op jit(solution)/shard_map/ppermute | solution.py:34
  517.9 36.6 %all-gather.15.cloned.1.call-done = bf16[896,1600]{1,0:T(8,128)(2,1)} async-done(((bf16[56,1600]{1,0:T(8,128)(2,1)}), bf16[896,1600]{1,0:T(8,128)(2,1)}) %all-gather.15.cloned.1.call-update) | async-done | bytes 2867216 | tf_op jit(solution)/shard_map/all_gather | solution.py:58
  647.0 11.6 %all-to-all-done.8.own_ref = bf16[16,16,1600]{2,1,0:T(8,128)(2,1)S(1)} async-done(((bf16[16,16,1600]{2,1,0:T(8,128)(2,1)}), bf16[16,16,1600]{2,1,0:T(8,128)(2,1)S(1)}, u32[]{:S(2)}, u32[]{:S(2)}) %all-to-all-start.8) | async-done | bytes 819232 | tf_op jit(solution)/shard_map/all_to_all | solution.py:54
  669.9 8.9 %fc_total.1 = f32[200,6400]{1,0:T(8,128)} custom-call(s32[8]{0:T(128)} %stack.39.place_ref, bf16[2,4,32,800]{3,2,1,0:T(8,128)(2,1)} %fc_both.1.refs_0_, bf16[2,4,32,800]{3,2,1,0:T(8,128)(2,1)} %collective-permute-done.50.refs_1_, bf16[2,4,32,800]{3,2,1,0:T(8,128)(2,1)} %copy-done.17, bf16[2,4,32,800]{3,2,1,0:T(8,128)(2,1)} %copy-done.16, ...), custom_call_target="tpu_custom_call" | custom-call | bytes 8396832 | tf_op jit(solution)/shard_map/fc_total/pallas_call | solution.py:114
  679.6 9.1 %qkv_total.1 = f32[200,4800]{1,0:T(8,128)} custom-call(s32[8]{0:T(128)} %stack.39.place_ref, bf16[2,4,32,768]{3,2,1,0:T(8,128)(2,1)} %qkv_both.1.refs_0_, bf16[2,4,32,768]{3,2,1,0:T(8,128)(2,1)} %collective-permute-done.58.refs_1_, bf16[2,4,32,768]{3,2,1,0:T(8,128)(2,1)} %collective-permute-done.59.refs_2_, ...), custom_call_target="tpu_custom_call" | custom-call | bytes 6985760 | tf_op jit(solution)/shard_map/qkv_total/pallas_call | solution.py:114
  (334 shorter events, 328.0 us)
Async XLA Ops:
  7.2 170.2 %all-gather.9.cloned.1.call-start = ((), (), s32[]{:S(2)}) async-start(), calls=%async_computation.16 | async-start | bytes 3833856 | tf_op jit(solution)/shard_map/all_gather | solution.py:58
  32.4 188.2 %all-gather.13.cloned.1.call-start = ((), (), s32[]{:S(2)}) async-start(), calls=%async_computation.18 | async-start | bytes 3833856 | tf_op jit(solution)/shard_map/all_gather | solution.py:58
  96.5 103.0 %collective-permute-start.7 = (bf16[800,1600]{1,0:T(8,128)(2,1)}, bf16[800,1600]{1,0:T(8,128)(2,1)}, u32[]{:S(2)}, u32[]{:S(2)}) collective-permute-start(bf16[800,1600]{1,0:T(8,128)(2,1)} %param.27), channel_id=1, source_target_pairs={{0,0},{1,8},{8,1},{9,9},{2,2},{3,10},{10,3},{11,11},{4,4},{5,12},{... | collective-permute-start | bytes 7680008 | tf_op jit(solution)/shard_map/ppermute | solution.py:46
  99.6 39.2 %collective-permute-start.8 = (bf16[200,1600]{1,0:T(8,128)(2,1)S(1)}, bf16[200,1600]{1,0:T(8,128)(2,1)S(1)}, u32[]{:S(2)}, u32[]{:S(2)}) collective-permute-start(bf16[200,1600]{1,0:T(8,128)(2,1)S(1)} %copy-done.37), channel_id=1, source_target_pairs={{0,0},{1,8},{8,1},{9,9},{2,2},{3,10},{10,3},{11,11},{4,4},{5,12},{... | collective-permute-start | bytes 1920008 | tf_op jit(solution)/shard_map/ppermute | solution.py:46
  199.5 51.2 %all-gather.11.cloned.1.call-start = ((), (), s32[]{:S(2)}) async-start(), calls=%async_computation.17 | async-start | bytes 3833856 | tf_op jit(solution)/shard_map/all_gather | solution.py:58
  228.5 70.7 %reduce-scatter.4.cloned.1.call-start = ((), (), s32[]{:S(2)}) async-start(), calls=%async_computation.13 | async-start | bytes 3833856 | tf_op jit(solution)/shard_map/reduce_scatter | solution.py:62
  265.5 121.8 %reduce-scatter.6.cloned.1.call-start = ((), (), s32[]{:S(2)}) async-start(), calls=%async_computation.14 | async-start | bytes 3833856 | tf_op jit(solution)/shard_map/reduce_scatter | solution.py:62
  320.4 46.2 %collective-permute-start.25 = (bf16[4,4,32,800]{3,2,1,0:T(8,128)(2,1)}, bf16[4,4,32,800]{3,2,1,0:T(8,128)(2,1)S(1)}, u32[]{:S(2)}, u32[]{:S(2)}) collective-permute-start(bf16[4,4,32,800]{3,2,1,0:T(8,128)(2,1)} %get-tuple-element.150), channel_id=1, source_target_pairs={{32,0},{64,32},{96,64},{0,96},{33,1},{65,33},{97,65},{1,97},{34,2}... | collective-permute-start | bytes 2457608 | tf_op jit(solution)/shard_map/ppermute | solution.py:34
  322.8 43.8 %collective-permute-start.26 = (bf16[4,4,32,800]{3,2,1,0:T(8,128)(2,1)}, bf16[4,4,32,800]{3,2,1,0:T(8,128)(2,1)S(1)}, u32[]{:S(2)}, u32[]{:S(2)}) collective-permute-start(bf16[4,4,32,800]{3,2,1,0:T(8,128)(2,1)} %get-tuple-element.151), channel_id=1, source_target_pairs={{64,0},{96,32},{0,64},{32,96},{65,1},{97,33},{1,65},{33,97},{66,2}... | collective-permute-start | bytes 2457608 | tf_op jit(solution)/shard_map/ppermute | solution.py:34
  323.4 43.3 %collective-permute-start.27 = (bf16[4,4,32,800]{3,2,1,0:T(8,128)(2,1)}, bf16[4,4,32,800]{3,2,1,0:T(8,128)(2,1)S(1)}, u32[]{:S(2)}, u32[]{:S(2)}) collective-permute-start(bf16[4,4,32,800]{3,2,1,0:T(8,128)(2,1)} %get-tuple-element.152), channel_id=1, source_target_pairs={{96,0},{0,32},{32,64},{64,96},{97,1},{1,33},{33,65},{65,97},{98,2}... | collective-permute-start | bytes 2457608 | tf_op jit(solution)/shard_map/ppermute | solution.py:34
  357.9 65.8 %reduce-scatter.8.cloned.1.call-start = ((), (), s32[]{:S(2)}) async-start(), calls=%async_computation.15 | async-start | bytes 3833856 | tf_op jit(solution)/shard_map/reduce_scatter | solution.py:62
  389.3 165.1 %all-gather.15.cloned.1.call-start = ((), (), s32[]{:S(2)}) async-start(), calls=%async_computation.19 | async-start | bytes 3168256 | tf_op jit(solution)/shard_map/all_gather | solution.py:58
  425.7 144.1 %all-to-all-start.4 = ((bf16[16,4,32,768]{3,2,1,0:T(8,128)(2,1)}), bf16[16,4,32,768]{3,2,1,0:T(8,128)(2,1)S(1)}, u32[]{:S(2)}, u32[]{:S(2)}) async-start(bf16[16,4,32,768]{3,2,1,0:T(8,128)(2,1)} %qkv_grad.1), calls=%async_computation.7 | async-start | bytes 6291456 | tf_op jit(solution)/shard_map/all_to_all | solution.py:54
  432.4 59.8 %collective-permute-start.31 = (bf16[4,32,800]{2,1,0:T(8,128)(2,1)}, bf16[4,32,800]{2,1,0:T(8,128)(2,1)}, u32[]{:S(2)}, u32[]{:S(2)}) collective-permute-start(bf16[4,32,800]{2,1,0:T(8,128)(2,1)} %get-tuple-element.170), channel_id=1, source_target_pairs={{16,0},{1,16},{17,1},{0,17},{18,2},{3,18},{19,3},{2,19},{20,4},{5,... | collective-permute-start | bytes 614408 | tf_op jit(solution)/shard_map/ppermute | solution.py:34
  434.9 78.1 %collective-permute-start.41 = (bf16[128,1600]{1,0:T(8,128)(2,1)}, bf16[128,1600]{1,0:T(8,128)(2,1)}, u32[]{:S(2)}, u32[]{:S(2)}) collective-permute-start(bf16[128,1600]{1,0:T(8,128)(2,1)} %get-tuple-element.187.refs_0_), channel_id=1, source_target_pairs={{6,0},{0,2},{2,4},{4,6},{7,1},{1,3},{3,5},{5,7},{14,8},{8,10},{10,... | collective-permute-start | bytes 1228808 | tf_op jit(solution)/shard_map/ppermute | solution.py:34
  438.1 76.3 %collective-permute-start.40 = (bf16[128,1600]{1,0:T(8,128)(2,1)}, bf16[128,1600]{1,0:T(8,128)(2,1)}, u32[]{:S(2)}, u32[]{:S(2)}) collective-permute-start(bf16[128,1600]{1,0:T(8,128)(2,1)} %get-tuple-element.187.refs_0_), channel_id=1, source_target_pairs={{4,0},{6,2},{0,4},{2,6},{5,1},{7,3},{1,5},{3,7},{12,8},{14,10},{8,... | collective-permute-start | bytes 1228808 | tf_op jit(solution)/shard_map/ppermute | solution.py:34
  438.1 76.4 %collective-permute-start.39 = (bf16[128,1600]{1,0:T(8,128)(2,1)}, bf16[128,1600]{1,0:T(8,128)(2,1)}, u32[]{:S(2)}, u32[]{:S(2)}) collective-permute-start(bf16[128,1600]{1,0:T(8,128)(2,1)} %get-tuple-element.187.refs_0_), channel_id=1, source_target_pairs={{2,0},{4,2},{6,4},{0,6},{3,1},{5,3},{7,5},{1,7},{10,8},{12,10},{14... | collective-permute-start | bytes 1228808 | tf_op jit(solution)/shard_map/ppermute | solution.py:34
  439.3 55.3 %collective-permute-start.32 = (bf16[4,32,800]{2,1,0:T(8,128)(2,1)}, bf16[4,32,800]{2,1,0:T(8,128)(2,1)}, u32[]{:S(2)}, u32[]{:S(2)}) collective-permute-start(bf16[4,32,800]{2,1,0:T(8,128)(2,1)} %get-tuple-element.171), channel_id=1, source_target_pairs={{1,0},{17,16},{0,1},{16,17},{3,2},{19,18},{2,3},{18,19},{5,4},{21,... | collective-permute-start | bytes 614408 | tf_op jit(solution)/shard_map/ppermute | solution.py:34
  494.5 67.2 %collective-permute-start.42 = (bf16[128,1600]{1,0:T(8,128)(2,1)}, bf16[128,1600]{1,0:T(8,128)(2,1)}, u32[]{:S(2)}, u32[]{:S(2)}) collective-permute-start(bf16[128,1600]{1,0:T(8,128)(2,1)} %get-tuple-element.187.refs_0_), channel_id=1, source_target_pairs={{0,8},{8,0},{1,9},{9,1},{2,10},{10,2},{3,11},{11,3},{4,12},{12,4},... | collective-permute-start | bytes 1228808 | tf_op jit(solution)/shard_map/ppermute | solution.py:50
  513.1 51.9 %collective-permute-start.45 = (bf16[128,1600]{1,0:T(8,128)(2,1)}, bf16[128,1600]{1,0:T(8,128)(2,1)}, u32[]{:S(2)}, u32[]{:S(2)}) collective-permute-start(bf16[128,1600]{1,0:T(8,128)(2,1)} %collective-permute-done.41.refs_3_), channel_id=1, source_target_pairs={{0,8},{8,0},{1,9},{9,1},{2,10},{10,2},{3,11},{11,3},{4,12},{12,4},... | collective-permute-start | bytes 1228808 | tf_op jit(solution)/shard_map/ppermute | solution.py:50
  514.3 50.7 %collective-permute-start.44 = (bf16[128,1600]{1,0:T(8,128)(2,1)}, bf16[128,1600]{1,0:T(8,128)(2,1)}, u32[]{:S(2)}, u32[]{:S(2)}) collective-permute-start(bf16[128,1600]{1,0:T(8,128)(2,1)} %collective-permute-done.40.refs_2_), channel_id=1, source_target_pairs={{0,8},{8,0},{1,9},{9,1},{2,10},{10,2},{3,11},{11,3},{4,12},{12,4},... | collective-permute-start | bytes 1228808 | tf_op jit(solution)/shard_map/ppermute | solution.py:50
  514.4 50.6 %collective-permute-start.43 = (bf16[128,1600]{1,0:T(8,128)(2,1)}, bf16[128,1600]{1,0:T(8,128)(2,1)}, u32[]{:S(2)}, u32[]{:S(2)}) collective-permute-start(bf16[128,1600]{1,0:T(8,128)(2,1)} %collective-permute-done.39.refs_1_), channel_id=1, source_target_pairs={{0,8},{8,0},{1,9},{9,1},{2,10},{10,2},{3,11},{11,3},{4,12},{12,4},... | collective-permute-start | bytes 1228808 | tf_op jit(solution)/shard_map/ppermute | solution.py:50
  554.4 139.2 %collective-permute-start.66 = (bf16[16,56,1600]{2,1,0:T(8,128)(2,1)}, bf16[16,56,1600]{2,1,0:T(8,128)(2,1)}, u32[]{:S(2)}, u32[]{:S(2)}) collective-permute-start(bf16[16,56,1600]{2,1,0:T(8,128)(2,1)} %bitcast.40), channel_id=1, source_target_pairs={{0,8},{8,0},{1,9},{9,1},{2,10},{10,2},{3,11},{11,3},{4,12},{12,4},... | collective-permute-start | bytes 8601608 | tf_op jit(solution)/shard_map/ppermute | solution.py:50
  561.8 47.0 %collective-permute-start.37 = (bf16[128,1600]{1,0:T(8,128)(2,1)}, bf16[128,1600]{1,0:T(8,128)(2,1)}, u32[]{:S(2)}, u32[]{:S(2)}) collective-permute-start(bf16[128,1600]{1,0:T(8,128)(2,1)} %add_convert_fusion), channel_id=1, source_target_pairs={{0,0},{1,8},{8,1},{9,9},{2,2},{3,10},{10,3},{11,11},{4,4},{5,12},{... | collective-permute-start | bytes 1228808 | tf_op jit(solution)/shard_map/ppermute | solution.py:46
  (112 other events, 2387.9 us)
Sparse Core Ops, SparseCore 0:
  21.4 29.4 all-gather.8
  66.6 26.7 all-gather.12
  212.1 32.8 all-gather.10
  265.6 33.5 reduce-scatter.3
  302.0 35.4 reduce-scatter.5
  389.4 34.2 reduce-scatter.7
  425.8 128.5 all-gather.14

commit v5 on v4

--- a/solution.py
+++ b/solution.py
@@ -46,6 +46,10 @@
     return lax.ppermute(value, ("c", "zh"), ROLES)
 
 
+def swap_selected(value, stays):
+    return jnp.where(stays, value, lax.ppermute(value, ("c", "zh"), ROLES[1:3]))
+
+
 def other_core(value):
     return lax.ppermute(value, "c", [(0, 1), (1, 0)])
 
@@ -59,7 +63,7 @@
 
 
 def team_sum(parts):
-    return lax.psum_scatter(parts.astype(bf16), TEAM, scatter_dimension=0, tiled=True).astype(f32)
+    return lax.psum_scatter(parts.astype(bf16), TEAM, scatter_dimension=0, tiled=True)
 
 
 def windows(rows, count):
@@ -119,7 +123,7 @@
         scratch_shapes=list(scratch),
         compiler_params=pltpu.CompilerParams(vmem_limit_bytes=56 * 2**20),
         cost_estimate=pl.CostEstimate(
-            flops=int(flops), bytes_accessed=int(moved), transcendentals=0
+            flops=int(3 * flops), bytes_accessed=int(moved), transcendentals=0
         ),
         name=name,
     )(*operands)
@@ -169,29 +173,33 @@
         out_ref[2 * y + 1 - zh] = refs[4 + k][...]
 
 
-def branch_kernel(place_ref, slots_ref, tokens_ref, norm_ref, *refs):
-    rows_refs, (middle_ref, second_ref, parts_ref, flat_ref) = refs[:8], refs[8:]
-    c = place_ref[C]
-    shard = rows_refs[0].shape[0]
+def branch_kernel(
+    slots_ref, tokens_ref, norm_ref, rows_ref, middle_ref, second_ref, parts_ref, flat_ref
+):
+    shard = parts_ref.shape[2]
     for rank in range(8):
         wide = STRIDE if rank < 7 else SLOT_WIDTH
         flat_ref[:, STRIDE * rank : STRIDE * rank + wide] = slots_ref[rank, :, :wide]
     for rank in range(8):
         parts_ref[rank] = flat_ref[:, shard * rank : shard * (rank + 1)]
-    total = tokens_ref[...].astype(f32) + norm_ref[4:5, :]
-    for k in range(4):
-        y = lax.rem(place_ref[Y] + k, 4)
-        total = total + dot(parts_ref[2 * y + c], rows_refs[k][...])
-        total = total + dot(parts_ref[2 * y + 1 - c], rows_refs[4 + k][...])
+    total = tokens_ref[...].astype(f32) + norm_ref[4:5, :] + dot(flat_ref[...], rows_ref[...])
     middle_ref[...] = total
     second_ref[...] = norm_parts(total, norm_ref[5:6, :], norm_ref[6:7, :])[0].astype(bf16)
 
 
-def branch_back_kernel(place_ref, grad_ref, middle_ref, cot_ref, norm_ref, *refs):
-    rows_refs = refs[:8]
-    grad_middle_ref, branch_ref, slots_ref, sums_ref, parts_ref, flat_ref = refs[8:]
-    c = place_ref[C]
-    shard = rows_refs[0].shape[0]
+def branch_back_kernel(
+    place_ref,
+    grad_ref,
+    middle_ref,
+    cot_ref,
+    norm_ref,
+    rows_ref,
+    grad_middle_ref,
+    branch_ref,
+    slots_ref,
+    sums_ref,
+    flat_ref,
+):
     gain = norm_ref[5:6, :]
     _, normed, factor = norm_parts(middle_ref[...], gain, gain)
     grad = grad_ref[...].astype(f32)
@@ -200,12 +208,7 @@
     branch = grad_middle.astype(bf16)
     grad_middle_ref[...] = grad_middle
     branch_ref[...] = branch
-    for k in range(4):
-        y = lax.rem(place_ref[Y] + k, 4)
-        parts_ref[2 * y + c] = dot_cols(branch, rows_refs[k][...]).astype(bf16)
-        parts_ref[2 * y + 1 - c] = dot_cols(branch, rows_refs[4 + k][...]).astype(bf16)
-    for rank in range(8):
-        flat_ref[:, shard * rank : shard * (rank + 1)] = parts_ref[rank]
+    flat_ref[...] = dot_cols(branch, rows_ref[...]).astype(bf16)
     for rank in range(8):
         slots_ref[rank] = flat_ref[:, STRIDE * rank : STRIDE * rank + SLOT_WIDTH]
     sums_ref[0:1, :] = jnp.sum(branch.astype(f32), axis=0, keepdims=True)
@@ -239,20 +242,13 @@
                 out_refs[k][z, y] = held_ref[pl.ds(at, size), :].astype(bf16)
 
 
-def row_start(rows, index):
-    return pl.multiple_of(lax.div(rows // 8 * index, 16) * 8, 8)
-
-
-def row_ring_kernel(place_ref, left_ref, right_ref, *refs):
-    out_refs, held_ref = refs[:4], refs[4]
+def row_grad_kernel(left_ref, right_ref, out_ref):
     rows = left_ref.shape[1]
-    size = windows(rows, 16)[0]
-    held_ref[...] = dot_rows(left_ref[...], right_ref[...])
-    for k in range(4):
-        z = lax.rem(place_ref[Z] + 4 - k, 4)
-        for x in range(4):
-            at = row_start(rows, (lax.rem(z, 2) * 4 + x) * 2 + lax.div(z, 2))
-            out_refs[k][x] = held_ref[pl.ds(at, size), :].astype(bf16)
+    size, starts = windows(rows, 16)
+    grad = dot_rows(left_ref[...], right_ref[...])
+    for i, start in enumerate(starts):
+        zl, x, zh = i // 8, i // 2 % 4, i % 2
+        out_ref[2 * zl + zh, x] = grad[start : start + size].astype(bf16)
 
 
 def out_grad_kernel(place_ref, left_ref, *refs):
@@ -279,6 +275,15 @@
         for j in range(1, 4):
             total = total + refs[j][at].astype(f32)
         refs[4 + k][...] = total.astype(bf16)
+
+
+def fold_stack_kernel(which, place_ref, parts_ref, *refs):
+    for k in range(4):
+        at = lax.rem(place_ref[which] + 4 - k, 4)
+        total = parts_ref[0, at].astype(f32)
+        for j in range(1, 4):
+            total = total + parts_ref[j, at].astype(f32)
+        refs[k][...] = total.astype(bf16)
 
 
 def stack_kernel(*refs):
@@ -473,13 +478,9 @@
         [y, c, rank, zh, zh * 2 + zl, x, zl, (c == zh).astype(jnp.int32)]
     ).astype(jnp.int32)
 
+    stays = c == zh
     own_tokens = swap_roles(tokens.reshape(span, width))
-    small = jnp.concatenate(
-        [ln1_gain, ln1_bias, bias_q, bias_v, bias_out, ln2_gain, ln2_bias, bias_proj, bias_fc]
-    ).reshape(3, hidden)
-    small_all = exchange(jnp.broadcast_to(small, (8, 3, hidden)), GRP)
     all_tokens = gather(own_tokens, TEAM).reshape(length, width)
-    place = after(place, small_all)
     qkv_parts = call(
         qkv_columns_kernel,
         "qkv_columns",
@@ -490,9 +491,15 @@
     )
     qkv_own = ring_all(qkv_parts, "y")
     qkv_other = [flipped(part, "zh") for part in qkv_own]
+    small = jnp.concatenate(
+        [ln1_gain, ln1_bias, bias_q, bias_v, bias_out, ln2_gain, ln2_bias, bias_proj, bias_fc]
+    ).reshape(3, hidden)
+    small_all = exchange(
+        after(jnp.broadcast_to(small, (8, 3, hidden)), qkv_parts[0]), GRP
+    )
     out_rows = swap_roles(after(w_out, small_all))
-    own_cot = swap_roles(after(cotangent, qkv_parts[0]).reshape(span, width))
-    place = after(place, qkv_parts[0])
+    own_cot = swap_roles(after(cotangent, out_rows).reshape(span, width))
+    place = after(place, small_all)
     fc_parts = call(
         fc_columns_kernel,
         "fc_columns",
@@ -514,12 +521,10 @@
         ]
     ).reshape(1, slots)
 
-    out_own = ring_all([after(out_rows, *qkv_own)] * 4, "y")
-    out_other = [other_core(part) for part in out_own]
-    all_cot = gather(after(own_cot, *qkv_own), TEAM).reshape(length, width)
-    proj_rows = swap_roles(after(w_proj, *qkv_other))
-    fc_own = ring_all([after(part, *out_own) for part in fc_parts], "y")
-    fc_other = [flipped(after(part, proj_rows), "zh") for part in fc_own]
+    out_all = gather(after(out_rows, *qkv_own), TEAM).reshape(width, width)
+    all_cot = gather(after(own_cot, *qkv_other), TEAM).reshape(length, width)
+    proj_rows = swap_selected(after(w_proj, *qkv_other), stays)
+    fc_own = ring_all([after(part, *qkv_other) for part in fc_parts], "y")
 
     first, qkv, attended_slots, top, qkv_cols = call(
         attend_kernel,
@@ -540,6 +545,7 @@
         flops=2 * length * width * slots,
     )
     qkv_cols = qkv_cols.reshape(width, slots)
+    fc_other = [flipped(after(part, qkv), "zh") for part in fc_own]
     attended = exchange(attended_slots.reshape(8, span, SLOT_WIDTH), TEAM)
     middle, second, attended_parts = call(
         branch_kernel,
@@ -549,12 +555,10 @@
             struct((span, width), bf16),
             struct((8, span, shard), bf16),
         ),
-        after(place, proj_rows, *fc_own),
         attended,
         own_tokens,
         vectors,
-        *out_own,
-        *out_other,
+        out_all,
         scratch=[pltpu.VMEM((span, width), bf16)],
         flops=2 * span * width * width,
     )
@@ -602,17 +606,15 @@
     fc_grad = ring_all(fc_grad, "x")
     row_window = windows(hidden, 16)[0]
     proj_grad = call(
-        row_ring_kernel,
+        row_grad_kernel,
         "proj_grad",
-        [struct((4, row_window, width), bf16)] * 4,
-        place,
+        struct((4, 4, row_window, width), bf16),
         active,
         all_cot,
-        scratch=[pltpu.VMEM((hidden, width), f32)],
         flops=2 * length * width * hidden,
     )
-    proj_grad = ring_all(proj_grad, Z_RING)
     down_parts = dot(active, proj_rows).astype(bf16)
+    grad_second = after(grad_second, fc_grad[0], proj_grad, down_parts)
 
     grad_middle, grad_branch, grad_slots, branch_sums = call(
         branch_back_kernel,
@@ -623,19 +625,18 @@
             struct((8, span, SLOT_WIDTH), bf16),
             struct((4, width), f32),
         ),
-        after(place, fc_grad[0], proj_grad[0], down_parts),
+        place,
         grad_second,
         middle,
         own_cot,
         vectors,
-        *out_own,
-        *out_other,
-        scratch=[pltpu.VMEM((8, span, shard), bf16), pltpu.VMEM((span, width), bf16)],
+        out_all,
+        scratch=[pltpu.VMEM((span, width), bf16)],
         flops=2 * span * width * width,
     )
     grad_heads = exchange(grad_slots, TEAM).reshape(length, SLOT_WIDTH)
     down = team_sum(after(down_parts, grad_second))
-    branch_own = ring_all([after(grad_branch, grad_heads)] * 4, "y")
+    proj_grad = exchange(after(proj_grad, grad_heads), Z_RING)
 
     def fold(which, parts, name, *behind):
         parts = [after(parts[0], *behind)] + parts[1:]
@@ -647,8 +648,6 @@
             *parts,
         )
 
-    fc_grad = ring_all(fold(Z, fc_grad, "fc_fold", grad_slots), Z_RING)
-    proj_grad = ring_all(fold(X, proj_grad, "proj_fold", grad_slots), "x")
     grad_mixed, first_parts, mixed_sums = call(
         attend_back_kernel,
         "attend_back",
@@ -657,7 +656,7 @@
             struct((length, width), bf16),
             struct((1, slots), f32),
         ),
-        after(place, fc_grad[0], proj_grad[0]),
+        place,
         qkv,
         grad_heads,
         attended_slots,
@@ -667,16 +666,31 @@
         flops=2 * length * width * slots,
     )
     grad_first = team_sum(after(first_parts, down))
+    place = after(place, grad_mixed)
+    proj_grad = ring_all(
+        call(
+            functools.partial(fold_stack_kernel, X),
+            "proj_fold",
+            [struct((row_window, width), bf16)] * 4,
+            place,
+            proj_grad,
+        ),
+        "x",
+    )
+    fc_grad = fold(Z, fc_grad, "fc_fold", place)
     qkv_grad = call(
         column_grad_kernel,
         "qkv_grad",
         struct((16, 4, window, slots), bf16),
-        first,
+        after(first, fc_grad[0], proj_grad[0]),
         grad_mixed,
         flops=2 * length * width * slots,
     )
     place = after(place, qkv_grad)
-    qkv_grad = exchange(qkv_grad, REPLICAS)
+    fc_grad = ring_all(fc_grad, Z_RING)
+    branch_own = ring_all([after(grad_branch, grad_mixed)] * 4, "y")
+    qkv_grad = exchange(after(qkv_grad, *fc_grad, *proj_grad), REPLICAS)
+    grad_first = after(grad_first, qkv_grad)
 
     def replica_sum(parts):
         return jnp.sum(parts.astype(f32), axis=0).astype(bf16)
@@ -688,17 +702,30 @@
 
     def column_spread(near, name):
         both = stacked([near, flipped(near, "zl")], name + "_both")
-        own = ring_all([both] * 4, "x")
-        return own + [other_core(part) for part in own]
-
-    def row_total(whole, rows, name):
+        return ring_all([both] * 4, "x")
+
+    def row_total(whole, rows, name, *behind):
+        whole = after(whole, *behind)
         return call(
             row_total_kernel, name, struct((rows, width), f32), place, whole, other_core(whole)
         )
 
     fc_grad = ring_all(fold(Y, fc_grad, "fc_fold_last", place), "y")
-    proj_grad = [after(proj_grad[0], place)] + proj_grad[1:]
     proj_sum = sum(part.astype(f32) for part in proj_grad).astype(bf16)
+    proj_whole = gather(after(proj_sum, grad_first), REPLICAS)
+    fc_own_pieces = column_spread(stacked(fc_grad, "fc_near"), "fc")
+    branch_other = [other_core(part) for part in branch_own]
+    out_grad = call(
+        out_grad_kernel,
+        "out_grad",
+        struct((16, windows(shard, 16)[0], width), bf16),
+        after(place, fc_grad[1]),
+        attended_own,
+        *branch_own,
+        *branch_other,
+        scratch=[pltpu.VMEM((shard, width), f32)],
+        flops=2 * length * width * shard,
+    )
     grad_inputs, first_sums = call(
         input_back_kernel,
         "input_back",
@@ -706,31 +733,19 @@
         grad_first,
         own_tokens,
         grad_middle,
-        after(vectors, fc_grad[0], proj_sum),
+        after(vectors, qkv_grad, out_grad, *fc_own_pieces),
     )
     inputs_home = swap_roles(grad_inputs).astype(f32).reshape(1, span, width)
-    output = middle + (after(down, grad_inputs) + vectors[7])
+    output = middle + (after(down, grad_inputs).astype(f32) + vectors[7])
     output_home = swap_roles(output.astype(bf16)).reshape(1, span, width)
-    proj_whole = gather(after(proj_sum, grad_first), REPLICAS)
     place = after(place, grad_inputs)
-    fc_pieces = column_spread(stacked([after(fc_grad[0], place)] + fc_grad[1:], "fc_near"), "fc")
-
-    branch_other = [other_core(part) for part in branch_own]
-    out_grad = call(
-        out_grad_kernel,
-        "out_grad",
-        struct((16, windows(shard, 16)[0], width), bf16),
-        place,
-        attended_own,
-        *branch_own,
-        *branch_other,
-        scratch=[pltpu.VMEM((shard, width), f32)],
-        flops=2 * length * width * shard,
-    )
+    fc_own_pieces = [after(part, grad_inputs) for part in fc_own_pieces]
+    fc_pieces = fc_own_pieces + [other_core(part) for part in fc_own_pieces]
     place = after(place, out_grad)
     qkv_sum = exchange(replica_sum(after(qkv_grad, place)), "y")
     out_grad = exchange(after(out_grad, qkv_sum), REPLICAS)
     qkv_pieces = column_spread(qkv_sum, "qkv")
+    qkv_pieces = qkv_pieces + [other_core(part) for part in qkv_pieces]
 
     blank = jnp.zeros((1, width), f32)
     at = (0, STRIDE * rank)
@@ -764,7 +779,7 @@
         after(place, qkv_sum),
         *fc_pieces,
     )
-    proj_total = row_total(proj_whole, hidden, "proj_total")
+    proj_total = row_total(proj_whole, hidden, "proj_total", out_whole)
     out_total = row_total(out_whole, shard, "out_total")
     qkv_spans = [
         [

time: 720 us -> 674 us (0.936)
  waiting for transfers between devices: 323 us -> 268 us
  blocking collectives: 0 us -> 49 us
  starting transfers between devices: 165 us -> 142 us
  other arithmetic: 12.3 us -> 4.7 us
    all_to_all x0 -> x4, blocking collectives: none -> 49 us  [exchange(): return lax.all_to_all(parts, axes, 0, 0)]
    all_to_all x10 -> x7, waiting for transfers between devices: 22.5 us -> 67.9 us  [exchange(): return lax.all_to_all(parts, axes, 0, 0)]
    all_gather x4 -> x5, waiting for transfers between devices: 36.6 us -> 0.03 us  [gather(): return lax.all_gather(block, axes, axis=0)]
    ppermute x6 -> x5, waiting for transfers between devices: 41 us -> 5.81 us  [swap_roles(): return lax.ppermute(value, ('c', 'zh'), ROLES)]
    reduce_scatter x3, waiting for transfers between devices: 44 us -> 12.8 us  [team_sum(): lax.psum_scatter(parts.astype(bf16), TEAM, scatter_dimension=0, tiled=True)]
    ppermute x10, waiting for transfers between devices: 35.5 us -> 53.3 us  [flipped(): return lax.ppermute(value, axis, [(0, 1), (1, 0)])]
    ppermute x33 -> x27, waiting for transfers between devices: 144 us -> 128 us  [ring(): lax.ppermute(value, axis, [(index[(i + step) % 4], index[i]) for i in ran...]
    all_to_all x10 -> x7, starting transfers between devices: 62.1 us -> 47.8 us  [exchange(): return lax.all_to_all(parts, axes, 0, 0)]
  transfers between devices with their start and end apart: 84 -> 72, of which waited for: 35 -> 33; matrix products, arithmetic and copies ran while one was open for 7% -> 6% of each run, Pallas kernels for 17% -> 18%
where the time goes in v5:
time: 674 us; the launch traced here: 666 us
  waiting for transfers between devices  268 us (40%)
  starting transfers between devices  142 us (21%)
  Pallas kernels  139 us (21%)
  blocking collectives  49 us (7%)
  local copies, waits for them, and re-layouts  32.4 us (5%)
  matrix products  15.7 us (2%)
  between operations  15 us (2%)
    pallas_call x23, Pallas kernels, call(): pl.pallas_call(kernel, out_shape=out_shape, in_specs=specs, out_specs=out...  139 us
    ppermute x27, waiting for transfers between devices, ring(): lax.ppermute(value, axis, [(index[(i + step) % 4], index[i]) for i in ran...  128 us
    all_to_all x7, waiting for transfers between devices, exchange(): return lax.all_to_all(parts, axes, 0, 0)  67.9 us
    ppermute x10, waiting for transfers between devices, flipped(): return lax.ppermute(value, axis, [(0, 1), (1, 0)])  53.3 us
    all_to_all x4, blocking collectives, exchange(): return lax.all_to_all(parts, axes, 0, 0)  49 us
    all_to_all x7, starting transfers between devices, exchange(): return lax.all_to_all(parts, axes, 0, 0)  47.8 us
    ppermute x27, starting transfers between devices, ring(): lax.ppermute(value, axis, [(index[(i + step) % 4], index[i]) for i in ran...  33.4 us
    ppermute x14, starting transfers between devices, other_core(): return lax.ppermute(value, 'c', [(0, 1), (1, 0)])  23.6 us
  transfers between devices with their start and end apart: 72, of which 33 were waited for; matrix products, arithmetic and copies ran while one was open for 6% of the time, Pallas kernels for 18%

profile of v5, /device:TPU:17, one launch (start us, length us, event | category | flops | bytes accessed | tf_op | source)
XLA Modules:
  0.0 665.7 jit_solution(1838910727657793972)
XLA Ops:
  31.9 9.2 %all_to_all.55 = bf16[8,3,800]{2,1,0:T(4,128)(2,1)S(1)} all-to-all(bf16[8,3,800]{2,1,0:T(4,128)(2,1)S(1)} %broadcast_in_dim.21), channel_id=1, replica_groups=mesh['x'=4,'zl'=2,'c'=2,'y'=4,'zh'=2] {'y','zh'}, dimensions={0} | all-to-all | bytes 76800 | tf_op jit(solution)/shard_map/all_to_all | solution.py:58
  107.2 15.6 %attend.1 = (bf16[1024,1600]{1,0:T(8,128)(2,1)}, bf16[1024,768]{1,0:T(8,128)(2,1)}, bf16[1024,256]{1,0:T(8,128)(2,1)}, f32[1024,4]{1,0:T(8,128)}, bf16[8,200,768]{2,1,0:T(8,128)(2,1)}) custom-call(s32[8]{0:T(128)} %stack.39.place_ref, bf16[1024,1600]{1,0:T(8,128)(2,1)} %all-gather.11.cloned.1.call-done.tokens_ref, f32[8,1600]{1,0:T(8,128)} %reshape.104.norm_ref, ...), custom_call_target="tpu_custom_call" | custom-call | flops 7549747200 | bytes 13636640 | tf_op jit(solution)/shard_map/attend/pallas_call | solution.py:118
  122.8 18.4 %all_to_all.56.slots_ref = bf16[8,128,256]{2,1,0:T(8,128)(2,1)} all-to-all(bf16[8,128,256]{2,1,0:T(8,128)(2,1)} %bitcast.41), channel_id=1, replica_groups=mesh['x'=4,'zl'=2,'c'=2,'y'=4,'zh'=2] {'y','c'}, dimensions={0} | all-to-all | bytes 1048576 | tf_op jit(solution)/shard_map/all_to_all | solution.py:58
  157.5 16.8 %collective-permute-done.10.refs_2_ = bf16[200,800]{1,0:T(8,128)(2,1)S(1)} collective-permute-done((bf16[200,800]{1,0:T(8,128)(2,1)S(1)}, bf16[200,800]{1,0:T(8,128)(2,1)S(1)}, u32[]{:S(2)}, u32[]{:S(2)}) %collective-permute-start.10) | collective-permute-done | bytes 320032 | tf_op jit(solution)/shard_map/ppermute | solution.py:34
  182.9 14.1 %all-to-all-start.2 = ((bf16[8,128,200]{1,2,0:T(8,128)(2,1)}), bf16[8,128,200]{1,2,0:T(8,128)(2,1)S(1)}, u32[]{:S(2)}, u32[]{:S(2)}) async-start(bf16[8,128,200]{1,2,0:T(8,128)(2,1)} %copy.70), calls=%async_computation.2 | async-start | bytes 819200 | tf_op jit(solution)/shard_map/all_to_all | solution.py:58
  196.9 8.5 %fusion.grad_ref = f32[1024,800]{1,0:T(8,128)} fusion(bf16[1024,1600]{1,0:T(8,128)(2,1)} %all-gather.17.cloned.1.call-done.right_ref, bf16[800,1600]{1,0:T(8,128)(2,1)} %param.27, bf16[800,1600]{1,0:T(8,128)(2,1)} %collective-permute-done.17, pred[]{:T(512)S(6)} %eq.4), kind=kOutput, calls=%fused_computation.2 | convolution fusion | flops 2622720000 | bytes 11673601 | tf_op jit(solution)/shard_map/dot_general | solution.py:107
  214.1 14.8 %hidden.1 = (bf16[1024,800]{1,0:T(8,128)(2,1)}, bf16[1024,800]{1,0:T(8,128)(2,1)}, f32[1,800]{1,0:T(1,128)}, bf16[1024,1600]{1,0:T(8,128)(2,1)}) custom-call(s32[8]{0:T(128)} %stack.39.place_ref, bf16[1024,1600]{1,0:T(8,128)(2,1)} %all-gather.15.cloned.1.call-done.second_ref.left_ref, bf16[1600,800]{1,0:T(8,128)(2,1)} %bitcast.40, ...), custom_call_target="tpu_custom_call" | custom-call | flops 15728640000 | bytes 15673632 | tf_op jit(solution)/shard_map/hidden/pallas_call | solution.py:118
  236.4 9.2 %fc_grad.1 = (bf16[4,4,32,800]{3,2,1,0:T(8,128)(2,1)}, bf16[4,4,32,800]{3,2,1,0:T(8,128)(2,1)}, bf16[4,4,32,800]{3,2,1,0:T(8,128)(2,1)}, bf16[4,4,32,800]{3,2,1,0:T(8,128)(2,1)}) custom-call(s32[8]{0:T(128)} %stack.39.place_ref, bf16[1024,1600]{1,0:T(8,128)(2,1)} %all-gather.15.cloned.1.call-done.second_ref.left_ref, ...), custom_call_target="tpu_custom_call" | custom-call | flops 7864320000 | bytes 8192032 | tf_op jit(solution)/shard_map/fc_grad/pallas_call | solution.py:118
  252.7 10.6 %reduce-scatter.4.cloned.1.call-done.grad_ref = bf16[128,1600]{1,0:T(8,128)(2,1)} async-done(((bf16[1024,1600]{1,0:T(8,128)(2,1)}), bf16[128,1600]{1,0:T(8,128)(2,1)}) %reduce-scatter.4.cloned.1.call-update) | async-done | bytes 409616 | tf_op jit(solution)/shard_map/reduce_scatter | solution.py:66
  269.8 8.1 %all-to-all-start.3 = ((bf16[8,128,256]{2,1,0:T(8,128)(2,1)}), bf16[8,128,256]{2,1,0:T(8,128)(2,1)S(1)}, u32[]{:S(2)}, u32[]{:S(2)}) async-start(bf16[8,128,256]{2,1,0:T(8,128)(2,1)} %get-tuple-element.149), calls=%async_computation.5 | async-start | bytes 1048576 | tf_op jit(solution)/shard_map/all_to_all | solution.py:58
  279.0 8.7 %all-to-all-done.3 = bf16[8,128,256]{2,1,0:T(8,128)(2,1)S(1)} async-done(((bf16[8,128,256]{2,1,0:T(8,128)(2,1)}), bf16[8,128,256]{2,1,0:T(8,128)(2,1)S(1)}, u32[]{:S(2)}, u32[]{:S(2)}) %all-to-all-start.3) | async-done | bytes 524320 | tf_op jit(solution)/shard_map/all_to_all | solution.py:58
  288.5 15.3 %attend_back.1 = (bf16[1024,768]{1,0:T(8,128)(2,1)}, bf16[1024,1600]{1,0:T(8,128)(2,1)}, f32[1,768]{1,0:T(1,128)}) custom-call(s32[8]{0:T(128)} %stack.39.place_ref, bf16[1024,768]{1,0:T(8,128)(2,1)} %get-tuple-element.134.qkv_ref, bf16[1024,256]{1,0:T(8,128)(2,1)} %bitcast.42, bf16[1024,256]{1,0:T(8,128)(2,1)} %get-tuple-element.119.out_ref, ...), custom_call_target="tpu_custom_call" | custom-call | flops 7549747200 | bytes 9948192 | tf_op jit(solution)/shard_map/attend_back/pallas_call | solution.py:118
  314.2 18.9 %collective-permute-done.18.refs_1_ = bf16[4,4,32,800]{3,2,1,0:T(8,128)(2,1)S(1)} collective-permute-done((bf16[4,4,32,800]{3,2,1,0:T(8,128)(2,1)}, bf16[4,4,32,800]{3,2,1,0:T(8,128)(2,1)S(1)}, u32[]{:S(2)}, u32[]{:S(2)}) %collective-permute-start.18) | collective-permute-done | bytes 819232 | tf_op jit(solution)/shard_map/ppermute | solution.py:34
  335.6 20.8 %collective-permute-done.20.refs_3_ = bf16[4,4,32,800]{3,2,1,0:T(8,128)(2,1)S(1)} collective-permute-done((bf16[4,4,32,800]{3,2,1,0:T(8,128)(2,1)}, bf16[4,4,32,800]{3,2,1,0:T(8,128)(2,1)S(1)}, u32[]{:S(2)}, u32[]{:S(2)}) %collective-permute-start.20) | collective-permute-done | bytes 819232 | tf_op jit(solution)/shard_map/ppermute | solution.py:34
  389.0 44.3 %all-to-all-done.5 = bf16[16,4,32,768]{3,2,1,0:T(8,128)(2,1)S(1)} async-done(((bf16[16,4,32,768]{3,2,1,0:T(8,128)(2,1)}), bf16[16,4,32,768]{3,2,1,0:T(8,128)(2,1)S(1)}, u32[]{:S(2)}, u32[]{:S(2)}) %all-to-all-start.5) | async-done | bytes 3145760 | tf_op jit(solution)/shard_map/all_to_all | solution.py:58
  472.1 13.6 %collective-permute-done.37.refs_1_ = bf16[4,32,800]{2,1,0:T(8,128)(2,1)S(1)} collective-permute-done((bf16[4,32,800]{2,1,0:T(8,128)(2,1)}, bf16[4,32,800]{2,1,0:T(8,128)(2,1)S(1)}, u32[]{:S(2)}, u32[]{:S(2)}) %collective-permute-start.37) | collective-permute-done | bytes 204832 | tf_op jit(solution)/shard_map/ppermute | solution.py:42
  499.9 8.2 %collective-permute-done.39.refs_2_ = bf16[2,4,32,800]{3,2,1,0:T(8,128)(2,1)} collective-permute-done((bf16[2,4,32,800]{3,2,1,0:T(8,128)(2,1)}, bf16[2,4,32,800]{3,2,1,0:T(8,128)(2,1)}, u32[]{:S(2)}, u32[]{:S(2)}) %collective-permute-start.39) | collective-permute-done | bytes 409632 | tf_op jit(solution)/shard_map/ppermute | solution.py:34
  508.1 11.6 %collective-permute-done.38.refs_1_ = bf16[2,4,32,800]{3,2,1,0:T(8,128)(2,1)} collective-permute-done((bf16[2,4,32,800]{3,2,1,0:T(8,128)(2,1)}, bf16[2,4,32,800]{3,2,1,0:T(8,128)(2,1)}, u32[]{:S(2)}, u32[]{:S(2)}) %collective-permute-start.38) | collective-permute-done | bytes 409632 | tf_op jit(solution)/shard_map/ppermute | solution.py:34
  539.3 10.1 %all-to-all-done.7 = bf16[16,16,1600]{2,1,0:T(8,128)(2,1)S(1)} async-done(((bf16[16,16,1600]{2,1,0:T(8,128)(2,1)}), bf16[16,16,1600]{2,1,0:T(8,128)(2,1)S(1)}, u32[]{:S(2)}, u32[]{:S(2)}) %all-to-all-start.7) | async-done | bytes 819232 | tf_op jit(solution)/shard_map/all_to_all | solution.py:58
  560.1 13.4 %all_to_all.58.own_ref = bf16[16,16,1600]{2,1,0:T(8,128)(2,1)S(1)} all-to-all(bf16[16,16,1600]{2,1,0:T(8,128)(2,1)S(1)} %broadcast_in_dim.26), channel_id=1, replica_groups=mesh['x'=4,'zl'=2,'c'=2,'y'=4,'zh'=2] {'zl','x','zh'}, dimensions={0} | all-to-all | bytes 1638400 | tf_op jit(solution)/shard_map/all_to_all | solution.py:58
  588.4 10.1 %collective-permute-done.47.refs_1_ = bf16[4,32,768]{2,1,0:T(8,128)(2,1)S(1)} collective-permute-done((bf16[4,32,768]{2,1,0:T(8,128)(2,1)S(1)}, bf16[4,32,768]{2,1,0:T(8,128)(2,1)S(1)}, u32[]{:S(2)}, u32[]{:S(2)}) %collective-permute-start.47) | collective-permute-done | bytes 196640 | tf_op jit(solution)/shard_map/ppermute | solution.py:42
  610.2 10.5 %collective-permute-done.50.refs_3_ = bf16[2,4,32,768]{3,2,1,0:T(8,128)(2,1)} collective-permute-done((bf16[2,4,32,768]{3,2,1,0:T(8,128)(2,1)}, bf16[2,4,32,768]{3,2,1,0:T(8,128)(2,1)}, u32[]{:S(2)}, u32[]{:S(2)}) %collective-permute-start.50) | collective-permute-done | bytes 393248 | tf_op jit(solution)/shard_map/ppermute | solution.py:34
  629.9 9.1 %fc_total.1 = f32[200,6400]{1,0:T(8,128)} custom-call(s32[8]{0:T(128)} %stack.39.place_ref, bf16[2,4,32,800]{3,2,1,0:T(8,128)(2,1)} %fc_both.1.refs_0_, bf16[2,4,32,800]{3,2,1,0:T(8,128)(2,1)} %collective-permute-done.38.refs_1_, bf16[2,4,32,800]{3,2,1,0:T(8,128)(2,1)} %collective-permute-done.39.refs_2_, ...), custom_call_target="tpu_custom_call" | custom-call | bytes 8396832 | tf_op jit(solution)/shard_map/fc_total/pallas_call | solution.py:118
  639.1 9.1 %qkv_total.1 = f32[200,4800]{1,0:T(8,128)} custom-call(s32[8]{0:T(128)} %stack.39.place_ref, bf16[2,4,32,768]{3,2,1,0:T(8,128)(2,1)} %qkv_both.1.refs_0_, bf16[2,4,32,768]{3,2,1,0:T(8,128)(2,1)} %collective-permute-done.48.refs_1_, bf16[2,4,32,768]{3,2,1,0:T(8,128)(2,1)} %collective-permute-done.49.refs_2_, ...), custom_call_target="tpu_custom_call" | custom-call | bytes 6985760 | tf_op jit(solution)/shard_map/qkv_total/pallas_call | solution.py:118
  (314 shorter events, 321.6 us)
Async XLA Ops:
  7.2 99.9 %all-gather.11.cloned.1.call-start = ((), (), s32[]{:S(2)}) async-start(), calls=%async_computation.17 | async-start | bytes 3833856 | tf_op jit(solution)/shard_map/all_gather | solution.py:62
  21.2 120.0 %all-gather.13.cloned.1.call-start = ((), (), s32[]{:S(2)}) async-start(), calls=%async_computation.18 | async-start | bytes 5990400 | tf_op jit(solution)/shard_map/all_gather | solution.py:62
  66.2 116.7 %all-gather.17.cloned.1.call-start = ((), (), s32[]{:S(2)}) async-start(), calls=%async_computation.20 | async-start | bytes 3833856 | tf_op jit(solution)/shard_map/all_gather | solution.py:62
  66.5 33.3 %collective-permute-start.16 = (bf16[128,1600]{1,0:T(8,128)(2,1)S(1)}, bf16[128,1600]{1,0:T(8,128)(2,1)S(1)}, u32[]{:S(2)}, u32[]{:S(2)}) collective-permute-start(bf16[128,1600]{1,0:T(8,128)(2,1)S(1)} %bitcast.43), channel_id=1, source_target_pairs={{0,0},{1,8},{8,1},{9,9},{2,2},{3,10},{10,3},{11,11},{4,4},{5,12},{... | collective-permute-start | bytes 1228808 | tf_op jit(solution)/shard_map/ppermute | solution.py:46
  100.7 113.3 %all-gather.15.cloned.1.call-start = ((), (), s32[]{:S(2)}) async-start(), calls=%async_computation.19 | async-start | bytes 3833856 | tf_op jit(solution)/shard_map/all_gather | solution.py:62
  146.5 50.5 %collective-permute-start.17 = (bf16[800,1600]{1,0:T(8,128)(2,1)}, bf16[800,1600]{1,0:T(8,128)(2,1)}, u32[]{:S(2)}, u32[]{:S(2)}) collective-permute-start(bf16[800,1600]{1,0:T(8,128)(2,1)} %param.27), channel_id=1, source_target_pairs={{1,8},{8,1},{3,10},{10,3},{5,12},{12,5},{7,14},{14,7},{17,24},{24,... | collective-permute-start | bytes 7680008 | tf_op jit(solution)/shard_map/ppermute | solution.py:50
  174.9 30.5 %collective-permute-start.12 = (bf16[200,800]{1,0:T(8,128)(2,1)S(1)}, bf16[200,800]{1,0:T(8,128)(2,1)S(1)}, u32[]{:S(2)}, u32[]{:S(2)}) collective-permute-start(bf16[200,800]{1,0:T(8,128)(2,1)S(1)} %copy-done.20), channel_id=1, source_target_pairs={{0,1},{1,0},{2,3},{3,2},{4,5},{5,4},{6,7},{7,6},{8,9},{9,8},{10,11... | collective-permute-start | bytes 960008 | tf_op jit(solution)/shard_map/ppermute | solution.py:42
  174.9 30.6 %collective-permute-start.13 = (bf16[200,800]{1,0:T(8,128)(2,1)S(1)}, bf16[200,800]{1,0:T(8,128)(2,1)S(1)}, u32[]{:S(2)}, u32[]{:S(2)}) collective-permute-start(bf16[200,800]{1,0:T(8,128)(2,1)S(1)} %collective-permute-done.9.refs_1_), channel_id=1, source_target_pairs={{0,1},{1,0},{2,3},{3,2},{4,5},{5,4},{6,7},{7,6},{8,9},{9,8},{10,11... | collective-permute-start | bytes 960008 | tf_op jit(solution)/shard_map/ppermute | solution.py:42
  178.0 31.8 %collective-permute-start.15 = (bf16[200,800]{1,0:T(8,128)(2,1)S(1)}, bf16[200,800]{1,0:T(8,128)(2,1)S(1)}, u32[]{:S(2)}, u32[]{:S(2)}) collective-permute-start(bf16[200,800]{1,0:T(8,128)(2,1)S(1)} %collective-permute-done.11.refs_3_), channel_id=1, source_target_pairs={{0,1},{1,0},{2,3},{3,2},{4,5},{5,4},{6,7},{7,6},{8,9},{9,8},{10,11... | collective-permute-start | bytes 960008 | tf_op jit(solution)/shard_map/ppermute | solution.py:42
  182.9 31.2 %all-to-all-start.2 = ((bf16[8,128,200]{1,2,0:T(8,128)(2,1)}), bf16[8,128,200]{1,2,0:T(8,128)(2,1)S(1)}, u32[]{:S(2)}, u32[]{:S(2)}) async-start(bf16[8,128,200]{1,2,0:T(8,128)(2,1)} %copy.70), calls=%async_computation.2 | async-start | bytes 819200 | tf_op jit(solution)/shard_map/all_to_all | solution.py:58
  196.9 66.4 %reduce-scatter.4.cloned.1.call-start = ((), (), s32[]{:S(2)}) async-start(), calls=%async_computation.14 | async-start | bytes 3833856 | tf_op jit(solution)/shard_map/reduce_scatter | solution.py:66
  228.8 77.2 %reduce-scatter.6.cloned.1.call-start = ((), (), s32[]{:S(2)}) async-start(), calls=%async_computation.15 | async-start | bytes 3833856 | tf_op jit(solution)/shard_map/reduce_scatter | solution.py:66
  278.0 155.3 %reduce-scatter.8.cloned.1.call-start = ((), (), s32[]{:S(2)}) async-start(), calls=%async_computation.16 | async-start | bytes 3833856 | tf_op jit(solution)/shard_map/reduce_scatter | solution.py:66
  306.1 58.2 %all-to-all-start.4 = ((bf16[4,4,56,1600]{3,2,1,0:T(8,128)(2,1)}), bf16[4,4,56,1600]{3,2,1,0:T(8,128)(2,1)S(1)}, u32[]{:S(2)}, u32[]{:S(2)}) async-start(bf16[4,4,56,1600]{3,2,1,0:T(8,128)(2,1)} %proj_grad.1), calls=%async_computation.7 | async-start | bytes 5963776 | tf_op jit(solution)/shard_map/all_to_all | solution.py:58
  313.2 43.1 %collective-permute-start.20 = (bf16[4,4,32,800]{3,2,1,0:T(8,128)(2,1)}, bf16[4,4,32,800]{3,2,1,0:T(8,128)(2,1)S(1)}, u32[]{:S(2)}, u32[]{:S(2)}) collective-permute-start(bf16[4,4,32,800]{3,2,1,0:T(8,128)(2,1)} %get-tuple-element.160), channel_id=1, source_target_pairs={{96,0},{0,32},{32,64},{64,96},{97,1},{1,33},{33,65},{65,97},{98,2}... | collective-permute-start | bytes 2457608 | tf_op jit(solution)/shard_map/ppermute | solution.py:34
  381.7 51.6 %all-to-all-start.5 = ((bf16[16,4,32,768]{3,2,1,0:T(8,128)(2,1)}), bf16[16,4,32,768]{3,2,1,0:T(8,128)(2,1)S(1)}, u32[]{:S(2)}, u32[]{:S(2)}) async-start(bf16[16,4,32,768]{3,2,1,0:T(8,128)(2,1)} %qkv_grad.1), calls=%async_computation.8 | async-start | bytes 6291456 | tf_op jit(solution)/shard_map/all_to_all | solution.py:58
  387.0 186.5 %all-gather.19.cloned.1.call-start = ((), (), s32[]{:S(2)}) async-start(), calls=%async_computation.21 | async-start | bytes 3168256 | tf_op jit(solution)/shard_map/all_gather | solution.py:62
  436.1 33.6 %collective-permute-start.29 = (bf16[128,1600]{1,0:T(8,128)(2,1)}, bf16[128,1600]{1,0:T(8,128)(2,1)}, u32[]{:S(2)}, u32[]{:S(2)}) collective-permute-start(bf16[128,1600]{1,0:T(8,128)(2,1)} %get-tuple-element.179.refs_0_), channel_id=1, source_target_pairs={{4,0},{6,2},{0,4},{2,6},{5,1},{7,3},{1,5},{3,7},{12,8},{14,10},{8,... | collective-permute-start | bytes 1228808 | tf_op jit(solution)/shard_map/ppermute | solution.py:34
  436.1 35.9 %collective-permute-start.28 = (bf16[128,1600]{1,0:T(8,128)(2,1)}, bf16[128,1600]{1,0:T(8,128)(2,1)}, u32[]{:S(2)}, u32[]{:S(2)}) collective-permute-start(bf16[128,1600]{1,0:T(8,128)(2,1)} %get-tuple-element.179.refs_0_), channel_id=1, source_target_pairs={{2,0},{4,2},{6,4},{0,6},{3,1},{5,3},{7,5},{1,7},{10,8},{12,10},{14... | collective-permute-start | bytes 1228808 | tf_op jit(solution)/shard_map/ppermute | solution.py:34
  437.4 51.7 %collective-permute-start.31 = (bf16[128,1600]{1,0:T(8,128)(2,1)}, bf16[128,1600]{1,0:T(8,128)(2,1)S(1)}, u32[]{:S(2)}, u32[]{:S(2)}) collective-permute-start(bf16[128,1600]{1,0:T(8,128)(2,1)} %get-tuple-element.179.refs_0_), channel_id=1, source_target_pairs={{0,8},{8,0},{1,9},{9,1},{2,10},{10,2},{3,11},{11,3},{4,12},{12,4},... | collective-permute-start | bytes 1228808 | tf_op jit(solution)/shard_map/ppermute | solution.py:54
  443.7 45.7 %collective-permute-start.34 = (bf16[128,1600]{1,0:T(8,128)(2,1)S(1)}, bf16[128,1600]{1,0:T(8,128)(2,1)S(1)}, u32[]{:S(2)}, u32[]{:S(2)}) collective-permute-start(bf16[128,1600]{1,0:T(8,128)(2,1)S(1)} %collective-permute-done.30.refs_3_), channel_id=1, source_target_pairs={{0,8},{8,0},{1,9},{9,1},{2,10},{10,2},{3,11},{11,3},{4,12},{12,4},... | collective-permute-start | bytes 1228808 | tf_op jit(solution)/shard_map/ppermute | solution.py:54
  490.6 29.1 %collective-permute-start.38 = (bf16[2,4,32,800]{3,2,1,0:T(8,128)(2,1)}, bf16[2,4,32,800]{3,2,1,0:T(8,128)(2,1)}, u32[]{:S(2)}, u32[]{:S(2)}) collective-permute-start(bf16[2,4,32,800]{3,2,1,0:T(8,128)(2,1)} %fc_both.1.refs_0_), channel_id=1, source_target_pairs={{32,0},{64,32},{96,64},{0,96},{33,1},{65,33},{97,65},{1,97},{34,2}... | collective-permute-start | bytes 1228808 | tf_op jit(solution)/shard_map/ppermute | solution.py:34
  573.5 79.6 %collective-permute-start.56 = (bf16[16,56,1600]{2,1,0:T(8,128)(2,1)}, bf16[16,56,1600]{2,1,0:T(8,128)(2,1)}, u32[]{:S(2)}, u32[]{:S(2)}) collective-permute-start(bf16[16,56,1600]{2,1,0:T(8,128)(2,1)} %bitcast.38), channel_id=1, source_target_pairs={{0,8},{8,0},{1,9},{9,1},{2,10},{10,2},{3,11},{11,3},{4,12},{12,4},... | collective-permute-start | bytes 8601608 | tf_op jit(solution)/shard_map/ppermute | solution.py:54
  606.1 42.1 %all-to-all-start.10 = ((f32[16,3,800]{2,1,0:T(4,128)}), f32[16,3,800]{2,1,0:T(4,128)S(1)}, u32[]{:S(2)}, u32[]{:S(2)}) async-start(f32[16,3,800]{2,1,0:T(4,128)} %broadcast_in_dim.27), calls=%async_computation.13 | async-start | bytes 458752 | tf_op jit(solution)/shard_map/all_to_all | solution.py:58
  (101 other events, 1781.2 us)
Sparse Core Ops, SparseCore 0:
  21.4 29.7 all-gather.10
  66.3 34.9 all-gather.12
  103.0 28.6 all-gather.16
  146.6 38.1 all-gather.14
  229.0 34.3 reduce-scatter.3
  266.2 39.7 reduce-scatter.5
  309.0 35.7 reduce-scatter.7
  433.4 93.6 all-gather.18

commit v6 on v5

--- a/solution.py
+++ b/solution.py
@@ -23,15 +23,11 @@
 REP = ("x", "zl", "c")
 GRP = ("y", "zh")
 TEAM = ("y", "c")
-REPLICAS = ("zl", "x", "zh")
-Z_RING = ("zl", "zh")
-Z_PLACES = (0, 2, 1, 3)
 ROLES = [(0, 0), (1, 2), (2, 1), (3, 3)]
 
 
 def ring(value, axis, step):
-    index = Z_PLACES if axis == Z_RING else range(4)
-    return lax.ppermute(value, axis, [(index[(i + step) % 4], index[i]) for i in range(4)])
+    return lax.ppermute(value, axis, [((i + step) % 4, i) for i in range(4)])
 
 
 def ring_all(values, axis):
@@ -64,20 +60,6 @@
 
 def team_sum(parts):
     return lax.psum_scatter(parts.astype(bf16), TEAM, scatter_dimension=0, tiled=True)
-
-
-def windows(rows, count):
-    tiles = rows // 8
-    starts = [tiles * i // count for i in range(count)]
-    size = max(b - a for a, b in zip(starts, starts[1:] + [tiles]))
-    return size * 8, [8 * s for s in starts]
-
-
-def joined(parts, starts, rows, axis):
-    ends = starts[1:] + [rows]
-    return jnp.concatenate(
-        [lax.slice_in_dim(p, 0, e - s, axis=axis) for p, s, e in zip(parts, starts, ends)], axis
-    )
 
 
 def norm_parts(value, gain, shift):
@@ -136,41 +118,29 @@
 Y, C, RANK, ZH, Z, X, ZL, MINE = range(8)
 
 
-def qkv_columns_kernel(place_ref, weight_ref, *refs):
-    out_refs, held_ref = refs[:4], refs[4]
+def qkv_columns_kernel(place_ref, weight_ref, out_ref):
     c = place_ref[C]
     width = weight_ref.shape[1] // 3
     for part in range(3):
-        lanes = slice(part * SLOT_WIDTH, (part + 1) * SLOT_WIDTH)
         for y in range(4):
             start = part * width + 2 * STRIDE * y
             even = weight_ref[:, start : start + SLOT_WIDTH]
             odd = weight_ref[:, start + STRIDE : start + STRIDE + SLOT_WIDTH]
-            held_ref[y, :, lanes] = jnp.where(c == 0, even, odd)
-    for k in range(4):
-        out_refs[k][...] = held_ref[lax.rem(place_ref[Y] + 4 - k, 4)]
-
-
-def fc_columns_kernel(place_ref, weight_ref, *refs):
-    out_refs, held_ref = refs[:4], refs[4]
+            block = jnp.where(c == 0, even, odd)
+            for zh in range(2):
+                out_ref[2 * y + zh, :, part * SLOT_WIDTH : (part + 1) * SLOT_WIDTH] = block
+
+
+def fc_columns_kernel(place_ref, weight_ref, out_ref):
     c = place_ref[C]
     hidden = weight_ref.shape[1] // 8
     for y in range(4):
         start = 2 * hidden * y
         even = weight_ref[:, start : start + hidden]
         odd = weight_ref[:, start + hidden : start + 2 * hidden]
-        held_ref[y] = jnp.where(c == 0, even, odd)
-    for k in range(4):
-        out_refs[k][...] = held_ref[lax.rem(place_ref[Y] + 4 - k, 4)]
-
-
-def fc_whole_kernel(place_ref, *refs):
-    out_ref = refs[8]
-    zh = place_ref[ZH]
-    for k in range(4):
-        y = lax.rem(place_ref[Y] + k, 4)
-        out_ref[2 * y + zh] = refs[k][...]
-        out_ref[2 * y + 1 - zh] = refs[4 + k][...]
+        block = jnp.where(c == 0, even, odd)
+        for zh in range(2):
+            out_ref[2 * y + zh] = block
 
 
 def branch_kernel(
@@ -217,45 +187,14 @@
     sums_ref[3:4, :] = jnp.sum(cot, axis=0, keepdims=True)
 
 
-def column_grad_kernel(left_ref, right_ref, out_ref):
-    shard = left_ref.shape[1] // 8
-    size, starts = windows(shard, 8)
-    grad = dot_rows(left_ref[...], right_ref[...])
-    for y in range(4):
-        for zh in range(2):
-            base = (2 * y + zh) * shard
-            for i, start in enumerate(starts):
-                out_ref[2 * i + zh, y] = grad[base + start : base + start + size].astype(bf16)
-
-
-def column_ring_kernel(place_ref, left_ref, right_ref, *refs):
-    out_refs, held_ref = refs[:4], refs[4]
-    shard = left_ref.shape[1] // 8
-    size, starts = windows(shard, 8)
-    held_ref[...] = dot_rows(left_ref[...], right_ref[...])
-    for k in range(4):
-        x = lax.rem(place_ref[X] + 4 - k, 4)
-        for z in range(4):
-            for y in range(4):
-                base = (2 * y + z // 2) * shard + starts[4 * (z % 2)]
-                at = pl.multiple_of(base + starts[1] * x, 8)
-                out_refs[k][z, y] = held_ref[pl.ds(at, size), :].astype(bf16)
-
-
-def row_grad_kernel(left_ref, right_ref, out_ref):
-    rows = left_ref.shape[1]
-    size, starts = windows(rows, 16)
-    grad = dot_rows(left_ref[...], right_ref[...])
-    for i, start in enumerate(starts):
-        zl, x, zh = i // 8, i // 2 % 4, i % 2
-        out_ref[2 * zl + zh, x] = grad[start : start + size].astype(bf16)
+def weight_grad_kernel(left_ref, right_ref, out_ref):
+    out_ref[...] = dot_rows(left_ref[...], right_ref[...]).astype(bf16)
 
 
 def out_grad_kernel(place_ref, left_ref, *refs):
     blocks, out_ref, held_ref = refs[:8], refs[8], refs[9]
     c = place_ref[C]
-    rows = left_ref.shape[2]
-    size, starts = windows(rows, 16)
+    rows = held_ref.shape[0]
     for k in range(4):
         y = lax.rem(place_ref[Y] + k, 4)
         term = dot_rows(left_ref[2 * y + c], blocks[k][...])
@@ -264,89 +203,36 @@
             held_ref[...] = term
         else:
             held_ref[...] += term
-    for i, start in enumerate(starts):
-        out_ref[i] = held_ref[start : start + size, :].astype(bf16)
-
-
-def fold_kernel(which, place_ref, *refs):
-    for k in range(4):
-        at = lax.rem(place_ref[which] + 4 - k, 4)
-        total = refs[0][at].astype(f32)
-        for j in range(1, 4):
-            total = total + refs[j][at].astype(f32)
-        refs[4 + k][...] = total.astype(bf16)
-
-
-def fold_stack_kernel(which, place_ref, parts_ref, *refs):
-    for k in range(4):
-        at = lax.rem(place_ref[which] + 4 - k, 4)
-        total = parts_ref[0, at].astype(f32)
-        for j in range(1, 4):
-            total = total + parts_ref[j, at].astype(f32)
-        refs[k][...] = total.astype(bf16)
-
-
-def stack_kernel(*refs):
-    for k, ref in enumerate(refs[:-1]):
-        refs[-1][k] = ref[...]
-
-
-def column_total_kernel(spans, ringed, place_ref, *refs):
-    out_ref = refs[8]
-    shard = out_ref.shape[0]
-    _, starts = windows(shard, 8)
-    step = starts[1]
-    for j in range(4):
-        x = lax.rem(place_ref[X] + j, 4)
-        for flip in range(2):
-            window = (place_ref[ZL] if flip == 0 else 1 - place_ref[ZL]) * 4 + x
-            at = pl.multiple_of(window * step, 8)
-            for rank in range(8):
-                k = lax.rem(rank // 2 + 4 - place_ref[Y], 4) if ringed else rank // 2
-                block = jnp.where(
-                    place_ref[C] == rank % 2, refs[j][flip, k], refs[4 + j][flip, k]
-                ).astype(f32)
-                for source, target, wide in spans[rank]:
-                    out_ref[pl.ds(at, step), target : target + wide] = block[
-                        :step, source : source + wide
-                    ]
-
-                @pl.when(window == 7)
-                def _(block=block, rank=rank):
-                    for source, target, wide in spans[rank]:
-                        out_ref[7 * step + step :, target : target + wide] = block[
-                            step:, source : source + wide
-                        ]
+    out_ref[:rows, :] = held_ref[...].astype(bf16)
+    out_ref[rows:, :] = jnp.zeros((out_ref.shape[0] - rows, out_ref.shape[1]), bf16)
+
+
+def column_total_kernel(spans, place_ref, own_ref, other_ref, out_ref):
+    c = place_ref[C]
+    for rank in range(8):
+        own, other = own_ref[rank % 4], other_ref[rank % 4]
+        block = jnp.where(c == rank // 4, own, other).astype(f32)
+        for source, target, wide in spans[rank]:
+            out_ref[:, target : target + wide] = block[:, source : source + wide]
 
 
 def row_total_kernel(place_ref, own_ref, other_ref, out_ref):
-    mine = place_ref[MINE]
-    _, starts = windows(out_ref.shape[0], 16)
-    ends = starts[1:] + [out_ref.shape[0]]
-    for i, (start, end) in enumerate(zip(starts, ends)):
-        block = jnp.where(mine == 1, own_ref[i], other_ref[i])
-        out_ref[start:end, :] = block[: end - start].astype(f32)
-
-
-def attend_kernel(place_ref, tokens_ref, norm_ref, bias_ref, *refs):
-    pieces, (first_ref, qkv_ref, out_ref, top_ref, cols_ref) = refs[:8], refs[8:]
+    c = place_ref[C]
+    rows, half = out_ref.shape[0], own_ref.shape[0]
+    for part in range(2):
+        block = jnp.where(c == part, own_ref[...], other_ref[...]).astype(f32)
+        out_ref[part * half : min(rows, (part + 1) * half), :] = block[: rows - part * half]
+
+
+def attend_kernel(tokens_ref, cols_ref, norm_ref, bias_ref, first_ref, qkv_ref, out_ref, top_ref):
     length = tokens_ref.shape[0]
-    shard = cols_ref.shape[1]
-    zh = place_ref[ZH]
-    for k in range(4):
-        y = lax.rem(place_ref[Y] + k, 4)
-        cols_ref[2 * y + zh] = pieces[k][...]
-        cols_ref[2 * y + 1 - zh] = pieces[4 + k][...]
     gain = norm_ref[0:1, :]
     shift = norm_ref[1:2, :]
     for block in range(length // BLOCK):
         rows = slice(block * BLOCK, (block + 1) * BLOCK)
         first = norm_parts(tokens_ref[rows, :].astype(f32), gain, shift)[0].astype(bf16)
         first_ref[rows, :] = first
-        mixed = bias_ref[...]
-        for g in range(8):
-            mixed = mixed + dot(first[:, g * shard : (g + 1) * shard], cols_ref[g])
-        qkv_ref[rows, :] = mixed.astype(bf16)
+        qkv_ref[rows, :] = (dot(first, cols_ref[...]) + bias_ref[...]).astype(bf16)
     for head in range(SLOTS):
         lanes = slice(head * HEAD_DIM, (head + 1) * HEAD_DIM)
         keys = qkv_ref[:, SLOT_WIDTH + head * HEAD_DIM : SLOT_WIDTH + (head + 1) * HEAD_DIM]
@@ -482,33 +368,17 @@
     own_tokens = swap_roles(tokens.reshape(span, width))
     all_tokens = gather(own_tokens, TEAM).reshape(length, width)
     qkv_parts = call(
-        qkv_columns_kernel,
-        "qkv_columns",
-        [struct((shard, slots), bf16)] * 4,
-        place,
-        w_qkv,
-        scratch=[pltpu.VMEM((4, shard, slots), bf16)],
-    )
-    qkv_own = ring_all(qkv_parts, "y")
-    qkv_other = [flipped(part, "zh") for part in qkv_own]
+        qkv_columns_kernel, "qkv_columns", struct((8, shard, slots), bf16), place, w_qkv
+    )
+    qkv_cols = exchange(qkv_parts, GRP).reshape(width, slots)
+    place = after(place, qkv_parts)
+    fc_parts = call(fc_columns_kernel, "fc_columns", struct((8, shard, hidden), bf16), place, w_fc)
+    out_rows = swap_roles(after(w_out, qkv_parts))
     small = jnp.concatenate(
         [ln1_gain, ln1_bias, bias_q, bias_v, bias_out, ln2_gain, ln2_bias, bias_proj, bias_fc]
     ).reshape(3, hidden)
-    small_all = exchange(
-        after(jnp.broadcast_to(small, (8, 3, hidden)), qkv_parts[0]), GRP
-    )
-    out_rows = swap_roles(after(w_out, small_all))
-    own_cot = swap_roles(after(cotangent, out_rows).reshape(span, width))
-    place = after(place, small_all)
-    fc_parts = call(
-        fc_columns_kernel,
-        "fc_columns",
-        [struct((shard, hidden), bf16)] * 4,
-        place,
-        w_fc,
-        scratch=[pltpu.VMEM((4, shard, hidden), bf16)],
-    )
-    place = after(place, fc_parts[0])
+    small_all = exchange(after(jnp.broadcast_to(small, (8, 3, hidden)), qkv_cols), GRP)
+    own_cot = swap_roles(after(cotangent, qkv_cols).reshape(span, width))
 
     small_all = small_all.astype(f32)
     hidden_bias = lax.dynamic_index_in_dim(small_all, rank, 0, keepdims=False)[2:3]
@@ -521,12 +391,11 @@
         ]
     ).reshape(1, slots)
 
-    out_all = gather(after(out_rows, *qkv_own), TEAM).reshape(width, width)
-    all_cot = gather(after(own_cot, *qkv_other), TEAM).reshape(length, width)
-    proj_rows = swap_selected(after(w_proj, *qkv_other), stays)
-    fc_own = ring_all([after(part, *qkv_other) for part in fc_parts], "y")
-
-    first, qkv, attended_slots, top, qkv_cols = call(
+    out_all = gather(out_rows, TEAM).reshape(width, width)
+    all_cot = gather(after(own_cot, out_rows), TEAM).reshape(length, width)
+    proj_rows = swap_selected(after(w_proj, small_all), stays)
+
+    first, qkv, attended_slots, top = call(
         attend_kernel,
         "attend",
         (
@@ -534,19 +403,16 @@
             struct((length, slots), bf16),
             struct((length, SLOT_WIDTH), bf16),
             struct((length, SLOTS), f32),
-            struct((8, shard, slots), bf16),
         ),
-        after(place, bias_slots),
         all_tokens,
+        qkv_cols,
         vectors,
-        bias_slots,
-        *qkv_own,
-        *qkv_other,
+        after(bias_slots, fc_parts),
         flops=2 * length * width * slots,
     )
-    qkv_cols = qkv_cols.reshape(width, slots)
-    fc_other = [flipped(after(part, qkv), "zh") for part in fc_own]
-    attended = exchange(attended_slots.reshape(8, span, SLOT_WIDTH), TEAM)
+    attended = exchange(
+        after(attended_slots, proj_rows).reshape(8, span, SLOT_WIDTH), TEAM
+    )
     middle, second, attended_parts = call(
         branch_kernel,
         "branch",
@@ -564,17 +430,8 @@
     )
 
     second_all = gather(second, TEAM).reshape(length, width)
-    attended_own = exchange(attended_parts, TEAM)
+    fc_cols = exchange(after(fc_parts, second), GRP).reshape(width, hidden)
     grad_active = dot_cols(after(all_cot, second), proj_rows)
-    fc_cols = call(
-        fc_whole_kernel,
-        "fc_whole",
-        struct((8, shard, hidden), bf16),
-        place,
-        after(fc_own[0], second),
-        *fc_own[1:],
-        *fc_other,
-    ).reshape(width, hidden)
     active, grad_hidden, hidden_sums, second_parts = call(
         hidden_kernel,
         "hidden",
@@ -584,7 +441,7 @@
             struct((1, hidden), f32),
             struct((length, width), bf16),
         ),
-        after(place, attended_own),
+        place,
         second_all,
         fc_cols,
         hidden_bias,
@@ -592,29 +449,25 @@
         flops=4 * length * width * hidden,
     )
     grad_second = team_sum(second_parts)
-    window = windows(shard, 8)[0]
     fc_grad = call(
-        column_ring_kernel,
+        weight_grad_kernel,
         "fc_grad",
-        [struct((4, 4, window, hidden), bf16)] * 4,
-        place,
+        struct((width, hidden), bf16),
         second_all,
         grad_hidden,
-        scratch=[pltpu.VMEM((width, hidden), f32)],
         flops=2 * length * width * hidden,
     )
-    fc_grad = ring_all(fc_grad, "x")
-    row_window = windows(hidden, 16)[0]
+    fc_grad = swap_roles(fc_grad)
     proj_grad = call(
-        row_grad_kernel,
+        weight_grad_kernel,
         "proj_grad",
-        struct((4, 4, row_window, width), bf16),
+        struct((hidden, width), bf16),
         active,
         all_cot,
         flops=2 * length * width * hidden,
     )
     down_parts = dot(active, proj_rows).astype(bf16)
-    grad_second = after(grad_second, fc_grad[0], proj_grad, down_parts)
+    grad_second = after(grad_second, fc_grad, proj_grad, down_parts)
 
     grad_middle, grad_branch, grad_slots, branch_sums = call(
         branch_back_kernel,
@@ -636,17 +489,9 @@
     )
     grad_heads = exchange(grad_slots, TEAM).reshape(length, SLOT_WIDTH)
     down = team_sum(after(down_parts, grad_second))
-    proj_grad = exchange(after(proj_grad, grad_heads), Z_RING)
-
-    def fold(which, parts, name, *behind):
-        parts = [after(parts[0], *behind)] + parts[1:]
-        return call(
-            functools.partial(fold_kernel, which),
-            name,
-            [struct(parts[0].shape[1:], bf16)] * 4,
-            place,
-            *parts,
-        )
+    attended_own = exchange(after(attended_parts, fc_grad), TEAM)
+    proj_grad = swap_roles(after(proj_grad, grad_heads))
+    fc_grad = exchange(after(fc_grad, grad_heads).reshape(8, shard, hidden), GRP)
 
     grad_mixed, first_parts, mixed_sums = call(
         attend_back_kernel,
@@ -666,66 +511,46 @@
         flops=2 * length * width * slots,
     )
     grad_first = team_sum(after(first_parts, down))
-    place = after(place, grad_mixed)
-    proj_grad = ring_all(
-        call(
-            functools.partial(fold_stack_kernel, X),
-            "proj_fold",
-            [struct((row_window, width), bf16)] * 4,
-            place,
-            proj_grad,
-        ),
-        "x",
-    )
-    fc_grad = fold(Z, fc_grad, "fc_fold", place)
     qkv_grad = call(
-        column_grad_kernel,
+        weight_grad_kernel,
         "qkv_grad",
-        struct((16, 4, window, slots), bf16),
-        after(first, fc_grad[0], proj_grad[0]),
+        struct((width, slots), bf16),
+        after(first, down),
         grad_mixed,
         flops=2 * length * width * slots,
     )
     place = after(place, qkv_grad)
-    fc_grad = ring_all(fc_grad, Z_RING)
-    branch_own = ring_all([after(grad_branch, grad_mixed)] * 4, "y")
-    qkv_grad = exchange(after(qkv_grad, *fc_grad, *proj_grad), REPLICAS)
-    grad_first = after(grad_first, qkv_grad)
-
-    def replica_sum(parts):
-        return jnp.sum(parts.astype(f32), axis=0).astype(bf16)
-
-    def stacked(parts, name):
-        return call(
-            stack_kernel, name, struct((len(parts),) + parts[0].shape, bf16), *parts
-        )
-
-    def column_spread(near, name):
-        both = stacked([near, flipped(near, "zl")], name + "_both")
-        return ring_all([both] * 4, "x")
-
-    def row_total(whole, rows, name, *behind):
-        whole = after(whole, *behind)
-        return call(
-            row_total_kernel, name, struct((rows, width), f32), place, whole, other_core(whole)
-        )
-
-    fc_grad = ring_all(fold(Y, fc_grad, "fc_fold_last", place), "y")
-    proj_sum = sum(part.astype(f32) for part in proj_grad).astype(bf16)
-    proj_whole = gather(after(proj_sum, grad_first), REPLICAS)
-    fc_own_pieces = column_spread(stacked(fc_grad, "fc_near"), "fc")
+    qkv_grad = swap_roles(qkv_grad)
+
+    def halved(parts):
+        give = lax.dynamic_index_in_dim(parts, 1 - c, 0, keepdims=False)
+        keep = lax.dynamic_index_in_dim(parts, c, 0, keepdims=False)
+        return (keep.astype(f32) + other_core(give).astype(f32)).astype(bf16)
+
+    fc_half = halved(fc_grad.reshape(2, 4, shard, hidden))
+    proj_half = halved(proj_grad.reshape(2, hidden // 2, width))
+    fc_half, proj_half = lax.psum(after((fc_half, proj_half), grad_first), ("x", "zl"))
+
+    branch_own = ring_all([after(grad_branch, qkv_grad)] * 4, "y")
     branch_other = [other_core(part) for part in branch_own]
+    pad = shard // 2 // 8 * 8 + 8
     out_grad = call(
         out_grad_kernel,
         "out_grad",
-        struct((16, windows(shard, 16)[0], width), bf16),
-        after(place, fc_grad[1]),
+        struct((2 * pad, width), bf16),
+        place,
         attended_own,
         *branch_own,
         *branch_other,
         scratch=[pltpu.VMEM((shard, width), f32)],
         flops=2 * length * width * shard,
     )
+    qkv_grad = exchange(qkv_grad.reshape(8, shard, slots), GRP)
+    out_grad = swap_roles(out_grad)
+    qkv_half = halved(qkv_grad.reshape(2, 4, shard, slots))
+    out_half = halved(out_grad.reshape(2, pad, width))
+    qkv_half, out_half = lax.psum(after((qkv_half, out_half), fc_half), ("x", "zl"))
+
     grad_inputs, first_sums = call(
         input_back_kernel,
         "input_back",
@@ -733,19 +558,11 @@
         grad_first,
         own_tokens,
         grad_middle,
-        after(vectors, qkv_grad, out_grad, *fc_own_pieces),
+        after(vectors, qkv_grad),
     )
     inputs_home = swap_roles(grad_inputs).astype(f32).reshape(1, span, width)
-    output = middle + (after(down, grad_inputs).astype(f32) + vectors[7])
+    output = middle + (down.astype(f32) + vectors[7])
     output_home = swap_roles(output.astype(bf16)).reshape(1, span, width)
-    place = after(place, grad_inputs)
-    fc_own_pieces = [after(part, grad_inputs) for part in fc_own_pieces]
-    fc_pieces = fc_own_pieces + [other_core(part) for part in fc_own_pieces]
-    place = after(place, out_grad)
-    qkv_sum = exchange(replica_sum(after(qkv_grad, place)), "y")
-    out_grad = exchange(after(out_grad, qkv_sum), REPLICAS)
-    qkv_pieces = column_spread(qkv_sum, "qkv")
-    qkv_pieces = qkv_pieces + [other_core(part) for part in qkv_pieces]
 
     blank = jnp.zeros((1, width), f32)
     at = (0, STRIDE * rank)
@@ -762,25 +579,28 @@
     )
     small_terms = small_terms.reshape(8, 8, shard).transpose(1, 0, 2).reshape(8, 2, hidden)
     small_terms = jnp.concatenate([small_terms, hidden_term[:, None]], axis=1)
-    small_sum = jnp.sum(exchange(after(small_terms, out_grad), GRP), axis=0)
-    out_sum = replica_sum(out_grad)
-    out_whole = exchange(
-        after(jnp.broadcast_to(out_sum, (16,) + out_sum.shape), small_sum), REPLICAS
-    )
-    small_sum = jnp.broadcast_to(after(small_sum, out_whole), (16, 3, hidden))
-    small_sum = jnp.sum(exchange(small_sum, REP), axis=0)
+    small_sum = jnp.sum(exchange(small_terms, GRP), axis=0)
+    small_sum = jnp.sum(exchange(jnp.broadcast_to(small_sum, (16, 3, hidden)), REP), axis=0)
     owned = small_sum[:2].reshape(8, shard)
 
-    fc_spans = [[(0, rank * hidden, hidden)] for rank in range(8)]
-    fc_total = call(
-        functools.partial(column_total_kernel, fc_spans, True),
-        "fc_total",
-        struct((shard, 8 * hidden), f32),
-        after(place, qkv_sum),
-        *fc_pieces,
-    )
-    proj_total = row_total(proj_whole, hidden, "proj_total", out_whole)
-    out_total = row_total(out_whole, shard, "out_total")
+    def column_total(half, spans, name):
+        count = max(target + wide for span in spans for _, target, wide in span)
+        return call(
+            functools.partial(column_total_kernel, spans),
+            name,
+            struct((shard, count), f32),
+            place,
+            half,
+            other_core(half),
+        )
+
+    def row_total(half, rows, name):
+        return call(
+            row_total_kernel, name, struct((rows, width), f32), place, half, other_core(half)
+        )
+
+    fc_total = column_total(fc_half, [[(0, r * hidden, hidden)] for r in range(8)], "fc_total")
+    proj_total = row_total(proj_half, hidden, "proj_total")
     qkv_spans = [
         [
             (p * SLOT_WIDTH, p * width + STRIDE * r, STRIDE if r < 7 else SLOT_WIDTH)
@@ -788,13 +608,8 @@
         ]
         for r in range(8)
     ]
-    qkv_total = call(
-        functools.partial(column_total_kernel, qkv_spans, False),
-        "qkv_total",
-        struct((shard, 3 * width), f32),
-        after(place, fc_total),
-        *qkv_pieces,
-    )
+    qkv_total = column_total(qkv_half, qkv_spans, "qkv_total")
+    out_total = row_total(out_half, shard, "out_total")
     return (
         output_home,
         inputs_home,

time: 674 us -> 805 us (1.19)
  waiting for transfers between devices: 268 us -> 412 us
  Pallas kernels: 139 us -> 109 us
  blocking collectives: 49 us -> 71.8 us
  starting transfers between devices: 142 us -> 122 us
  other arithmetic: 4.7 us -> 16.9 us
    psum x0 -> x2, waiting for transfers between devices: none -> 201 us  [the longest x1 131 us: per_device(): lax.psum(after((qkv_half, out_half), fc_half), ('x', 'zl'))]
    ppermute x37 -> x3, waiting for transfers between devices: 181 us -> 14.7 us  [ring(): return lax.ppermute(value, axis, [((i + step) % 4, i) for i in range(4)])]
    ppermute x5 -> x9, waiting for transfers between devices: 5.81 us -> 86.4 us  [swap_roles(): return lax.ppermute(value, ('c', 'zh'), ROLES)]
    ppermute x37 -> x3, starting transfers between devices: 46.5 us -> 2.13 us  [ring(): return lax.ppermute(value, axis, [((i + step) % 4, i) for i in range(4)])]
    pallas_call x23 -> x16, Pallas kernels: 139 us -> 109 us  [call(): pl.pallas_call(kernel, out_shape=out_shape, in_specs=specs, out_specs=out...]
    ppermute x1, waiting for transfers between devices: 0.01 us -> 23.6 us  [swap_selected(): return jnp.where(stays, value, lax.ppermute(value, ('c', 'zh'), ROLES[1:3]))]
    all_to_all x4, blocking collectives: 49 us -> 71.8 us  [exchange(): return lax.all_to_all(parts, axes, 0, 0)]
    ppermute x5 -> x9, starting transfers between devices: 21.4 us -> 42.7 us  [swap_roles(): return lax.ppermute(value, ('c', 'zh'), ROLES)]
  transfers between devices with their start and end apart: 72 -> 40, of which waited for: 33 -> 19; matrix products, arithmetic and copies ran while one was open for 6% -> 7% of each run, Pallas kernels for 18% -> 11%
where the time goes in v6:
time: 805 us; the launch traced here: 793 us
  waiting for transfers between devices  412 us (51%)
  starting transfers between devices  122 us (15%)
  Pallas kernels  109 us (14%)
  blocking collectives  71.8 us (9%)
  local copies, waits for them, and re-layouts  32.5 us (4%)
  other arithmetic  16.9 us (2%)
  matrix products  15.7 us (2%)
  between operations  14.6 us (2%)
    psum x1, waiting for transfers between devices, per_device(): lax.psum(after((qkv_half, out_half), fc_half), ('x', 'zl'))  131 us
    pallas_call x16, Pallas kernels, call(): pl.pallas_call(kernel, out_shape=out_shape, in_specs=specs, out_specs=out...  109 us
    ppermute x9, waiting for transfers between devices, swap_roles(): return lax.ppermute(value, ('c', 'zh'), ROLES)  86.4 us
    all_to_all x6, waiting for transfers between devices, exchange(): return lax.all_to_all(parts, axes, 0, 0)  81.4 us
    all_to_all x4, blocking collectives, exchange(): return lax.all_to_all(parts, axes, 0, 0)  71.8 us
    psum x1, waiting for transfers between devices, per_device(): lax.psum(after((fc_half, proj_half), grad_first), ('x', 'zl'))  70.5 us
    all_to_all x6, starting transfers between devices, exchange(): return lax.all_to_all(parts, axes, 0, 0)  57.4 us
    ppermute x9, starting transfers between devices, swap_roles(): return lax.ppermute(value, ('c', 'zh'), ROLES)  42.7 us
  transfers between devices with their start and end apart: 40, of which 19 were waited for; matrix products, arithmetic and copies ran while one was open for 7% of the time, Pallas kernels for 11%

profile of v6, /device:TPU:17, one launch (start us, length us, event | category | flops | bytes accessed | tf_op | source)
XLA Modules:
  0.0 793.5 jit_solution(8938067441080382383)
XLA Ops:
  31.0 8.4 %collective-permute-done.2 = bf16[200,1600]{1,0:T(8,128)(2,1)S(1)} collective-permute-done((bf16[200,1600]{1,0:T(8,128)(2,1)S(1)}, bf16[200,1600]{1,0:T(8,128)(2,1)S(1)}, u32[]{:S(2)}, u32[]{:S(2)}) %collective-permute-start.2) | collective-permute-done | bytes 640032 | tf_op jit(solution)/shard_map/ppermute | solution.py:42
  40.4 39.7 %all_to_all.50 = bf16[8,200,768]{2,1,0:T(8,128)(2,1)} all-to-all(bf16[8,200,768]{2,1,0:T(8,128)(2,1)} %qkv_columns.1), channel_id=1, replica_groups=mesh['x'=4,'zl'=2,'c'=2,'y'=4,'zh'=2] {'y','zh'}, dimensions={0} | all-to-all | bytes 4915200 | tf_op jit(solution)/shard_map/all_to_all | solution.py:54
  80.4 8.6 %collective-permute-start.3 = (bf16[128,1600]{1,0:T(8,128)(2,1)S(1)}, bf16[128,1600]{1,0:T(8,128)(2,1)S(1)}, u32[]{:S(2)}, u32[]{:S(2)}) collective-permute-start(bf16[128,1600]{1,0:T(8,128)(2,1)S(1)} %bitcast.77), channel_id=1, source_target_pairs={{0,0},{1,8},{8,1},{9,9},{2,2},{3,10},{10,3},{11,11},{4,4},{5,12},{... | collective-permute-start | bytes 1228808 | tf_op jit(solution)/shard_map/ppermute | solution.py:42
  95.9 8.7 %all_to_all.51 = bf16[8,3,800]{2,1,0:T(4,128)(2,1)S(1)} all-to-all(bf16[8,3,800]{2,1,0:T(4,128)(2,1)S(1)} %broadcast_in_dim.18), channel_id=1, replica_groups=mesh['x'=4,'zl'=2,'c'=2,'y'=4,'zh'=2] {'y','zh'}, dimensions={0} | all-to-all | bytes 76800 | tf_op jit(solution)/shard_map/all_to_all | solution.py:54
  117.4 23.6 %collective-permute-done.1 = bf16[800,1600]{1,0:T(8,128)(2,1)} collective-permute-done((bf16[800,1600]{1,0:T(8,128)(2,1)S(1)}, bf16[800,1600]{1,0:T(8,128)(2,1)}, u32[]{:S(2)}, u32[]{:S(2)}) %collective-permute-start.1) | collective-permute-done | bytes 2560032 | tf_op jit(solution)/shard_map/ppermute | solution.py:46
  144.6 14.2 %attend.1 = (bf16[1024,1600]{1,0:T(8,128)(2,1)}, bf16[1024,768]{1,0:T(8,128)(2,1)}, bf16[1024,256]{1,0:T(8,128)(2,1)}, f32[1024,4]{1,0:T(8,128)}) custom-call(bf16[1024,1600]{1,0:T(8,128)(2,1)} %all-gather.9.cloned.1.call-done.tokens_ref, bf16[1600,768]{1,0:T(8,128)(2,1)} %bitcast.69, f32[8,1600]{1,0:T(8,128)} %reshape.130.norm_ref, f32[1,768]{1,0:T(1,128)} %reshape.131.bias_ref), custom_call_target="tpu_custom_call" | custom-call | flops 7549747200 | bytes 11179008 | tf_op jit(solution)/shard_map/attend/pallas_call | solution.py:100
  158.8 12.0 %all_to_all.52.slots_ref = bf16[8,128,256]{2,1,0:T(8,128)(2,1)} all-to-all(bf16[8,128,256]{2,1,0:T(8,128)(2,1)} %bitcast.73), channel_id=1, replica_groups=mesh['x'=4,'zl'=2,'c'=2,'y'=4,'zh'=2] {'y','c'}, dimensions={0} | all-to-all | bytes 1048576 | tf_op jit(solution)/shard_map/all_to_all | solution.py:54
  175.9 9.0 %all-to-all-start.3 = ((bf16[8,200,800]{2,1,0:T(8,128)(2,1)}), bf16[8,200,800]{2,1,0:T(8,128)(2,1)S(1)}, u32[]{:S(2)}, u32[]{:S(2)}) async-start(bf16[8,200,800]{2,1,0:T(8,128)(2,1)} %fc_columns.1), calls=%async_computation.3 | async-start | bytes 5734400 | tf_op jit(solution)/shard_map/all_to_all | solution.py:54
  185.9 8.5 %fusion.6.grad_ref = f32[1024,800]{1,0:T(8,128)} fusion(bf16[1024,1600]{1,0:T(8,128)(2,1)} %all-gather.15.cloned.1.call-done.right_ref, bf16[800,1600]{1,0:T(8,128)(2,1)} %broadcast_select_fusion), kind=kOutput, calls=%fused_computation.28 | convolution fusion | flops 2621440000 | bytes 9113600 | tf_op jit(solution)/shard_map/dot_general | solution.py:89
  194.4 37.4 %all-to-all-done.3 = bf16[8,200,800]{2,1,0:T(8,128)(2,1)S(1)} async-done(((bf16[8,200,800]{2,1,0:T(8,128)(2,1)}), bf16[8,200,800]{2,1,0:T(8,128)(2,1)S(1)}, u32[]{:S(2)}, u32[]{:S(2)}) %all-to-all-start.3) | async-done | bytes 2560032 | tf_op jit(solution)/shard_map/all_to_all | solution.py:54
  234.6 14.8 %hidden.1 = (bf16[1024,800]{1,0:T(8,128)(2,1)}, bf16[1024,800]{1,0:T(8,128)(2,1)}, f32[1,800]{1,0:T(1,128)}, bf16[1024,1600]{1,0:T(8,128)(2,1)}) custom-call(s32[8]{0:T(128)} %stack.39.place_ref, bf16[1024,1600]{1,0:T(8,128)(2,1)} %all-gather.13.cloned.1.call-done.second_ref.left_ref, bf16[1600,800]{1,0:T(8,128)(2,1)} %bitcast.68, ...), custom_call_target="tpu_custom_call" | custom-call | flops 15728640000 | bytes 15673632 | tf_op jit(solution)/shard_map/hidden/pallas_call | solution.py:100
  249.6 7.7 fc_grad.1
  280.6 17.3 %collective-permute-done.4 = bf16[1600,800]{0,1:T(8,128)(2,1)} collective-permute-done((bf16[1600,800]{0,1:T(8,128)(2,1)}, bf16[1600,800]{0,1:T(8,128)(2,1)}, u32[]{:S(2)}, u32[]{:S(2)}) %collective-permute-start.4) | collective-permute-done | bytes 2560032 | tf_op jit(solution)/shard_map/ppermute | solution.py:42
  304.3 8.2 %all-to-all-start.4 = ((bf16[8,128,256]{2,1,0:T(8,128)(2,1)}), bf16[8,128,256]{2,1,0:T(8,128)(2,1)S(1)}, u32[]{:S(2)}, u32[]{:S(2)}) async-start(bf16[8,128,256]{2,1,0:T(8,128)(2,1)} %get-tuple-element.78), calls=%async_computation.6 | async-start | bytes 1048576 | tf_op jit(solution)/shard_map/all_to_all | solution.py:54
  313.5 8.8 %all-to-all-done.4 = bf16[8,128,256]{2,1,0:T(8,128)(2,1)S(1)} async-done(((bf16[8,128,256]{2,1,0:T(8,128)(2,1)}), bf16[8,128,256]{2,1,0:T(8,128)(2,1)S(1)}, u32[]{:S(2)}, u32[]{:S(2)}) %all-to-all-start.4) | async-done | bytes 524320 | tf_op jit(solution)/shard_map/all_to_all | solution.py:54
  323.1 15.4 %attend_back.1 = (bf16[1024,768]{1,0:T(8,128)(2,1)}, bf16[1024,1600]{1,0:T(8,128)(2,1)}, f32[1,768]{1,0:T(1,128)}) custom-call(s32[8]{0:T(128)} %stack.39.place_ref, bf16[1024,768]{1,0:T(8,128)(2,1)} %get-tuple-element.77.qkv_ref, bf16[1024,256]{1,0:T(8,128)(2,1)} %bitcast.74, bf16[1024,256]{1,0:T(8,128)(2,1)} %get-tuple-element.64.out_ref, ...), custom_call_target="tpu_custom_call" | custom-call | flops 7549747200 | bytes 9948192 | tf_op jit(solution)/shard_map/attend_back/pallas_call | solution.py:100
  340.5 7.3 all-to-all-start.8
  361.7 21.3 %all-to-all-start.9 = ((bf16[8,200,800]{2,1,0:T(8,128)(2,1)}), bf16[8,200,800]{2,1,0:T(8,128)(2,1)S(1)}, u32[]{:S(2)}, u32[]{:S(2)}) async-start(bf16[8,200,800]{2,1,0:T(8,128)(2,1)} %bitcast.67), calls=%async_computation.12 | async-start | bytes 5734400 | tf_op jit(solution)/shard_map/all_to_all | solution.py:54
  389.4 31.7 %all-to-all-done.9 = bf16[8,200,800]{2,1,0:T(8,128)(2,1)S(1)} async-done(((bf16[8,200,800]{2,1,0:T(8,128)(2,1)}), bf16[8,200,800]{2,1,0:T(8,128)(2,1)S(1)}, u32[]{:S(2)}, u32[]{:S(2)}) %all-to-all-start.9) | async-done | bytes 2560032 | tf_op jit(solution)/shard_map/all_to_all | solution.py:54
  430.3 39.4 %collective-permute-done.19 = bf16[800,1600]{1,0:T(8,128)(2,1)} collective-permute-done((bf16[800,1600]{1,0:T(8,128)(2,1)}, bf16[800,1600]{1,0:T(8,128)(2,1)}, u32[]{:S(2)}, u32[]{:S(2)}) %collective-permute-start.19) | collective-permute-done | bytes 2560032 | tf_op jit(solution)/shard_map/ppermute | solution.py:42
  475.8 7.7 collective-permute-done.11.refs_3_
  523.7 70.5 %all-reduce.4.cloned.1.call-done.own_ref = bf16[4,200,800]{2,1,0:T(8,128)(2,1)} async-done(((bf16[4,200,800]{2,1,0:T(8,128)(2,1)}), bf16[4,200,800]{2,1,0:T(8,128)(2,1)}) %all-reduce.4.cloned.1.call-update) | async-done | bytes 1280016 | tf_op jit(solution)/shard_map/psum | solution.py:532
  606.1 130.6 %all-reduce.6.cloned.1.call-done = (bf16[4,200,768]{2,1,0:T(8,128)(2,1)}, bf16[104,1600]{1,0:T(8,128)(2,1)}, bf16[400,1600]{1,0:T(8,128)(2,1)}) async-done(((bf16[4,200,768]{2,1,0:T(8,128)(2,1)}, bf16[104,1600]{1,0:T(8,128)(2,1)}, bf16[400,1600]{1,0:T(8,128)(2,1)}), (bf16[4,200,768]{2,1,0:T(8,128)(2,1)}, bf16[104,1600]{1,0:T(8,128)(2,1)}, bf16[400,1600]{1,0:T(8,128)(2,1)})) %all-reduce.6.cloned.1.call-update) | async-done | bytes 2841616 | tf_op jit(solution)/shard_map/psum | solution.py:552
  739.5 11.3 %all_to_all.53 = f32[8,3,800]{2,1,0:T(4,128)S(1)} all-to-all(f32[8,3,800]{2,1,0:T(4,128)S(1)} %pad_maximum_fusion), channel_id=1, replica_groups=mesh['x'=4,'zl'=2,'c'=2,'y'=4,'zh'=2] {'y','zh'}, dimensions={0} | all-to-all | bytes 153600 | tf_op jit(solution)/shard_map/all_to_all | solution.py:54
  (197 shorter events, 216.9 us)
Async XLA Ops:
  7.2 137.4 %all-gather.9.cloned.1.call-start = ((), (), s32[]{:S(2)}) async-start(), calls=%async_computation.17 | async-start | bytes 3833856 | tf_op jit(solution)/shard_map/all_gather | solution.py:58
  21.2 149.6 %all-gather.11.cloned.1.call-start = ((), (), s32[]{:S(2)}) async-start(), calls=%async_computation.18 | async-start | bytes 5990400 | tf_op jit(solution)/shard_map/all_gather | solution.py:58
  40.3 145.6 %all-gather.15.cloned.1.call-start = ((), (), s32[]{:S(2)}) async-start(), calls=%async_computation.20 | async-start | bytes 3833856 | tf_op jit(solution)/shard_map/all_gather | solution.py:58
  95.6 139.1 %all-gather.13.cloned.1.call-start = ((), (), s32[]{:S(2)}) async-start(), calls=%async_computation.19 | async-start | bytes 3833856 | tf_op jit(solution)/shard_map/all_gather | solution.py:58
  104.7 36.4 %collective-permute-start.1 = (bf16[800,1600]{1,0:T(8,128)(2,1)S(1)}, bf16[800,1600]{1,0:T(8,128)(2,1)}, u32[]{:S(2)}, u32[]{:S(2)}) collective-permute-start(bf16[800,1600]{1,0:T(8,128)(2,1)S(1)} %copy-done.1), channel_id=1, source_target_pairs={{1,8},{8,1},{3,10},{10,3},{5,12},{12,5},{7,14},{14,7},{17,24},{24,... | collective-permute-start | bytes 7680008 | tf_op jit(solution)/shard_map/ppermute | solution.py:46
  175.9 55.9 %all-to-all-start.3 = ((bf16[8,200,800]{2,1,0:T(8,128)(2,1)}), bf16[8,200,800]{2,1,0:T(8,128)(2,1)S(1)}, u32[]{:S(2)}, u32[]{:S(2)}) async-start(bf16[8,200,800]{2,1,0:T(8,128)(2,1)} %fc_columns.1), calls=%async_computation.3 | async-start | bytes 5734400 | tf_op jit(solution)/shard_map/all_to_all | solution.py:54
  184.9 113.0 %reduce-scatter.4.cloned.1.call-start = ((), (), s32[]{:S(2)}) async-start(), calls=%async_computation.13 | async-start | bytes 3833856 | tf_op jit(solution)/shard_map/reduce_scatter | solution.py:62
  249.4 89.1 %reduce-scatter.6.cloned.1.call-start = ((), (), s32[]{:S(2)}) async-start(), calls=%async_computation.14 | async-start | bytes 3833856 | tf_op jit(solution)/shard_map/reduce_scatter | solution.py:62
  262.6 35.2 %collective-permute-start.4 = (bf16[1600,800]{0,1:T(8,128)(2,1)}, bf16[1600,800]{0,1:T(8,128)(2,1)}, u32[]{:S(2)}, u32[]{:S(2)}) collective-permute-start(bf16[1600,800]{0,1:T(8,128)(2,1)} %copy.90), channel_id=1, source_target_pairs={{0,0},{1,8},{8,1},{9,9},{2,2},{3,10},{10,3},{11,11},{4,4},{5,12},{... | collective-permute-start | bytes 7680008 | tf_op jit(solution)/shard_map/ppermute | solution.py:42
  312.5 198.5 %reduce-scatter.8.cloned.1.call-start = ((), (), s32[]{:S(2)}) async-start(), calls=%async_computation.15 | async-start | bytes 3833856 | tf_op jit(solution)/shard_map/reduce_scatter | solution.py:62
  340.5 21.2 %all-to-all-start.8 = ((bf16[8,128,200]{1,2,0:T(8,128)(2,1)}), bf16[8,128,200]{1,2,0:T(8,128)(2,1)S(1)}, u32[]{:S(2)}, u32[]{:S(2)}) async-start(bf16[8,128,200]{1,2,0:T(8,128)(2,1)} %copy.94), calls=%async_computation.11 | async-start | bytes 819200 | tf_op jit(solution)/shard_map/all_to_all | solution.py:54
  354.5 66.6 %collective-permute-start.6 = (bf16[1600,768]{1,0:T(8,128)(2,1)}, bf16[1600,768]{1,0:T(8,128)(2,1)}, u32[]{:S(2)}, u32[]{:S(2)}) collective-permute-start(bf16[1600,768]{1,0:T(8,128)(2,1)} %qkv_grad.1), channel_id=1, source_target_pairs={{0,0},{1,8},{8,1},{9,9},{2,2},{3,10},{10,3},{11,11},{4,4},{5,12},{... | collective-permute-start | bytes 7372808 | tf_op jit(solution)/shard_map/ppermute | solution.py:42
  361.7 59.4 %all-to-all-start.9 = ((bf16[8,200,800]{2,1,0:T(8,128)(2,1)}), bf16[8,200,800]{2,1,0:T(8,128)(2,1)S(1)}, u32[]{:S(2)}, u32[]{:S(2)}) async-start(bf16[8,200,800]{2,1,0:T(8,128)(2,1)} %bitcast.67), calls=%async_computation.12 | async-start | bytes 5734400 | tf_op jit(solution)/shard_map/all_to_all | solution.py:54
  382.9 86.8 %collective-permute-start.19 = (bf16[800,1600]{1,0:T(8,128)(2,1)}, bf16[800,1600]{1,0:T(8,128)(2,1)}, u32[]{:S(2)}, u32[]{:S(2)}) collective-permute-start(bf16[800,1600]{1,0:T(8,128)(2,1)} %proj_grad.1), channel_id=1, source_target_pairs={{0,0},{1,8},{8,1},{9,9},{2,2},{3,10},{10,3},{11,11},{4,4},{5,12},{... | collective-permute-start | bytes 7680008 | tf_op jit(solution)/shard_map/ppermute | solution.py:42
  421.1 85.4 %all-to-all-start.5 = ((bf16[8,200,768]{2,1,0:T(8,128)(2,1)}), bf16[8,200,768]{2,1,0:T(8,128)(2,1)}, u32[]{:S(2)}, u32[]{:S(2)}) async-start(bf16[8,200,768]{2,1,0:T(8,128)(2,1)} %bitcast.18), calls=%async_computation.8 | async-start | bytes 4915200 | tf_op jit(solution)/shard_map/all_to_all | solution.py:54
  427.8 166.3 %all-reduce.4.cloned.1.call-start = ((), (), s32[]{:S(2)}) async-start(), calls=%async_computation.16 | async-start | bytes 2867200 | tf_op jit(solution)/shard_map/psum | solution.py:532
  428.0 46.4 %collective-permute-start.18 = (bf16[4,200,800]{2,1,0:T(8,128)(2,1)S(1)}, bf16[4,200,800]{2,1,0:T(8,128)(2,1)}, u32[]{:S(2)}, u32[]{:S(2)}) collective-permute-start(bf16[4,200,800]{2,1,0:T(8,128)(2,1)S(1)} %dynamic-slice_bitcast_fusion), channel_id=1, source_target_pairs={{0,8},{8,0},{1,9},{9,1},{2,10},{10,2},{3,11},{11,3},{4,12},{12,4},... | collective-permute-start | bytes 3840008 | tf_op jit(solution)/shard_map/ppermute | solution.py:50
  472.3 35.7 %collective-permute-start.20 = (bf16[400,1600]{1,0:T(8,128)(2,1)}, bf16[400,1600]{1,0:T(8,128)(2,1)}, u32[]{:S(2)}, u32[]{:S(2)}) collective-permute-start(bf16[400,1600]{1,0:T(8,128)(2,1)} %dynamic-slice_bitcast_fusion.1), channel_id=1, source_target_pairs={{0,8},{8,0},{1,9},{9,1},{2,10},{10,2},{3,11},{11,3},{4,12},{12,4},... | collective-permute-start | bytes 3840008 | tf_op jit(solution)/shard_map/ppermute | solution.py:50
  474.4 25.2 %collective-permute-start.12 = (bf16[128,1600]{1,0:T(8,128)(2,1)}, bf16[128,1600]{1,0:T(8,128)(2,1)}, u32[]{:S(2)}, u32[]{:S(2)}) collective-permute-start(bf16[128,1600]{1,0:T(8,128)(2,1)} %get-tuple-element.96.refs_0_), channel_id=1, source_target_pairs={{0,8},{8,0},{1,9},{9,1},{2,10},{10,2},{3,11},{11,3},{4,12},{12,4},... | collective-permute-start | bytes 1228808 | tf_op jit(solution)/shard_map/ppermute | solution.py:50
  511.1 225.5 %all-reduce.6.cloned.1.call-start = ((), (), s32[]{:S(2)}) async-start(), calls=%async_computation.21 | async-start | bytes 5812224 | tf_op jit(solution)/shard_map/psum | solution.py:552
  596.8 162.3 %collective-permute-start.5 = (bf16[128,1600]{1,0:T(8,128)(2,1)}, bf16[128,1600]{1,0:T(8,128)(2,1)S(1)}, u32[]{:S(2)}, u32[]{:S(2)}) collective-permute-start(bf16[128,1600]{1,0:T(8,128)(2,1)} %add_convert_fusion), channel_id=1, source_target_pairs={{0,0},{1,8},{8,1},{9,9},{2,2},{3,10},{10,3},{11,11},{4,4},{5,12},{... | collective-permute-start | bytes 1228808 | tf_op jit(solution)/shard_map/ppermute | solution.py:42
  606.1 164.1 %collective-permute-start.23 = (bf16[4,200,800]{2,1,0:T(8,128)(2,1)S(1)}, bf16[4,200,800]{2,1,0:T(8,128)(2,1)}, u32[]{:S(2)}, u32[]{:S(2)}) collective-permute-start(bf16[4,200,800]{2,1,0:T(8,128)(2,1)S(1)} %copy-done.4), channel_id=1, source_target_pairs={{0,8},{8,0},{1,9},{9,1},{2,10},{10,2},{3,11},{11,3},{4,12},{12,4},... | collective-permute-start | bytes 3840008 | tf_op jit(solution)/shard_map/ppermute | solution.py:50
  736.6 40.6 %collective-permute-start.21 = (bf16[4,200,768]{2,1,0:T(8,128)(2,1)}, bf16[4,200,768]{2,1,0:T(8,128)(2,1)S(1)}, u32[]{:S(2)}, u32[]{:S(2)}) collective-permute-start(bf16[4,200,768]{2,1,0:T(8,128)(2,1)} %get-tuple-element.196.own_ref), channel_id=1, source_target_pairs={{0,8},{8,0},{1,9},{9,1},{2,10},{10,2},{3,11},{11,3},{4,12},{12,4},... | collective-permute-start | bytes 3686408 | tf_op jit(solution)/shard_map/ppermute | solution.py:50
  738.4 43.9 %collective-permute-start.24 = (bf16[400,1600]{1,0:T(8,128)(2,1)}, bf16[400,1600]{1,0:T(8,128)(2,1)}, u32[]{:S(2)}, u32[]{:S(2)}) collective-permute-start(bf16[400,1600]{1,0:T(8,128)(2,1)} %get-tuple-element.198.own_ref), channel_id=1, source_target_pairs={{0,8},{8,0},{1,9},{9,1},{2,10},{10,2},{3,11},{11,3},{4,12},{12,4},... | collective-permute-start | bytes 3840008 | tf_op jit(solution)/shard_map/ppermute | solution.py:50
  (42 other events, 1300.6 us)
Sparse Core Ops, SparseCore 0:
  21.3 29.9 all-gather.8
  53.6 44.6 all-gather.10
  100.0 28.7 all-gather.14
  176.0 58.5 all-gather.12
  249.5 32.5 reduce-scatter.3
  298.0 38.3 reduce-scatter.5
  339.4 36.5 reduce-scatter.7
  511.2 82.9 all-reduce.3
  598.1 138.5 all-reduce.5

commit v7 on v5

--- a/solution.py
+++ b/solution.py
@@ -123,7 +123,7 @@
         scratch_shapes=list(scratch),
         compiler_params=pltpu.CompilerParams(vmem_limit_bytes=56 * 2**20),
         cost_estimate=pl.CostEstimate(
-            flops=int(3 * flops), bytes_accessed=int(moved), transcendentals=0
+            flops=int(flops), bytes_accessed=int(moved), transcendentals=0
         ),
         name=name,
     )(*operands)
@@ -242,13 +242,17 @@
                 out_refs[k][z, y] = held_ref[pl.ds(at, size), :].astype(bf16)
 
 
-def row_grad_kernel(left_ref, right_ref, out_ref):
+def row_grad_kernel(place_ref, left_ref, right_ref, *refs):
+    out_refs, held_ref = refs[:4], refs[4]
     rows = left_ref.shape[1]
-    size, starts = windows(rows, 16)
-    grad = dot_rows(left_ref[...], right_ref[...])
-    for i, start in enumerate(starts):
-        zl, x, zh = i // 8, i // 2 % 4, i % 2
-        out_ref[2 * zl + zh, x] = grad[start : start + size].astype(bf16)
+    size = windows(rows, 16)[0]
+    held_ref[...] = dot_rows(left_ref[...], right_ref[...])
+    for k in range(4):
+        z = lax.rem(place_ref[Z] + 4 - k, 4)
+        for x in range(4):
+            window = (lax.rem(z, 2) * 4 + x) * 2 + lax.div(z, 2)
+            at = pl.multiple_of(lax.div(rows // 8 * window, 16) * 8, 8)
+            out_refs[k][x] = held_ref[pl.ds(at, size), :].astype(bf16)
 
 
 def out_grad_kernel(place_ref, left_ref, *refs):
@@ -275,15 +279,6 @@
         for j in range(1, 4):
             total = total + refs[j][at].astype(f32)
         refs[4 + k][...] = total.astype(bf16)
-
-
-def fold_stack_kernel(which, place_ref, parts_ref, *refs):
-    for k in range(4):
-        at = lax.rem(place_ref[which] + 4 - k, 4)
-        total = parts_ref[0, at].astype(f32)
-        for j in range(1, 4):
-            total = total + parts_ref[j, at].astype(f32)
-        refs[k][...] = total.astype(bf16)
 
 
 def stack_kernel(*refs):
@@ -392,7 +387,17 @@
 
 
 def attend_back_kernel(
-    place_ref, qkv_ref, grad_ref, out_ref, top_ref, cols_ref, mixed_ref, first_ref, sums_ref, query_ref
+    place_ref,
+    qkv_ref,
+    grad_ref,
+    out_ref,
+    top_ref,
+    cols_ref,
+    down_ref,
+    mixed_ref,
+    parts_ref,
+    sums_ref,
+    query_ref,
 ):
     length = qkv_ref.shape[0]
     scale = 1.0 / math.sqrt(HEAD_DIM)
@@ -433,15 +438,23 @@
         rows = slice(block * BLOCK, (block + 1) * BLOCK)
         mixed = mixed_ref[rows, :]
         sums = sums + jnp.sum(mixed.astype(f32), axis=0, keepdims=True)
-        first_ref[rows, :] = dot_cols(mixed, cols_ref[...]).astype(bf16)
+        first = dot_cols(mixed, cols_ref[...]).astype(bf16)
+        for half in range(2):
+            rank = 2 * block + half
+            parts_ref[rank, 0] = first[half * BLOCK // 2 : (half + 1) * BLOCK // 2]
+            parts_ref[rank, 1] = down_ref[rank]
     sums_ref[...] = sums
 
 
-def input_back_kernel(grad_ref, tokens_ref, middle_ref, norm_ref, out_ref, sums_ref):
+def input_back_kernel(
+    parts_ref, tokens_ref, middle_ref, grad_ref, norm_ref, out_ref, sums_ref
+):
     gain = norm_ref[0:1, :]
     _, normed, factor = norm_parts(tokens_ref[...].astype(f32), gain, gain)
-    grad = grad_ref[...].astype(f32)
-    out_ref[...] = (middle_ref[...] + norm_back(grad, normed, factor, gain)).astype(bf16)
+    grad = parts_ref[0].astype(f32)
+    out_ref[0] = (grad_ref[...] + norm_back(grad, normed, factor, gain)).astype(bf16)
+    down = parts_ref[1].astype(f32) + norm_ref[7:8, :]
+    out_ref[1] = (middle_ref[...] + down).astype(bf16)
     sums_ref[0:1, :] = jnp.sum(grad * normed, axis=0, keepdims=True)
     sums_ref[1:2, :] = jnp.sum(grad, axis=0, keepdims=True)
 
@@ -481,6 +494,8 @@
     stays = c == zh
     own_tokens = swap_roles(tokens.reshape(span, width))
     all_tokens = gather(own_tokens, TEAM).reshape(length, width)
+    out_rows = swap_roles(w_out)
+    proj_came = lax.ppermute(after(w_proj, own_tokens), ("c", "zh"), ROLES[1:3])
     qkv_parts = call(
         qkv_columns_kernel,
         "qkv_columns",
@@ -490,15 +505,13 @@
         scratch=[pltpu.VMEM((4, shard, slots), bf16)],
     )
     qkv_own = ring_all(qkv_parts, "y")
-    qkv_other = [flipped(part, "zh") for part in qkv_own]
     small = jnp.concatenate(
         [ln1_gain, ln1_bias, bias_q, bias_v, bias_out, ln2_gain, ln2_bias, bias_proj, bias_fc]
     ).reshape(3, hidden)
     small_all = exchange(
         after(jnp.broadcast_to(small, (8, 3, hidden)), qkv_parts[0]), GRP
     )
-    out_rows = swap_roles(after(w_out, small_all))
-    own_cot = swap_roles(after(cotangent, out_rows).reshape(span, width))
+    qkv_other = [flipped(after(part, proj_came, out_rows), "zh") for part in qkv_own]
     place = after(place, small_all)
     fc_parts = call(
         fc_columns_kernel,
@@ -508,7 +521,7 @@
         w_fc,
         scratch=[pltpu.VMEM((4, shard, hidden), bf16)],
     )
-    place = after(place, fc_parts[0])
+    own_cot = swap_roles(after(cotangent, *qkv_other).reshape(span, width))
 
     small_all = small_all.astype(f32)
     hidden_bias = lax.dynamic_index_in_dim(small_all, rank, 0, keepdims=False)[2:3]
@@ -521,9 +534,9 @@
         ]
     ).reshape(1, slots)
 
-    out_all = gather(after(out_rows, *qkv_own), TEAM).reshape(width, width)
-    all_cot = gather(after(own_cot, *qkv_other), TEAM).reshape(length, width)
-    proj_rows = swap_selected(after(w_proj, *qkv_other), stays)
+    out_all = gather(out_rows, TEAM).reshape(width, width)
+    all_cot = gather(after(own_cot, out_rows), TEAM).reshape(length, width)
+    proj_rows = jnp.where(stays, w_proj, after(proj_came, *qkv_other))
     fc_own = ring_all([after(part, *qkv_other) for part in fc_parts], "y")
 
     first, qkv, attended_slots, top, qkv_cols = call(
@@ -545,8 +558,8 @@
         flops=2 * length * width * slots,
     )
     qkv_cols = qkv_cols.reshape(width, slots)
-    fc_other = [flipped(after(part, qkv), "zh") for part in fc_own]
-    attended = exchange(attended_slots.reshape(8, span, SLOT_WIDTH), TEAM)
+    fc_other = [flipped(part, "zh") for part in fc_own]
+    attended = exchange(after(attended_slots, *fc_own).reshape(8, span, SLOT_WIDTH), TEAM)
     middle, second, attended_parts = call(
         branch_kernel,
         "branch",
@@ -564,7 +577,7 @@
     )
 
     second_all = gather(second, TEAM).reshape(length, width)
-    attended_own = exchange(attended_parts, TEAM)
+    attended_own = exchange(after(attended_parts, *fc_other), TEAM)
     grad_active = dot_cols(after(all_cot, second), proj_rows)
     fc_cols = call(
         fc_whole_kernel,
@@ -608,13 +621,14 @@
     proj_grad = call(
         row_grad_kernel,
         "proj_grad",
-        struct((4, 4, row_window, width), bf16),
+        [struct((4, row_window, width), bf16)] * 4,
+        place,
         active,
         all_cot,
+        scratch=[pltpu.VMEM((hidden, width), f32)],
         flops=2 * length * width * hidden,
     )
     down_parts = dot(active, proj_rows).astype(bf16)
-    grad_second = after(grad_second, fc_grad[0], proj_grad, down_parts)
 
     grad_middle, grad_branch, grad_slots, branch_sums = call(
         branch_back_kernel,
@@ -625,7 +639,7 @@
             struct((8, span, SLOT_WIDTH), bf16),
             struct((4, width), f32),
         ),
-        place,
+        after(place, fc_grad[0], proj_grad[0], down_parts),
         grad_second,
         middle,
         own_cot,
@@ -635,8 +649,6 @@
         flops=2 * span * width * width,
     )
     grad_heads = exchange(grad_slots, TEAM).reshape(length, SLOT_WIDTH)
-    down = team_sum(after(down_parts, grad_second))
-    proj_grad = exchange(after(proj_grad, grad_heads), Z_RING)
 
     def fold(which, parts, name, *behind):
         parts = [after(parts[0], *behind)] + parts[1:]
@@ -648,49 +660,39 @@
             *parts,
         )
 
-    grad_mixed, first_parts, mixed_sums = call(
+    fc_grad = fold(Z, fc_grad, "fc_fold", grad_slots)
+    proj_grad = ring_all([after(part, fc_grad[0]) for part in proj_grad], Z_RING)
+    grad_mixed, last_parts, mixed_sums = call(
         attend_back_kernel,
         "attend_back",
         (
             struct((length, slots), bf16),
-            struct((length, width), bf16),
+            struct((8, 2, span, width), bf16),
             struct((1, slots), f32),
         ),
-        place,
+        after(place, fc_grad[0]),
         qkv,
         grad_heads,
         attended_slots,
         top.T,
         qkv_cols,
+        down_parts.reshape(8, span, width),
         scratch=[pltpu.VMEM((length, HEAD_DIM), f32)],
         flops=2 * length * width * slots,
     )
-    grad_first = team_sum(after(first_parts, down))
-    place = after(place, grad_mixed)
-    proj_grad = ring_all(
-        call(
-            functools.partial(fold_stack_kernel, X),
-            "proj_fold",
-            [struct((row_window, width), bf16)] * 4,
-            place,
-            proj_grad,
-        ),
-        "x",
-    )
-    fc_grad = fold(Z, fc_grad, "fc_fold", place)
+    last = team_sum(last_parts.reshape(2 * length, width)).reshape(2, span, width)
     qkv_grad = call(
         column_grad_kernel,
         "qkv_grad",
         struct((16, 4, window, slots), bf16),
-        after(first, fc_grad[0], proj_grad[0]),
+        first,
         grad_mixed,
         flops=2 * length * width * slots,
     )
     place = after(place, qkv_grad)
-    fc_grad = ring_all(fc_grad, Z_RING)
-    branch_own = ring_all([after(grad_branch, grad_mixed)] * 4, "y")
-    qkv_grad = exchange(after(qkv_grad, *fc_grad, *proj_grad), REPLICAS)
-    grad_first = after(grad_first, qkv_grad)
+    qkv_grad = exchange(qkv_grad, REPLICAS)
+    fc_grad = ring_all([after(part, place) for part in fc_grad], Z_RING)
+    branch_own = ring_all([after(grad_branch, qkv_grad)] * 4, "y")
 
     def replica_sum(parts):
         return jnp.sum(parts.astype(f32), axis=0).astype(bf16)
@@ -699,10 +701,6 @@
         return call(
             stack_kernel, name, struct((len(parts),) + parts[0].shape, bf16), *parts
         )
-
-    def column_spread(near, name):
-        both = stacked([near, flipped(near, "zl")], name + "_both")
-        return ring_all([both] * 4, "x")
 
     def row_total(whole, rows, name, *behind):
         whole = after(whole, *behind)
@@ -711,41 +709,41 @@
         )
 
     fc_grad = ring_all(fold(Y, fc_grad, "fc_fold_last", place), "y")
-    proj_sum = sum(part.astype(f32) for part in proj_grad).astype(bf16)
-    proj_whole = gather(after(proj_sum, grad_first), REPLICAS)
-    fc_own_pieces = column_spread(stacked(fc_grad, "fc_near"), "fc")
+    fc_near = stacked(fc_grad, "fc_near")
+    fc_both = stacked([fc_near, flipped(fc_near, "zl")], "fc_both")
     branch_other = [other_core(part) for part in branch_own]
     out_grad = call(
         out_grad_kernel,
         "out_grad",
         struct((16, windows(shard, 16)[0], width), bf16),
-        after(place, fc_grad[1]),
+        place,
         attended_own,
         *branch_own,
         *branch_other,
         scratch=[pltpu.VMEM((shard, width), f32)],
         flops=2 * length * width * shard,
     )
-    grad_inputs, first_sums = call(
+
+    place = after(place, qkv_grad)
+    qkv_sum = exchange(replica_sum(after(qkv_grad, fc_both)), "y")
+    proj_grad = ring_all(fold(X, proj_grad, "proj_fold", place), "x")
+    proj_sum = sum(part.astype(f32) for part in proj_grad).astype(bf16)
+    proj_whole = gather(proj_sum, REPLICAS)
+    qkv_both = stacked([qkv_sum, flipped(qkv_sum, "zl")], "qkv_both")
+    qkv_pieces = ring_all([qkv_both] * 4, "x")
+    out_grad = exchange(after(out_grad, qkv_both), REPLICAS)
+    fc_pieces = ring_all([after(fc_both, *qkv_pieces)] * 4, "x")
+    results, first_sums = call(
         input_back_kernel,
         "input_back",
-        (struct((span, width), bf16), struct((2, width), f32)),
-        grad_first,
+        (struct((2, span, width), bf16), struct((2, width), f32)),
+        last,
         own_tokens,
+        middle,
         grad_middle,
-        after(vectors, qkv_grad, out_grad, *fc_own_pieces),
-    )
-    inputs_home = swap_roles(grad_inputs).astype(f32).reshape(1, span, width)
-    output = middle + (after(down, grad_inputs).astype(f32) + vectors[7])
-    output_home = swap_roles(output.astype(bf16)).reshape(1, span, width)
-    place = after(place, grad_inputs)
-    fc_own_pieces = [after(part, grad_inputs) for part in fc_own_pieces]
-    fc_pieces = fc_own_pieces + [other_core(part) for part in fc_own_pieces]
-    place = after(place, out_grad)
-    qkv_sum = exchange(replica_sum(after(qkv_grad, place)), "y")
-    out_grad = exchange(after(out_grad, qkv_sum), REPLICAS)
-    qkv_pieces = column_spread(qkv_sum, "qkv")
-    qkv_pieces = qkv_pieces + [other_core(part) for part in qkv_pieces]
+        after(vectors, *qkv_pieces),
+    )
+    results_home = swap_roles(results)
 
     blank = jnp.zeros((1, width), f32)
     at = (0, STRIDE * rank)
@@ -771,16 +769,7 @@
     small_sum = jnp.sum(exchange(small_sum, REP), axis=0)
     owned = small_sum[:2].reshape(8, shard)
 
-    fc_spans = [[(0, rank * hidden, hidden)] for rank in range(8)]
-    fc_total = call(
-        functools.partial(column_total_kernel, fc_spans, True),
-        "fc_total",
-        struct((shard, 8 * hidden), f32),
-        after(place, qkv_sum),
-        *fc_pieces,
-    )
-    proj_total = row_total(proj_whole, hidden, "proj_total", out_whole)
-    out_total = row_total(out_whole, shard, "out_total")
+    qkv_pieces = qkv_pieces + [other_core(part) for part in qkv_pieces]
     qkv_spans = [
         [
             (p * SLOT_WIDTH, p * width + STRIDE * r, STRIDE if r < 7 else SLOT_WIDTH)
@@ -792,12 +781,23 @@
         functools.partial(column_total_kernel, qkv_spans, False),
         "qkv_total",
         struct((shard, 3 * width), f32),
-        after(place, fc_total),
+        after(place, results, out_grad),
         *qkv_pieces,
     )
+    fc_pieces = fc_pieces + [other_core(after(part, qkv_total)) for part in fc_pieces]
+    fc_spans = [[(0, rank * hidden, hidden)] for rank in range(8)]
+    fc_total = call(
+        functools.partial(column_total_kernel, fc_spans, True),
+        "fc_total",
+        struct((shard, 8 * hidden), f32),
+        after(place, out_whole, small_sum),
+        *fc_pieces,
+    )
+    out_total = row_total(out_whole, shard, "out_total", fc_total)
+    proj_total = row_total(proj_whole, hidden, "proj_total", fc_total)
     return (
-        output_home,
-        inputs_home,
+        results_home[1].reshape(1, span, width),
+        results_home[0].astype(f32).reshape(1, span, width),
         owned[0],
         owned[1],
         qkv_total,

time: 674 us -> 662 us (0.982)
  blocking collectives: 49 us -> 35.4 us
  waiting for transfers between devices: 268 us -> 276 us
  local copies, waits for them, and re-layouts: 32.4 us -> 24.9 us
    ppermute x27 -> x30, waiting for transfers between devices: 128 us -> 88.5 us  [ring(): lax.ppermute(value, axis, [(index[(i + step) % 4], index[i]) for i in ran...]
    ppermute x5 -> x4, waiting for transfers between devices: 5.81 us -> 33.4 us  [swap_roles(): return lax.ppermute(value, ('c', 'zh'), ROLES)]
    ppermute x1, waiting for transfers between devices: 0.01 us -> 19.8 us  [per_device(): proj_came = lax.ppermute(after(w_proj, own_tokens), ('c', 'zh'), ROLES[1:3])]
    ppermute x10, waiting for transfers between devices: 53.3 us -> 71.1 us  [flipped(): return lax.ppermute(value, axis, [(0, 1), (1, 0)])]
    all_to_all x7, waiting for transfers between devices: 67.9 us -> 53.5 us  [exchange(): return lax.all_to_all(parts, axes, 0, 0)]
    all_to_all x4 -> x3, blocking collectives: 49 us -> 35.4 us  [exchange(): return lax.all_to_all(parts, axes, 0, 0)]
    all_to_all x7, starting transfers between devices: 47.8 us -> 39.1 us  [exchange(): return lax.all_to_all(parts, axes, 0, 0)]
    unnamed x109 -> x113, local copies, waits for them, and re-layouts: 15.5 us -> 8.49 us
  transfers between devices with their start and end apart: 72 -> 73, of which waited for: 33 -> 38; matrix products, arithmetic and copies ran while one was open for 6% -> 6% of each run, Pallas kernels for 18% -> 16%
where the time goes in v7:
time: 662 us; the launch traced here: 652 us
  waiting for transfers between devices  276 us (42%)
  Pallas kernels  143 us (22%)
  starting transfers between devices  138 us (21%)
  blocking collectives  35.4 us (5%)
  local copies, waits for them, and re-layouts  24.9 us (4%)
  between operations  15.1 us (2%)
  matrix products  14.2 us (2%)
    pallas_call x23, Pallas kernels, call(): pl.pallas_call(kernel, out_shape=out_shape, in_specs=specs, out_specs=out...  143 us
    ppermute x30, waiting for transfers between devices, ring(): lax.ppermute(value, axis, [(index[(i + step) % 4], index[i]) for i in ran...  88.5 us
    ppermute x10, waiting for transfers between devices, flipped(): return lax.ppermute(value, axis, [(0, 1), (1, 0)])  71.1 us
    all_to_all x7, waiting for transfers between devices, exchange(): return lax.all_to_all(parts, axes, 0, 0)  53.5 us
    ppermute x30, starting transfers between devices, ring(): lax.ppermute(value, axis, [(index[(i + step) % 4], index[i]) for i in ran...  39.2 us
    all_to_all x7, starting transfers between devices, exchange(): return lax.all_to_all(parts, axes, 0, 0)  39.1 us
    all_to_all x3, blocking collectives, exchange(): return lax.all_to_all(parts, axes, 0, 0)  35.4 us
    ppermute x4, waiting for transfers between devices, swap_roles(): return lax.ppermute(value, ('c', 'zh'), ROLES)  33.4 us
  transfers between devices with their start and end apart: 73, of which 38 were waited for; matrix products, arithmetic and copies ran while one was open for 6% of the time, Pallas kernels for 16%

profile of v7, /device:TPU:17, one launch (start us, length us, event | category | flops | bytes accessed | tf_op | source)
XLA Modules:
  0.0 652.5 jit_solution(17641770902463585883)
XLA Ops:
  26.6 8.6 %collective-permute-done.5 = bf16[200,1600]{1,0:T(8,128)(2,1)S(1)} collective-permute-done((bf16[200,1600]{1,0:T(8,128)(2,1)}, bf16[200,1600]{1,0:T(8,128)(2,1)S(1)}, u32[]{:S(2)}, u32[]{:S(2)}) %collective-permute-start.5) | collective-permute-done | bytes 640032 | tf_op jit(solution)/shard_map/ppermute | solution.py:46
  51.5 19.8 %collective-permute-done.4 = bf16[800,1600]{1,0:T(8,128)(2,1)} collective-permute-done((bf16[800,1600]{1,0:T(8,128)(2,1)}, bf16[800,1600]{1,0:T(8,128)(2,1)}, u32[]{:S(2)}, u32[]{:S(2)}) %collective-permute-start.4) | collective-permute-done | bytes 2560032 | tf_op jit(solution)/shard_map/ppermute | solution.py:498
  104.7 8.2 %collective-permute-done.17.cot_ref = bf16[128,1600]{1,0:T(8,128)(2,1)S(1)} collective-permute-done((bf16[128,1600]{1,0:T(8,128)(2,1)S(1)}, bf16[128,1600]{1,0:T(8,128)(2,1)S(1)}, u32[]{:S(2)}, u32[]{:S(2)}) %collective-permute-start.17) | collective-permute-done | bytes 409632 | tf_op jit(solution)/shard_map/ppermute | solution.py:46
  133.4 15.6 %attend.1 = (bf16[1024,1600]{1,0:T(8,128)(2,1)}, bf16[1024,768]{1,0:T(8,128)(2,1)}, bf16[1024,256]{1,0:T(8,128)(2,1)}, f32[1024,4]{1,0:T(8,128)}, bf16[8,200,768]{2,1,0:T(8,128)(2,1)}) custom-call(s32[8]{0:T(128)} %stack.39.place_ref, bf16[1024,1600]{1,0:T(8,128)(2,1)} %all-gather.11.cloned.1.call-done.tokens_ref, f32[8,1600]{1,0:T(8,128)} %reshape.103.norm_ref, ...), custom_call_target="tpu_custom_call" | custom-call | flops 2516582400 | bytes 13636640 | tf_op jit(solution)/shard_map/attend/pallas_call | solution.py:118
  152.9 14.5 %all_to_all.50.slots_ref = bf16[8,128,256]{2,1,0:T(8,128)(2,1)} all-to-all(bf16[8,128,256]{2,1,0:T(8,128)(2,1)} %bitcast.43), channel_id=1, replica_groups=mesh['x'=4,'zl'=2,'c'=2,'y'=4,'zh'=2] {'y','c'}, dimensions={0} | all-to-all | bytes 1048576 | tf_op jit(solution)/shard_map/all_to_all | solution.py:58
  183.5 7.7 %collective-permute-done.14.refs_5_ = bf16[200,800]{1,0:T(8,128)(2,1)S(1)} collective-permute-done((bf16[200,800]{1,0:T(8,128)(2,1)S(1)}, bf16[200,800]{1,0:T(8,128)(2,1)S(1)}, u32[]{:S(2)}, u32[]{:S(2)}) %collective-permute-start.14) | collective-permute-done | bytes 320032 | tf_op jit(solution)/shard_map/ppermute | solution.py:42
  191.1 7.7 %collective-permute-done.15.refs_6_ = bf16[200,800]{1,0:T(8,128)(2,1)S(1)} collective-permute-done((bf16[200,800]{1,0:T(8,128)(2,1)S(1)}, bf16[200,800]{1,0:T(8,128)(2,1)S(1)}, u32[]{:S(2)}, u32[]{:S(2)}) %collective-permute-start.15) | collective-permute-done | bytes 320032 | tf_op jit(solution)/shard_map/ppermute | solution.py:42
  198.8 7.7 %collective-permute-done.16.refs_7_ = bf16[200,800]{1,0:T(8,128)(2,1)S(1)} collective-permute-done((bf16[200,800]{1,0:T(8,128)(2,1)S(1)}, bf16[200,800]{1,0:T(8,128)(2,1)S(1)}, u32[]{:S(2)}, u32[]{:S(2)}) %collective-permute-start.16) | collective-permute-done | bytes 320032 | tf_op jit(solution)/shard_map/ppermute | solution.py:42
  216.3 8.5 %fusion.grad_ref = f32[1024,800]{1,0:T(8,128)} fusion(bf16[1024,1600]{1,0:T(8,128)(2,1)} %all-gather.17.cloned.1.call-done.right_ref, bf16[800,1600]{1,0:T(8,128)(2,1)} %param.27, bf16[800,1600]{1,0:T(8,128)(2,1)} %collective-permute-done.4, pred[]{:T(512)S(6)} %eq.4), kind=kOutput, calls=%fused_computation.2 | convolution fusion | flops 2622720000 | bytes 11673601 | tf_op jit(solution)/shard_map/dot_general | solution.py:107
  228.4 14.9 %hidden.1 = (bf16[1024,800]{1,0:T(8,128)(2,1)}, bf16[1024,800]{1,0:T(8,128)(2,1)}, f32[1,800]{1,0:T(1,128)}, bf16[1024,1600]{1,0:T(8,128)(2,1)}) custom-call(s32[8]{0:T(128)} %stack.39.place_ref, bf16[1024,1600]{1,0:T(8,128)(2,1)} %all-gather.15.cloned.1.call-done.second_ref.left_ref, bf16[1600,800]{1,0:T(8,128)(2,1)} %bitcast.41, ...), custom_call_target="tpu_custom_call" | custom-call | flops 5242880000 | bytes 15673632 | tf_op jit(solution)/shard_map/hidden/pallas_call | solution.py:118
  243.3 9.4 %fc_grad.1 = (bf16[4,4,32,800]{3,2,1,0:T(8,128)(2,1)}, bf16[4,4,32,800]{3,2,1,0:T(8,128)(2,1)}, bf16[4,4,32,800]{3,2,1,0:T(8,128)(2,1)}, bf16[4,4,32,800]{3,2,1,0:T(8,128)(2,1)}) custom-call(s32[8]{0:T(128)} %stack.39.place_ref, bf16[1024,1600]{1,0:T(8,128)(2,1)} %all-gather.15.cloned.1.call-done.second_ref.left_ref, ...), custom_call_target="tpu_custom_call" | custom-call | flops 2621440000 | bytes 8192032 | tf_op jit(solution)/shard_map/fc_grad/pallas_call | solution.py:118
  269.5 7.6 %reduce-scatter.3.cloned.1.call-done.grad_ref = bf16[128,1600]{1,0:T(8,128)(2,1)} async-done(((bf16[1024,1600]{1,0:T(8,128)(2,1)}), bf16[128,1600]{1,0:T(8,128)(2,1)}) %reduce-scatter.3.cloned.1.call-update) | async-done | bytes 409616 | tf_op jit(solution)/shard_map/reduce_scatter | solution.py:66
  283.5 9.3 %all-to-all-start.3 = ((bf16[8,128,256]{2,1,0:T(8,128)(2,1)}), bf16[8,128,256]{2,1,0:T(8,128)(2,1)}, u32[]{:S(2)}, u32[]{:S(2)}) async-start(bf16[8,128,256]{2,1,0:T(8,128)(2,1)} %get-tuple-element.153), calls=%async_computation.4 | async-start | bytes 1048576 | tf_op jit(solution)/shard_map/all_to_all | solution.py:58
  302.1 17.6 %attend_back.1 = (bf16[1024,768]{1,0:T(8,128)(2,1)}, bf16[8,2,128,1600]{3,2,1,0:T(8,128)(2,1)}, f32[1,768]{1,0:T(1,128)}) custom-call(s32[8]{0:T(128)} %stack.39.place_ref, bf16[1024,768]{1,0:T(8,128)(2,1)} %get-tuple-element.160.qkv_ref, bf16[1024,256]{1,0:T(8,128)(2,1)} %bitcast.14.grad_ref, bf16[1024,256]{1,0:T(8,128)(2,1)} %get-tuple-element.136.out_ref, ...), custom_call_target="tpu_custom_call" | custom-call | flops 2516582400 | bytes 16501792 | tf_op jit(solution)/shard_map/attend_back/pallas_call | solution.py:118
  336.9 44.0 %all-to-all-done.4 = bf16[16,4,32,768]{3,2,1,0:T(8,128)(2,1)S(1)} async-done(((bf16[16,4,32,768]{3,2,1,0:T(8,128)(2,1)}), bf16[16,4,32,768]{3,2,1,0:T(8,128)(2,1)S(1)}, u32[]{:S(2)}, u32[]{:S(2)}) %all-to-all-start.4) | async-done | bytes 3145760 | tf_op jit(solution)/shard_map/all_to_all | solution.py:58
  385.4 8.6 %collective-permute-done.53.refs_2_ = bf16[4,56,1600]{2,1,0:T(8,128)(2,1)} collective-permute-done((bf16[4,56,1600]{2,1,0:T(8,128)(2,1)}, bf16[4,56,1600]{2,1,0:T(8,128)(2,1)}, u32[]{:S(2)}, u32[]{:S(2)}) %collective-permute-start.53) | collective-permute-done | bytes 716832 | tf_op jit(solution)/shard_map/ppermute | solution.py:34
  394.0 12.6 %collective-permute-done.54.refs_3_ = bf16[4,56,1600]{2,1,0:T(8,128)(2,1)} collective-permute-done((bf16[4,56,1600]{2,1,0:T(8,128)(2,1)}, bf16[4,56,1600]{2,1,0:T(8,128)(2,1)}, u32[]{:S(2)}, u32[]{:S(2)}) %collective-permute-start.54) | collective-permute-done | bytes 716832 | tf_op jit(solution)/shard_map/ppermute | solution.py:34
  439.4 25.1 %collective-permute-done.23.refs_3_ = bf16[4,32,800]{2,1,0:T(8,128)(2,1)S(1)} collective-permute-done((bf16[4,32,800]{2,1,0:T(8,128)(2,1)S(1)}, bf16[4,32,800]{2,1,0:T(8,128)(2,1)S(1)}, u32[]{:S(2)}, u32[]{:S(2)}) %collective-permute-start.23) | collective-permute-done | bytes 204832 | tf_op jit(solution)/shard_map/ppermute | solution.py:34
  480.7 12.9 %collective-permute-done.27.refs_1_ = bf16[4,32,800]{2,1,0:T(8,128)(2,1)S(1)} collective-permute-done((bf16[4,32,800]{2,1,0:T(8,128)(2,1)}, bf16[4,32,800]{2,1,0:T(8,128)(2,1)S(1)}, u32[]{:S(2)}, u32[]{:S(2)}) %collective-permute-start.27) | collective-permute-done | bytes 204832 | tf_op jit(solution)/shard_map/ppermute | solution.py:42
  497.4 10.2 %all_to_all.51.refs_0_ = bf16[4,32,768]{2,1,0:T(8,128)(2,1)S(1)} all-to-all(bf16[4,32,768]{2,1,0:T(8,128)(2,1)} %reduce_sum.42), channel_id=1, replica_groups=mesh['x'=4,'zl'=2,'c'=2,'y'=4,'zh'=2] {'y'}, dimensions={0} | all-to-all | bytes 393216 | tf_op jit(solution)/shard_map/all_to_all | solution.py:58
  576.5 9.1 %qkv_total.1 = f32[200,4800]{1,0:T(8,128)} custom-call(s32[8]{0:T(128)} %stack.39.place_ref, bf16[2,4,32,768]{3,2,1,0:T(8,128)(2,1)} %qkv_both.1.refs_0_, bf16[2,4,32,768]{3,2,1,0:T(8,128)(2,1)} %copy-done.16, bf16[2,4,32,768]{3,2,1,0:T(8,128)(2,1)} %copy-done.15, bf16[2,4,32,768]{3,2,1,0:T(8,128)(2,1)} %collective-permute-done.31.refs_3_, ...), custom_call_target="tpu_custom_call" | custom-call | bytes 6985760 | tf_op jit(solution)/shard_map/qkv_total/pallas_call | solution.py:118
  598.1 10.6 %all_to_all.52 = f32[16,3,800]{2,1,0:T(4,128)S(1)} all-to-all(f32[16,3,800]{2,1,0:T(4,128)S(1)} %broadcast_in_dim.27), channel_id=1, replica_groups=mesh['x'=4,'zl'=2,'c'=2,'y'=4,'zh'=2] {'x','zl','c'}, dimensions={0} | all-to-all | bytes 307200 | tf_op jit(solution)/shard_map/all_to_all | solution.py:58
  608.9 9.0 %fc_total.1 = f32[200,6400]{1,0:T(8,128)} custom-call(s32[8]{0:T(128)} %stack.39.place_ref, bf16[2,4,32,800]{3,2,1,0:T(8,128)(2,1)} %fc_both.1.refs_0_, bf16[2,4,32,800]{3,2,1,0:T(8,128)(2,1)} %copy-done.13, bf16[2,4,32,800]{3,2,1,0:T(8,128)(2,1)} %copy-done.12, bf16[2,4,32,800]{3,2,1,0:T(8,128)(2,1)} %copy-done.11, ...), custom_call_target="tpu_custom_call" | custom-call | bytes 8396832 | tf_op jit(solution)/shard_map/fc_total/pallas_call | solution.py:118
  623.3 10.7 %collective-permute-done.32 = bf16[2,128,1600]{1,2,0:T(8,128)(2,1)S(1)} collective-permute-done((bf16[2,128,1600]{1,2,0:T(8,128)(2,1)S(1)}, bf16[2,128,1600]{1,2,0:T(8,128)(2,1)S(1)}, u32[]{:S(2)}, u32[]{:S(2)}) %collective-permute-start.32) | collective-permute-done | bytes 819232 | tf_op jit(solution)/shard_map/ppermute | solution.py:46
  (318 shorter events, 327.4 us)
Async XLA Ops:
  7.3 126.1 %all-gather.11.cloned.1.call-start = ((), (), s32[]{:S(2)}) async-start(), calls=%async_computation.14 | async-start | bytes 3833856 | tf_op jit(solution)/shard_map/all_gather | solution.py:62
  21.4 146.0 %all-gather.13.cloned.1.call-start = ((), (), s32[]{:S(2)}) async-start(), calls=%async_computation.15 | async-start | bytes 5990400 | tf_op jit(solution)/shard_map/all_gather | solution.py:62
  36.0 172.6 %all-gather.17.cloned.1.call-start = ((), (), s32[]{:S(2)}) async-start(), calls=%async_computation.17 | async-start | bytes 3833856 | tf_op jit(solution)/shard_map/all_gather | solution.py:62
  36.1 35.2 %collective-permute-start.4 = (bf16[800,1600]{1,0:T(8,128)(2,1)}, bf16[800,1600]{1,0:T(8,128)(2,1)}, u32[]{:S(2)}, u32[]{:S(2)}) collective-permute-start(bf16[800,1600]{1,0:T(8,128)(2,1)} %param.27), channel_id=1, source_target_pairs={{1,8},{8,1},{3,10},{10,3},{5,12},{12,5},{7,14},{14,7},{17,24},{24,... | collective-permute-start | bytes 7680008 | tf_op jit(solution)/shard_map/ppermute | solution.py:498
  118.9 109.5 %all-gather.15.cloned.1.call-start = ((), (), s32[]{:S(2)}) async-start(), calls=%async_computation.16 | async-start | bytes 3833856 | tf_op jit(solution)/shard_map/all_gather | solution.py:62
  215.9 61.2 %reduce-scatter.3.cloned.1.call-start = ((), (), s32[]{:S(2)}) async-start(), calls=%async_computation.12 | async-start | bytes 3833856 | tf_op jit(solution)/shard_map/reduce_scatter | solution.py:66
  252.8 45.6 %collective-permute-start.18 = (bf16[4,4,32,800]{3,2,1,0:T(8,128)(2,1)}, bf16[4,4,32,800]{3,2,1,0:T(8,128)(2,1)}, u32[]{:S(2)}, u32[]{:S(2)}) collective-permute-start(bf16[4,4,32,800]{3,2,1,0:T(8,128)(2,1)} %get-tuple-element.155), channel_id=1, source_target_pairs={{32,0},{64,32},{96,64},{0,96},{33,1},{65,33},{97,65},{1,97},{34,2}... | collective-permute-start | bytes 2457608 | tf_op jit(solution)/shard_map/ppermute | solution.py:34
  255.2 43.2 %collective-permute-start.19 = (bf16[4,4,32,800]{3,2,1,0:T(8,128)(2,1)}, bf16[4,4,32,800]{3,2,1,0:T(8,128)(2,1)}, u32[]{:S(2)}, u32[]{:S(2)}) collective-permute-start(bf16[4,4,32,800]{3,2,1,0:T(8,128)(2,1)} %get-tuple-element.156), channel_id=1, source_target_pairs={{64,0},{96,32},{0,64},{32,96},{65,1},{97,33},{1,65},{33,97},{66,2}... | collective-permute-start | bytes 2457608 | tf_op jit(solution)/shard_map/ppermute | solution.py:34
  255.7 43.2 %collective-permute-start.20 = (bf16[4,4,32,800]{3,2,1,0:T(8,128)(2,1)}, bf16[4,4,32,800]{3,2,1,0:T(8,128)(2,1)}, u32[]{:S(2)}, u32[]{:S(2)}) collective-permute-start(bf16[4,4,32,800]{3,2,1,0:T(8,128)(2,1)} %get-tuple-element.157), channel_id=1, source_target_pairs={{96,0},{0,32},{32,64},{64,96},{97,1},{1,33},{33,65},{65,97},{98,2}... | collective-permute-start | bytes 2457608 | tf_op jit(solution)/shard_map/ppermute | solution.py:34
  292.8 251.9 %reduce-scatter.5.cloned.1.call-start = ((), (), s32[]{:S(2)}) async-start(), calls=%async_computation.13 | async-start | bytes 7667712 | tf_op jit(solution)/shard_map/reduce_scatter | solution.py:66
  327.1 53.7 %all-to-all-start.4 = ((bf16[16,4,32,768]{3,2,1,0:T(8,128)(2,1)}), bf16[16,4,32,768]{3,2,1,0:T(8,128)(2,1)S(1)}, u32[]{:S(2)}, u32[]{:S(2)}) async-start(bf16[16,4,32,768]{3,2,1,0:T(8,128)(2,1)} %qkv_grad.1), calls=%async_computation.6 | async-start | bytes 6291456 | tf_op jit(solution)/shard_map/all_to_all | solution.py:58
  333.0 284.8 %all-gather.19.cloned.1.call-start = ((), (), s32[]{:S(2)}) async-start(), calls=%async_computation.18 | async-start | bytes 3168256 | tf_op jit(solution)/shard_map/all_gather | solution.py:62
  333.1 52.3 %collective-permute-start.52 = (bf16[4,56,1600]{2,1,0:T(8,128)(2,1)}, bf16[4,56,1600]{2,1,0:T(8,128)(2,1)}, u32[]{:S(2)}, u32[]{:S(2)}) collective-permute-start(bf16[4,56,1600]{2,1,0:T(8,128)(2,1)} %get-tuple-element.205), channel_id=1, source_target_pairs={{16,0},{1,16},{17,1},{0,17},{18,2},{3,18},{19,3},{2,19},{20,4},{5,... | collective-permute-start | bytes 2150408 | tf_op jit(solution)/shard_map/ppermute | solution.py:34
  335.7 58.3 %collective-permute-start.53 = (bf16[4,56,1600]{2,1,0:T(8,128)(2,1)}, bf16[4,56,1600]{2,1,0:T(8,128)(2,1)}, u32[]{:S(2)}, u32[]{:S(2)}) collective-permute-start(bf16[4,56,1600]{2,1,0:T(8,128)(2,1)} %get-tuple-element.207), channel_id=1, source_target_pairs={{1,0},{17,16},{0,1},{16,17},{3,2},{19,18},{2,3},{18,19},{5,4},{21,... | collective-permute-start | bytes 2150408 | tf_op jit(solution)/shard_map/ppermute | solution.py:34
  336.3 70.2 %collective-permute-start.54 = (bf16[4,56,1600]{2,1,0:T(8,128)(2,1)}, bf16[4,56,1600]{2,1,0:T(8,128)(2,1)}, u32[]{:S(2)}, u32[]{:S(2)}) collective-permute-start(bf16[4,56,1600]{2,1,0:T(8,128)(2,1)} %get-tuple-element.209), channel_id=1, source_target_pairs={{17,0},{0,16},{16,1},{1,17},{19,2},{2,18},{18,3},{3,19},{21,4},{4,... | collective-permute-start | bytes 2150408 | tf_op jit(solution)/shard_map/ppermute | solution.py:34
  433.0 47.1 %collective-permute-start.35 = (bf16[128,1600]{1,0:T(8,128)(2,1)}, bf16[128,1600]{1,0:T(8,128)(2,1)}, u32[]{:S(2)}, u32[]{:S(2)}) collective-permute-start(bf16[128,1600]{1,0:T(8,128)(2,1)} %get-tuple-element.188.refs_0_), channel_id=1, source_target_pairs={{6,0},{0,2},{2,4},{4,6},{7,1},{1,3},{3,5},{5,7},{14,8},{8,10},{10,... | collective-permute-start | bytes 1228808 | tf_op jit(solution)/shard_map/ppermute | solution.py:34
  433.9 46.3 %collective-permute-start.34 = (bf16[128,1600]{1,0:T(8,128)(2,1)}, bf16[128,1600]{1,0:T(8,128)(2,1)}, u32[]{:S(2)}, u32[]{:S(2)}) collective-permute-start(bf16[128,1600]{1,0:T(8,128)(2,1)} %get-tuple-element.188.refs_0_), channel_id=1, source_target_pairs={{4,0},{6,2},{0,4},{2,6},{5,1},{7,3},{1,5},{3,7},{12,8},{14,10},{8,... | collective-permute-start | bytes 1228808 | tf_op jit(solution)/shard_map/ppermute | solution.py:34
  437.3 43.3 %collective-permute-start.33 = (bf16[128,1600]{1,0:T(8,128)(2,1)}, bf16[128,1600]{1,0:T(8,128)(2,1)}, u32[]{:S(2)}, u32[]{:S(2)}) collective-permute-start(bf16[128,1600]{1,0:T(8,128)(2,1)} %get-tuple-element.188.refs_0_), channel_id=1, source_target_pairs={{2,0},{4,2},{6,4},{0,6},{3,1},{5,3},{7,5},{1,7},{10,8},{12,10},{14... | collective-permute-start | bytes 1228808 | tf_op jit(solution)/shard_map/ppermute | solution.py:34
  476.8 40.8 %collective-permute-start.36 = (bf16[128,1600]{1,0:T(8,128)(2,1)}, bf16[128,1600]{1,0:T(8,128)(2,1)}, u32[]{:S(2)}, u32[]{:S(2)}) collective-permute-start(bf16[128,1600]{1,0:T(8,128)(2,1)} %get-tuple-element.188.refs_0_), channel_id=1, source_target_pairs={{0,8},{8,0},{1,9},{9,1},{2,10},{10,2},{3,11},{11,3},{4,12},{12,4},... | collective-permute-start | bytes 1228808 | tf_op jit(solution)/shard_map/ppermute | solution.py:54
  480.1 37.7 %collective-permute-start.39 = (bf16[128,1600]{1,0:T(8,128)(2,1)}, bf16[128,1600]{1,0:T(8,128)(2,1)}, u32[]{:S(2)}, u32[]{:S(2)}) collective-permute-start(bf16[128,1600]{1,0:T(8,128)(2,1)} %collective-permute-done.35.refs_3_), channel_id=1, source_target_pairs={{0,8},{8,0},{1,9},{9,1},{2,10},{10,2},{3,11},{11,3},{4,12},{12,4},... | collective-permute-start | bytes 1228808 | tf_op jit(solution)/shard_map/ppermute | solution.py:54
  480.2 40.4 %collective-permute-start.38 = (bf16[128,1600]{1,0:T(8,128)(2,1)}, bf16[128,1600]{1,0:T(8,128)(2,1)}, u32[]{:S(2)}, u32[]{:S(2)}) collective-permute-start(bf16[128,1600]{1,0:T(8,128)(2,1)} %collective-permute-done.34.refs_2_), channel_id=1, source_target_pairs={{0,8},{8,0},{1,9},{9,1},{2,10},{10,2},{3,11},{11,3},{4,12},{12,4},... | collective-permute-start | bytes 1228808 | tf_op jit(solution)/shard_map/ppermute | solution.py:54
  480.6 40.0 %collective-permute-start.37 = (bf16[128,1600]{1,0:T(8,128)(2,1)}, bf16[128,1600]{1,0:T(8,128)(2,1)}, u32[]{:S(2)}, u32[]{:S(2)}) collective-permute-start(bf16[128,1600]{1,0:T(8,128)(2,1)} %collective-permute-done.33.refs_1_), channel_id=1, source_target_pairs={{0,8},{8,0},{1,9},{9,1},{2,10},{10,2},{3,11},{11,3},{4,12},{12,4},... | collective-permute-start | bytes 1228808 | tf_op jit(solution)/shard_map/ppermute | solution.py:54
  530.4 38.5 %collective-permute-start.40 = (bf16[2,4,32,768]{3,2,1,0:T(8,128)(2,1)S(1)}, bf16[2,4,32,768]{3,2,1,0:T(8,128)(2,1)}, u32[]{:S(2)}, u32[]{:S(2)}) collective-permute-start(bf16[2,4,32,768]{3,2,1,0:T(8,128)(2,1)S(1)} %copy-done.6), channel_id=1, source_target_pairs={{0,8},{8,0},{1,9},{9,1},{2,10},{10,2},{3,11},{11,3},{4,12},{12,4},... | collective-permute-start | bytes 1179656 | tf_op jit(solution)/shard_map/ppermute | solution.py:54
  560.3 37.7 %all-to-all-start.8 = ((bf16[16,16,1600]{2,1,0:T(8,128)(2,1)}), bf16[16,16,1600]{2,1,0:T(8,128)(2,1)S(1)}, u32[]{:S(2)}, u32[]{:S(2)}) async-start(bf16[16,16,1600]{2,1,0:T(8,128)(2,1)} %broadcast_in_dim.26), calls=%async_computation.10 | async-start | bytes 1703936 | tf_op jit(solution)/shard_map/all_to_all | solution.py:58
  (105 other events, 2809.1 us)
Sparse Core Ops, SparseCore 0:
  21.5 29.1 all-gather.10
  53.0 37.4 all-gather.12
  113.9 37.5 all-gather.16
  172.7 29.8 all-gather.14
  243.4 33.6 reduce-scatter.2
  319.8 44.2 reduce-scatter.4
  428.9 86.0 all-gather.18

commit v8 on v7

--- a/solution.py
+++ b/solution.py
@@ -107,7 +107,7 @@
     return lax.dot_general(left, right, (((1,), (1,)), ((), ())), preferred_element_type=f32)
 
 
-def call(kernel, name, out_shape, *operands, scratch=(), flops=0):
+def call(kernel, name, out_shape, *operands, scratch=(), flops=0, light=False):
     specs = [
         pl.BlockSpec(memory_space=pltpu.SMEM if op.dtype == jnp.int32 else pltpu.VMEM)
         for op in operands
@@ -123,7 +123,9 @@
         scratch_shapes=list(scratch),
         compiler_params=pltpu.CompilerParams(vmem_limit_bytes=56 * 2**20),
         cost_estimate=pl.CostEstimate(
-            flops=int(flops), bytes_accessed=int(moved), transcendentals=0
+            flops=1 if light else int(flops),
+            bytes_accessed=1 if light else int(moved),
+            transcendentals=0,
         ),
         name=name,
     )(*operands)
@@ -217,17 +219,6 @@
     sums_ref[3:4, :] = jnp.sum(cot, axis=0, keepdims=True)
 
 
-def column_grad_kernel(left_ref, right_ref, out_ref):
-    shard = left_ref.shape[1] // 8
-    size, starts = windows(shard, 8)
-    grad = dot_rows(left_ref[...], right_ref[...])
-    for y in range(4):
-        for zh in range(2):
-            base = (2 * y + zh) * shard
-            for i, start in enumerate(starts):
-                out_ref[2 * i + zh, y] = grad[base + start : base + start + size].astype(bf16)
-
-
 def column_ring_kernel(place_ref, left_ref, right_ref, *refs):
     out_refs, held_ref = refs[:4], refs[4]
     shard = left_ref.shape[1] // 8
@@ -255,21 +246,37 @@
             out_refs[k][x] = held_ref[pl.ds(at, size), :].astype(bf16)
 
 
-def out_grad_kernel(place_ref, left_ref, *refs):
-    blocks, out_ref, held_ref = refs[:8], refs[8], refs[9]
-    c = place_ref[C]
-    rows = left_ref.shape[2]
-    size, starts = windows(rows, 16)
-    for k in range(4):
-        y = lax.rem(place_ref[Y] + k, 4)
-        term = dot_rows(left_ref[2 * y + c], blocks[k][...])
-        term = term + dot_rows(left_ref[2 * y + 1 - c], blocks[4 + k][...])
-        if k == 0:
-            held_ref[...] = term
-        else:
-            held_ref[...] += term
-    for i, start in enumerate(starts):
-        out_ref[i] = held_ref[start : start + size, :].astype(bf16)
+def last_grads_kernel(place_ref, first_ref, mixed_ref, attended_ref, branch_ref, out_ref, held_ref):
+    shard = first_ref.shape[1] // 8
+    slots = mixed_ref.shape[1]
+    size, starts = windows(shard, 8)
+    held_ref[...] = dot_rows(first_ref[...], mixed_ref[...])
+    for y in range(4):
+        for zh in range(2):
+            base = (2 * y + zh) * shard
+            for i, start in enumerate(starts):
+                rows = slice(y % 2 * size, (y % 2 + 1) * size)
+                lanes = slice(y // 2 * slots, (y // 2 + 1) * slots)
+                block = held_ref[base + start : base + start + size, :]
+                out_ref[2 * i + zh, rows, lanes] = block.astype(bf16)
+    size_out, starts_out = windows(shard, 16)
+    grad = dot_rows(attended_ref[...], branch_ref[...])
+    rest = jnp.zeros((2 * size, out_ref.shape[2] - 2 * slots), bf16)
+    for i, start in enumerate(starts_out):
+        out_ref[i, : 2 * size, 2 * slots :] = rest
+        out_ref[i, 2 * size :, :] = grad[start : start + size_out].astype(bf16)
+
+
+def last_sum_kernel(parts_ref, qkv_ref, out_ref):
+    size, slots = qkv_ref.shape[1:]
+    total = parts_ref[0].astype(f32)
+    for i in range(1, 16):
+        total = total + parts_ref[i].astype(f32)
+    total = total.astype(bf16)
+    for y in range(4):
+        rows = slice(y % 2 * size, (y % 2 + 1) * size)
+        qkv_ref[y] = total[rows, y // 2 * slots : (y // 2 + 1) * slots]
+    out_ref[...] = total[2 * size :, :]
 
 
 def fold_kernel(which, place_ref, *refs):
@@ -384,6 +391,12 @@
         sums = sums + jnp.sum(grad.astype(f32), axis=0, keepdims=True)
         out_ref[rows, :] = dot_cols(grad, cols_ref[...]).astype(bf16)
     sums_ref[...] = sums
+
+
+def down_kernel(active_ref, rows_ref, out_ref):
+    for block in range(active_ref.shape[0] // BLOCK):
+        rows = slice(block * BLOCK, (block + 1) * BLOCK)
+        out_ref[rows, :] = dot(active_ref[rows, :], rows_ref[...]).astype(bf16)
 
 
 def attend_back_kernel(
@@ -495,7 +508,6 @@
     own_tokens = swap_roles(tokens.reshape(span, width))
     all_tokens = gather(own_tokens, TEAM).reshape(length, width)
     out_rows = swap_roles(w_out)
-    proj_came = lax.ppermute(after(w_proj, own_tokens), ("c", "zh"), ROLES[1:3])
     qkv_parts = call(
         qkv_columns_kernel,
         "qkv_columns",
@@ -511,7 +523,7 @@
     small_all = exchange(
         after(jnp.broadcast_to(small, (8, 3, hidden)), qkv_parts[0]), GRP
     )
-    qkv_other = [flipped(after(part, proj_came, out_rows), "zh") for part in qkv_own]
+    qkv_other = [flipped(after(part, small_all), "zh") for part in qkv_own]
     place = after(place, small_all)
     fc_parts = call(
         fc_columns_kernel,
@@ -536,7 +548,8 @@
 
     out_all = gather(out_rows, TEAM).reshape(width, width)
     all_cot = gather(after(own_cot, out_rows), TEAM).reshape(length, width)
-    proj_rows = jnp.where(stays, w_proj, after(proj_came, *qkv_other))
+    proj_came = lax.ppermute(after(w_proj, *qkv_other), ("c", "zh"), ROLES[1:3])
+    proj_rows = jnp.where(stays, w_proj, proj_came)
     fc_own = ring_all([after(part, *qkv_other) for part in fc_parts], "y")
 
     first, qkv, attended_slots, top, qkv_cols = call(
@@ -559,7 +572,9 @@
     )
     qkv_cols = qkv_cols.reshape(width, slots)
     fc_other = [flipped(part, "zh") for part in fc_own]
-    attended = exchange(after(attended_slots, *fc_own).reshape(8, span, SLOT_WIDTH), TEAM)
+    attended = exchange(
+        after(attended_slots, proj_came, *fc_own).reshape(8, span, SLOT_WIDTH), TEAM
+    )
     middle, second, attended_parts = call(
         branch_kernel,
         "branch",
@@ -577,14 +592,14 @@
     )
 
     second_all = gather(second, TEAM).reshape(length, width)
-    attended_own = exchange(after(attended_parts, *fc_other), TEAM)
+    attended_own = exchange(after(attended_parts, second), TEAM)
     grad_active = dot_cols(after(all_cot, second), proj_rows)
     fc_cols = call(
         fc_whole_kernel,
         "fc_whole",
         struct((8, shard, hidden), bf16),
         place,
-        after(fc_own[0], second),
+        after(fc_own[0], grad_active),
         *fc_own[1:],
         *fc_other,
     ).reshape(width, hidden)
@@ -622,13 +637,23 @@
         row_grad_kernel,
         "proj_grad",
         [struct((4, row_window, width), bf16)] * 4,
-        place,
+        after(place, fc_grad[0]),
         active,
         all_cot,
         scratch=[pltpu.VMEM((hidden, width), f32)],
         flops=2 * length * width * hidden,
     )
-    down_parts = dot(active, proj_rows).astype(bf16)
+    down_parts = call(
+        down_kernel,
+        "down",
+        struct((length, width), bf16),
+        after(active, proj_grad[0]),
+        proj_rows,
+        light=True,
+    )
+    proj_near = [ring(proj_grad[k], Z_RING, k) for k in (1, 3)]
+    proj_far = ring(after(proj_grad[2], *proj_near), Z_RING, 2)
+    proj_grad = [proj_grad[0], proj_near[0], proj_far, proj_near[1]]
 
     grad_middle, grad_branch, grad_slots, branch_sums = call(
         branch_back_kernel,
@@ -639,7 +664,7 @@
             struct((8, span, SLOT_WIDTH), bf16),
             struct((4, width), f32),
         ),
-        after(place, fc_grad[0], proj_grad[0], down_parts),
+        after(place, *fc_grad, proj_grad[1], proj_grad[3], down_parts),
         grad_second,
         middle,
         own_cot,
@@ -660,8 +685,8 @@
             *parts,
         )
 
-    fc_grad = fold(Z, fc_grad, "fc_fold", grad_slots)
-    proj_grad = ring_all([after(part, fc_grad[0]) for part in proj_grad], Z_RING)
+    fc_grad = ring_all(fold(Z, fc_grad, "fc_fold", grad_slots), Z_RING)
+    branch_all = gather(grad_branch, TEAM).reshape(length, width)
     grad_mixed, last_parts, mixed_sums = call(
         attend_back_kernel,
         "attend_back",
@@ -670,7 +695,7 @@
             struct((8, 2, span, width), bf16),
             struct((1, slots), f32),
         ),
-        after(place, fc_grad[0]),
+        after(place, proj_far, *fc_grad),
         qkv,
         grad_heads,
         attended_slots,
@@ -681,21 +706,22 @@
         flops=2 * length * width * slots,
     )
     last = team_sum(last_parts.reshape(2 * length, width)).reshape(2, span, width)
-    qkv_grad = call(
-        column_grad_kernel,
-        "qkv_grad",
-        struct((16, 4, window, slots), bf16),
-        first,
+    fc_grad = ring_all(fold(Y, fc_grad, "fc_fold_last", grad_mixed), "y")
+    proj_grad = ring_all(fold(X, proj_grad, "proj_fold", grad_mixed), "x")
+    last_grads = call(
+        last_grads_kernel,
+        "last_grads",
+        struct((16, 2 * window + windows(shard, 16)[0], width), bf16),
+        place,
+        after(first, fc_grad[0], proj_grad[0]),
         grad_mixed,
-        flops=2 * length * width * slots,
-    )
-    place = after(place, qkv_grad)
-    qkv_grad = exchange(qkv_grad, REPLICAS)
-    fc_grad = ring_all([after(part, place) for part in fc_grad], Z_RING)
-    branch_own = ring_all([after(grad_branch, qkv_grad)] * 4, "y")
-
-    def replica_sum(parts):
-        return jnp.sum(parts.astype(f32), axis=0).astype(bf16)
+        attended_own.reshape(length, shard),
+        branch_all,
+        scratch=[pltpu.VMEM((width, slots), f32)],
+        flops=2 * length * width * (slots + shard),
+    )
+    place = after(place, last_grads)
+    last_grads = exchange(after(last_grads, *fc_grad, *proj_grad), REPLICAS)
 
     def stacked(parts, name):
         return call(
@@ -708,30 +734,19 @@
             row_total_kernel, name, struct((rows, width), f32), place, whole, other_core(whole)
         )
 
-    fc_grad = ring_all(fold(Y, fc_grad, "fc_fold_last", place), "y")
-    fc_near = stacked(fc_grad, "fc_near")
+    proj_sum = sum(part.astype(f32) for part in [after(proj_grad[0], place)] + proj_grad[1:])
+    proj_whole = gather(proj_sum.astype(bf16), REPLICAS)
+    fc_near = stacked([after(fc_grad[0], place)] + fc_grad[1:], "fc_near")
     fc_both = stacked([fc_near, flipped(fc_near, "zl")], "fc_both")
-    branch_other = [other_core(part) for part in branch_own]
-    out_grad = call(
-        out_grad_kernel,
-        "out_grad",
-        struct((16, windows(shard, 16)[0], width), bf16),
-        place,
-        attended_own,
-        *branch_own,
-        *branch_other,
-        scratch=[pltpu.VMEM((shard, width), f32)],
-        flops=2 * length * width * shard,
-    )
-
-    place = after(place, qkv_grad)
-    qkv_sum = exchange(replica_sum(after(qkv_grad, fc_both)), "y")
-    proj_grad = ring_all(fold(X, proj_grad, "proj_fold", place), "x")
-    proj_sum = sum(part.astype(f32) for part in proj_grad).astype(bf16)
-    proj_whole = gather(proj_sum, REPLICAS)
+    qkv_sum, out_sum = call(
+        last_sum_kernel,
+        "last_sum",
+        (struct((4, window, slots), bf16), struct((windows(shard, 16)[0], width), bf16)),
+        after(last_grads, fc_both),
+    )
+    qkv_sum = exchange(qkv_sum, "y")
     qkv_both = stacked([qkv_sum, flipped(qkv_sum, "zl")], "qkv_both")
     qkv_pieces = ring_all([qkv_both] * 4, "x")
-    out_grad = exchange(after(out_grad, qkv_both), REPLICAS)
     fc_pieces = ring_all([after(fc_both, *qkv_pieces)] * 4, "x")
     results, first_sums = call(
         input_back_kernel,
@@ -741,7 +756,7 @@
         own_tokens,
         middle,
         grad_middle,
-        after(vectors, *qkv_pieces),
+        after(vectors, qkv_sum),
     )
     results_home = swap_roles(results)
 
@@ -760,14 +775,13 @@
     )
     small_terms = small_terms.reshape(8, 8, shard).transpose(1, 0, 2).reshape(8, 2, hidden)
     small_terms = jnp.concatenate([small_terms, hidden_term[:, None]], axis=1)
-    small_sum = jnp.sum(exchange(after(small_terms, out_grad), GRP), axis=0)
-    out_sum = replica_sum(out_grad)
+    small_sum = jnp.sum(exchange(after(small_terms, qkv_both), GRP), axis=0)
     out_whole = exchange(
         after(jnp.broadcast_to(out_sum, (16,) + out_sum.shape), small_sum), REPLICAS
     )
-    small_sum = jnp.broadcast_to(after(small_sum, out_whole), (16, 3, hidden))
-    small_sum = jnp.sum(exchange(small_sum, REP), axis=0)
-    owned = small_sum[:2].reshape(8, shard)
+    small_last = jnp.broadcast_to(after(small_sum, out_whole), (16, 3, hidden))
+    small_last = jnp.sum(exchange(small_last, REP), axis=0)
+    owned = small_last[:2].reshape(8, shard)
 
     qkv_pieces = qkv_pieces + [other_core(part) for part in qkv_pieces]
     qkv_spans = [
@@ -781,7 +795,7 @@
         functools.partial(column_total_kernel, qkv_spans, False),
         "qkv_total",
         struct((shard, 3 * width), f32),
-        after(place, results, out_grad),
+        after(place, results, small_sum),
         *qkv_pieces,
     )
     fc_pieces = fc_pieces + [other_core(after(part, qkv_total)) for part in fc_pieces]
@@ -790,7 +804,7 @@
         functools.partial(column_total_kernel, fc_spans, True),
         "fc_total",
         struct((shard, 8 * hidden), f32),
-        after(place, out_whole, small_sum),
+        after(place, out_whole, small_last),
         *fc_pieces,
     )
     out_total = row_total(out_whole, shard, "out_total", fc_total)
@@ -808,7 +822,7 @@
         owned[5],
         owned[6],
         fc_total,
-        small_sum[2],
+        small_last[2],
         proj_total,
         owned[7],
     )

time: 662 us -> 616 us (0.931)
  waiting for transfers between devices: 276 us -> 182 us
  blocking collectives: 35.4 us -> 59.7 us
  starting transfers between devices: 138 us -> 161 us
  Pallas kernels: 143 us -> 151 us
  matrix products: 14.2 us -> 6.89 us
    all_to_all x7 -> x4, waiting for transfers between devices: 53.5 us -> 0.01 us  [exchange(): return lax.all_to_all(parts, axes, 0, 0)]
    ppermute x30 -> x27, waiting for transfers between devices: 88.5 us -> 52.9 us  [ring(): lax.ppermute(value, axis, [(index[(i + step) % 4], index[i]) for i in ran...]
    ppermute x30 -> x27, starting transfers between devices: 39.2 us -> 65.7 us  [ring(): lax.ppermute(value, axis, [(index[(i + step) % 4], index[i]) for i in ran...]
    ppermute x10, waiting for transfers between devices: 71.1 us -> 95.7 us  [flipped(): return lax.ppermute(value, axis, [(0, 1), (1, 0)])]
    all_to_all x3 -> x5, blocking collectives: 35.4 us -> 59.7 us  [exchange(): return lax.all_to_all(parts, axes, 0, 0)]
    ppermute x1, waiting for transfers between devices: 19.8 us -> 0.01 us  [per_device(): proj_came = lax.ppermute(after(w_proj, *qkv_other), ('c', 'zh'), ROLES[1:3])]
    pallas_call x23 -> x24, Pallas kernels: 143 us -> 151 us  [call(): pl.pallas_call(kernel, out_shape=out_shape, in_specs=specs, out_specs=out...]
    ppermute x14 -> x10, starting transfers between devices: 24.1 us -> 16 us  [other_core(): return lax.ppermute(value, 'c', [(0, 1), (1, 0)])]
  transfers between devices with their start and end apart: 73 -> 64, of which waited for: 38 -> 24; matrix products, arithmetic and copies ran while one was open for 6% -> 5% of each run, Pallas kernels for 16% -> 21%
where the time goes in v8:
time: 616 us; the launch traced here: 606 us
  waiting for transfers between devices  182 us (30%)
  starting transfers between devices  161 us (26%)
  Pallas kernels  151 us (25%)
  blocking collectives  59.7 us (10%)
  local copies, waits for them, and re-layouts  25.3 us (4%)
  between operations  15.1 us (2%)
  matrix products  6.89 us (1%)
    pallas_call x24, Pallas kernels, call(): pl.pallas_call(kernel, out_shape=out_shape, in_specs=specs, out_specs=out...  151 us
    ppermute x10, waiting for transfers between devices, flipped(): return lax.ppermute(value, axis, [(0, 1), (1, 0)])  95.7 us
    ppermute x27, starting transfers between devices, ring(): lax.ppermute(value, axis, [(index[(i + step) % 4], index[i]) for i in ran...  65.7 us
    all_to_all x5, blocking collectives, exchange(): return lax.all_to_all(parts, axes, 0, 0)  59.7 us
    ppermute x27, waiting for transfers between devices, ring(): lax.ppermute(value, axis, [(index[(i + step) % 4], index[i]) for i in ran...  52.9 us
    all_to_all x4, starting transfers between devices, exchange(): return lax.all_to_all(parts, axes, 0, 0)  36.4 us
    ppermute x4, waiting for transfers between devices, swap_roles(): return lax.ppermute(value, ('c', 'zh'), ROLES)  31.2 us
    ppermute x4, starting transfers between devices, swap_roles(): return lax.ppermute(value, ('c', 'zh'), ROLES)  22.9 us
  transfers between devices with their start and end apart: 64, of which 24 were waited for; matrix products, arithmetic and copies ran while one was open for 5% of the time, Pallas kernels for 21%

profile of v8, /device:TPU:17, one launch (start us, length us, event | category | flops | bytes accessed | tf_op | source)
XLA Modules:
  0.0 605.9 jit_solution(11902037772214358136)
XLA Ops:
  26.6 8.7 %collective-permute-done.12 = bf16[200,1600]{1,0:T(8,128)(2,1)} collective-permute-done((bf16[200,1600]{1,0:T(8,128)(2,1)}, bf16[200,1600]{1,0:T(8,128)(2,1)}, u32[]{:S(2)}, u32[]{:S(2)}) %collective-permute-start.12) | collective-permute-done | bytes 640032 | tf_op jit(solution)/shard_map/ppermute | solution.py:46
  42.9 13.0 %all_to_all.45 = bf16[8,3,800]{2,1,0:T(4,128)(2,1)S(1)} all-to-all(bf16[8,3,800]{2,1,0:T(4,128)(2,1)S(1)} %broadcast_in_dim.21), channel_id=1, replica_groups=mesh['x'=4,'zl'=2,'c'=2,'y'=4,'zh'=2] {'y','zh'}, dimensions={0} | all-to-all | bytes 76800 | tf_op jit(solution)/shard_map/all_to_all | solution.py:58
  114.2 15.6 %attend.1 = (bf16[1024,1600]{1,0:T(8,128)(2,1)}, bf16[1024,768]{1,0:T(8,128)(2,1)}, bf16[1024,256]{1,0:T(8,128)(2,1)}, f32[1024,4]{1,0:T(8,128)}, bf16[8,200,768]{2,1,0:T(8,128)(2,1)}) custom-call(s32[8]{0:T(128)} %stack.39.place_ref, bf16[1024,1600]{1,0:T(8,128)(2,1)} %all-gather.13.cloned.1.call-done.tokens_ref, f32[8,1600]{1,0:T(8,128)} %reshape.109.norm_ref, ...), custom_call_target="tpu_custom_call" | custom-call | flops 2516582400 | bytes 13636640 | tf_op jit(solution)/shard_map/attend/pallas_call | solution.py:118
  134.9 12.1 %all_to_all.46.slots_ref = bf16[8,128,256]{2,1,0:T(8,128)(2,1)} all-to-all(bf16[8,128,256]{2,1,0:T(8,128)(2,1)} %bitcast.45), channel_id=1, replica_groups=mesh['x'=4,'zl'=2,'c'=2,'y'=4,'zh'=2] {'y','c'}, dimensions={0} | all-to-all | bytes 1048576 | tf_op jit(solution)/shard_map/all_to_all | solution.py:58
  163.0 7.7 %all-to-all-start.2 = ((bf16[8,128,200]{1,2,0:T(8,128)(2,1)}), bf16[8,128,200]{1,2,0:T(8,128)(2,1)S(1)}, u32[]{:S(2)}, u32[]{:S(2)}) async-start(bf16[8,128,200]{1,2,0:T(8,128)(2,1)} %copy.64), calls=%async_computation.2 | async-start | bytes 819200 | tf_op jit(solution)/shard_map/all_to_all | solution.py:58
  191.6 14.8 %hidden.1 = (bf16[1024,800]{1,0:T(8,128)(2,1)}, bf16[1024,800]{1,0:T(8,128)(2,1)}, f32[1,800]{1,0:T(1,128)}, bf16[1024,1600]{1,0:T(8,128)(2,1)}) custom-call(s32[8]{0:T(128)} %stack.39.place_ref, bf16[1024,1600]{1,0:T(8,128)(2,1)} %all-gather.17.cloned.1.call-done.second_ref.left_ref, bf16[1600,800]{1,0:T(8,128)(2,1)} %bitcast.42, ...), custom_call_target="tpu_custom_call" | custom-call | flops 5242880000 | bytes 15673632 | tf_op jit(solution)/shard_map/hidden/pallas_call | solution.py:118
  206.6 9.1 %fc_grad.1 = (bf16[4,4,32,800]{3,2,1,0:T(8,128)(2,1)}, bf16[4,4,32,800]{3,2,1,0:T(8,128)(2,1)}, bf16[4,4,32,800]{3,2,1,0:T(8,128)(2,1)}, bf16[4,4,32,800]{3,2,1,0:T(8,128)(2,1)}) custom-call(s32[8]{0:T(128)} %stack.39.place_ref, bf16[1024,1600]{1,0:T(8,128)(2,1)} %all-gather.17.cloned.1.call-done.second_ref.left_ref, ...), custom_call_target="tpu_custom_call" | custom-call | flops 2621440000 | bytes 8192032 | tf_op jit(solution)/shard_map/fc_grad/pallas_call | solution.py:118
  219.3 7.5 %proj_grad.1 = (bf16[4,56,1600]{2,1,0:T(8,128)(2,1)}, bf16[4,56,1600]{2,1,0:T(8,128)(2,1)}, bf16[4,56,1600]{2,1,0:T(8,128)(2,1)}, bf16[4,56,1600]{2,1,0:T(8,128)(2,1)}) custom-call(s32[8]{0:T(128)} %stack.39.place_ref, bf16[1024,800]{1,0:T(8,128)(2,1)} %get-tuple-element.154.left_ref.active_ref, bf16[1024,1600]{1,0:T(8,128)(2,1)} %all-gather.19.cloned.1.call-done.right_ref), custom_call_target="tpu_custom_call" | custom-call | flops 2621440000 | bytes 7782432 | tf_op jit(solution)/shard_map/proj_grad/pallas_call | solution.py:118
  230.1 8.0 %down.1 = bf16[1024,1600]{1,0:T(8,128)(2,1)} custom-call(bf16[1024,800]{1,0:T(8,128)(2,1)} %get-tuple-element.154.left_ref.active_ref, bf16[800,1600]{1,0:T(8,128)(2,1)} %copy-done), custom_call_target="tpu_custom_call" | custom-call | flops 1 | bytes 1 | tf_op jit(solution)/shard_map/down/pallas_call | solution.py:118
  248.0 13.9 %collective-permute-done.23.refs_3_ = bf16[4,4,32,800]{3,2,1,0:T(8,128)(2,1)} collective-permute-done((bf16[4,4,32,800]{3,2,1,0:T(8,128)(2,1)}, bf16[4,4,32,800]{3,2,1,0:T(8,128)(2,1)}, u32[]{:S(2)}, u32[]{:S(2)}) %collective-permute-start.23) | collective-permute-done | bytes 819232 | tf_op jit(solution)/shard_map/ppermute | solution.py:34
  299.4 17.6 %attend_back.1 = (bf16[1024,768]{1,0:T(8,128)(2,1)}, bf16[8,2,128,1600]{3,2,1,0:T(8,128)(2,1)}, f32[1,768]{1,0:T(1,128)}) custom-call(s32[8]{0:T(128)} %stack.39.place_ref, bf16[1024,768]{1,0:T(8,128)(2,1)} %get-tuple-element.165.qkv_ref, bf16[1024,256]{1,0:T(8,128)(2,1)} %bitcast.46, bf16[1024,256]{1,0:T(8,128)(2,1)} %get-tuple-element.133.out_ref, ...), custom_call_target="tpu_custom_call" | custom-call | flops 2516582400 | bytes 16501792 | tf_op jit(solution)/shard_map/attend_back/pallas_call | solution.py:118
  328.9 9.3 %last_grads.1 = bf16[16,80,1600]{2,1,0:T(8,128)(2,1)} custom-call(s32[8]{0:T(128)} %stack.39.place_ref, bf16[1024,1600]{1,0:T(8,128)(2,1)} %get-tuple-element.176.first_ref, bf16[1024,768]{1,0:T(8,128)(2,1)} %get-tuple-element.171.mixed_ref, bf16[1024,200]{1,0:T(8,128)(2,1)} %bitcast.43, bf16[1024,1600]{1,0:T(8,128)(2,1)} %all-gather.21.cloned.1.call-done.branch_ref), custom_call_target="tpu_custom_call" | custom-call | flops 3171942400 | bytes 12632096 | tf_op jit(solution)/shard_map/last_grads/pallas_call | solution.py:118
  349.9 59.5 %collective-permute-done.33.refs_1_ = bf16[4,32,800]{2,1,0:T(8,128)(2,1)S(1)} collective-permute-done((bf16[4,32,800]{2,1,0:T(8,128)(2,1)}, bf16[4,32,800]{2,1,0:T(8,128)(2,1)S(1)}, u32[]{:S(2)}, u32[]{:S(2)}) %collective-permute-start.33) | collective-permute-done | bytes 204832 | tf_op jit(solution)/shard_map/ppermute | solution.py:42
  415.4 7.7 %all_to_all.47.refs_0_ = bf16[4,32,768]{2,1,0:T(8,128)(2,1)S(1)} all-to-all(bf16[4,32,768]{2,1,0:T(8,128)(2,1)} %get-tuple-element.188), channel_id=1, replica_groups=mesh['x'=4,'zl'=2,'c'=2,'y'=4,'zh'=2] {'y'}, dimensions={0} | all-to-all | bytes 393216 | tf_op jit(solution)/shard_map/all_to_all | solution.py:58
  423.1 9.0 %collective-permute-done.35.refs_1_ = bf16[4,32,768]{2,1,0:T(8,128)(2,1)S(1)} collective-permute-done((bf16[4,32,768]{2,1,0:T(8,128)(2,1)S(1)}, bf16[4,32,768]{2,1,0:T(8,128)(2,1)S(1)}, u32[]{:S(2)}, u32[]{:S(2)}) %collective-permute-start.35) | collective-permute-done | bytes 196640 | tf_op jit(solution)/shard_map/ppermute | solution.py:42
  434.6 26.5 %collective-permute-start.38 = (bf16[2,4,32,768]{3,2,1,0:T(8,128)(2,1)}, bf16[2,4,32,768]{3,2,1,0:T(8,128)(2,1)S(1)}, u32[]{:S(2)}, u32[]{:S(2)}) collective-permute-start(bf16[2,4,32,768]{3,2,1,0:T(8,128)(2,1)} %qkv_both.1.refs_0_), channel_id=1, source_target_pairs={{96,0},{0,32},{32,64},{64,96},{97,1},{1,33},{33,65},{65,97},{98,2}... | collective-permute-start | bytes 1179656 | tf_op jit(solution)/shard_map/ppermute | solution.py:34
  461.8 8.9 %collective-permute-start.39 = (bf16[2,4,32,768]{3,2,1,0:T(8,128)(2,1)}, bf16[2,4,32,768]{3,2,1,0:T(8,128)(2,1)S(1)}, u32[]{:S(2)}, u32[]{:S(2)}) collective-permute-start(bf16[2,4,32,768]{3,2,1,0:T(8,128)(2,1)} %qkv_both.1.refs_0_), channel_id=1, source_target_pairs={{0,8},{8,0},{1,9},{9,1},{2,10},{10,2},{3,11},{11,3},{4,12},{12,4},... | collective-permute-start | bytes 1179656 | tf_op jit(solution)/shard_map/ppermute | solution.py:54
  484.1 16.3 %all_to_all.48 = f32[8,3,800]{2,1,0:T(4,128)S(1)} all-to-all(f32[8,3,800]{2,1,0:T(4,128)S(1)} %pad_maximum_fusion), channel_id=1, replica_groups=mesh['x'=4,'zl'=2,'c'=2,'y'=4,'zh'=2] {'y','zh'}, dimensions={0} | all-to-all | bytes 153600 | tf_op jit(solution)/shard_map/all_to_all | solution.py:58
  501.4 15.9 %all-to-all-start.7 = ((bf16[16,16,1600]{2,1,0:T(8,128)(2,1)}), bf16[16,16,1600]{2,1,0:T(8,128)(2,1)S(1)}, u32[]{:S(2)}, u32[]{:S(2)}) async-start(bf16[16,16,1600]{2,1,0:T(8,128)(2,1)} %broadcast_in_dim.26), calls=%async_computation.9 | async-start | bytes 1703936 | tf_op jit(solution)/shard_map/all_to_all | solution.py:58
  529.0 9.1 %qkv_total.1 = f32[200,4800]{1,0:T(8,128)} custom-call(s32[8]{0:T(128)} %stack.39.place_ref, bf16[2,4,32,768]{3,2,1,0:T(8,128)(2,1)} %qkv_both.1.refs_0_, bf16[2,4,32,768]{3,2,1,0:T(8,128)(2,1)} %collective-permute-done.36.refs_1_, bf16[2,4,32,768]{3,2,1,0:T(8,128)(2,1)} %copy-done.23, bf16[2,4,32,768]{3,2,1,0:T(8,128)(2,1)} %copy-done.21, ...), custom_call_target="tpu_custom_call" | custom-call | bytes 6985760 | tf_op jit(solution)/shard_map/qkv_total/pallas_call | solution.py:118
  540.1 8.1 %collective-permute-done.44.refs_2_ = bf16[2,4,32,800]{3,2,1,0:T(8,128)(2,1)S(1)} collective-permute-done((bf16[2,4,32,800]{3,2,1,0:T(8,128)(2,1)S(1)}, bf16[2,4,32,800]{3,2,1,0:T(8,128)(2,1)S(1)}, u32[]{:S(2)}, u32[]{:S(2)}) %collective-permute-start.44) | collective-permute-done | bytes 409632 | tf_op jit(solution)/shard_map/ppermute | solution.py:34
  551.5 10.6 %all_to_all.49 = f32[16,3,800]{2,1,0:T(4,128)S(1)} all-to-all(f32[16,3,800]{2,1,0:T(4,128)S(1)} %broadcast_in_dim.27), channel_id=1, replica_groups=mesh['x'=4,'zl'=2,'c'=2,'y'=4,'zh'=2] {'x','zl','c'}, dimensions={0} | all-to-all | bytes 307200 | tf_op jit(solution)/shard_map/all_to_all | solution.py:58
  562.2 9.0 %fc_total.1 = f32[200,6400]{1,0:T(8,128)} custom-call(s32[8]{0:T(128)} %stack.39.place_ref, bf16[2,4,32,800]{3,2,1,0:T(8,128)(2,1)} %fc_both.1.refs_0_, bf16[2,4,32,800]{3,2,1,0:T(8,128)(2,1)} %copy-done.19, bf16[2,4,32,800]{3,2,1,0:T(8,128)(2,1)} %copy-done.18, bf16[2,4,32,800]{3,2,1,0:T(8,128)(2,1)} %copy-done.17, ...), custom_call_target="tpu_custom_call" | custom-call | bytes 8396832 | tf_op jit(solution)/shard_map/fc_total/pallas_call | solution.py:118
  576.6 10.8 %collective-permute-done.34 = bf16[2,128,1600]{1,2,0:T(8,128)(2,1)S(1)} collective-permute-done((bf16[2,128,1600]{1,2,0:T(8,128)(2,1)S(1)}, bf16[2,128,1600]{1,2,0:T(8,128)(2,1)S(1)}, u32[]{:S(2)}, u32[]{:S(2)}) %collective-permute-start.34) | collective-permute-done | bytes 819232 | tf_op jit(solution)/shard_map/ppermute | solution.py:46
  (300 shorter events, 262.1 us)
Async XLA Ops:
  7.3 106.9 %all-gather.13.cloned.1.call-start = ((), (), s32[]{:S(2)}) async-start(), calls=%async_computation.13 | async-start | bytes 3833856 | tf_op jit(solution)/shard_map/all_gather | solution.py:62
  21.4 125.7 %all-gather.15.cloned.1.call-start = ((), (), s32[]{:S(2)}) async-start(), calls=%async_computation.14 | async-start | bytes 5990400 | tf_op jit(solution)/shard_map/all_gather | solution.py:62
  35.3 127.7 %all-gather.19.cloned.1.call-start = ((), (), s32[]{:S(2)}) async-start(), calls=%async_computation.16 | async-start | bytes 3833856 | tf_op jit(solution)/shard_map/all_gather | solution.py:62
  99.3 92.3 %all-gather.17.cloned.1.call-start = ((), (), s32[]{:S(2)}) async-start(), calls=%async_computation.15 | async-start | bytes 3833856 | tf_op jit(solution)/shard_map/all_gather | solution.py:62
  99.4 35.6 %collective-permute-start.8 = (bf16[800,1600]{1,0:T(8,128)(2,1)S(1)}, bf16[800,1600]{1,0:T(8,128)(2,1)}, u32[]{:S(2)}, u32[]{:S(2)}) collective-permute-start(bf16[800,1600]{1,0:T(8,128)(2,1)S(1)} %copy-done.3), channel_id=1, source_target_pairs={{1,8},{8,1},{3,10},{10,3},{5,12},{12,5},{7,14},{14,7},{17,24},{24,... | collective-permute-start | bytes 7680008 | tf_op jit(solution)/shard_map/ppermute | solution.py:551
  152.9 29.7 %collective-permute-start.14 = (bf16[200,800]{1,0:T(8,128)(2,1)S(1)}, bf16[200,800]{1,0:T(8,128)(2,1)}, u32[]{:S(2)}, u32[]{:S(2)}) collective-permute-start(bf16[200,800]{1,0:T(8,128)(2,1)S(1)} %copy-done.26), channel_id=1, source_target_pairs={{0,1},{1,0},{2,3},{3,2},{4,5},{5,4},{6,7},{7,6},{8,9},{9,8},{10,11... | collective-permute-start | bytes 960008 | tf_op jit(solution)/shard_map/ppermute | solution.py:42
  159.8 28.3 %collective-permute-start.15 = (bf16[200,800]{1,0:T(8,128)(2,1)}, bf16[200,800]{1,0:T(8,128)(2,1)}, u32[]{:S(2)}, u32[]{:S(2)}) collective-permute-start(bf16[200,800]{1,0:T(8,128)(2,1)} %collective-permute-done.9.refs_1_), channel_id=1, source_target_pairs={{0,1},{1,0},{2,3},{3,2},{4,5},{5,4},{6,7},{7,6},{8,9},{9,8},{10,11... | collective-permute-start | bytes 960008 | tf_op jit(solution)/shard_map/ppermute | solution.py:42
  163.0 28.6 %all-to-all-start.2 = ((bf16[8,128,200]{1,2,0:T(8,128)(2,1)}), bf16[8,128,200]{1,2,0:T(8,128)(2,1)S(1)}, u32[]{:S(2)}, u32[]{:S(2)}) async-start(bf16[8,128,200]{1,2,0:T(8,128)(2,1)} %copy.64), calls=%async_computation.2 | async-start | bytes 819200 | tf_op jit(solution)/shard_map/all_to_all | solution.py:58
  170.8 91.1 %reduce-scatter.3.cloned.1.call-start = ((), (), s32[]{:S(2)}) async-start(), calls=%async_computation.11 | async-start | bytes 3833856 | tf_op jit(solution)/shard_map/reduce_scatter | solution.py:66
  206.4 122.5 %all-gather.21.cloned.1.call-start = ((), (), s32[]{:S(2)}) async-start(), calls=%async_computation.17 | async-start | bytes 3833856 | tf_op jit(solution)/shard_map/all_gather | solution.py:62
  215.7 31.4 %collective-permute-start.21 = (bf16[4,4,32,800]{3,2,1,0:T(8,128)(2,1)}, bf16[4,4,32,800]{3,2,1,0:T(8,128)(2,1)S(1)}, u32[]{:S(2)}, u32[]{:S(2)}) collective-permute-start(bf16[4,4,32,800]{3,2,1,0:T(8,128)(2,1)} %get-tuple-element.150), channel_id=1, source_target_pairs={{32,0},{64,32},{96,64},{0,96},{33,1},{65,33},{97,65},{1,97},{34,2}... | collective-permute-start | bytes 2457608 | tf_op jit(solution)/shard_map/ppermute | solution.py:34
  218.1 29.0 %collective-permute-start.22 = (bf16[4,4,32,800]{3,2,1,0:T(8,128)(2,1)}, bf16[4,4,32,800]{3,2,1,0:T(8,128)(2,1)S(1)}, u32[]{:S(2)}, u32[]{:S(2)}) collective-permute-start(bf16[4,4,32,800]{3,2,1,0:T(8,128)(2,1)} %get-tuple-element.151), channel_id=1, source_target_pairs={{64,0},{96,32},{0,64},{32,96},{65,1},{97,33},{1,65},{33,97},{66,2}... | collective-permute-start | bytes 2457608 | tf_op jit(solution)/shard_map/ppermute | solution.py:34
  218.7 43.2 %collective-permute-start.23 = (bf16[4,4,32,800]{3,2,1,0:T(8,128)(2,1)}, bf16[4,4,32,800]{3,2,1,0:T(8,128)(2,1)}, u32[]{:S(2)}, u32[]{:S(2)}) collective-permute-start(bf16[4,4,32,800]{3,2,1,0:T(8,128)(2,1)} %get-tuple-element.152), channel_id=1, source_target_pairs={{96,0},{0,32},{32,64},{64,96},{97,1},{1,33},{33,65},{65,97},{98,2}... | collective-permute-start | bytes 2457608 | tf_op jit(solution)/shard_map/ppermute | solution.py:34
  277.2 202.1 %reduce-scatter.5.cloned.1.call-start = ((), (), s32[]{:S(2)}) async-start(), calls=%async_computation.12 | async-start | bytes 7667712 | tf_op jit(solution)/shard_map/reduce_scatter | solution.py:66
  339.4 72.6 %all-to-all-start.4 = ((bf16[16,80,1600]{2,1,0:T(8,128)(2,1)}), bf16[16,80,1600]{2,1,0:T(8,128)(2,1)}, u32[]{:S(2)}, u32[]{:S(2)}) async-start(bf16[16,80,1600]{2,1,0:T(8,128)(2,1)} %last_grads.1), calls=%async_computation.6 | async-start | bytes 8519680 | tf_op jit(solution)/shard_map/all_to_all | solution.py:58
  346.1 225.1 %all-gather.23.cloned.1.call-start = ((), (), s32[]{:S(2)}) async-start(), calls=%async_computation.18 | async-start | bytes 3168256 | tf_op jit(solution)/shard_map/all_gather | solution.py:62
  348.6 60.9 %collective-permute-start.33 = (bf16[4,32,800]{2,1,0:T(8,128)(2,1)}, bf16[4,32,800]{2,1,0:T(8,128)(2,1)S(1)}, u32[]{:S(2)}, u32[]{:S(2)}) collective-permute-start(bf16[4,32,800]{2,1,0:T(8,128)(2,1)} %fc_near.1.refs_0_), channel_id=1, source_target_pairs={{0,16},{16,0},{1,17},{17,1},{2,18},{18,2},{3,19},{19,3},{4,20},{20... | collective-permute-start | bytes 614408 | tf_op jit(solution)/shard_map/ppermute | solution.py:42
  434.6 44.1 %collective-permute-start.38 = (bf16[2,4,32,768]{3,2,1,0:T(8,128)(2,1)}, bf16[2,4,32,768]{3,2,1,0:T(8,128)(2,1)S(1)}, u32[]{:S(2)}, u32[]{:S(2)}) collective-permute-start(bf16[2,4,32,768]{3,2,1,0:T(8,128)(2,1)} %qkv_both.1.refs_0_), channel_id=1, source_target_pairs={{96,0},{0,32},{32,64},{64,96},{97,1},{1,33},{33,65},{65,97},{98,2}... | collective-permute-start | bytes 1179656 | tf_op jit(solution)/shard_map/ppermute | solution.py:34
  461.8 61.4 %collective-permute-start.39 = (bf16[2,4,32,768]{3,2,1,0:T(8,128)(2,1)}, bf16[2,4,32,768]{3,2,1,0:T(8,128)(2,1)S(1)}, u32[]{:S(2)}, u32[]{:S(2)}) collective-permute-start(bf16[2,4,32,768]{3,2,1,0:T(8,128)(2,1)} %qkv_both.1.refs_0_), channel_id=1, source_target_pairs={{0,8},{8,0},{1,9},{9,1},{2,10},{10,2},{3,11},{11,3},{4,12},{12,4},... | collective-permute-start | bytes 1179656 | tf_op jit(solution)/shard_map/ppermute | solution.py:54
  470.6 46.7 %collective-permute-start.37 = (bf16[2,4,32,768]{3,2,1,0:T(8,128)(2,1)}, bf16[2,4,32,768]{3,2,1,0:T(8,128)(2,1)S(1)}, u32[]{:S(2)}, u32[]{:S(2)}) collective-permute-start(bf16[2,4,32,768]{3,2,1,0:T(8,128)(2,1)} %qkv_both.1.refs_0_), channel_id=1, source_target_pairs={{64,0},{96,32},{0,64},{32,96},{65,1},{97,33},{1,65},{33,97},{66,2}... | collective-permute-start | bytes 1179656 | tf_op jit(solution)/shard_map/ppermute | solution.py:34
  476.3 41.7 %collective-permute-start.36 = (bf16[2,4,32,768]{3,2,1,0:T(8,128)(2,1)}, bf16[2,4,32,768]{3,2,1,0:T(8,128)(2,1)}, u32[]{:S(2)}, u32[]{:S(2)}) collective-permute-start(bf16[2,4,32,768]{3,2,1,0:T(8,128)(2,1)} %qkv_both.1.refs_0_), channel_id=1, source_target_pairs={{32,0},{64,32},{96,64},{0,96},{33,1},{65,33},{97,65},{1,97},{34,2}... | collective-permute-start | bytes 1179656 | tf_op jit(solution)/shard_map/ppermute | solution.py:34
  478.7 47.2 %collective-permute-start.42 = (bf16[2,4,32,768]{3,2,1,0:T(8,128)(2,1)S(1)}, bf16[2,4,32,768]{3,2,1,0:T(8,128)(2,1)}, u32[]{:S(2)}, u32[]{:S(2)}) collective-permute-start(bf16[2,4,32,768]{3,2,1,0:T(8,128)(2,1)S(1)} %collective-permute-done.38.refs_3_), channel_id=1, source_target_pairs={{0,8},{8,0},{1,9},{9,1},{2,10},{10,2},{3,11},{11,3},{4,12},{12,4},... | collective-permute-start | bytes 1179656 | tf_op jit(solution)/shard_map/ppermute | solution.py:54
  501.4 50.1 %all-to-all-start.7 = ((bf16[16,16,1600]{2,1,0:T(8,128)(2,1)}), bf16[16,16,1600]{2,1,0:T(8,128)(2,1)S(1)}, u32[]{:S(2)}, u32[]{:S(2)}) async-start(bf16[16,16,1600]{2,1,0:T(8,128)(2,1)} %broadcast_in_dim.26), calls=%async_computation.9 | async-start | bytes 1703936 | tf_op jit(solution)/shard_map/all_to_all | solution.py:58
  519.4 28.9 %collective-permute-start.44 = (bf16[2,4,32,800]{3,2,1,0:T(8,128)(2,1)S(1)}, bf16[2,4,32,800]{3,2,1,0:T(8,128)(2,1)S(1)}, u32[]{:S(2)}, u32[]{:S(2)}) collective-permute-start(bf16[2,4,32,800]{3,2,1,0:T(8,128)(2,1)S(1)} %copy-done.4), channel_id=1, source_target_pairs={{64,0},{96,32},{0,64},{32,96},{65,1},{97,33},{1,65},{33,97},{66,2}... | collective-permute-start | bytes 1228808 | tf_op jit(solution)/shard_map/ppermute | solution.py:34
  (95 other events, 1945.5 us)
Sparse Core Ops, SparseCore 0:
  21.5 33.3 all-gather.12
  56.6 36.4 all-gather.14
  99.4 36.4 all-gather.18
  152.4 36.0 all-gather.16
  206.5 35.5 reduce-scatter.2
  268.5 32.0 all-gather.20
  317.1 45.0 reduce-scatter.4
  363.9 117.1 all-gather.22

commit v9 on v8

--- a/solution.py
+++ b/solution.py
@@ -27,6 +27,10 @@
 Z_RING = ("zl", "zh")
 Z_PLACES = (0, 2, 1, 3)
 ROLES = [(0, 0), (1, 2), (2, 1), (3, 3)]
+OWNERS = [
+    [(l * 4 + k * 2 + h, (h ^ i) * 4 + l * 2 + k) for l in range(2) for k in range(2) for h in range(2)]
+    for i in range(2)
+]
 
 
 def ring(value, axis, step):
@@ -293,32 +297,39 @@
         refs[-1][k] = ref[...]
 
 
-def column_total_kernel(spans, ringed, place_ref, *refs):
-    out_ref = refs[8]
-    shard = out_ref.shape[0]
-    _, starts = windows(shard, 8)
-    step = starts[1]
-    for j in range(4):
-        x = lax.rem(place_ref[X] + j, 4)
-        for flip in range(2):
-            window = (place_ref[ZL] if flip == 0 else 1 - place_ref[ZL]) * 4 + x
-            at = pl.multiple_of(window * step, 8)
-            for rank in range(8):
-                k = lax.rem(rank // 2 + 4 - place_ref[Y], 4) if ringed else rank // 2
-                block = jnp.where(
-                    place_ref[C] == rank % 2, refs[j][flip, k], refs[4 + j][flip, k]
-                ).astype(f32)
-                for source, target, wide in spans[rank]:
-                    out_ref[pl.ds(at, step), target : target + wide] = block[
-                        :step, source : source + wide
-                    ]
-
-                @pl.when(window == 7)
-                def _(block=block, rank=rank):
-                    for source, target, wide in spans[rank]:
-                        out_ref[7 * step + step :, target : target + wide] = block[
-                            step:, source : source + wide
-                        ]
+def column_total_kernel(spans, ringed, place_ref, own_ref, other_ref, out_ref):
+    _, starts = windows(out_ref.shape[0], 8)
+    ends = starts[1:] + [out_ref.shape[0]]
+    for rank in range(8):
+        y = lax.rem(rank // 2 + 4 - place_ref[Y], 4) if ringed else rank // 2
+        mine = place_ref[C] == rank % 2
+        rows = [
+            jnp.where(mine, own_ref[i, y], other_ref[i, y]).astype(f32)[: end - start]
+            for i, (start, end) in enumerate(zip(starts, ends))
+        ]
+        block = jnp.concatenate(rows, axis=0)
+        for source, target, wide in spans[rank]:
+            out_ref[:, target : target + wide] = block[:, source : source + wide]
+
+
+def proj_total_kernel(place_ref, own_ref, other_ref, out_ref):
+    tiles = out_ref.shape[0] // 8
+    small = tiles // 16 * 8
+    for part, ref in enumerate((own_ref, other_ref)):
+        zl = place_ref[C] if part == 0 else 1 - place_ref[C]
+        for x in range(4):
+            for i in range(2):
+                zh = place_ref[ZL] if i == 0 else 1 - place_ref[ZL]
+                window = (zl * 4 + x) * 2 + zh
+                start = lax.div(tiles * window, 16)
+                wide = lax.div(tiles * (window + 1), 16) - start > small // 8
+                at = pl.multiple_of(start * 8, 8)
+                block = ref[x, i].astype(f32)
+                out_ref[pl.ds(at, small), :] = block[:small]
+
+                @pl.when(wide)
+                def _(at=at, block=block):
+                    out_ref[pl.ds(pl.multiple_of(at + small, 8), 8), :] = block[small:]
 
 
 def row_total_kernel(place_ref, own_ref, other_ref, out_ref):
@@ -573,7 +584,7 @@
     qkv_cols = qkv_cols.reshape(width, slots)
     fc_other = [flipped(part, "zh") for part in fc_own]
     attended = exchange(
-        after(attended_slots, proj_came, *fc_own).reshape(8, span, SLOT_WIDTH), TEAM
+        after(attended_slots, *fc_own).reshape(8, span, SLOT_WIDTH), TEAM
     )
     middle, second, attended_parts = call(
         branch_kernel,
@@ -583,7 +594,7 @@
             struct((span, width), bf16),
             struct((8, span, shard), bf16),
         ),
-        attended,
+        after(attended, proj_came),
         own_tokens,
         vectors,
         out_all,
@@ -664,14 +675,14 @@
             struct((8, span, SLOT_WIDTH), bf16),
             struct((4, width), f32),
         ),
-        after(place, *fc_grad, proj_grad[1], proj_grad[3], down_parts),
+        after(place, fc_grad[0], *proj_near, down_parts),
         grad_second,
         middle,
         own_cot,
         vectors,
         out_all,
         scratch=[pltpu.VMEM((span, width), bf16)],
-        flops=2 * span * width * width,
+        light=True,
     )
     grad_heads = exchange(grad_slots, TEAM).reshape(length, SLOT_WIDTH)
 
@@ -683,6 +694,7 @@
             [struct(parts[0].shape[1:], bf16)] * 4,
             place,
             *parts,
+            light=True,
         )
 
     fc_grad = ring_all(fold(Z, fc_grad, "fc_fold", grad_slots), Z_RING)
@@ -703,7 +715,7 @@
         qkv_cols,
         down_parts.reshape(8, span, width),
         scratch=[pltpu.VMEM((length, HEAD_DIM), f32)],
-        flops=2 * length * width * slots,
+        flops=20 * length * width * slots,
     )
     last = team_sum(last_parts.reshape(2 * length, width)).reshape(2, span, width)
     fc_grad = ring_all(fold(Y, fc_grad, "fc_fold_last", grad_mixed), "y")
@@ -735,19 +747,18 @@
         )
 
     proj_sum = sum(part.astype(f32) for part in [after(proj_grad[0], place)] + proj_grad[1:])
-    proj_whole = gather(proj_sum.astype(bf16), REPLICAS)
+    proj_sum = proj_sum.astype(bf16)
+    proj_both = [lax.ppermute(proj_sum, ("zl", "c", "zh"), owners) for owners in OWNERS]
+    proj_whole = gather(stacked(proj_both, "proj_both"), "x")
     fc_near = stacked([after(fc_grad[0], place)] + fc_grad[1:], "fc_near")
-    fc_both = stacked([fc_near, flipped(fc_near, "zl")], "fc_both")
     qkv_sum, out_sum = call(
         last_sum_kernel,
         "last_sum",
         (struct((4, window, slots), bf16), struct((windows(shard, 16)[0], width), bf16)),
-        after(last_grads, fc_both),
-    )
-    qkv_sum = exchange(qkv_sum, "y")
-    qkv_both = stacked([qkv_sum, flipped(qkv_sum, "zl")], "qkv_both")
-    qkv_pieces = ring_all([qkv_both] * 4, "x")
-    fc_pieces = ring_all([after(fc_both, *qkv_pieces)] * 4, "x")
+        last_grads,
+    )
+    qkv_sum = exchange(after(qkv_sum, last), "y")
+    qkv_whole = gather(qkv_sum, ("zl", "x"))
     results, first_sums = call(
         input_back_kernel,
         "input_back",
@@ -775,7 +786,7 @@
     )
     small_terms = small_terms.reshape(8, 8, shard).transpose(1, 0, 2).reshape(8, 2, hidden)
     small_terms = jnp.concatenate([small_terms, hidden_term[:, None]], axis=1)
-    small_sum = jnp.sum(exchange(after(small_terms, qkv_both), GRP), axis=0)
+    small_sum = jnp.sum(exchange(after(small_terms, qkv_sum), GRP), axis=0)
     out_whole = exchange(
         after(jnp.broadcast_to(out_sum, (16,) + out_sum.shape), small_sum), REPLICAS
     )
@@ -783,7 +794,6 @@
     small_last = jnp.sum(exchange(small_last, REP), axis=0)
     owned = small_last[:2].reshape(8, shard)
 
-    qkv_pieces = qkv_pieces + [other_core(part) for part in qkv_pieces]
     qkv_spans = [
         [
             (p * SLOT_WIDTH, p * width + STRIDE * r, STRIDE if r < 7 else SLOT_WIDTH)
@@ -791,24 +801,34 @@
         ]
         for r in range(8)
     ]
+    proj_whole = after(proj_whole, qkv_sum)
+    proj_total = call(
+        proj_total_kernel,
+        "proj_total",
+        struct((hidden, width), f32),
+        after(place, small_sum),
+        proj_whole,
+        other_core(proj_whole),
+    )
     qkv_total = call(
         functools.partial(column_total_kernel, qkv_spans, False),
         "qkv_total",
         struct((shard, 3 * width), f32),
-        after(place, results, small_sum),
-        *qkv_pieces,
-    )
-    fc_pieces = fc_pieces + [other_core(after(part, qkv_total)) for part in fc_pieces]
+        after(place, results, small_last),
+        qkv_whole,
+        other_core(qkv_whole),
+    )
+    out_total = row_total(out_whole, shard, "out_total")
+    fc_whole = gather(after(fc_near, qkv_whole, small_last), ("zl", "x"))
     fc_spans = [[(0, rank * hidden, hidden)] for rank in range(8)]
     fc_total = call(
         functools.partial(column_total_kernel, fc_spans, True),
         "fc_total",
         struct((shard, 8 * hidden), f32),
-        after(place, out_whole, small_last),
-        *fc_pieces,
-    )
-    out_total = row_total(out_whole, shard, "out_total", fc_total)
-    proj_total = row_total(proj_whole, hidden, "proj_total", fc_total)
+        after(place, qkv_total, out_total, proj_total),
+        fc_whole,
+        other_core(fc_whole),
+    )
     return (
         results_home[1].reshape(1, span, width),
         results_home[0].astype(f32).reshape(1, span, width),

time: 616 us -> 586 us (0.951)
  starting transfers between devices: 161 us -> 107 us
  blocking collectives: 59.7 us -> 111 us
  waiting for transfers between devices: 182 us -> 161 us
  Pallas kernels: 151 us -> 139 us
    ppermute x10 -> x8, waiting for transfers between devices: 95.7 us -> 25.5 us  [flipped(): return lax.ppermute(value, axis, [(0, 1), (1, 0)])]
    all_to_all x5, blocking collectives: 59.7 us -> 111 us  [exchange(): return lax.all_to_all(parts, axes, 0, 0)]
    all_gather x6 -> x8, waiting for transfers between devices: 0.01 us -> 41.4 us  [gather(): return lax.all_gather(block, axes, axis=0)]
    ppermute x27 -> x21, starting transfers between devices: 65.7 us -> 25 us  [ring(): lax.ppermute(value, axis, [(index[(i + step) % 4], index[i]) for i in ran...]
    all_to_all x4, waiting for transfers between devices: 0.01 us -> 12.2 us  [exchange(): return lax.all_to_all(parts, axes, 0, 0)]
    pallas_call x24 -> x23, Pallas kernels: 151 us -> 139 us  [call(): pl.pallas_call(kernel, out_shape=out_shape, in_specs=specs, out_specs=out...]
    ppermute x4, waiting for transfers between devices: 31.2 us -> 20.4 us  [swap_roles(): return lax.ppermute(value, ('c', 'zh'), ROLES)]
    ppermute x10 -> x4, starting transfers between devices: 16 us -> 6.95 us  [other_core(): return lax.ppermute(value, 'c', [(0, 1), (1, 0)])]
  transfers between devices with their start and end apart: 64 -> 54, of which waited for: 24 -> 24; matrix products, arithmetic and copies ran while one was open for 5% -> 6% of each run, Pallas kernels for 21% -> 20%
where the time goes in v9:
time: 586 us; the launch traced here: 576 us
  waiting for transfers between devices  161 us (27%)
  Pallas kernels  139 us (24%)
  blocking collectives  111 us (19%)
  starting transfers between devices  107 us (18%)
  local copies, waits for them, and re-layouts  31.4 us (5%)
  between operations  14.9 us (3%)
  matrix products  6.89 us (1%)
    pallas_call x23, Pallas kernels, call(): pl.pallas_call(kernel, out_shape=out_shape, in_specs=specs, out_specs=out...  139 us
    all_to_all x5, blocking collectives, exchange(): return lax.all_to_all(parts, axes, 0, 0)  111 us
    ppermute x21, waiting for transfers between devices, ring(): lax.ppermute(value, axis, [(index[(i + step) % 4], index[i]) for i in ran...  58.3 us
    all_gather x8, waiting for transfers between devices, gather(): return lax.all_gather(block, axes, axis=0)  41.4 us
    all_to_all x4, starting transfers between devices, exchange(): return lax.all_to_all(parts, axes, 0, 0)  27.8 us
    ppermute x8, waiting for transfers between devices, flipped(): return lax.ppermute(value, axis, [(0, 1), (1, 0)])  25.5 us
    ppermute x21, starting transfers between devices, ring(): lax.ppermute(value, axis, [(index[(i + step) % 4], index[i]) for i in ran...  25 us
    ppermute x4, starting transfers between devices, swap_roles(): return lax.ppermute(value, ('c', 'zh'), ROLES)  23.5 us
  transfers between devices with their start and end apart: 54, of which 24 were waited for; matrix products, arithmetic and copies ran while one was open for 6% of the time, Pallas kernels for 20%

profile of v9, /device:TPU:17, one launch (start us, length us, event | category | flops | bytes accessed | tf_op | source)
XLA Modules:
  0.0 576.4 jit_solution(11503698197785284566)
XLA Ops:
  26.6 8.6 %collective-permute-done.12 = bf16[200,1600]{1,0:T(8,128)(2,1)S(1)} collective-permute-done((bf16[200,1600]{1,0:T(8,128)(2,1)}, bf16[200,1600]{1,0:T(8,128)(2,1)S(1)}, u32[]{:S(2)}, u32[]{:S(2)}) %collective-permute-start.12) | collective-permute-done | bytes 640032 | tf_op jit(solution)/shard_map/ppermute | solution.py:50
  43.7 12.5 %all_to_all.45 = bf16[8,3,800]{2,1,0:T(4,128)(2,1)S(1)} all-to-all(bf16[8,3,800]{2,1,0:T(4,128)(2,1)S(1)} %broadcast_in_dim.21), channel_id=1, replica_groups=mesh['x'=4,'zl'=2,'c'=2,'y'=4,'zh'=2] {'y','zh'}, dimensions={0} | all-to-all | bytes 76800 | tf_op jit(solution)/shard_map/all_to_all | solution.py:62
  64.4 6.5 %collective-permute-done.5.refs_5_ = bf16[200,768]{1,0:T(8,128)(2,1)S(1)} collective-permute-done((bf16[200,768]{1,0:T(8,128)(2,1)S(1)}, bf16[200,768]{1,0:T(8,128)(2,1)S(1)}, u32[]{:S(2)}, u32[]{:S(2)}) %collective-permute-start.5) | collective-permute-done | bytes 307232 | tf_op jit(solution)/shard_map/ppermute | solution.py:46
  70.9 6.6 %collective-permute-done.6.refs_6_ = bf16[200,768]{1,0:T(8,128)(2,1)S(1)} collective-permute-done((bf16[200,768]{1,0:T(8,128)(2,1)S(1)}, bf16[200,768]{1,0:T(8,128)(2,1)S(1)}, u32[]{:S(2)}, u32[]{:S(2)}) %collective-permute-start.6) | collective-permute-done | bytes 307232 | tf_op jit(solution)/shard_map/ppermute | solution.py:46
  86.1 7.3 %collective-permute-start.13 = (bf16[128,1600]{1,0:T(8,128)(2,1)}, bf16[128,1600]{1,0:T(8,128)(2,1)S(1)}, u32[]{:S(2)}, u32[]{:S(2)}) collective-permute-start(bf16[128,1600]{1,0:T(8,128)(2,1)} %bitcast.53), channel_id=1, source_target_pairs={{0,0},{1,8},{8,1},{9,9},{2,2},{3,10},{10,3},{11,11},{4,4},{5,12},{... | collective-permute-start | bytes 1228808 | tf_op jit(solution)/shard_map/ppermute | solution.py:50
  115.1 15.6 %attend.1 = (bf16[1024,1600]{1,0:T(8,128)(2,1)}, bf16[1024,768]{1,0:T(8,128)(2,1)}, bf16[1024,256]{1,0:T(8,128)(2,1)}, f32[1024,4]{1,0:T(8,128)}, bf16[8,200,768]{2,1,0:T(8,128)(2,1)}) custom-call(s32[8]{0:T(128)} %stack.39.place_ref, bf16[1024,1600]{1,0:T(8,128)(2,1)} %all-gather.17.cloned.1.call-done.tokens_ref, f32[8,1600]{1,0:T(8,128)} %reshape.109.norm_ref, ...), custom_call_target="tpu_custom_call" | custom-call | flops 2516582400 | bytes 13636640 | tf_op jit(solution)/shard_map/attend/pallas_call | solution.py:122
  140.9 6.7 %all-to-all-done.1.slots_ref = bf16[8,128,256]{2,1,0:T(8,128)(2,1)} async-done(((bf16[8,128,256]{2,1,0:T(8,128)(2,1)}), bf16[8,128,256]{2,1,0:T(8,128)(2,1)}, u32[]{:S(2)}, u32[]{:S(2)}) %all-to-all-start.1) | async-done | bytes 524320 | tf_op jit(solution)/shard_map/all_to_all | solution.py:62
  163.9 7.9 %all-to-all-start.2 = ((bf16[8,128,200]{1,2,0:T(8,128)(2,1)}), bf16[8,128,200]{1,2,0:T(8,128)(2,1)S(1)}, u32[]{:S(2)}, u32[]{:S(2)}) async-start(bf16[8,128,200]{1,2,0:T(8,128)(2,1)} %copy.64), calls=%async_computation.2 | async-start | bytes 819200 | tf_op jit(solution)/shard_map/all_to_all | solution.py:62
  171.7 6.9 %fusion.2 = f32[1024,800]{0,1:T(8,128)} fusion(bf16[1024,1600]{1,0:T(8,128)(2,1)} %all-gather.23.cloned.1.call-done.right_ref, bf16[800,1600]{1,0:T(8,128)(2,1)S(1)} %broadcast_select_fusion.rows_ref), kind=kOutput, calls=%fused_computation.14 | convolution fusion | flops 2621440000 | bytes 9113600 | tf_op jit(solution)/shard_map/dot_general | solution.py:111
  191.2 14.8 %hidden.1 = (bf16[1024,800]{1,0:T(8,128)(2,1)}, bf16[1024,800]{1,0:T(8,128)(2,1)}, f32[1,800]{1,0:T(1,128)}, bf16[1024,1600]{1,0:T(8,128)(2,1)}) custom-call(s32[8]{0:T(128)} %stack.39.place_ref, bf16[1024,1600]{1,0:T(8,128)(2,1)} %all-gather.21.cloned.1.call-done.second_ref.left_ref, bf16[1600,800]{1,0:T(8,128)(2,1)} %bitcast.42, ...), custom_call_target="tpu_custom_call" | custom-call | flops 5242880000 | bytes 15673632 | tf_op jit(solution)/shard_map/hidden/pallas_call | solution.py:122
  206.2 9.1 %fc_grad.1 = (bf16[4,4,32,800]{3,2,1,0:T(8,128)(2,1)}, bf16[4,4,32,800]{3,2,1,0:T(8,128)(2,1)}, bf16[4,4,32,800]{3,2,1,0:T(8,128)(2,1)}, bf16[4,4,32,800]{3,2,1,0:T(8,128)(2,1)}) custom-call(s32[8]{0:T(128)} %stack.39.place_ref, bf16[1024,1600]{1,0:T(8,128)(2,1)} %all-gather.21.cloned.1.call-done.second_ref.left_ref, ...), custom_call_target="tpu_custom_call" | custom-call | flops 2621440000 | bytes 8192032 | tf_op jit(solution)/shard_map/fc_grad/pallas_call | solution.py:122
  215.3 7.4 %proj_grad.1 = (bf16[4,56,1600]{2,1,0:T(8,128)(2,1)}, bf16[4,56,1600]{2,1,0:T(8,128)(2,1)}, bf16[4,56,1600]{2,1,0:T(8,128)(2,1)}, bf16[4,56,1600]{2,1,0:T(8,128)(2,1)}) custom-call(s32[8]{0:T(128)} %stack.39.place_ref, bf16[1024,800]{1,0:T(8,128)(2,1)} %get-tuple-element.149.left_ref.active_ref, bf16[1024,1600]{1,0:T(8,128)(2,1)} %all-gather.23.cloned.1.call-done.right_ref), custom_call_target="tpu_custom_call" | custom-call | flops 2621440000 | bytes 7782432 | tf_op jit(solution)/shard_map/proj_grad/pallas_call | solution.py:122
  224.5 8.0 %down.1 = bf16[1024,1600]{1,0:T(8,128)(2,1)} custom-call(bf16[1024,800]{1,0:T(8,128)(2,1)} %get-tuple-element.149.left_ref.active_ref, bf16[800,1600]{1,0:T(8,128)(2,1)} %copy-done), custom_call_target="tpu_custom_call" | custom-call | flops 1 | bytes 1 | tf_op jit(solution)/shard_map/down/pallas_call | solution.py:122
  232.5 7.3 %collective-permute-done.18.refs_1_ = bf16[4,56,1600]{2,1,0:T(8,128)(2,1)} collective-permute-done((bf16[4,56,1600]{2,1,0:T(8,128)(2,1)}, bf16[4,56,1600]{2,1,0:T(8,128)(2,1)}, u32[]{:S(2)}, u32[]{:S(2)}) %collective-permute-start.18) | collective-permute-done | bytes 716832 | tf_op jit(solution)/shard_map/ppermute | solution.py:38
  254.2 9.6 %all-to-all-start.3 = ((bf16[8,128,256]{2,1,0:T(8,128)(2,1)}), bf16[8,128,256]{2,1,0:T(8,128)(2,1)}, u32[]{:S(2)}, u32[]{:S(2)}) async-start(bf16[8,128,256]{2,1,0:T(8,128)(2,1)} %get-tuple-element.153), calls=%async_computation.4 | async-start | bytes 1048576 | tf_op jit(solution)/shard_map/all_to_all | solution.py:62
  271.6 23.1 %collective-permute-done.23.refs_3_ = bf16[4,4,32,800]{3,2,1,0:T(8,128)(2,1)S(1)} collective-permute-done((bf16[4,4,32,800]{3,2,1,0:T(8,128)(2,1)}, bf16[4,4,32,800]{3,2,1,0:T(8,128)(2,1)S(1)}, u32[]{:S(2)}, u32[]{:S(2)}) %collective-permute-start.23) | collective-permute-done | bytes 819232 | tf_op jit(solution)/shard_map/ppermute | solution.py:38
  314.7 17.6 %attend_back.1 = (bf16[1024,768]{1,0:T(8,128)(2,1)}, bf16[8,2,128,1600]{3,2,1,0:T(8,128)(2,1)}, f32[1,768]{1,0:T(1,128)}) custom-call(s32[8]{0:T(128)} %stack.39.place_ref, bf16[1024,768]{1,0:T(8,128)(2,1)} %get-tuple-element.163.qkv_ref, bf16[1024,256]{1,0:T(8,128)(2,1)} %bitcast.14.grad_ref, bf16[1024,256]{1,0:T(8,128)(2,1)} %get-tuple-element.129.out_ref, ...), custom_call_target="tpu_custom_call" | custom-call | flops 25165824000 | bytes 16501792 | tf_op jit(solution)/shard_map/attend_back/pallas_call | solution.py:122
  345.6 9.3 %last_grads.1 = bf16[16,80,1600]{2,1,0:T(8,128)(2,1)} custom-call(s32[8]{0:T(128)} %stack.39.place_ref, bf16[1024,1600]{1,0:T(8,128)(2,1)} %get-tuple-element.174.first_ref, bf16[1024,768]{1,0:T(8,128)(2,1)} %get-tuple-element.169.mixed_ref, bf16[1024,200]{1,0:T(8,128)(2,1)} %bitcast.43, bf16[1024,1600]{1,0:T(8,128)(2,1)} %all-gather.25.cloned.1.call-done.branch_ref), custom_call_target="tpu_custom_call" | custom-call | flops 3171942400 | bytes 12632096 | tf_op jit(solution)/shard_map/last_grads/pallas_call | solution.py:122
  356.8 55.5 %all_to_all.46.parts_ref = bf16[16,80,1600]{2,1,0:T(8,128)(2,1)} all-to-all(bf16[16,80,1600]{2,1,0:T(8,128)(2,1)} %last_grads.1), channel_id=1, replica_groups=mesh['x'=4,'zl'=2,'c'=2,'y'=4,'zh'=2] {'zl','x','zh'}, dimensions={0} | all-to-all | bytes 8192000 | tf_op jit(solution)/shard_map/all_to_all | solution.py:62
  415.7 8.5 %all_to_all.47 = bf16[4,32,768]{2,1,0:T(8,128)(2,1)} all-to-all(bf16[4,32,768]{2,1,0:T(8,128)(2,1)} %get-tuple-element.184), channel_id=1, replica_groups=mesh['x'=4,'zl'=2,'c'=2,'y'=4,'zh'=2] {'y'}, dimensions={0} | all-to-all | bytes 393216 | tf_op jit(solution)/shard_map/all_to_all | solution.py:62
  429.6 11.6 %all_to_all.49 = f32[8,3,800]{2,1,0:T(4,128)S(1)} all-to-all(f32[8,3,800]{2,1,0:T(4,128)S(1)} %pad_maximum_fusion), channel_id=1, replica_groups=mesh['x'=4,'zl'=2,'c'=2,'y'=4,'zh'=2] {'y','zh'}, dimensions={0} | all-to-all | bytes 153600 | tf_op jit(solution)/shard_map/all_to_all | solution.py:62
  441.4 23.0 %all_to_all.48.own_ref = bf16[16,16,1600]{2,1,0:T(8,128)(2,1)S(1)} all-to-all(bf16[16,16,1600]{2,1,0:T(8,128)(2,1)S(1)} %broadcast_in_dim.26), channel_id=1, replica_groups=mesh['x'=4,'zl'=2,'c'=2,'y'=4,'zh'=2] {'zl','x','zh'}, dimensions={0} | all-to-all | bytes 1638400 | tf_op jit(solution)/shard_map/all_to_all | solution.py:62
  495.9 15.1 %all-gather.31.cloned.1.call-done = bf16[32,32,800]{2,1,0:T(8,128)(2,1)} async-done(((bf16[4,32,800]{2,1,0:T(8,128)(2,1)}), bf16[32,32,800]{2,1,0:T(8,128)(2,1)}) %all-gather.31.cloned.1.call-update) | async-done | bytes 1638416 | tf_op jit(solution)/shard_map/all_gather | solution.py:66
  517.3 26.2 %all-gather.29.cloned.1.call-done = bf16[8,56,1600]{2,1,0:T(8,128)(2,1)} async-done(((bf16[2,56,1600]{2,1,0:T(8,128)(2,1)}), bf16[8,56,1600]{2,1,0:T(8,128)(2,1)}) %all-gather.29.cloned.1.call-update) | async-done | bytes 1433616 | tf_op jit(solution)/shard_map/all_gather | solution.py:66
  (255 shorter events, 236.6 us)
Async XLA Ops:
  7.3 107.8 %all-gather.17.cloned.1.call-start = ((), (), s32[]{:S(2)}) async-start(), calls=%async_computation.13 | async-start | bytes 3833856 | tf_op jit(solution)/shard_map/all_gather | solution.py:66
  21.4 126.2 %all-gather.19.cloned.1.call-start = ((), (), s32[]{:S(2)}) async-start(), calls=%async_computation.14 | async-start | bytes 5990400 | tf_op jit(solution)/shard_map/all_gather | solution.py:66
  36.0 127.8 %all-gather.23.cloned.1.call-start = ((), (), s32[]{:S(2)}) async-start(), calls=%async_computation.16 | async-start | bytes 3833856 | tf_op jit(solution)/shard_map/all_gather | solution.py:66
  100.3 40.6 %collective-permute-start.11 = (bf16[800,1600]{1,0:T(8,128)(2,1)S(1)}, bf16[800,1600]{1,0:T(8,128)(2,1)}, u32[]{:S(2)}, u32[]{:S(2)}) collective-permute-start(bf16[800,1600]{1,0:T(8,128)(2,1)S(1)} %copy-done.3), channel_id=1, source_target_pairs={{1,8},{8,1},{3,10},{10,3},{5,12},{12,5},{7,14},{14,7},{17,24},{24,... | collective-permute-start | bytes 7680008 | tf_op jit(solution)/shard_map/ppermute | solution.py:562
  111.6 23.2 %collective-permute-start.9 = (bf16[200,800]{1,0:T(8,128)(2,1)}, bf16[200,800]{1,0:T(8,128)(2,1)}, u32[]{:S(2)}, u32[]{:S(2)}) collective-permute-start(bf16[200,800]{1,0:T(8,128)(2,1)} %get-tuple-element.126), channel_id=1, source_target_pairs={{4,0},{6,2},{0,4},{2,6},{5,1},{7,3},{1,5},{3,7},{12,8},{14,10},{8,... | collective-permute-start | bytes 960008 | tf_op jit(solution)/shard_map/ppermute | solution.py:38
  112.8 23.1 %collective-permute-start.8 = (bf16[200,800]{1,0:T(8,128)(2,1)}, bf16[200,800]{1,0:T(8,128)(2,1)}, u32[]{:S(2)}, u32[]{:S(2)}) collective-permute-start(bf16[200,800]{1,0:T(8,128)(2,1)} %get-tuple-element.124), channel_id=1, source_target_pairs={{2,0},{4,2},{6,4},{0,6},{3,1},{5,3},{7,5},{1,7},{10,8},{12,10},{14... | collective-permute-start | bytes 960008 | tf_op jit(solution)/shard_map/ppermute | solution.py:38
  140.5 50.7 %all-gather.21.cloned.1.call-start = ((), (), s32[]{:S(2)}) async-start(), calls=%async_computation.15 | async-start | bytes 3833856 | tf_op jit(solution)/shard_map/all_gather | solution.py:66
  153.4 30.1 %collective-permute-start.14 = (bf16[200,800]{1,0:T(8,128)(2,1)S(1)}, bf16[200,800]{1,0:T(8,128)(2,1)}, u32[]{:S(2)}, u32[]{:S(2)}) collective-permute-start(bf16[200,800]{1,0:T(8,128)(2,1)S(1)} %copy-done.12), channel_id=1, source_target_pairs={{0,1},{1,0},{2,3},{3,2},{4,5},{5,4},{6,7},{7,6},{8,9},{9,8},{10,11... | collective-permute-start | bytes 960008 | tf_op jit(solution)/shard_map/ppermute | solution.py:46
  156.4 27.1 %collective-permute-start.17 = (bf16[200,800]{1,0:T(8,128)(2,1)}, bf16[200,800]{1,0:T(8,128)(2,1)}, u32[]{:S(2)}, u32[]{:S(2)}) collective-permute-start(bf16[200,800]{1,0:T(8,128)(2,1)} %collective-permute-done.10.refs_3_), channel_id=1, source_target_pairs={{0,1},{1,0},{2,3},{3,2},{4,5},{5,4},{6,7},{7,6},{8,9},{9,8},{10,11... | collective-permute-start | bytes 960008 | tf_op jit(solution)/shard_map/ppermute | solution.py:46
  156.4 27.1 %collective-permute-start.16 = (bf16[200,800]{1,0:T(8,128)(2,1)}, bf16[200,800]{1,0:T(8,128)(2,1)}, u32[]{:S(2)}, u32[]{:S(2)}) collective-permute-start(bf16[200,800]{1,0:T(8,128)(2,1)} %collective-permute-done.9.refs_2_), channel_id=1, source_target_pairs={{0,1},{1,0},{2,3},{3,2},{4,5},{5,4},{6,7},{7,6},{8,9},{9,8},{10,11... | collective-permute-start | bytes 960008 | tf_op jit(solution)/shard_map/ppermute | solution.py:46
  159.4 28.3 %collective-permute-start.15 = (bf16[200,800]{1,0:T(8,128)(2,1)}, bf16[200,800]{1,0:T(8,128)(2,1)}, u32[]{:S(2)}, u32[]{:S(2)}) collective-permute-start(bf16[200,800]{1,0:T(8,128)(2,1)} %collective-permute-done.8.refs_1_), channel_id=1, source_target_pairs={{0,1},{1,0},{2,3},{3,2},{4,5},{5,4},{6,7},{7,6},{8,9},{9,8},{10,11... | collective-permute-start | bytes 960008 | tf_op jit(solution)/shard_map/ppermute | solution.py:46
  163.9 27.3 %all-to-all-start.2 = ((bf16[8,128,200]{1,2,0:T(8,128)(2,1)}), bf16[8,128,200]{1,2,0:T(8,128)(2,1)S(1)}, u32[]{:S(2)}, u32[]{:S(2)}) async-start(bf16[8,128,200]{1,2,0:T(8,128)(2,1)} %copy.64), calls=%async_computation.2 | async-start | bytes 819200 | tf_op jit(solution)/shard_map/all_to_all | solution.py:62
  171.7 70.4 %reduce-scatter.3.cloned.1.call-start = ((), (), s32[]{:S(2)}) async-start(), calls=%async_computation.11 | async-start | bytes 3833856 | tf_op jit(solution)/shard_map/reduce_scatter | solution.py:70
  206.0 139.6 %all-gather.25.cloned.1.call-start = ((), (), s32[]{:S(2)}) async-start(), calls=%async_computation.17 | async-start | bytes 3833856 | tf_op jit(solution)/shard_map/all_gather | solution.py:66
  251.6 43.1 %collective-permute-start.23 = (bf16[4,4,32,800]{3,2,1,0:T(8,128)(2,1)}, bf16[4,4,32,800]{3,2,1,0:T(8,128)(2,1)S(1)}, u32[]{:S(2)}, u32[]{:S(2)}) collective-permute-start(bf16[4,4,32,800]{3,2,1,0:T(8,128)(2,1)} %get-tuple-element.157), channel_id=1, source_target_pairs={{96,0},{0,32},{32,64},{64,96},{97,1},{1,33},{33,65},{65,97},{98,2}... | collective-permute-start | bytes 2457608 | tf_op jit(solution)/shard_map/ppermute | solution.py:38
  252.2 51.7 %collective-permute-start.20 = (bf16[4,56,1600]{2,1,0:T(8,128)(2,1)}, bf16[4,56,1600]{2,1,0:T(8,128)(2,1)}, u32[]{:S(2)}, u32[]{:S(2)}) collective-permute-start(bf16[4,56,1600]{2,1,0:T(8,128)(2,1)} %get-tuple-element.147), channel_id=1, source_target_pairs={{1,0},{17,16},{0,1},{16,17},{3,2},{19,18},{2,3},{18,19},{5,4},{21,... | collective-permute-start | bytes 2150408 | tf_op jit(solution)/shard_map/ppermute | solution.py:38
  254.2 60.5 %all-to-all-start.3 = ((bf16[8,128,256]{2,1,0:T(8,128)(2,1)}), bf16[8,128,256]{2,1,0:T(8,128)(2,1)}, u32[]{:S(2)}, u32[]{:S(2)}) async-start(bf16[8,128,256]{2,1,0:T(8,128)(2,1)} %get-tuple-element.153), calls=%async_computation.4 | async-start | bytes 1048576 | tf_op jit(solution)/shard_map/all_to_all | solution.py:62
  263.8 151.9 %reduce-scatter.5.cloned.1.call-start = ((), (), s32[]{:S(2)}) async-start(), calls=%async_computation.12 | async-start | bytes 7667712 | tf_op jit(solution)/shard_map/reduce_scatter | solution.py:70
  332.3 145.7 %all-gather.27.cloned.1.call-start = ((), (), s32[]{:S(2)}) async-start(), calls=%async_computation.18 | async-start | bytes 1769472 | tf_op jit(solution)/shard_map/all_gather | solution.py:66
  470.9 40.1 %all-gather.31.cloned.1.call-start = ((), (), s32[]{:S(2)}) async-start(), calls=%async_computation.20 | async-start | bytes 2064384 | tf_op jit(solution)/shard_map/all_gather | solution.py:66
  478.1 65.4 %all-gather.29.cloned.1.call-start = ((), (), s32[]{:S(2)}) async-start(), calls=%async_computation.19 | async-start | bytes 1863680 | tf_op jit(solution)/shard_map/all_gather | solution.py:66
  490.9 53.3 %collective-permute-start.33 = (bf16[2,128,1600]{1,2,0:T(8,128)(2,1)}, bf16[2,128,1600]{1,2,0:T(8,128)(2,1)}, u32[]{:S(2)}, u32[]{:S(2)}) collective-permute-start(bf16[2,128,1600]{1,2,0:T(8,128)(2,1)} %copy.69), channel_id=1, source_target_pairs={{0,0},{1,8},{8,1},{9,9},{2,2},{3,10},{10,3},{11,11},{4,4},{5,12},{... | collective-permute-start | bytes 2457608 | tf_op jit(solution)/shard_map/ppermute | solution.py:50
  511.0 52.1 %collective-permute-start.39 = (bf16[8,4,32,800]{3,2,1,0:T(8,128)(2,1)}, bf16[8,4,32,800]{3,2,1,0:T(8,128)(2,1)S(1)}, u32[]{:S(2)}, u32[]{:S(2)}) collective-permute-start(bf16[8,4,32,800]{3,2,1,0:T(8,128)(2,1)} %bitcast.44), channel_id=1, source_target_pairs={{0,8},{8,0},{1,9},{9,1},{2,10},{10,2},{3,11},{11,3},{4,12},{12,4},... | collective-permute-start | bytes 4915208 | tf_op jit(solution)/shard_map/ppermute | solution.py:58
  517.3 41.6 %collective-permute-start.34 = (bf16[8,4,32,768]{3,2,1,0:T(8,128)(2,1)}, bf16[8,4,32,768]{3,2,1,0:T(8,128)(2,1)}, u32[]{:S(2)}, u32[]{:S(2)}) collective-permute-start(bf16[8,4,32,768]{3,2,1,0:T(8,128)(2,1)} %bitcast.46), channel_id=1, source_target_pairs={{0,8},{8,0},{1,9},{9,1},{2,10},{10,2},{3,11},{11,3},{4,12},{12,4},... | collective-permute-start | bytes 4718600 | tf_op jit(solution)/shard_map/ppermute | solution.py:58
  (72 other events, 1465.0 us)
Sparse Core Ops, SparseCore 0:
  21.5 33.0 all-gather.16
  56.9 36.3 all-gather.18
  100.4 36.5 all-gather.22
  152.9 34.4 all-gather.20
  206.1 35.1 reduce-scatter.2
  248.7 35.4 all-gather.24
  332.5 44.5 reduce-scatter.4
  424.4 39.8 all-gather.26
  478.2 32.7 all-gather.30
  513.1 30.3 all-gather.28

commit v10 on v9

--- a/solution.py
+++ b/solution.py
@@ -517,8 +517,6 @@
 
     stays = c == zh
     own_tokens = swap_roles(tokens.reshape(span, width))
-    all_tokens = gather(own_tokens, TEAM).reshape(length, width)
-    out_rows = swap_roles(w_out)
     qkv_parts = call(
         qkv_columns_kernel,
         "qkv_columns",
@@ -527,14 +525,16 @@
         w_qkv,
         scratch=[pltpu.VMEM((4, shard, slots), bf16)],
     )
+    all_tokens = gather(after(own_tokens, qkv_parts[0]), TEAM).reshape(length, width)
     qkv_own = ring_all(qkv_parts, "y")
+    qkv_other = [flipped(part, "zh") for part in qkv_own]
+    out_rows = swap_roles(after(w_out, *qkv_own))
     small = jnp.concatenate(
         [ln1_gain, ln1_bias, bias_q, bias_v, bias_out, ln2_gain, ln2_bias, bias_proj, bias_fc]
     ).reshape(3, hidden)
     small_all = exchange(
-        after(jnp.broadcast_to(small, (8, 3, hidden)), qkv_parts[0]), GRP
-    )
-    qkv_other = [flipped(after(part, small_all), "zh") for part in qkv_own]
+        after(jnp.broadcast_to(small, (8, 3, hidden)), qkv_other[0]), GRP
+    )
     place = after(place, small_all)
     fc_parts = call(
         fc_columns_kernel,
@@ -675,7 +675,7 @@
             struct((8, span, SLOT_WIDTH), bf16),
             struct((4, width), f32),
         ),
-        after(place, fc_grad[0], *proj_near, down_parts),
+        after(place, *fc_grad, *proj_near, down_parts),
         grad_second,
         middle,
         own_cot,
@@ -707,7 +707,7 @@
             struct((8, 2, span, width), bf16),
             struct((1, slots), f32),
         ),
-        after(place, proj_far, *fc_grad),
+        place,
         qkv,
         grad_heads,
         attended_slots,
@@ -718,14 +718,12 @@
         flops=20 * length * width * slots,
     )
     last = team_sum(last_parts.reshape(2 * length, width)).reshape(2, span, width)
-    fc_grad = ring_all(fold(Y, fc_grad, "fc_fold_last", grad_mixed), "y")
-    proj_grad = ring_all(fold(X, proj_grad, "proj_fold", grad_mixed), "x")
     last_grads = call(
         last_grads_kernel,
         "last_grads",
         struct((16, 2 * window + windows(shard, 16)[0], width), bf16),
         place,
-        after(first, fc_grad[0], proj_grad[0]),
+        first,
         grad_mixed,
         attended_own.reshape(length, shard),
         branch_all,
@@ -733,7 +731,7 @@
         flops=2 * length * width * (slots + shard),
     )
     place = after(place, last_grads)
-    last_grads = exchange(after(last_grads, *fc_grad, *proj_grad), REPLICAS)
+    last_grads = exchange(last_grads, REPLICAS)
 
     def stacked(parts, name):
         return call(
@@ -746,19 +744,20 @@
             row_total_kernel, name, struct((rows, width), f32), place, whole, other_core(whole)
         )
 
-    proj_sum = sum(part.astype(f32) for part in [after(proj_grad[0], place)] + proj_grad[1:])
-    proj_sum = proj_sum.astype(bf16)
-    proj_both = [lax.ppermute(proj_sum, ("zl", "c", "zh"), owners) for owners in OWNERS]
-    proj_whole = gather(stacked(proj_both, "proj_both"), "x")
-    fc_near = stacked([after(fc_grad[0], place)] + fc_grad[1:], "fc_near")
     qkv_sum, out_sum = call(
         last_sum_kernel,
         "last_sum",
         (struct((4, window, slots), bf16), struct((windows(shard, 16)[0], width), bf16)),
-        last_grads,
+        after(last_grads, proj_far, *fc_grad),
     )
     qkv_sum = exchange(after(qkv_sum, last), "y")
     qkv_whole = gather(qkv_sum, ("zl", "x"))
+    fc_grad = ring_all(fold(Y, fc_grad, "fc_fold_last", qkv_sum), "y")
+    proj_grad = ring_all(fold(X, proj_grad, "proj_fold", qkv_sum), "x")
+    proj_sum = sum(part.astype(f32) for part in proj_grad).astype(bf16)
+    proj_both = [lax.ppermute(proj_sum, ("zl", "c", "zh"), owners) for owners in OWNERS]
+    proj_whole = gather(stacked(proj_both, "proj_both"), "x")
+    fc_near = stacked(fc_grad, "fc_near")
     results, first_sums = call(
         input_back_kernel,
         "input_back",
@@ -801,7 +800,10 @@
         ]
         for r in range(8)
     ]
-    proj_whole = after(proj_whole, qkv_sum)
+    fc_whole = gather(after(fc_near, qkv_whole), ("zl", "x"))
+    qkv_whole, fc_whole, proj_whole, out_whole = [
+        after(whole, small_last) for whole in (qkv_whole, fc_whole, proj_whole, out_whole)
+    ]
     proj_total = call(
         proj_total_kernel,
         "proj_total",
@@ -819,7 +821,6 @@
         other_core(qkv_whole),
     )
     out_total = row_total(out_whole, shard, "out_total")
-    fc_whole = gather(after(fc_near, qkv_whole, small_last), ("zl", "x"))
     fc_spans = [[(0, rank * hidden, hidden)] for rank in range(8)]
     fc_total = call(
         functools.partial(column_total_kernel, fc_spans, True),

time: 586 us -> 619 us (1.056)
  waiting for transfers between devices: 161 us -> 245 us
  blocking collectives: 111 us -> 39.4 us
  starting transfers between devices: 107 us -> 122 us
    all_to_all x5 -> x3, blocking collectives: 111 us -> 39.4 us  [exchange(): return lax.all_to_all(parts, axes, 0, 0)]
    ppermute x21, waiting for transfers between devices: 58.3 us -> 116 us  [ring(): lax.ppermute(value, axis, [(index[(i + step) % 4], index[i]) for i in ran...]
    all_to_all x4 -> x6, waiting for transfers between devices: 12.2 us -> 39.9 us  [exchange(): return lax.all_to_all(parts, axes, 0, 0)]
    all_to_all x4 -> x6, starting transfers between devices: 27.8 us -> 48.7 us  [exchange(): return lax.all_to_all(parts, axes, 0, 0)]
    all_gather x8, waiting for transfers between devices: 41.4 us -> 28.4 us  [gather(): return lax.all_gather(block, axes, axis=0)]
  transfers between devices with their start and end apart: 54 -> 56, of which waited for: 24 -> 31; matrix products, arithmetic and copies ran while one was open for 6% -> 6% of each run, Pallas kernels for 20% -> 19%
where the time goes in v10:
time: 619 us; the launch traced here: 608 us
  waiting for transfers between devices  245 us (40%)
  Pallas kernels  140 us (23%)
  starting transfers between devices  122 us (20%)
  blocking collectives  39.4 us (6%)
  local copies, waits for them, and re-layouts  33.4 us (5%)
  between operations  15 us (2%)
  matrix products  6.89 us (1%)
  other arithmetic  6.28 us (1%)
    pallas_call x23, Pallas kernels, call(): pl.pallas_call(kernel, out_shape=out_shape, in_specs=specs, out_specs=out...  140 us
    ppermute x21, waiting for transfers between devices, ring(): lax.ppermute(value, axis, [(index[(i + step) % 4], index[i]) for i in ran...  116 us
    all_to_all x6, starting transfers between devices, exchange(): return lax.all_to_all(parts, axes, 0, 0)  48.7 us
    all_to_all x6, waiting for transfers between devices, exchange(): return lax.all_to_all(parts, axes, 0, 0)  39.9 us
    all_to_all x3, blocking collectives, exchange(): return lax.all_to_all(parts, axes, 0, 0)  39.4 us
    all_gather x8, waiting for transfers between devices, gather(): return lax.all_gather(block, axes, axis=0)  28.4 us
    ppermute x8, waiting for transfers between devices, flipped(): return lax.ppermute(value, axis, [(0, 1), (1, 0)])  27.4 us
    ppermute x21, starting transfers between devices, ring(): lax.ppermute(value, axis, [(index[(i + step) % 4], index[i]) for i in ran...  25.6 us
  transfers between devices with their start and end apart: 56, of which 31 were waited for; matrix products, arithmetic and copies ran while one was open for 6% of the time, Pallas kernels for 19%

profile of v10, /device:TPU:17, one launch (start us, length us, event | category | flops | bytes accessed | tf_op | source)
XLA Modules:
  0.0 608.1 jit_solution(5976354164217995115)
XLA Ops:
  39.7 8.6 %collective-permute-done.12 = bf16[200,1600]{1,0:T(8,128)(2,1)S(1)} collective-permute-done((bf16[200,1600]{1,0:T(8,128)(2,1)}, bf16[200,1600]{1,0:T(8,128)(2,1)S(1)}, u32[]{:S(2)}, u32[]{:S(2)}) %collective-permute-start.12) | collective-permute-done | bytes 640032 | tf_op jit(solution)/shard_map/ppermute | solution.py:50
  83.6 8.2 %collective-permute-done.13.cot_ref = bf16[128,1600]{1,0:T(8,128)(2,1)S(1)} collective-permute-done((bf16[128,1600]{1,0:T(8,128)(2,1)S(1)}, bf16[128,1600]{1,0:T(8,128)(2,1)S(1)}, u32[]{:S(2)}, u32[]{:S(2)}) %collective-permute-start.13) | collective-permute-done | bytes 409632 | tf_op jit(solution)/shard_map/ppermute | solution.py:50
  102.1 22.8 %all-to-all-done = bf16[8,3,800]{2,1,0:T(4,128)(2,1)S(1)} async-done(((bf16[8,3,800]{2,1,0:T(4,128)(2,1)}), bf16[8,3,800]{2,1,0:T(4,128)(2,1)S(1)}, u32[]{:S(2)}, u32[]{:S(2)}) %all-to-all-start) | async-done | bytes 38432 | tf_op jit(solution)/shard_map/all_to_all | solution.py:62
  135.3 15.5 %attend.1 = (bf16[1024,1600]{1,0:T(8,128)(2,1)}, bf16[1024,768]{1,0:T(8,128)(2,1)}, bf16[1024,256]{1,0:T(8,128)(2,1)}, f32[1024,4]{1,0:T(8,128)}, bf16[8,200,768]{2,1,0:T(8,128)(2,1)}) custom-call(s32[8]{0:T(128)} %stack.39.place_ref, bf16[1024,1600]{1,0:T(8,128)(2,1)} %all-gather.17.cloned.1.call-done.tokens_ref, f32[8,1600]{1,0:T(8,128)} %reshape.109.norm_ref, ...), custom_call_target="tpu_custom_call" | custom-call | flops 2516582400 | bytes 13636640 | tf_op jit(solution)/shard_map/attend/pallas_call | solution.py:122
  150.9 9.2 %all-to-all-start.1 = ((bf16[8,128,256]{2,1,0:T(8,128)(2,1)}), bf16[8,128,256]{2,1,0:T(8,128)(2,1)}, u32[]{:S(2)}, u32[]{:S(2)}) async-start(bf16[8,128,256]{2,1,0:T(8,128)(2,1)} %bitcast.51), calls=%async_computation.1 | async-start | bytes 1048576 | tf_op jit(solution)/shard_map/all_to_all | solution.py:62
  183.2 8.1 %all-to-all-start.2 = ((bf16[8,128,200]{1,2,0:T(8,128)(2,1)}), bf16[8,128,200]{1,2,0:T(8,128)(2,1)S(1)}, u32[]{:S(2)}, u32[]{:S(2)}) async-start(bf16[8,128,200]{1,2,0:T(8,128)(2,1)} %copy.64), calls=%async_computation.2 | async-start | bytes 819200 | tf_op jit(solution)/shard_map/all_to_all | solution.py:62
  191.3 6.9 %fusion.2 = f32[1024,800]{0,1:T(8,128)} fusion(bf16[1024,1600]{1,0:T(8,128)(2,1)} %all-gather.23.cloned.1.call-done.right_ref, bf16[800,1600]{1,0:T(8,128)(2,1)S(1)} %broadcast_select_fusion.rows_ref), kind=kOutput, calls=%fused_computation.14 | convolution fusion | flops 2621440000 | bytes 9113600 | tf_op jit(solution)/shard_map/dot_general | solution.py:111
  210.3 14.8 %hidden.1 = (bf16[1024,800]{1,0:T(8,128)(2,1)}, bf16[1024,800]{1,0:T(8,128)(2,1)}, f32[1,800]{1,0:T(1,128)}, bf16[1024,1600]{1,0:T(8,128)(2,1)}) custom-call(s32[8]{0:T(128)} %stack.39.place_ref, bf16[1024,1600]{1,0:T(8,128)(2,1)} %all-gather.21.cloned.1.call-done.second_ref.left_ref, bf16[1600,800]{1,0:T(8,128)(2,1)} %bitcast.42, ...), custom_call_target="tpu_custom_call" | custom-call | flops 5242880000 | bytes 15673632 | tf_op jit(solution)/shard_map/hidden/pallas_call | solution.py:122
  225.3 9.1 %fc_grad.1 = (bf16[4,4,32,800]{3,2,1,0:T(8,128)(2,1)}, bf16[4,4,32,800]{3,2,1,0:T(8,128)(2,1)}, bf16[4,4,32,800]{3,2,1,0:T(8,128)(2,1)}, bf16[4,4,32,800]{3,2,1,0:T(8,128)(2,1)}) custom-call(s32[8]{0:T(128)} %stack.39.place_ref, bf16[1024,1600]{1,0:T(8,128)(2,1)} %all-gather.21.cloned.1.call-done.second_ref.left_ref, ...), custom_call_target="tpu_custom_call" | custom-call | flops 2621440000 | bytes 8192032 | tf_op jit(solution)/shard_map/fc_grad/pallas_call | solution.py:122
  238.0 7.5 %proj_grad.1 = (bf16[4,56,1600]{2,1,0:T(8,128)(2,1)}, bf16[4,56,1600]{2,1,0:T(8,128)(2,1)}, bf16[4,56,1600]{2,1,0:T(8,128)(2,1)}, bf16[4,56,1600]{2,1,0:T(8,128)(2,1)}) custom-call(s32[8]{0:T(128)} %stack.39.place_ref, bf16[1024,800]{1,0:T(8,128)(2,1)} %get-tuple-element.146.left_ref.active_ref, bf16[1024,1600]{1,0:T(8,128)(2,1)} %all-gather.23.cloned.1.call-done.right_ref), custom_call_target="tpu_custom_call" | custom-call | flops 2621440000 | bytes 7782432 | tf_op jit(solution)/shard_map/proj_grad/pallas_call | solution.py:122
  247.4 8.0 %down.1 = bf16[1024,1600]{1,0:T(8,128)(2,1)} custom-call(bf16[1024,800]{1,0:T(8,128)(2,1)} %get-tuple-element.146.left_ref.active_ref, bf16[800,1600]{1,0:T(8,128)(2,1)} %copy-done), custom_call_target="tpu_custom_call" | custom-call | flops 1 | bytes 1 | tf_op jit(solution)/shard_map/down/pallas_call | solution.py:122
  255.4 6.9 %collective-permute-done.21.refs_1_ = bf16[4,56,1600]{2,1,0:T(8,128)(2,1)S(1)} collective-permute-done((bf16[4,56,1600]{2,1,0:T(8,128)(2,1)}, bf16[4,56,1600]{2,1,0:T(8,128)(2,1)S(1)}, u32[]{:S(2)}, u32[]{:S(2)}) %collective-permute-start.21) | collective-permute-done | bytes 716832 | tf_op jit(solution)/shard_map/ppermute | solution.py:38
  264.6 16.0 %collective-permute-done.20.refs_3_ = bf16[4,4,32,800]{3,2,1,0:T(8,128)(2,1)S(1)} collective-permute-done((bf16[4,4,32,800]{3,2,1,0:T(8,128)(2,1)}, bf16[4,4,32,800]{3,2,1,0:T(8,128)(2,1)S(1)}, u32[]{:S(2)}, u32[]{:S(2)}) %collective-permute-start.20) | collective-permute-done | bytes 819232 | tf_op jit(solution)/shard_map/ppermute | solution.py:38
  295.7 7.9 %all-to-all-done.3 = bf16[8,128,256]{2,1,0:T(8,128)(2,1)S(1)} async-done(((bf16[8,128,256]{2,1,0:T(8,128)(2,1)}), bf16[8,128,256]{2,1,0:T(8,128)(2,1)S(1)}, u32[]{:S(2)}, u32[]{:S(2)}) %all-to-all-start.3) | async-done | bytes 524320 | tf_op jit(solution)/shard_map/all_to_all | solution.py:62
  304.4 17.7 %attend_back.1 = (bf16[1024,768]{1,0:T(8,128)(2,1)}, bf16[8,2,128,1600]{3,2,1,0:T(8,128)(2,1)}, f32[1,768]{1,0:T(1,128)}) custom-call(s32[8]{0:T(128)} %stack.39.place_ref, bf16[1024,768]{1,0:T(8,128)(2,1)} %get-tuple-element.114.qkv_ref, bf16[1024,256]{1,0:T(8,128)(2,1)} %bitcast.52, bf16[1024,256]{1,0:T(8,128)(2,1)} %get-tuple-element.124.out_ref, ...), custom_call_target="tpu_custom_call" | custom-call | flops 25165824000 | bytes 16501792 | tf_op jit(solution)/shard_map/attend_back/pallas_call | solution.py:122
  323.2 9.4 %last_grads.1 = bf16[16,80,1600]{2,1,0:T(8,128)(2,1)} custom-call(s32[8]{0:T(128)} %stack.39.place_ref, bf16[1024,1600]{1,0:T(8,128)(2,1)} %get-tuple-element.155.first_ref, bf16[1024,768]{1,0:T(8,128)(2,1)} %get-tuple-element.156.mixed_ref, bf16[1024,200]{1,0:T(8,128)(2,1)} %bitcast.43, bf16[1024,1600]{1,0:T(8,128)(2,1)} %all-gather.25.cloned.1.call-done.branch_ref), custom_call_target="tpu_custom_call" | custom-call | flops 3171942400 | bytes 12632096 | tf_op jit(solution)/shard_map/last_grads/pallas_call | solution.py:122
  345.7 66.7 %collective-permute-done.23.refs_2_ = bf16[4,56,1600]{2,1,0:T(8,128)(2,1)S(1)} collective-permute-done((bf16[4,56,1600]{2,1,0:T(8,128)(2,1)S(1)}, bf16[4,56,1600]{2,1,0:T(8,128)(2,1)S(1)}, u32[]{:S(2)}, u32[]{:S(2)}) %collective-permute-start.23) | collective-permute-done | bytes 716832 | tf_op jit(solution)/shard_map/ppermute | solution.py:38
  422.5 13.2 %all_to_all.45 = bf16[4,32,768]{2,1,0:T(8,128)(2,1)} all-to-all(bf16[4,32,768]{2,1,0:T(8,128)(2,1)} %get-tuple-element.167), channel_id=1, replica_groups=mesh['x'=4,'zl'=2,'c'=2,'y'=4,'zh'=2] {'y'}, dimensions={0} | all-to-all | bytes 393216 | tf_op jit(solution)/shard_map/all_to_all | solution.py:62
  446.9 28.4 %all-gather.27.cloned.1.call-done = bf16[32,32,768]{2,1,0:T(8,128)(2,1)} async-done(((bf16[4,32,768]{2,1,0:T(8,128)(2,1)}), bf16[32,32,768]{2,1,0:T(8,128)(2,1)}) %all-gather.27.cloned.1.call-update) | async-done | bytes 1572880 | tf_op jit(solution)/shard_map/all_gather | solution.py:66
  489.4 8.5 %collective-permute-start.34 = (bf16[56,1600]{1,0:T(8,128)(2,1)S(1)}, bf16[56,1600]{1,0:T(8,128)(2,1)S(1)}, u32[]{:S(2)}, u32[]{:S(2)}) collective-permute-start(bf16[56,1600]{1,0:T(8,128)(2,1)S(1)} %add_convert_fusion), channel_id=1, source_target_pairs={{0,16},{1,0},{8,17},{9,1},{16,24},{17,8},{24,25},{25,9},{2,18},{3,... | collective-permute-start | bytes 537608 | tf_op jit(solution)/shard_map/ppermute | solution.py:758
  501.9 7.5 %collective-permute-done.33.refs_0_ = bf16[56,1600]{1,0:T(8,128)(2,1)S(1)} collective-permute-done((bf16[56,1600]{1,0:T(8,128)(2,1)S(1)}, bf16[56,1600]{1,0:T(8,128)(2,1)S(1)}, u32[]{:S(2)}, u32[]{:S(2)}) %collective-permute-start.33) | collective-permute-done | bytes 179232 | tf_op jit(solution)/shard_map/ppermute | solution.py:758
  517.2 11.0 %all_to_all.47 = f32[8,3,800]{2,1,0:T(4,128)S(1)} all-to-all(f32[8,3,800]{2,1,0:T(4,128)S(1)} %pad_maximum_fusion), channel_id=1, replica_groups=mesh['x'=4,'zl'=2,'c'=2,'y'=4,'zh'=2] {'y','zh'}, dimensions={0} | all-to-all | bytes 153600 | tf_op jit(solution)/shard_map/all_to_all | solution.py:62
  528.3 15.2 %all_to_all.46.own_ref = bf16[16,16,1600]{2,1,0:T(8,128)(2,1)S(1)} all-to-all(bf16[16,16,1600]{2,1,0:T(8,128)(2,1)S(1)} %broadcast_in_dim.26), channel_id=1, replica_groups=mesh['x'=4,'zl'=2,'c'=2,'y'=4,'zh'=2] {'zl','x','zh'}, dimensions={0} | all-to-all | bytes 1638400 | tf_op jit(solution)/shard_map/all_to_all | solution.py:62
  544.3 14.8 %all-to-all-start.8 = ((f32[16,3,800]{2,1,0:T(4,128)}), f32[16,3,800]{2,1,0:T(4,128)S(1)}, u32[]{:S(2)}, u32[]{:S(2)}) async-start(f32[16,3,800]{2,1,0:T(4,128)} %broadcast_in_dim.27), calls=%async_computation.10 | async-start | bytes 458752 | tf_op jit(solution)/shard_map/all_to_all | solution.py:62
  (263 shorter events, 251.2 us)
Async XLA Ops:
  7.3 128.0 %all-gather.17.cloned.1.call-start = ((), (), s32[]{:S(2)}) async-start(), calls=%async_computation.13 | async-start | bytes 3833856 | tf_op jit(solution)/shard_map/all_gather | solution.py:66
  21.4 145.7 %all-gather.19.cloned.1.call-start = ((), (), s32[]{:S(2)}) async-start(), calls=%async_computation.14 | async-start | bytes 5990400 | tf_op jit(solution)/shard_map/all_gather | solution.py:66
  49.1 134.1 %all-gather.23.cloned.1.call-start = ((), (), s32[]{:S(2)}) async-start(), calls=%async_computation.16 | async-start | bytes 3833856 | tf_op jit(solution)/shard_map/all_gather | solution.py:66
  52.3 27.3 %collective-permute-start.7 = (bf16[200,768]{1,0:T(8,128)(2,1)}, bf16[200,768]{1,0:T(8,128)(2,1)}, u32[]{:S(2)}, u32[]{:S(2)}) collective-permute-start(bf16[200,768]{1,0:T(8,128)(2,1)} %copy-done.41), channel_id=1, source_target_pairs={{0,1},{1,0},{2,3},{3,2},{4,5},{5,4},{6,7},{7,6},{8,9},{9,8},{10,11... | collective-permute-start | bytes 921608 | tf_op jit(solution)/shard_map/ppermute | solution.py:46
  92.6 67.8 %collective-permute-start.11 = (bf16[800,1600]{1,0:T(8,128)(2,1)S(1)}, bf16[800,1600]{1,0:T(8,128)(2,1)}, u32[]{:S(2)}, u32[]{:S(2)}) collective-permute-start(bf16[800,1600]{1,0:T(8,128)(2,1)S(1)} %copy-done.3), channel_id=1, source_target_pairs={{1,8},{8,1},{3,10},{10,3},{5,12},{12,5},{7,14},{14,7},{17,24},{24,... | collective-permute-start | bytes 7680008 | tf_op jit(solution)/shard_map/ppermute | solution.py:562
  96.2 28.7 %all-to-all-start = ((bf16[8,3,800]{2,1,0:T(4,128)(2,1)}), bf16[8,3,800]{2,1,0:T(4,128)(2,1)S(1)}, u32[]{:S(2)}, u32[]{:S(2)}) async-start(bf16[8,3,800]{2,1,0:T(4,128)(2,1)} %broadcast_in_dim.21), calls=%async_computation | async-start | bytes 114688 | tf_op jit(solution)/shard_map/all_to_all | solution.py:62
  160.0 50.3 %all-gather.21.cloned.1.call-start = ((), (), s32[]{:S(2)}) async-start(), calls=%async_computation.15 | async-start | bytes 3833856 | tf_op jit(solution)/shard_map/all_gather | solution.py:66
  172.8 30.2 %collective-permute-start.14 = (bf16[200,800]{1,0:T(8,128)(2,1)S(1)}, bf16[200,800]{1,0:T(8,128)(2,1)}, u32[]{:S(2)}, u32[]{:S(2)}) collective-permute-start(bf16[200,800]{1,0:T(8,128)(2,1)S(1)} %copy-done.16), channel_id=1, source_target_pairs={{0,1},{1,0},{2,3},{3,2},{4,5},{5,4},{6,7},{7,6},{8,9},{9,8},{10,11... | collective-permute-start | bytes 960008 | tf_op jit(solution)/shard_map/ppermute | solution.py:46
  173.5 29.5 %collective-permute-start.17 = (bf16[200,800]{1,0:T(8,128)(2,1)}, bf16[200,800]{1,0:T(8,128)(2,1)}, u32[]{:S(2)}, u32[]{:S(2)}) collective-permute-start(bf16[200,800]{1,0:T(8,128)(2,1)} %collective-permute-done.10.refs_3_), channel_id=1, source_target_pairs={{0,1},{1,0},{2,3},{3,2},{4,5},{5,4},{6,7},{7,6},{8,9},{9,8},{10,11... | collective-permute-start | bytes 960008 | tf_op jit(solution)/shard_map/ppermute | solution.py:46
  176.5 30.3 %collective-permute-start.15 = (bf16[200,800]{1,0:T(8,128)(2,1)}, bf16[200,800]{1,0:T(8,128)(2,1)}, u32[]{:S(2)}, u32[]{:S(2)}) collective-permute-start(bf16[200,800]{1,0:T(8,128)(2,1)} %collective-permute-done.8.refs_1_), channel_id=1, source_target_pairs={{0,1},{1,0},{2,3},{3,2},{4,5},{5,4},{6,7},{7,6},{8,9},{9,8},{10,11... | collective-permute-start | bytes 960008 | tf_op jit(solution)/shard_map/ppermute | solution.py:46
  191.3 89.3 %reduce-scatter.3.cloned.1.call-start = ((), (), s32[]{:S(2)}) async-start(), calls=%async_computation.11 | async-start | bytes 3833856 | tf_op jit(solution)/shard_map/reduce_scatter | solution.py:70
  225.1 98.1 %all-gather.25.cloned.1.call-start = ((), (), s32[]{:S(2)}) async-start(), calls=%async_computation.17 | async-start | bytes 3833856 | tf_op jit(solution)/shard_map/all_gather | solution.py:66
  234.4 29.3 %collective-permute-start.18 = (bf16[4,4,32,800]{3,2,1,0:T(8,128)(2,1)}, bf16[4,4,32,800]{3,2,1,0:T(8,128)(2,1)S(1)}, u32[]{:S(2)}, u32[]{:S(2)}) collective-permute-start(bf16[4,4,32,800]{3,2,1,0:T(8,128)(2,1)} %get-tuple-element.138), channel_id=1, source_target_pairs={{32,0},{64,32},{96,64},{0,96},{33,1},{65,33},{97,65},{1,97},{34,2}... | collective-permute-start | bytes 2457608 | tf_op jit(solution)/shard_map/ppermute | solution.py:38
  237.4 43.1 %collective-permute-start.20 = (bf16[4,4,32,800]{3,2,1,0:T(8,128)(2,1)}, bf16[4,4,32,800]{3,2,1,0:T(8,128)(2,1)S(1)}, u32[]{:S(2)}, u32[]{:S(2)}) collective-permute-start(bf16[4,4,32,800]{3,2,1,0:T(8,128)(2,1)} %get-tuple-element.140), channel_id=1, source_target_pairs={{96,0},{0,32},{32,64},{64,96},{97,1},{1,33},{33,65},{65,97},{98,2}... | collective-permute-start | bytes 2457608 | tf_op jit(solution)/shard_map/ppermute | solution.py:38
  293.4 129.1 %reduce-scatter.5.cloned.1.call-start = ((), (), s32[]{:S(2)}) async-start(), calls=%async_computation.12 | async-start | bytes 7667712 | tf_op jit(solution)/shard_map/reduce_scatter | solution.py:70
  332.6 86.5 %all-to-all-start.4 = ((bf16[16,80,1600]{2,1,0:T(8,128)(2,1)}), bf16[16,80,1600]{2,1,0:T(8,128)(2,1)}, u32[]{:S(2)}, u32[]{:S(2)}) async-start(bf16[16,80,1600]{2,1,0:T(8,128)(2,1)} %last_grads.1), calls=%async_computation.6 | async-start | bytes 8519680 | tf_op jit(solution)/shard_map/all_to_all | solution.py:62
  337.3 138.0 %all-gather.27.cloned.1.call-start = ((), (), s32[]{:S(2)}) async-start(), calls=%async_computation.18 | async-start | bytes 1769472 | tf_op jit(solution)/shard_map/all_gather | solution.py:66
  337.4 75.0 %collective-permute-start.23 = (bf16[4,56,1600]{2,1,0:T(8,128)(2,1)S(1)}, bf16[4,56,1600]{2,1,0:T(8,128)(2,1)S(1)}, u32[]{:S(2)}, u32[]{:S(2)}) collective-permute-start(bf16[4,56,1600]{2,1,0:T(8,128)(2,1)S(1)} %copy-done.38), channel_id=1, source_target_pairs={{1,0},{17,16},{0,1},{16,17},{3,2},{19,18},{2,3},{18,19},{5,4},{21,... | collective-permute-start | bytes 2150408 | tf_op jit(solution)/shard_map/ppermute | solution.py:38
  343.4 73.2 %collective-permute-start.24 = (bf16[4,32,800]{2,1,0:T(8,128)(2,1)}, bf16[4,32,800]{2,1,0:T(8,128)(2,1)S(1)}, u32[]{:S(2)}, u32[]{:S(2)}) collective-permute-start(bf16[4,32,800]{2,1,0:T(8,128)(2,1)} %get-tuple-element.162), channel_id=1, source_target_pairs={{16,0},{1,16},{17,1},{0,17},{18,2},{3,18},{19,3},{2,19},{20,4},{5,... | collective-permute-start | bytes 614408 | tf_op jit(solution)/shard_map/ppermute | solution.py:38
  345.1 72.2 %collective-permute-start.25 = (bf16[4,32,800]{2,1,0:T(8,128)(2,1)}, bf16[4,32,800]{2,1,0:T(8,128)(2,1)S(1)}, u32[]{:S(2)}, u32[]{:S(2)}) collective-permute-start(bf16[4,32,800]{2,1,0:T(8,128)(2,1)} %get-tuple-element.163), channel_id=1, source_target_pairs={{1,0},{17,16},{0,1},{16,17},{3,2},{19,18},{2,3},{18,19},{5,4},{21,... | collective-permute-start | bytes 614408 | tf_op jit(solution)/shard_map/ppermute | solution.py:38
  345.5 73.6 %collective-permute-start.26 = (bf16[4,32,800]{2,1,0:T(8,128)(2,1)}, bf16[4,32,800]{2,1,0:T(8,128)(2,1)S(1)}, u32[]{:S(2)}, u32[]{:S(2)}) collective-permute-start(bf16[4,32,800]{2,1,0:T(8,128)(2,1)} %get-tuple-element.164), channel_id=1, source_target_pairs={{17,0},{0,16},{16,1},{1,17},{19,2},{2,18},{18,3},{3,19},{21,4},{4,... | collective-permute-start | bytes 614408 | tf_op jit(solution)/shard_map/ppermute | solution.py:38
  435.8 130.6 %all-gather.31.cloned.1.call-start = ((), (), s32[]{:S(2)}) async-start(), calls=%async_computation.20 | async-start | bytes 2064384 | tf_op jit(solution)/shard_map/all_gather | solution.py:66
  475.3 93.6 %all-gather.29.cloned.1.call-start = ((), (), s32[]{:S(2)}) async-start(), calls=%async_computation.19 | async-start | bytes 1863680 | tf_op jit(solution)/shard_map/all_gather | solution.py:66
  566.4 28.3 %collective-permute-start.39 = (bf16[8,4,32,800]{3,2,1,0:T(8,128)(2,1)}, bf16[8,4,32,800]{3,2,1,0:T(8,128)(2,1)S(1)}, u32[]{:S(2)}, u32[]{:S(2)}) collective-permute-start(bf16[8,4,32,800]{3,2,1,0:T(8,128)(2,1)} %bitcast.44), channel_id=1, source_target_pairs={{0,8},{8,0},{1,9},{9,1},{2,10},{10,2},{3,11},{11,3},{4,12},{12,4},... | collective-permute-start | bytes 4915208 | tf_op jit(solution)/shard_map/ppermute | solution.py:58
  (77 other events, 1847.5 us)
Sparse Core Ops, SparseCore 0:
  21.5 29.1 all-gather.16
  53.0 36.8 all-gather.18
  92.7 28.4 all-gather.22
  172.3 33.2 all-gather.20
  225.2 34.0 reduce-scatter.2
  287.4 29.2 all-gather.24
  322.3 43.8 reduce-scatter.4
  435.9 39.3 all-gather.26
  477.5 41.4 all-gather.30
  521.0 35.2 all-gather.28

commit v11 on v10

--- a/solution.py
+++ b/solution.py
@@ -297,11 +297,39 @@
         refs[-1][k] = ref[...]
 
 
-def column_total_kernel(spans, ringed, place_ref, own_ref, other_ref, out_ref):
+def column_ring_total_kernel(spans, place_ref, *refs):
+    out_ref = refs[8]
+    shard = out_ref.shape[0]
+    _, starts = windows(shard, 8)
+    step = starts[1]
+    for j in range(4):
+        x = lax.rem(place_ref[X] + j, 4)
+        for flip in range(2):
+            window = (place_ref[ZL] if flip == 0 else 1 - place_ref[ZL]) * 4 + x
+            at = pl.multiple_of(window * step, 8)
+            for rank in range(8):
+                k = lax.rem(rank // 2 + 4 - place_ref[Y], 4)
+                block = jnp.where(
+                    place_ref[C] == rank % 2, refs[j][flip, k], refs[4 + j][flip, k]
+                ).astype(f32)
+                for source, target, wide in spans[rank]:
+                    out_ref[pl.ds(at, step), target : target + wide] = block[
+                        :step, source : source + wide
+                    ]
+
+                @pl.when(window == 7)
+                def _(block=block, rank=rank):
+                    for source, target, wide in spans[rank]:
+                        out_ref[7 * step + step :, target : target + wide] = block[
+                            step:, source : source + wide
+                        ]
+
+
+def column_total_kernel(spans, place_ref, own_ref, other_ref, out_ref):
     _, starts = windows(out_ref.shape[0], 8)
     ends = starts[1:] + [out_ref.shape[0]]
     for rank in range(8):
-        y = lax.rem(rank // 2 + 4 - place_ref[Y], 4) if ringed else rank // 2
+        y = rank // 2
         mine = place_ref[C] == rank % 2
         rows = [
             jnp.where(mine, own_ref[i, y], other_ref[i, y]).astype(f32)[: end - start]
@@ -533,7 +561,7 @@
         [ln1_gain, ln1_bias, bias_q, bias_v, bias_out, ln2_gain, ln2_bias, bias_proj, bias_fc]
     ).reshape(3, hidden)
     small_all = exchange(
-        after(jnp.broadcast_to(small, (8, 3, hidden)), qkv_other[0]), GRP
+        after(jnp.broadcast_to(small, (8, 3, hidden)), qkv_own[1]), GRP
     )
     place = after(place, small_all)
     fc_parts = call(
@@ -707,7 +735,7 @@
             struct((8, 2, span, width), bf16),
             struct((1, slots), f32),
         ),
-        place,
+        after(place, proj_far, *fc_grad),
         qkv,
         grad_heads,
         attended_slots,
@@ -732,6 +760,8 @@
     )
     place = after(place, last_grads)
     last_grads = exchange(last_grads, REPLICAS)
+    fc_grad = ring_all(fold(Y, fc_grad, "fc_fold_last", grad_mixed), "y")
+    proj_grad = ring_all(fold(X, proj_grad, "proj_fold", grad_mixed), "x")
 
     def stacked(parts, name):
         return call(
@@ -744,20 +774,23 @@
             row_total_kernel, name, struct((rows, width), f32), place, whole, other_core(whole)
         )
 
+    proj_sum = sum(part.astype(f32) for part in proj_grad)
+    proj_sum = proj_sum.astype(bf16)
     qkv_sum, out_sum = call(
         last_sum_kernel,
         "last_sum",
         (struct((4, window, slots), bf16), struct((windows(shard, 16)[0], width), bf16)),
-        after(last_grads, proj_far, *fc_grad),
+        after(last_grads, proj_sum, *fc_grad),
     )
     qkv_sum = exchange(after(qkv_sum, last), "y")
     qkv_whole = gather(qkv_sum, ("zl", "x"))
-    fc_grad = ring_all(fold(Y, fc_grad, "fc_fold_last", qkv_sum), "y")
-    proj_grad = ring_all(fold(X, proj_grad, "proj_fold", qkv_sum), "x")
-    proj_sum = sum(part.astype(f32) for part in proj_grad).astype(bf16)
+    proj_sum = after(proj_sum, qkv_sum)
     proj_both = [lax.ppermute(proj_sum, ("zl", "c", "zh"), owners) for owners in OWNERS]
-    proj_whole = gather(stacked(proj_both, "proj_both"), "x")
-    fc_near = stacked(fc_grad, "fc_near")
+    proj_pair = stacked(proj_both, "proj_both")
+    fc_near = stacked([after(fc_grad[0], qkv_sum)] + fc_grad[1:], "fc_near")
+    fc_both = stacked([fc_near, flipped(fc_near, "zl")], "fc_both")
+    fc_pieces = ring_all([fc_both] * 4, "x")
+    fc_pieces = fc_pieces + [other_core(part) for part in fc_pieces]
     results, first_sums = call(
         input_back_kernel,
         "input_back",
@@ -766,7 +799,7 @@
         own_tokens,
         middle,
         grad_middle,
-        after(vectors, qkv_sum),
+        after(vectors, qkv_sum, fc_both),
     )
     results_home = swap_roles(results)
 
@@ -787,7 +820,8 @@
     small_terms = jnp.concatenate([small_terms, hidden_term[:, None]], axis=1)
     small_sum = jnp.sum(exchange(after(small_terms, qkv_sum), GRP), axis=0)
     out_whole = exchange(
-        after(jnp.broadcast_to(out_sum, (16,) + out_sum.shape), small_sum), REPLICAS
+        after(jnp.broadcast_to(out_sum, (16,) + out_sum.shape), small_sum, *fc_pieces[:4]),
+        REPLICAS,
     )
     small_last = jnp.broadcast_to(after(small_sum, out_whole), (16, 3, hidden))
     small_last = jnp.sum(exchange(small_last, REP), axis=0)
@@ -800,10 +834,8 @@
         ]
         for r in range(8)
     ]
-    fc_whole = gather(after(fc_near, qkv_whole), ("zl", "x"))
-    qkv_whole, fc_whole, proj_whole, out_whole = [
-        after(whole, small_last) for whole in (qkv_whole, fc_whole, proj_whole, out_whole)
-    ]
+    qkv_whole = after(qkv_whole, small_sum, *fc_pieces[:4])
+    proj_whole = after(gather(after(proj_pair, qkv_whole), "x"), small_last)
     proj_total = call(
         proj_total_kernel,
         "proj_total",
@@ -813,7 +845,7 @@
         other_core(proj_whole),
     )
     qkv_total = call(
-        functools.partial(column_total_kernel, qkv_spans, False),
+        functools.partial(column_total_kernel, qkv_spans),
         "qkv_total",
         struct((shard, 3 * width), f32),
         after(place, results, small_last),
@@ -823,12 +855,11 @@
     out_total = row_total(out_whole, shard, "out_total")
     fc_spans = [[(0, rank * hidden, hidden)] for rank in range(8)]
     fc_total = call(
-        functools.partial(column_total_kernel, fc_spans, True),
+        functools.partial(column_ring_total_kernel, fc_spans),
         "fc_total",
         struct((shard, 8 * hidden), f32),
         after(place, qkv_total, out_total, proj_total),
-        fc_whole,
-        other_core(fc_whole),
+        *fc_pieces,
     )
     return (
         results_home[1].reshape(1, span, width),

time: 619 us -> 577 us (0.932)
  waiting for transfers between devices: 245 us -> 204 us
  blocking collectives: 39.4 us -> 27.8 us
  starting transfers between devices: 122 us -> 131 us
    all_gather x8 -> x7, waiting for transfers between devices: 28.4 us -> 10.8 us  [gather(): return lax.all_gather(block, axes, axis=0)]
    all_to_all x3 -> x2, blocking collectives: 39.4 us -> 27.8 us  [exchange(): return lax.all_to_all(parts, axes, 0, 0)]
    ppermute x2, waiting for transfers between devices: 8.57 us -> 0.01 us  [per_device(): lax.ppermute(proj_sum, ('zl', 'c', 'zh'), owners)]
    ppermute x21 -> x24, waiting for transfers between devices: 116 us -> 108 us  [ring(): lax.ppermute(value, axis, [(index[(i + step) % 4], index[i]) for i in ran...]
    ppermute x4 -> x7, starting transfers between devices: 3.02 us -> 10.2 us  [other_core(): return lax.ppermute(value, 'c', [(0, 1), (1, 0)])]
    all_to_all x6 -> x7, waiting for transfers between devices: 39.9 us -> 33.1 us  [exchange(): return lax.all_to_all(parts, axes, 0, 0)]
    ppermute x8 -> x9, waiting for transfers between devices: 27.4 us -> 34 us  [flipped(): return lax.ppermute(value, axis, [(0, 1), (1, 0)])]
    ppermute x4, waiting for transfers between devices: 24.6 us -> 18.2 us  [swap_roles(): return lax.ppermute(value, ('c', 'zh'), ROLES)]
  transfers between devices with their start and end apart: 56 -> 63, of which waited for: 31 -> 27; matrix products, arithmetic and copies ran while one was open for 6% -> 6% of each run, Pallas kernels for 19% -> 20%
where the time goes in v11:
time: 577 us; the launch traced here: 567 us
  waiting for transfers between devices  204 us (35%)
  Pallas kernels  145 us (25%)
  starting transfers between devices  131 us (23%)
  local copies, waits for them, and re-layouts  30.5 us (5%)
  blocking collectives  27.8 us (5%)
  between operations  14.8 us (3%)
  matrix products  6.89 us (1%)
  other arithmetic  6.85 us (1%)
    pallas_call x24, Pallas kernels, call(): pl.pallas_call(kernel, out_shape=out_shape, in_specs=specs, out_specs=out...  145 us
    ppermute x24, waiting for transfers between devices, ring(): lax.ppermute(value, axis, [(index[(i + step) % 4], index[i]) for i in ran...  108 us
    all_to_all x7, starting transfers between devices, exchange(): return lax.all_to_all(parts, axes, 0, 0)  44.4 us
    ppermute x9, waiting for transfers between devices, flipped(): return lax.ppermute(value, axis, [(0, 1), (1, 0)])  34 us
    all_to_all x7, waiting for transfers between devices, exchange(): return lax.all_to_all(parts, axes, 0, 0)  33.1 us
    ppermute x24, starting transfers between devices, ring(): lax.ppermute(value, axis, [(index[(i + step) % 4], index[i]) for i in ran...  30.6 us
    all_to_all x2, blocking collectives, exchange(): return lax.all_to_all(parts, axes, 0, 0)  27.8 us
    ppermute x4, starting transfers between devices, swap_roles(): return lax.ppermute(value, ('c', 'zh'), ROLES)  19.1 us
  transfers between devices with their start and end apart: 63, of which 27 were waited for; matrix products, arithmetic and copies ran while one was open for 6% of the time, Pallas kernels for 20%

profile of v11, /device:TPU:17, one launch (start us, length us, event | category | flops | bytes accessed | tf_op | source)
XLA Modules:
  0.0 567.4 jit_solution(16600817712080669670)
XLA Ops:
  39.7 8.6 %collective-permute-done.12 = bf16[200,1600]{1,0:T(8,128)(2,1)S(1)} collective-permute-done((bf16[200,1600]{1,0:T(8,128)(2,1)}, bf16[200,1600]{1,0:T(8,128)(2,1)S(1)}, u32[]{:S(2)}, u32[]{:S(2)}) %collective-permute-start.12) | collective-permute-done | bytes 640032 | tf_op jit(solution)/shard_map/ppermute | solution.py:50
  59.8 6.6 %collective-permute-done.5.refs_5_ = bf16[200,768]{1,0:T(8,128)(2,1)S(1)} collective-permute-done((bf16[200,768]{1,0:T(8,128)(2,1)}, bf16[200,768]{1,0:T(8,128)(2,1)S(1)}, u32[]{:S(2)}, u32[]{:S(2)}) %collective-permute-start.5) | collective-permute-done | bytes 307232 | tf_op jit(solution)/shard_map/ppermute | solution.py:46
  66.4 6.6 %collective-permute-done.6.refs_6_ = bf16[200,768]{1,0:T(8,128)(2,1)S(1)} collective-permute-done((bf16[200,768]{1,0:T(8,128)(2,1)}, bf16[200,768]{1,0:T(8,128)(2,1)S(1)}, u32[]{:S(2)}, u32[]{:S(2)}) %collective-permute-start.6) | collective-permute-done | bytes 307232 | tf_op jit(solution)/shard_map/ppermute | solution.py:46
  83.6 8.2 %collective-permute-done.13.cot_ref = bf16[128,1600]{1,0:T(8,128)(2,1)S(1)} collective-permute-done((bf16[128,1600]{1,0:T(8,128)(2,1)S(1)}, bf16[128,1600]{1,0:T(8,128)(2,1)S(1)}, u32[]{:S(2)}, u32[]{:S(2)}) %collective-permute-start.13) | collective-permute-done | bytes 409632 | tf_op jit(solution)/shard_map/ppermute | solution.py:50
  102.2 22.8 %all-to-all-done = bf16[8,3,800]{2,1,0:T(4,128)(2,1)S(1)} async-done(((bf16[8,3,800]{2,1,0:T(4,128)(2,1)}), bf16[8,3,800]{2,1,0:T(4,128)(2,1)S(1)}, u32[]{:S(2)}, u32[]{:S(2)}) %all-to-all-start) | async-done | bytes 38432 | tf_op jit(solution)/shard_map/all_to_all | solution.py:62
  135.4 15.5 %attend.1 = (bf16[1024,1600]{1,0:T(8,128)(2,1)}, bf16[1024,768]{1,0:T(8,128)(2,1)}, bf16[1024,256]{1,0:T(8,128)(2,1)}, f32[1024,4]{1,0:T(8,128)}, bf16[8,200,768]{2,1,0:T(8,128)(2,1)}) custom-call(s32[8]{0:T(128)} %stack.39.place_ref, bf16[1024,1600]{1,0:T(8,128)(2,1)} %all-gather.15.cloned.1.call-done.tokens_ref, f32[8,1600]{1,0:T(8,128)} %reshape.109.norm_ref, ...), custom_call_target="tpu_custom_call" | custom-call | flops 2516582400 | bytes 13636640 | tf_op jit(solution)/shard_map/attend/pallas_call | solution.py:122
  151.0 9.2 %all-to-all-start.1 = ((bf16[8,128,256]{2,1,0:T(8,128)(2,1)}), bf16[8,128,256]{2,1,0:T(8,128)(2,1)}, u32[]{:S(2)}, u32[]{:S(2)}) async-start(bf16[8,128,256]{2,1,0:T(8,128)(2,1)} %bitcast.48), calls=%async_computation.1 | async-start | bytes 1048576 | tf_op jit(solution)/shard_map/all_to_all | solution.py:62
  160.6 6.6 %all-to-all-done.1.slots_ref = bf16[8,128,256]{2,1,0:T(8,128)(2,1)} async-done(((bf16[8,128,256]{2,1,0:T(8,128)(2,1)}), bf16[8,128,256]{2,1,0:T(8,128)(2,1)}, u32[]{:S(2)}, u32[]{:S(2)}) %all-to-all-start.1) | async-done | bytes 524320 | tf_op jit(solution)/shard_map/all_to_all | solution.py:62
  182.1 8.1 %all-to-all-start.2 = ((bf16[8,128,200]{1,2,0:T(8,128)(2,1)}), bf16[8,128,200]{1,2,0:T(8,128)(2,1)S(1)}, u32[]{:S(2)}, u32[]{:S(2)}) async-start(bf16[8,128,200]{1,2,0:T(8,128)(2,1)} %copy.64), calls=%async_computation.2 | async-start | bytes 819200 | tf_op jit(solution)/shard_map/all_to_all | solution.py:62
  190.2 6.9 %fusion.2 = f32[1024,800]{0,1:T(8,128)} fusion(bf16[1024,1600]{1,0:T(8,128)(2,1)} %all-gather.21.cloned.1.call-done.right_ref, bf16[800,1600]{1,0:T(8,128)(2,1)S(1)} %broadcast_select_fusion.rows_ref), kind=kOutput, calls=%fused_computation.14 | convolution fusion | flops 2621440000 | bytes 9113600 | tf_op jit(solution)/shard_map/dot_general | solution.py:111
  210.5 14.8 %hidden.1 = (bf16[1024,800]{1,0:T(8,128)(2,1)}, bf16[1024,800]{1,0:T(8,128)(2,1)}, f32[1,800]{1,0:T(1,128)}, bf16[1024,1600]{1,0:T(8,128)(2,1)}) custom-call(s32[8]{0:T(128)} %stack.39.place_ref, bf16[1024,1600]{1,0:T(8,128)(2,1)} %all-gather.19.cloned.1.call-done.second_ref.left_ref, bf16[1600,800]{1,0:T(8,128)(2,1)} %bitcast.41, ...), custom_call_target="tpu_custom_call" | custom-call | flops 5242880000 | bytes 15673632 | tf_op jit(solution)/shard_map/hidden/pallas_call | solution.py:122
  225.5 9.1 %fc_grad.1 = (bf16[4,4,32,800]{3,2,1,0:T(8,128)(2,1)}, bf16[4,4,32,800]{3,2,1,0:T(8,128)(2,1)}, bf16[4,4,32,800]{3,2,1,0:T(8,128)(2,1)}, bf16[4,4,32,800]{3,2,1,0:T(8,128)(2,1)}) custom-call(s32[8]{0:T(128)} %stack.39.place_ref, bf16[1024,1600]{1,0:T(8,128)(2,1)} %all-gather.19.cloned.1.call-done.second_ref.left_ref, ...), custom_call_target="tpu_custom_call" | custom-call | flops 2621440000 | bytes 8192032 | tf_op jit(solution)/shard_map/fc_grad/pallas_call | solution.py:122
  238.2 7.5 %proj_grad.1 = (bf16[4,56,1600]{2,1,0:T(8,128)(2,1)}, bf16[4,56,1600]{2,1,0:T(8,128)(2,1)}, bf16[4,56,1600]{2,1,0:T(8,128)(2,1)}, bf16[4,56,1600]{2,1,0:T(8,128)(2,1)}) custom-call(s32[8]{0:T(128)} %stack.39.place_ref, bf16[1024,800]{1,0:T(8,128)(2,1)} %get-tuple-element.148.left_ref.active_ref, bf16[1024,1600]{1,0:T(8,128)(2,1)} %all-gather.21.cloned.1.call-done.right_ref), custom_call_target="tpu_custom_call" | custom-call | flops 2621440000 | bytes 7782432 | tf_op jit(solution)/shard_map/proj_grad/pallas_call | solution.py:122
  247.6 8.0 %down.1 = bf16[1024,1600]{1,0:T(8,128)(2,1)} custom-call(bf16[1024,800]{1,0:T(8,128)(2,1)} %get-tuple-element.148.left_ref.active_ref, bf16[800,1600]{1,0:T(8,128)(2,1)} %copy-done), custom_call_target="tpu_custom_call" | custom-call | flops 1 | bytes 1 | tf_op jit(solution)/shard_map/down/pallas_call | solution.py:122
  255.6 7.0 %collective-permute-done.18.refs_1_ = bf16[4,56,1600]{2,1,0:T(8,128)(2,1)S(1)} collective-permute-done((bf16[4,56,1600]{2,1,0:T(8,128)(2,1)}, bf16[4,56,1600]{2,1,0:T(8,128)(2,1)S(1)}, u32[]{:S(2)}, u32[]{:S(2)}) %collective-permute-start.18) | collective-permute-done | bytes 716832 | tf_op jit(solution)/shard_map/ppermute | solution.py:38
  264.9 15.9 %collective-permute-done.23.refs_3_ = bf16[4,4,32,800]{3,2,1,0:T(8,128)(2,1)} collective-permute-done((bf16[4,4,32,800]{3,2,1,0:T(8,128)(2,1)}, bf16[4,4,32,800]{3,2,1,0:T(8,128)(2,1)}, u32[]{:S(2)}, u32[]{:S(2)}) %collective-permute-start.23) | collective-permute-done | bytes 819232 | tf_op jit(solution)/shard_map/ppermute | solution.py:38
  318.3 17.6 %attend_back.1 = (bf16[1024,768]{1,0:T(8,128)(2,1)}, bf16[8,2,128,1600]{3,2,1,0:T(8,128)(2,1)}, f32[1,768]{1,0:T(1,128)}) custom-call(s32[8]{0:T(128)} %stack.39.place_ref, bf16[1024,768]{1,0:T(8,128)(2,1)} %get-tuple-element.159.qkv_ref, bf16[1024,256]{1,0:T(8,128)(2,1)} %bitcast.49, bf16[1024,256]{1,0:T(8,128)(2,1)} %get-tuple-element.124.out_ref, ...), custom_call_target="tpu_custom_call" | custom-call | flops 25165824000 | bytes 16501792 | tf_op jit(solution)/shard_map/attend_back/pallas_call | solution.py:122
  336.9 9.4 %last_grads.1 = bf16[16,80,1600]{2,1,0:T(8,128)(2,1)} custom-call(s32[8]{0:T(128)} %stack.39.place_ref, bf16[1024,1600]{1,0:T(8,128)(2,1)} %get-tuple-element.164.first_ref, bf16[1024,768]{1,0:T(8,128)(2,1)} %get-tuple-element.165.mixed_ref, bf16[1024,200]{1,0:T(8,128)(2,1)} %bitcast.42, bf16[1024,1600]{1,0:T(8,128)(2,1)} %all-gather.23.cloned.1.call-done.branch_ref), custom_call_target="tpu_custom_call" | custom-call | flops 3171942400 | bytes 12632096 | tf_op jit(solution)/shard_map/last_grads/pallas_call | solution.py:122
  362.7 56.1 %collective-permute-done.27 = bf16[56,1600]{1,0:T(8,128)(2,1)S(1)} collective-permute-done((bf16[56,1600]{1,0:T(8,128)(2,1)}, bf16[56,1600]{1,0:T(8,128)(2,1)S(1)}, u32[]{:S(2)}, u32[]{:S(2)}) %collective-permute-start.27) | collective-permute-done | bytes 179232 | tf_op jit(solution)/shard_map/ppermute | solution.py:38
  429.6 9.7 %all_to_all.45 = bf16[4,32,768]{2,1,0:T(8,128)(2,1)} all-to-all(bf16[4,32,768]{2,1,0:T(8,128)(2,1)} %get-tuple-element.180), channel_id=1, replica_groups=mesh['x'=4,'zl'=2,'c'=2,'y'=4,'zh'=2] {'y'}, dimensions={0} | all-to-all | bytes 393216 | tf_op jit(solution)/shard_map/all_to_all | solution.py:62
  453.5 8.0 %collective-permute-start.41 = (bf16[56,1600]{1,0:T(8,128)(2,1)S(1)}, bf16[56,1600]{1,0:T(8,128)(2,1)S(1)}, u32[]{:S(2)}, u32[]{:S(2)}) collective-permute-start(bf16[56,1600]{1,0:T(8,128)(2,1)S(1)} %add_convert_fusion), channel_id=1, source_target_pairs={{0,16},{1,0},{8,17},{9,1},{16,24},{17,8},{24,25},{25,9},{2,18},{3,... | collective-permute-start | bytes 537608 | tf_op jit(solution)/shard_map/ppermute | solution.py:788
  481.4 10.8 %all-gather.25.cloned.1.call-done = bf16[32,32,768]{2,1,0:T(8,128)(2,1)} async-done(((bf16[4,32,768]{2,1,0:T(8,128)(2,1)}), bf16[32,32,768]{2,1,0:T(8,128)(2,1)}) %all-gather.25.cloned.1.call-update) | async-done | bytes 1572880 | tf_op jit(solution)/shard_map/all_gather | solution.py:66
  515.1 18.1 %all_to_all.46 = f32[16,3,800]{2,1,0:T(4,128)S(1)} all-to-all(f32[16,3,800]{2,1,0:T(4,128)S(1)} %broadcast_in_dim.27), channel_id=1, replica_groups=mesh['x'=4,'zl'=2,'c'=2,'y'=4,'zh'=2] {'x','zl','c'}, dimensions={0} | all-to-all | bytes 307200 | tf_op jit(solution)/shard_map/all_to_all | solution.py:62
  551.7 8.9 %fc_total.1 = f32[200,6400]{1,0:T(8,128)} custom-call(s32[8]{0:T(128)} %stack.39.place_ref, bf16[2,4,32,800]{3,2,1,0:T(8,128)(2,1)} %fc_both.1.refs_0_, bf16[2,4,32,800]{3,2,1,0:T(8,128)(2,1)} %copy-done.18, bf16[2,4,32,800]{3,2,1,0:T(8,128)(2,1)} %copy-done.17, bf16[2,4,32,800]{3,2,1,0:T(8,128)(2,1)} %copy-done.16, bf16[2,4,32,800]{3,2,1,0:T(8,128)(2,1)} %copy-done.19, ...), custom_call_target="tpu_custom_call" | custom-call | bytes 8396832 | tf_op jit(solution)/shard_map/fc_total/pallas_call | solution.py:122
  (288 shorter events, 252.7 us)
Async XLA Ops:
  7.3 128.1 %all-gather.15.cloned.1.call-start = ((), (), s32[]{:S(2)}) async-start(), calls=%async_computation.13 | async-start | bytes 3833856 | tf_op jit(solution)/shard_map/all_gather | solution.py:66
  21.4 145.8 %all-gather.17.cloned.1.call-start = ((), (), s32[]{:S(2)}) async-start(), calls=%async_computation.14 | async-start | bytes 5990400 | tf_op jit(solution)/shard_map/all_gather | solution.py:66
  49.1 133.0 %all-gather.21.cloned.1.call-start = ((), (), s32[]{:S(2)}) async-start(), calls=%async_computation.16 | async-start | bytes 3833856 | tf_op jit(solution)/shard_map/all_gather | solution.py:66
  92.7 68.0 %collective-permute-start.11 = (bf16[800,1600]{1,0:T(8,128)(2,1)S(1)}, bf16[800,1600]{1,0:T(8,128)(2,1)}, u32[]{:S(2)}, u32[]{:S(2)}) collective-permute-start(bf16[800,1600]{1,0:T(8,128)(2,1)S(1)} %copy-done.3), channel_id=1, source_target_pairs={{1,8},{8,1},{3,10},{10,3},{5,12},{12,5},{7,14},{14,7},{17,24},{24,... | collective-permute-start | bytes 7680008 | tf_op jit(solution)/shard_map/ppermute | solution.py:590
  160.1 50.3 %all-gather.19.cloned.1.call-start = ((), (), s32[]{:S(2)}) async-start(), calls=%async_computation.15 | async-start | bytes 3833856 | tf_op jit(solution)/shard_map/all_gather | solution.py:66
  176.6 30.4 %collective-permute-start.15 = (bf16[200,800]{1,0:T(8,128)(2,1)}, bf16[200,800]{1,0:T(8,128)(2,1)}, u32[]{:S(2)}, u32[]{:S(2)}) collective-permute-start(bf16[200,800]{1,0:T(8,128)(2,1)} %collective-permute-done.8.refs_1_), channel_id=1, source_target_pairs={{0,1},{1,0},{2,3},{3,2},{4,5},{5,4},{6,7},{7,6},{8,9},{9,8},{10,11... | collective-permute-start | bytes 960008 | tf_op jit(solution)/shard_map/ppermute | solution.py:46
  190.2 90.6 %reduce-scatter.3.cloned.1.call-start = ((), (), s32[]{:S(2)}) async-start(), calls=%async_computation.11 | async-start | bytes 3833856 | tf_op jit(solution)/shard_map/reduce_scatter | solution.py:70
  225.3 111.7 %all-gather.23.cloned.1.call-start = ((), (), s32[]{:S(2)}) async-start(), calls=%async_computation.17 | async-start | bytes 3833856 | tf_op jit(solution)/shard_map/all_gather | solution.py:66
  237.6 43.3 %collective-permute-start.23 = (bf16[4,4,32,800]{3,2,1,0:T(8,128)(2,1)}, bf16[4,4,32,800]{3,2,1,0:T(8,128)(2,1)}, u32[]{:S(2)}, u32[]{:S(2)}) collective-permute-start(bf16[4,4,32,800]{3,2,1,0:T(8,128)(2,1)} %get-tuple-element.146), channel_id=1, source_target_pairs={{96,0},{0,32},{32,64},{64,96},{97,1},{1,33},{33,65},{65,97},{98,2}... | collective-permute-start | bytes 2457608 | tf_op jit(solution)/shard_map/ppermute | solution.py:38
  287.9 29.6 %all-to-all-start.3 = ((bf16[8,128,256]{2,1,0:T(8,128)(2,1)}), bf16[8,128,256]{2,1,0:T(8,128)(2,1)S(1)}, u32[]{:S(2)}, u32[]{:S(2)}) async-start(bf16[8,128,256]{2,1,0:T(8,128)(2,1)} %get-tuple-element.152), calls=%async_computation.4 | async-start | bytes 1048576 | tf_op jit(solution)/shard_map/all_to_all | solution.py:62
  294.5 135.1 %reduce-scatter.5.cloned.1.call-start = ((), (), s32[]{:S(2)}) async-start(), calls=%async_computation.12 | async-start | bytes 7667712 | tf_op jit(solution)/shard_map/reduce_scatter | solution.py:70
  346.3 79.9 %all-to-all-start.4 = ((bf16[16,80,1600]{2,1,0:T(8,128)(2,1)}), bf16[16,80,1600]{2,1,0:T(8,128)(2,1)}, u32[]{:S(2)}, u32[]{:S(2)}) async-start(bf16[16,80,1600]{2,1,0:T(8,128)(2,1)} %last_grads.1), calls=%async_computation.6 | async-start | bytes 8519680 | tf_op jit(solution)/shard_map/all_to_all | solution.py:62
  350.9 141.2 %all-gather.25.cloned.1.call-start = ((), (), s32[]{:S(2)}) async-start(), calls=%async_computation.18 | async-start | bytes 1769472 | tf_op jit(solution)/shard_map/all_gather | solution.py:66
  353.9 64.8 %collective-permute-start.27 = (bf16[56,1600]{1,0:T(8,128)(2,1)}, bf16[56,1600]{1,0:T(8,128)(2,1)S(1)}, u32[]{:S(2)}, u32[]{:S(2)}) collective-permute-start(bf16[56,1600]{1,0:T(8,128)(2,1)} %get-tuple-element.170), channel_id=1, source_target_pairs={{32,0},{64,32},{96,64},{0,96},{33,1},{65,33},{97,65},{1,97},{34,2}... | collective-permute-start | bytes 537608 | tf_op jit(solution)/shard_map/ppermute | solution.py:38
  356.3 64.8 %collective-permute-start.28 = (bf16[56,1600]{1,0:T(8,128)(2,1)}, bf16[56,1600]{1,0:T(8,128)(2,1)S(1)}, u32[]{:S(2)}, u32[]{:S(2)}) collective-permute-start(bf16[56,1600]{1,0:T(8,128)(2,1)} %get-tuple-element.171), channel_id=1, source_target_pairs={{64,0},{96,32},{0,64},{32,96},{65,1},{97,33},{1,65},{33,97},{66,2}... | collective-permute-start | bytes 537608 | tf_op jit(solution)/shard_map/ppermute | solution.py:38
  356.9 68.2 %collective-permute-start.29 = (bf16[56,1600]{1,0:T(8,128)(2,1)}, bf16[56,1600]{1,0:T(8,128)(2,1)S(1)}, u32[]{:S(2)}, u32[]{:S(2)}) collective-permute-start(bf16[56,1600]{1,0:T(8,128)(2,1)} %get-tuple-element.172), channel_id=1, source_target_pairs={{96,0},{0,32},{32,64},{64,96},{97,1},{1,33},{33,65},{65,97},{98,2}... | collective-permute-start | bytes 537608 | tf_op jit(solution)/shard_map/ppermute | solution.py:38
  359.5 66.6 %collective-permute-start.30 = (bf16[32,800]{1,0:T(8,128)(2,1)}, bf16[32,800]{1,0:T(8,128)(2,1)S(1)}, u32[]{:S(2)}, u32[]{:S(2)}) collective-permute-start(bf16[32,800]{1,0:T(8,128)(2,1)} %get-tuple-element.175), channel_id=1, source_target_pairs={{2,0},{4,2},{6,4},{0,6},{3,1},{5,3},{7,5},{1,7},{10,8},{12,10},{14... | collective-permute-start | bytes 153608 | tf_op jit(solution)/shard_map/ppermute | solution.py:38
  360.9 65.3 %collective-permute-start.31 = (bf16[32,800]{1,0:T(8,128)(2,1)}, bf16[32,800]{1,0:T(8,128)(2,1)S(1)}, u32[]{:S(2)}, u32[]{:S(2)}) collective-permute-start(bf16[32,800]{1,0:T(8,128)(2,1)} %get-tuple-element.176), channel_id=1, source_target_pairs={{4,0},{6,2},{0,4},{2,6},{5,1},{7,3},{1,5},{3,7},{12,8},{14,10},{8,... | collective-permute-start | bytes 153608 | tf_op jit(solution)/shard_map/ppermute | solution.py:38
  449.0 31.6 %collective-permute-start.37 = (bf16[2,4,32,800]{3,2,1,0:T(8,128)(2,1)}, bf16[2,4,32,800]{3,2,1,0:T(8,128)(2,1)S(1)}, u32[]{:S(2)}, u32[]{:S(2)}) collective-permute-start(bf16[2,4,32,800]{3,2,1,0:T(8,128)(2,1)} %fc_both.1.refs_0_), channel_id=1, source_target_pairs={{96,0},{0,32},{32,64},{64,96},{97,1},{1,33},{33,65},{65,97},{98,2}... | collective-permute-start | bytes 1228808 | tf_op jit(solution)/shard_map/ppermute | solution.py:38
  450.5 30.0 %collective-permute-start.36 = (bf16[2,4,32,800]{3,2,1,0:T(8,128)(2,1)}, bf16[2,4,32,800]{3,2,1,0:T(8,128)(2,1)S(1)}, u32[]{:S(2)}, u32[]{:S(2)}) collective-permute-start(bf16[2,4,32,800]{3,2,1,0:T(8,128)(2,1)} %fc_both.1.refs_0_), channel_id=1, source_target_pairs={{64,0},{96,32},{0,64},{32,96},{65,1},{97,33},{1,65},{33,97},{66,2}... | collective-permute-start | bytes 1228808 | tf_op jit(solution)/shard_map/ppermute | solution.py:38
  450.6 30.0 %collective-permute-start.35 = (bf16[2,4,32,800]{3,2,1,0:T(8,128)(2,1)}, bf16[2,4,32,800]{3,2,1,0:T(8,128)(2,1)S(1)}, u32[]{:S(2)}, u32[]{:S(2)}) collective-permute-start(bf16[2,4,32,800]{3,2,1,0:T(8,128)(2,1)} %fc_both.1.refs_0_), channel_id=1, source_target_pairs={{32,0},{64,32},{96,64},{0,96},{33,1},{65,33},{97,65},{1,97},{34,2}... | collective-permute-start | bytes 1228808 | tf_op jit(solution)/shard_map/ppermute | solution.py:38
  475.5 57.9 %all-gather.27.cloned.1.call-start = ((), (), s32[]{:S(2)}) async-start(), calls=%async_computation.19 | async-start | bytes 1863680 | tf_op jit(solution)/shard_map/all_gather | solution.py:66
  497.8 36.9 %collective-permute-start.38 = (bf16[8,4,32,768]{3,2,1,0:T(8,128)(2,1)S(1)}, bf16[8,4,32,768]{3,2,1,0:T(8,128)(2,1)}, u32[]{:S(2)}, u32[]{:S(2)}) collective-permute-start(bf16[8,4,32,768]{3,2,1,0:T(8,128)(2,1)S(1)} %bitcast.44), channel_id=1, source_target_pairs={{0,8},{8,0},{1,9},{9,1},{2,10},{10,2},{3,11},{11,3},{4,12},{12,4},... | collective-permute-start | bytes 4718600 | tf_op jit(solution)/shard_map/ppermute | solution.py:58
  503.0 31.1 %collective-permute-start.34 = (bf16[2,128,1600]{1,2,0:T(8,128)(2,1)}, bf16[2,128,1600]{1,2,0:T(8,128)(2,1)}, u32[]{:S(2)}, u32[]{:S(2)}) collective-permute-start(bf16[2,128,1600]{1,2,0:T(8,128)(2,1)} %copy.69), channel_id=1, source_target_pairs={{0,0},{1,8},{8,1},{9,9},{2,2},{3,10},{10,3},{11,11},{4,4},{5,12},{... | collective-permute-start | bytes 2457608 | tf_op jit(solution)/shard_map/ppermute | solution.py:50
  (90 other events, 2101.4 us)
Sparse Core Ops, SparseCore 0:
  21.5 29.1 all-gather.14
  53.0 36.8 all-gather.16
  92.8 28.4 all-gather.20
  172.5 33.2 all-gather.18
  225.4 34.0 reduce-scatter.2
  287.4 30.3 all-gather.22
  336.0 44.6 reduce-scatter.4
  439.4 52.7 all-gather.24
  494.4 28.7 all-gather.26

commit v12 on v11

--- a/solution.py
+++ b/solution.py
@@ -555,14 +555,14 @@
     )
     all_tokens = gather(after(own_tokens, qkv_parts[0]), TEAM).reshape(length, width)
     qkv_own = ring_all(qkv_parts, "y")
-    qkv_other = [flipped(part, "zh") for part in qkv_own]
-    out_rows = swap_roles(after(w_out, *qkv_own))
     small = jnp.concatenate(
         [ln1_gain, ln1_bias, bias_q, bias_v, bias_out, ln2_gain, ln2_bias, bias_proj, bias_fc]
     ).reshape(3, hidden)
     small_all = exchange(
-        after(jnp.broadcast_to(small, (8, 3, hidden)), qkv_own[1]), GRP
-    )
+        after(jnp.broadcast_to(small, (8, 3, hidden)), qkv_parts[0]), GRP
+    )
+    qkv_other = [flipped(after(part, small_all), "zh") for part in qkv_own]
+    out_rows = swap_roles(after(w_out, *qkv_own))
     place = after(place, small_all)
     fc_parts = call(
         fc_columns_kernel,
@@ -746,12 +746,14 @@
         flops=20 * length * width * slots,
     )
     last = team_sum(last_parts.reshape(2 * length, width)).reshape(2, span, width)
+    fc_grad = ring_all(fold(Y, fc_grad, "fc_fold_last", grad_mixed), "y")
+    proj_grad = ring_all(fold(X, proj_grad, "proj_fold", grad_mixed), "x")
     last_grads = call(
         last_grads_kernel,
         "last_grads",
         struct((16, 2 * window + windows(shard, 16)[0], width), bf16),
         place,
-        first,
+        after(first, fc_grad[0], proj_grad[0]),
         grad_mixed,
         attended_own.reshape(length, shard),
         branch_all,
@@ -759,9 +761,7 @@
         flops=2 * length * width * (slots + shard),
     )
     place = after(place, last_grads)
-    last_grads = exchange(last_grads, REPLICAS)
-    fc_grad = ring_all(fold(Y, fc_grad, "fc_fold_last", grad_mixed), "y")
-    proj_grad = ring_all(fold(X, proj_grad, "proj_fold", grad_mixed), "x")
+    last_grads = exchange(after(last_grads, *fc_grad, *proj_grad), REPLICAS)
 
     def stacked(parts, name):
         return call(
@@ -780,7 +780,7 @@
         last_sum_kernel,
         "last_sum",
         (struct((4, window, slots), bf16), struct((windows(shard, 16)[0], width), bf16)),
-        after(last_grads, proj_sum, *fc_grad),
+        last_grads,
     )
     qkv_sum = exchange(after(qkv_sum, last), "y")
     qkv_whole = gather(qkv_sum, ("zl", "x"))
@@ -819,12 +819,12 @@
     small_terms = small_terms.reshape(8, 8, shard).transpose(1, 0, 2).reshape(8, 2, hidden)
     small_terms = jnp.concatenate([small_terms, hidden_term[:, None]], axis=1)
     small_sum = jnp.sum(exchange(after(small_terms, qkv_sum), GRP), axis=0)
+    small_last = jnp.broadcast_to(small_sum, (16, 3, hidden))
+    small_last = jnp.sum(exchange(small_last, REP), axis=0)
     out_whole = exchange(
-        after(jnp.broadcast_to(out_sum, (16,) + out_sum.shape), small_sum, *fc_pieces[:4]),
+        after(jnp.broadcast_to(out_sum, (16,) + out_sum.shape), small_last, *fc_pieces[:4]),
         REPLICAS,
     )
-    small_last = jnp.broadcast_to(after(small_sum, out_whole), (16, 3, hidden))
-    small_last = jnp.sum(exchange(small_last, REP), axis=0)
     owned = small_last[:2].reshape(8, shard)
 
     qkv_spans = [
@@ -835,32 +835,32 @@
         for r in range(8)
     ]
     qkv_whole = after(qkv_whole, small_sum, *fc_pieces[:4])
-    proj_whole = after(gather(after(proj_pair, qkv_whole), "x"), small_last)
-    proj_total = call(
-        proj_total_kernel,
-        "proj_total",
-        struct((hidden, width), f32),
-        after(place, small_sum),
-        proj_whole,
-        other_core(proj_whole),
-    )
-    qkv_total = call(
-        functools.partial(column_total_kernel, qkv_spans),
-        "qkv_total",
-        struct((shard, 3 * width), f32),
-        after(place, results, small_last),
-        qkv_whole,
-        other_core(qkv_whole),
-    )
-    out_total = row_total(out_whole, shard, "out_total")
+    proj_whole = after(gather(after(proj_pair, qkv_whole), "x"), out_whole)
     fc_spans = [[(0, rank * hidden, hidden)] for rank in range(8)]
     fc_total = call(
         functools.partial(column_ring_total_kernel, fc_spans),
         "fc_total",
         struct((shard, 8 * hidden), f32),
-        after(place, qkv_total, out_total, proj_total),
+        after(place, small_last),
         *fc_pieces,
     )
+    proj_total = call(
+        proj_total_kernel,
+        "proj_total",
+        struct((hidden, width), f32),
+        after(place, fc_total),
+        proj_whole,
+        other_core(proj_whole),
+    )
+    qkv_total = call(
+        functools.partial(column_total_kernel, qkv_spans),
+        "qkv_total",
+        struct((shard, 3 * width), f32),
+        after(place, results, fc_total),
+        qkv_whole,
+        other_core(qkv_whole),
+    )
+    out_total = row_total(out_whole, shard, "out_total", fc_total)
     return (
         results_home[1].reshape(1, span, width),
         results_home[0].astype(f32).reshape(1, span, width),

time: 577 us -> 558 us (0.967)
  waiting for transfers between devices: 204 us -> 140 us
  blocking collectives: 27.8 us -> 86.2 us
  starting transfers between devices: 131 us -> 117 us
    all_to_all x2 -> x4, blocking collectives: 27.8 us -> 86.2 us  [exchange(): return lax.all_to_all(parts, axes, 0, 0)]
    ppermute x24, waiting for transfers between devices: 108 us -> 53.7 us  [ring(): lax.ppermute(value, axis, [(index[(i + step) % 4], index[i]) for i in ran...]
    all_to_all x7 -> x5, starting transfers between devices: 44.4 us -> 30.1 us  [exchange(): return lax.all_to_all(parts, axes, 0, 0)]
    all_to_all x7 -> x5, waiting for transfers between devices: 33.1 us -> 28.7 us  [exchange(): return lax.all_to_all(parts, axes, 0, 0)]
    unnamed x103 -> x107, local copies, waits for them, and re-layouts: 12.2 us -> 12.5 us
  transfers between devices with their start and end apart: 63 -> 61, of which waited for: 27 -> 28; matrix products, arithmetic and copies ran while one was open for 6% -> 6% of each run, Pallas kernels for 20% -> 22%
where the time goes in v12:
time: 558 us; the launch traced here: 549 us
  Pallas kernels  145 us (26%)
  waiting for transfers between devices  140 us (25%)
  starting transfers between devices  117 us (21%)
  blocking collectives  86.2 us (15%)
  local copies, waits for them, and re-layouts  32 us (6%)
  between operations  14.8 us (3%)
  matrix products  6.89 us (1%)
  other arithmetic  5.92 us (1%)
    pallas_call x24, Pallas kernels, call(): pl.pallas_call(kernel, out_shape=out_shape, in_specs=specs, out_specs=out...  145 us
    all_to_all x4, blocking collectives, exchange(): return lax.all_to_all(parts, axes, 0, 0)  86.2 us
    ppermute x24, waiting for transfers between devices, ring(): lax.ppermute(value, axis, [(index[(i + step) % 4], index[i]) for i in ran...  53.7 us
    all_to_all x5, starting transfers between devices, exchange(): return lax.all_to_all(parts, axes, 0, 0)  30.1 us
    ppermute x24, starting transfers between devices, ring(): lax.ppermute(value, axis, [(index[(i + step) % 4], index[i]) for i in ran...  29.2 us
    ppermute x9, waiting for transfers between devices, flipped(): return lax.ppermute(value, axis, [(0, 1), (1, 0)])  29 us
    all_to_all x5, waiting for transfers between devices, exchange(): return lax.all_to_all(parts, axes, 0, 0)  28.7 us
    ppermute x4, starting transfers between devices, swap_roles(): return lax.ppermute(value, ('c', 'zh'), ROLES)  21.1 us
  transfers between devices with their start and end apart: 61, of which 28 were waited for; matrix products, arithmetic and copies ran while one was open for 6% of the time, Pallas kernels for 22%

profile of v12, /device:TPU:17, one launch (start us, length us, event | category | flops | bytes accessed | tf_op | source)
XLA Modules:
  0.0 549.1 jit_solution(15407608645023221711)
XLA Ops:
  39.7 8.6 %collective-permute-done.12 = bf16[200,1600]{1,0:T(8,128)(2,1)S(1)} collective-permute-done((bf16[200,1600]{1,0:T(8,128)(2,1)}, bf16[200,1600]{1,0:T(8,128)(2,1)S(1)}, u32[]{:S(2)}, u32[]{:S(2)}) %collective-permute-start.12) | collective-permute-done | bytes 640032 | tf_op jit(solution)/shard_map/ppermute | solution.py:50
  49.5 9.7 %all_to_all.45 = bf16[8,3,800]{2,1,0:T(4,128)(2,1)S(1)} all-to-all(bf16[8,3,800]{2,1,0:T(4,128)(2,1)S(1)} %broadcast_in_dim.21), channel_id=1, replica_groups=mesh['x'=4,'zl'=2,'c'=2,'y'=4,'zh'=2] {'y','zh'}, dimensions={0} | all-to-all | bytes 76800 | tf_op jit(solution)/shard_map/all_to_all | solution.py:62
  72.2 6.6 %collective-permute-done.6.refs_6_ = bf16[200,768]{1,0:T(8,128)(2,1)} collective-permute-done((bf16[200,768]{1,0:T(8,128)(2,1)}, bf16[200,768]{1,0:T(8,128)(2,1)}, u32[]{:S(2)}, u32[]{:S(2)}) %collective-permute-start.6) | collective-permute-done | bytes 307232 | tf_op jit(solution)/shard_map/ppermute | solution.py:46
  78.8 6.7 %collective-permute-done.7.refs_7_ = bf16[200,768]{1,0:T(8,128)(2,1)} collective-permute-done((bf16[200,768]{1,0:T(8,128)(2,1)}, bf16[200,768]{1,0:T(8,128)(2,1)}, u32[]{:S(2)}, u32[]{:S(2)}) %collective-permute-start.7) | collective-permute-done | bytes 307232 | tf_op jit(solution)/shard_map/ppermute | solution.py:46
  87.5 7.0 %collective-permute-start.13 = (bf16[128,1600]{1,0:T(8,128)(2,1)}, bf16[128,1600]{1,0:T(8,128)(2,1)S(1)}, u32[]{:S(2)}, u32[]{:S(2)}) collective-permute-start(bf16[128,1600]{1,0:T(8,128)(2,1)} %bitcast.51), channel_id=1, source_target_pairs={{0,0},{1,8},{8,1},{9,9},{2,2},{3,10},{10,3},{11,11},{4,4},{5,12},{... | collective-permute-start | bytes 1228808 | tf_op jit(solution)/shard_map/ppermute | solution.py:50
  116.5 15.6 %attend.1 = (bf16[1024,1600]{1,0:T(8,128)(2,1)}, bf16[1024,768]{1,0:T(8,128)(2,1)}, bf16[1024,256]{1,0:T(8,128)(2,1)}, f32[1024,4]{1,0:T(8,128)}, bf16[8,200,768]{2,1,0:T(8,128)(2,1)}) custom-call(s32[8]{0:T(128)} %stack.39.place_ref, bf16[1024,1600]{1,0:T(8,128)(2,1)} %all-gather.15.cloned.1.call-done.tokens_ref, f32[8,1600]{1,0:T(8,128)} %reshape.109.norm_ref, ...), custom_call_target="tpu_custom_call" | custom-call | flops 2516582400 | bytes 13636640 | tf_op jit(solution)/shard_map/attend/pallas_call | solution.py:122
  142.1 6.7 %all-to-all-done.1.slots_ref = bf16[8,128,256]{2,1,0:T(8,128)(2,1)} async-done(((bf16[8,128,256]{2,1,0:T(8,128)(2,1)}), bf16[8,128,256]{2,1,0:T(8,128)(2,1)}, u32[]{:S(2)}, u32[]{:S(2)}) %all-to-all-start.1) | async-done | bytes 524320 | tf_op jit(solution)/shard_map/all_to_all | solution.py:62
  165.2 7.9 %all-to-all-start.2 = ((bf16[8,128,200]{1,2,0:T(8,128)(2,1)}), bf16[8,128,200]{1,2,0:T(8,128)(2,1)S(1)}, u32[]{:S(2)}, u32[]{:S(2)}) async-start(bf16[8,128,200]{1,2,0:T(8,128)(2,1)} %copy.64), calls=%async_computation.2 | async-start | bytes 819200 | tf_op jit(solution)/shard_map/all_to_all | solution.py:62
  173.1 6.9 %fusion.2 = f32[1024,800]{0,1:T(8,128)} fusion(bf16[1024,1600]{1,0:T(8,128)(2,1)} %all-gather.21.cloned.1.call-done.right_ref, bf16[800,1600]{1,0:T(8,128)(2,1)S(1)} %broadcast_select_fusion.rows_ref), kind=kOutput, calls=%fused_computation.14 | convolution fusion | flops 2621440000 | bytes 9113600 | tf_op jit(solution)/shard_map/dot_general | solution.py:111
  192.5 14.8 %hidden.1 = (bf16[1024,800]{1,0:T(8,128)(2,1)}, bf16[1024,800]{1,0:T(8,128)(2,1)}, f32[1,800]{1,0:T(1,128)}, bf16[1024,1600]{1,0:T(8,128)(2,1)}) custom-call(s32[8]{0:T(128)} %stack.39.place_ref, bf16[1024,1600]{1,0:T(8,128)(2,1)} %all-gather.19.cloned.1.call-done.second_ref.left_ref, bf16[1600,800]{1,0:T(8,128)(2,1)} %bitcast.41, ...), custom_call_target="tpu_custom_call" | custom-call | flops 5242880000 | bytes 15673632 | tf_op jit(solution)/shard_map/hidden/pallas_call | solution.py:122
  207.5 9.1 %fc_grad.1 = (bf16[4,4,32,800]{3,2,1,0:T(8,128)(2,1)}, bf16[4,4,32,800]{3,2,1,0:T(8,128)(2,1)}, bf16[4,4,32,800]{3,2,1,0:T(8,128)(2,1)}, bf16[4,4,32,800]{3,2,1,0:T(8,128)(2,1)}) custom-call(s32[8]{0:T(128)} %stack.39.place_ref, bf16[1024,1600]{1,0:T(8,128)(2,1)} %all-gather.19.cloned.1.call-done.second_ref.left_ref, ...), custom_call_target="tpu_custom_call" | custom-call | flops 2621440000 | bytes 8192032 | tf_op jit(solution)/shard_map/fc_grad/pallas_call | solution.py:122
  220.2 7.4 %proj_grad.1 = (bf16[4,56,1600]{2,1,0:T(8,128)(2,1)}, bf16[4,56,1600]{2,1,0:T(8,128)(2,1)}, bf16[4,56,1600]{2,1,0:T(8,128)(2,1)}, bf16[4,56,1600]{2,1,0:T(8,128)(2,1)}) custom-call(s32[8]{0:T(128)} %stack.39.place_ref, bf16[1024,800]{1,0:T(8,128)(2,1)} %get-tuple-element.157.left_ref.active_ref, bf16[1024,1600]{1,0:T(8,128)(2,1)} %all-gather.21.cloned.1.call-done.right_ref), custom_call_target="tpu_custom_call" | custom-call | flops 2621440000 | bytes 7782432 | tf_op jit(solution)/shard_map/proj_grad/pallas_call | solution.py:122
  229.6 8.0 %down.1 = bf16[1024,1600]{1,0:T(8,128)(2,1)} custom-call(bf16[1024,800]{1,0:T(8,128)(2,1)} %get-tuple-element.157.left_ref.active_ref, bf16[800,1600]{1,0:T(8,128)(2,1)} %copy-done), custom_call_target="tpu_custom_call" | custom-call | flops 1 | bytes 1 | tf_op jit(solution)/shard_map/down/pallas_call | solution.py:122
  247.4 15.4 %collective-permute-done.23.refs_3_ = bf16[4,4,32,800]{3,2,1,0:T(8,128)(2,1)S(1)} collective-permute-done((bf16[4,4,32,800]{3,2,1,0:T(8,128)(2,1)}, bf16[4,4,32,800]{3,2,1,0:T(8,128)(2,1)S(1)}, u32[]{:S(2)}, u32[]{:S(2)}) %collective-permute-start.23) | collective-permute-done | bytes 819232 | tf_op jit(solution)/shard_map/ppermute | solution.py:38
  262.7 6.7 %branch_back.1 = (f32[128,1600]{1,0:T(8,128)}, bf16[128,1600]{1,0:T(8,128)(2,1)}, bf16[8,128,256]{2,1,0:T(8,128)(2,1)}, f32[4,1600]{1,0:T(4,128)}) custom-call(s32[8]{0:T(128)} %stack.39.place_ref, bf16[128,1600]{1,0:T(8,128)(2,1)} %reduce-scatter.3.cloned.1.call-done.grad_ref, f32[128,1600]{1,0:T(8,128)} %get-tuple-element.160.middle_ref, ...), custom_call_target="tpu_custom_call" | custom-call | flops 1 | bytes 1 | tf_op jit(solution)/shard_map/branch_back/pallas_call | solution.py:122
  300.5 17.6 %attend_back.1 = (bf16[1024,768]{1,0:T(8,128)(2,1)}, bf16[8,2,128,1600]{3,2,1,0:T(8,128)(2,1)}, f32[1,768]{1,0:T(1,128)}) custom-call(s32[8]{0:T(128)} %stack.39.place_ref, bf16[1024,768]{1,0:T(8,128)(2,1)} %get-tuple-element.168.qkv_ref, bf16[1024,256]{1,0:T(8,128)(2,1)} %bitcast.49, bf16[1024,256]{1,0:T(8,128)(2,1)} %get-tuple-element.133.out_ref, ...), custom_call_target="tpu_custom_call" | custom-call | flops 25165824000 | bytes 16501792 | tf_op jit(solution)/shard_map/attend_back/pallas_call | solution.py:122
  330.5 9.3 %last_grads.1 = bf16[16,80,1600]{2,1,0:T(8,128)(2,1)} custom-call(s32[8]{0:T(128)} %stack.39.place_ref, bf16[1024,1600]{1,0:T(8,128)(2,1)} %get-tuple-element.179.first_ref, bf16[1024,768]{1,0:T(8,128)(2,1)} %get-tuple-element.174.mixed_ref, bf16[1024,200]{1,0:T(8,128)(2,1)} %bitcast.42, bf16[1024,1600]{1,0:T(8,128)(2,1)} %all-gather.23.cloned.1.call-done.branch_ref), custom_call_target="tpu_custom_call" | custom-call | flops 3171942400 | bytes 12632096 | tf_op jit(solution)/shard_map/last_grads/pallas_call | solution.py:122
  340.9 56.4 %all_to_all.46.parts_ref = bf16[16,80,1600]{2,1,0:T(8,128)(2,1)} all-to-all(bf16[16,80,1600]{2,1,0:T(8,128)(2,1)} %last_grads.1), channel_id=1, replica_groups=mesh['x'=4,'zl'=2,'c'=2,'y'=4,'zh'=2] {'zl','x','zh'}, dimensions={0} | all-to-all | bytes 8192000 | tf_op jit(solution)/shard_map/all_to_all | solution.py:62
  400.7 7.4 %all_to_all.47 = bf16[4,32,768]{2,1,0:T(8,128)(2,1)} all-to-all(bf16[4,32,768]{2,1,0:T(8,128)(2,1)} %get-tuple-element.189), channel_id=1, replica_groups=mesh['x'=4,'zl'=2,'c'=2,'y'=4,'zh'=2] {'y'}, dimensions={0} | all-to-all | bytes 393216 | tf_op jit(solution)/shard_map/all_to_all | solution.py:62
  422.9 7.5 %collective-permute-start.45 = (bf16[56,1600]{1,0:T(8,128)(2,1)S(1)}, bf16[56,1600]{1,0:T(8,128)(2,1)S(1)}, u32[]{:S(2)}, u32[]{:S(2)}) collective-permute-start(bf16[56,1600]{1,0:T(8,128)(2,1)S(1)} %add_convert_fusion), channel_id=1, source_target_pairs={{0,16},{1,0},{8,17},{9,1},{16,24},{17,8},{24,25},{25,9},{2,18},{3,... | collective-permute-start | bytes 537608 | tf_op jit(solution)/shard_map/ppermute | solution.py:788
  451.1 10.8 %all-gather.25.cloned.1.call-done = bf16[32,32,768]{2,1,0:T(8,128)(2,1)} async-done(((bf16[4,32,768]{2,1,0:T(8,128)(2,1)}), bf16[32,32,768]{2,1,0:T(8,128)(2,1)}) %all-gather.25.cloned.1.call-update) | async-done | bytes 1572880 | tf_op jit(solution)/shard_map/all_gather | solution.py:66
  462.0 12.7 %all_to_all.48 = f32[16,3,800]{2,1,0:T(4,128)S(1)} all-to-all(f32[16,3,800]{2,1,0:T(4,128)S(1)} %broadcast_in_dim.26), channel_id=1, replica_groups=mesh['x'=4,'zl'=2,'c'=2,'y'=4,'zh'=2] {'x','zl','c'}, dimensions={0} | all-to-all | bytes 307200 | tf_op jit(solution)/shard_map/all_to_all | solution.py:62
  482.7 19.6 %all-to-all-done.8.own_ref = bf16[16,16,1600]{2,1,0:T(8,128)(2,1)S(1)} async-done(((bf16[16,16,1600]{2,1,0:T(8,128)(2,1)}), bf16[16,16,1600]{2,1,0:T(8,128)(2,1)S(1)}, u32[]{:S(2)}, u32[]{:S(2)}) %all-to-all-start.8) | async-done | bytes 819232 | tf_op jit(solution)/shard_map/all_to_all | solution.py:62
  517.1 8.9 %fc_total.1 = f32[200,6400]{1,0:T(8,128)} custom-call(s32[8]{0:T(128)} %stack.39.place_ref, bf16[2,4,32,800]{3,2,1,0:T(8,128)(2,1)} %fc_both.1.refs_0_, bf16[2,4,32,800]{3,2,1,0:T(8,128)(2,1)} %copy-done.19, bf16[2,4,32,800]{3,2,1,0:T(8,128)(2,1)} %copy-done.18, bf16[2,4,32,800]{3,2,1,0:T(8,128)(2,1)} %copy-done.17, ...), custom_call_target="tpu_custom_call" | custom-call | bytes 8396832 | tf_op jit(solution)/shard_map/fc_total/pallas_call | solution.py:122
  (290 shorter events, 247.3 us)
Async XLA Ops:
  7.3 109.2 %all-gather.15.cloned.1.call-start = ((), (), s32[]{:S(2)}) async-start(), calls=%async_computation.13 | async-start | bytes 3833856 | tf_op jit(solution)/shard_map/all_gather | solution.py:66
  21.4 127.4 %all-gather.17.cloned.1.call-start = ((), (), s32[]{:S(2)}) async-start(), calls=%async_computation.14 | async-start | bytes 5990400 | tf_op jit(solution)/shard_map/all_gather | solution.py:66
  49.2 116.0 %all-gather.21.cloned.1.call-start = ((), (), s32[]{:S(2)}) async-start(), calls=%async_computation.16 | async-start | bytes 3833856 | tf_op jit(solution)/shard_map/all_gather | solution.py:66
  101.3 40.9 %collective-permute-start.11 = (bf16[800,1600]{1,0:T(8,128)(2,1)S(1)}, bf16[800,1600]{1,0:T(8,128)(2,1)}, u32[]{:S(2)}, u32[]{:S(2)}) collective-permute-start(bf16[800,1600]{1,0:T(8,128)(2,1)S(1)} %copy-done.3), channel_id=1, source_target_pairs={{1,8},{8,1},{3,10},{10,3},{5,12},{12,5},{7,14},{14,7},{17,24},{24,... | collective-permute-start | bytes 7680008 | tf_op jit(solution)/shard_map/ppermute | solution.py:590
  141.7 50.8 %all-gather.19.cloned.1.call-start = ((), (), s32[]{:S(2)}) async-start(), calls=%async_computation.15 | async-start | bytes 3833856 | tf_op jit(solution)/shard_map/all_gather | solution.py:66
  154.6 30.3 %collective-permute-start.14 = (bf16[200,800]{1,0:T(8,128)(2,1)S(1)}, bf16[200,800]{1,0:T(8,128)(2,1)}, u32[]{:S(2)}, u32[]{:S(2)}) collective-permute-start(bf16[200,800]{1,0:T(8,128)(2,1)S(1)} %copy-done.22), channel_id=1, source_target_pairs={{0,1},{1,0},{2,3},{3,2},{4,5},{5,4},{6,7},{7,6},{8,9},{9,8},{10,11... | collective-permute-start | bytes 960008 | tf_op jit(solution)/shard_map/ppermute | solution.py:46
  157.7 27.1 %collective-permute-start.17 = (bf16[200,800]{1,0:T(8,128)(2,1)}, bf16[200,800]{1,0:T(8,128)(2,1)}, u32[]{:S(2)}, u32[]{:S(2)}) collective-permute-start(bf16[200,800]{1,0:T(8,128)(2,1)} %collective-permute-done.10.refs_3_), channel_id=1, source_target_pairs={{0,1},{1,0},{2,3},{3,2},{4,5},{5,4},{6,7},{7,6},{8,9},{9,8},{10,11... | collective-permute-start | bytes 960008 | tf_op jit(solution)/shard_map/ppermute | solution.py:46
  160.7 28.3 %collective-permute-start.15 = (bf16[200,800]{1,0:T(8,128)(2,1)}, bf16[200,800]{1,0:T(8,128)(2,1)}, u32[]{:S(2)}, u32[]{:S(2)}) collective-permute-start(bf16[200,800]{1,0:T(8,128)(2,1)} %collective-permute-done.8.refs_1_), channel_id=1, source_target_pairs={{0,1},{1,0},{2,3},{3,2},{4,5},{5,4},{6,7},{7,6},{8,9},{9,8},{10,11... | collective-permute-start | bytes 960008 | tf_op jit(solution)/shard_map/ppermute | solution.py:46
  165.2 27.3 %all-to-all-start.2 = ((bf16[8,128,200]{1,2,0:T(8,128)(2,1)}), bf16[8,128,200]{1,2,0:T(8,128)(2,1)S(1)}, u32[]{:S(2)}, u32[]{:S(2)}) async-start(bf16[8,128,200]{1,2,0:T(8,128)(2,1)} %copy.64), calls=%async_computation.2 | async-start | bytes 819200 | tf_op jit(solution)/shard_map/all_to_all | solution.py:62
  173.1 89.7 %reduce-scatter.3.cloned.1.call-start = ((), (), s32[]{:S(2)}) async-start(), calls=%async_computation.11 | async-start | bytes 3833856 | tf_op jit(solution)/shard_map/reduce_scatter | solution.py:70
  207.3 123.2 %all-gather.23.cloned.1.call-start = ((), (), s32[]{:S(2)}) async-start(), calls=%async_computation.17 | async-start | bytes 3833856 | tf_op jit(solution)/shard_map/all_gather | solution.py:66
  216.6 29.9 %collective-permute-start.21 = (bf16[4,4,32,800]{3,2,1,0:T(8,128)(2,1)}, bf16[4,4,32,800]{3,2,1,0:T(8,128)(2,1)S(1)}, u32[]{:S(2)}, u32[]{:S(2)}) collective-permute-start(bf16[4,4,32,800]{3,2,1,0:T(8,128)(2,1)} %get-tuple-element.153), channel_id=1, source_target_pairs={{32,0},{64,32},{96,64},{0,96},{33,1},{65,33},{97,65},{1,97},{34,2}... | collective-permute-start | bytes 2457608 | tf_op jit(solution)/shard_map/ppermute | solution.py:38
  219.1 27.4 %collective-permute-start.22 = (bf16[4,4,32,800]{3,2,1,0:T(8,128)(2,1)}, bf16[4,4,32,800]{3,2,1,0:T(8,128)(2,1)S(1)}, u32[]{:S(2)}, u32[]{:S(2)}) collective-permute-start(bf16[4,4,32,800]{3,2,1,0:T(8,128)(2,1)} %get-tuple-element.154), channel_id=1, source_target_pairs={{64,0},{96,32},{0,64},{32,96},{65,1},{97,33},{1,65},{33,97},{66,2}... | collective-permute-start | bytes 2457608 | tf_op jit(solution)/shard_map/ppermute | solution.py:38
  219.6 43.1 %collective-permute-start.23 = (bf16[4,4,32,800]{3,2,1,0:T(8,128)(2,1)}, bf16[4,4,32,800]{3,2,1,0:T(8,128)(2,1)S(1)}, u32[]{:S(2)}, u32[]{:S(2)}) collective-permute-start(bf16[4,4,32,800]{3,2,1,0:T(8,128)(2,1)} %get-tuple-element.155), channel_id=1, source_target_pairs={{96,0},{0,32},{32,64},{64,96},{97,1},{1,33},{33,65},{65,97},{98,2}... | collective-permute-start | bytes 2457608 | tf_op jit(solution)/shard_map/ppermute | solution.py:38
  272.2 27.5 %all-to-all-start.3 = ((bf16[8,128,256]{2,1,0:T(8,128)(2,1)}), bf16[8,128,256]{2,1,0:T(8,128)(2,1)S(1)}, u32[]{:S(2)}, u32[]{:S(2)}) async-start(bf16[8,128,256]{2,1,0:T(8,128)(2,1)} %get-tuple-element.161), calls=%async_computation.4 | async-start | bytes 1048576 | tf_op jit(solution)/shard_map/all_to_all | solution.py:62
  278.8 121.9 %reduce-scatter.5.cloned.1.call-start = ((), (), s32[]{:S(2)}) async-start(), calls=%async_computation.12 | async-start | bytes 7667712 | tf_op jit(solution)/shard_map/reduce_scatter | solution.py:70
  318.2 143.8 %all-gather.25.cloned.1.call-start = ((), (), s32[]{:S(2)}) async-start(), calls=%async_computation.18 | async-start | bytes 1769472 | tf_op jit(solution)/shard_map/all_gather | solution.py:66
  417.5 32.1 %collective-permute-start.37 = (bf16[2,4,32,800]{3,2,1,0:T(8,128)(2,1)}, bf16[2,4,32,800]{3,2,1,0:T(8,128)(2,1)S(1)}, u32[]{:S(2)}, u32[]{:S(2)}) collective-permute-start(bf16[2,4,32,800]{3,2,1,0:T(8,128)(2,1)} %fc_both.1.refs_0_), channel_id=1, source_target_pairs={{96,0},{0,32},{32,64},{64,96},{97,1},{1,33},{33,65},{65,97},{98,2}... | collective-permute-start | bytes 1228808 | tf_op jit(solution)/shard_map/ppermute | solution.py:38
  418.7 30.8 %collective-permute-start.36 = (bf16[2,4,32,800]{3,2,1,0:T(8,128)(2,1)}, bf16[2,4,32,800]{3,2,1,0:T(8,128)(2,1)S(1)}, u32[]{:S(2)}, u32[]{:S(2)}) collective-permute-start(bf16[2,4,32,800]{3,2,1,0:T(8,128)(2,1)} %fc_both.1.refs_0_), channel_id=1, source_target_pairs={{64,0},{96,32},{0,64},{32,96},{65,1},{97,33},{1,65},{33,97},{66,2}... | collective-permute-start | bytes 1228808 | tf_op jit(solution)/shard_map/ppermute | solution.py:38
  420.7 28.9 %collective-permute-start.35 = (bf16[2,4,32,800]{3,2,1,0:T(8,128)(2,1)}, bf16[2,4,32,800]{3,2,1,0:T(8,128)(2,1)S(1)}, u32[]{:S(2)}, u32[]{:S(2)}) collective-permute-start(bf16[2,4,32,800]{3,2,1,0:T(8,128)(2,1)} %fc_both.1.refs_0_), channel_id=1, source_target_pairs={{32,0},{64,32},{96,64},{0,96},{33,1},{65,33},{97,65},{1,97},{34,2}... | collective-permute-start | bytes 1228808 | tf_op jit(solution)/shard_map/ppermute | solution.py:38
  443.9 58.3 %all-gather.27.cloned.1.call-start = ((), (), s32[]{:S(2)}) async-start(), calls=%async_computation.19 | async-start | bytes 1863680 | tf_op jit(solution)/shard_map/all_gather | solution.py:66
  482.0 31.9 %collective-permute-start.41 = (bf16[2,4,32,800]{3,2,1,0:T(8,128)(2,1)S(1)}, bf16[2,4,32,800]{3,2,1,0:T(8,128)(2,1)}, u32[]{:S(2)}, u32[]{:S(2)}) collective-permute-start(bf16[2,4,32,800]{3,2,1,0:T(8,128)(2,1)S(1)} %collective-permute-done.37.refs_3_), channel_id=1, source_target_pairs={{0,8},{8,0},{1,9},{9,1},{2,10},{10,2},{3,11},{11,3},{4,12},{12,4},... | collective-permute-start | bytes 1228808 | tf_op jit(solution)/shard_map/ppermute | solution.py:58
  482.3 51.1 %collective-permute-start.42 = (bf16[8,4,32,768]{3,2,1,0:T(8,128)(2,1)S(1)}, bf16[8,4,32,768]{3,2,1,0:T(8,128)(2,1)}, u32[]{:S(2)}, u32[]{:S(2)}) collective-permute-start(bf16[8,4,32,768]{3,2,1,0:T(8,128)(2,1)S(1)} %bitcast.44), channel_id=1, source_target_pairs={{0,8},{8,0},{1,9},{9,1},{2,10},{10,2},{3,11},{11,3},{4,12},{12,4},... | collective-permute-start | bytes 4718600 | tf_op jit(solution)/shard_map/ppermute | solution.py:58
  502.3 35.3 %collective-permute-start.46 = (bf16[4,2,56,1600]{3,2,1,0:T(8,128)(2,1)}, bf16[4,2,56,1600]{3,2,1,0:T(8,128)(2,1)}, u32[]{:S(2)}, u32[]{:S(2)}) collective-permute-start(bf16[4,2,56,1600]{3,2,1,0:T(8,128)(2,1)} %bitcast.45), channel_id=1, source_target_pairs={{0,8},{8,0},{1,9},{9,1},{2,10},{10,2},{3,11},{11,3},{4,12},{12,4},... | collective-permute-start | bytes 4300808 | tf_op jit(solution)/shard_map/ppermute | solution.py:58
  (90 other events, 1677.5 us)
Sparse Core Ops, SparseCore 0:
  21.5 29.1 all-gather.14
  53.0 36.8 all-gather.16
  101.4 37.6 all-gather.20
  154.1 34.6 all-gather.18
  207.4 35.0 reduce-scatter.2
  269.6 32.4 all-gather.22
  318.3 44.5 reduce-scatter.4
  408.3 53.6 all-gather.24
  464.2 36.6 all-gather.26

commit v13 on v12

--- a/solution.py
+++ b/solution.py
@@ -799,9 +799,9 @@
         own_tokens,
         middle,
         grad_middle,
-        after(vectors, qkv_sum, fc_both),
-    )
-    results_home = swap_roles(results)
+        after(vectors, qkv_sum, fc_both, proj_pair),
+    )
+    results_home = swap_selected(results, stays)
 
     blank = jnp.zeros((1, width), f32)
     at = (0, STRIDE * rank)
@@ -835,7 +835,7 @@
         for r in range(8)
     ]
     qkv_whole = after(qkv_whole, small_sum, *fc_pieces[:4])
-    proj_whole = after(gather(after(proj_pair, qkv_whole), "x"), out_whole)
+    proj_whole = gather(after(proj_pair, qkv_whole), "x")
     fc_spans = [[(0, rank * hidden, hidden)] for rank in range(8)]
     fc_total = call(
         functools.partial(column_ring_total_kernel, fc_spans),
@@ -843,14 +843,7 @@
         struct((shard, 8 * hidden), f32),
         after(place, small_last),
         *fc_pieces,
-    )
-    proj_total = call(
-        proj_total_kernel,
-        "proj_total",
-        struct((hidden, width), f32),
-        after(place, fc_total),
-        proj_whole,
-        other_core(proj_whole),
+        light=True,
     )
     qkv_total = call(
         functools.partial(column_total_kernel, qkv_spans),
@@ -859,8 +852,18 @@
         after(place, results, fc_total),
         qkv_whole,
         other_core(qkv_whole),
-    )
-    out_total = row_total(out_whole, shard, "out_total", fc_total)
+        light=True,
+    )
+    proj_whole = after(proj_whole, qkv_total)
+    proj_total = call(
+        proj_total_kernel,
+        "proj_total",
+        struct((hidden, width), f32),
+        after(place, qkv_total),
+        proj_whole,
+        other_core(proj_whole),
+    )
+    out_total = row_total(out_whole, shard, "out_total", fc_total, qkv_total)
     return (
         results_home[1].reshape(1, span, width),
         results_home[0].astype(f32).reshape(1, span, width),

time: 558 us -> 533 us (0.955)
  waiting for transfers between devices: 140 us -> 124 us
    all_to_all x5, waiting for transfers between devices: 28.7 us -> 10.5 us  [exchange(): return lax.all_to_all(parts, axes, 0, 0)]
    ppermute x24, waiting for transfers between devices: 53.7 us -> 62.7 us  [ring(): lax.ppermute(value, axis, [(index[(i + step) % 4], index[i]) for i in ran...]
    ppermute x4 -> x3, starting transfers between devices: 21.1 us -> 18.4 us  [swap_roles(): return lax.ppermute(value, ('c', 'zh'), ROLES)]
    ppermute x4 -> x3, waiting for transfers between devices: 16.1 us -> 16 us  [swap_roles(): return lax.ppermute(value, ('c', 'zh'), ROLES)]
  transfers between devices with their start and end apart: 61 -> 61, of which waited for: 28 -> 26; matrix products, arithmetic and copies ran while one was open for 6% -> 6% of each run, Pallas kernels for 22% -> 23%
where the time goes in v13:
time: 533 us; the launch traced here: 525 us
  Pallas kernels  146 us (27%)
  waiting for transfers between devices  124 us (23%)
  starting transfers between devices  113 us (21%)
  blocking collectives  83.2 us (16%)
  local copies, waits for them, and re-layouts  34.1 us (6%)
  between operations  14.8 us (3%)
  matrix products  6.89 us (1%)
    pallas_call x24, Pallas kernels, call(): pl.pallas_call(kernel, out_shape=out_shape, in_specs=specs, out_specs=out...  146 us
    all_to_all x4, blocking collectives, exchange(): return lax.all_to_all(parts, axes, 0, 0)  83.2 us
    ppermute x24, waiting for transfers between devices, ring(): lax.ppermute(value, axis, [(index[(i + step) % 4], index[i]) for i in ran...  62.7 us
    all_to_all x5, starting transfers between devices, exchange(): return lax.all_to_all(parts, axes, 0, 0)  29.9 us
    ppermute x24, starting transfers between devices, ring(): lax.ppermute(value, axis, [(index[(i + step) % 4], index[i]) for i in ran...  27.9 us
    ppermute x9, waiting for transfers between devices, flipped(): return lax.ppermute(value, axis, [(0, 1), (1, 0)])  24.5 us
    ppermute x3, starting transfers between devices, swap_roles(): return lax.ppermute(value, ('c', 'zh'), ROLES)  18.4 us
    ppermute x3, waiting for transfers between devices, swap_roles(): return lax.ppermute(value, ('c', 'zh'), ROLES)  16 us
  transfers between devices with their start and end apart: 61, of which 26 were waited for; matrix products, arithmetic and copies ran while one was open for 6% of the time, Pallas kernels for 23%

profile of v13, /device:TPU:17, one launch (start us, length us, event | category | flops | bytes accessed | tf_op | source)
XLA Modules:
  0.0 524.8 jit_solution(6934969674797329118)
XLA Ops:
  39.7 8.6 %collective-permute-done.12 = bf16[200,1600]{1,0:T(8,128)(2,1)S(1)} collective-permute-done((bf16[200,1600]{1,0:T(8,128)(2,1)}, bf16[200,1600]{1,0:T(8,128)(2,1)S(1)}, u32[]{:S(2)}, u32[]{:S(2)}) %collective-permute-start.12) | collective-permute-done | bytes 640032 | tf_op jit(solution)/shard_map/ppermute | solution.py:50
  49.5 9.7 %all_to_all.45 = bf16[8,3,800]{2,1,0:T(4,128)(2,1)S(1)} all-to-all(bf16[8,3,800]{2,1,0:T(4,128)(2,1)S(1)} %broadcast_in_dim.21), channel_id=1, replica_groups=mesh['x'=4,'zl'=2,'c'=2,'y'=4,'zh'=2] {'y','zh'}, dimensions={0} | all-to-all | bytes 76800 | tf_op jit(solution)/shard_map/all_to_all | solution.py:62
  72.2 6.6 %collective-permute-done.6.refs_6_ = bf16[200,768]{1,0:T(8,128)(2,1)} collective-permute-done((bf16[200,768]{1,0:T(8,128)(2,1)}, bf16[200,768]{1,0:T(8,128)(2,1)}, u32[]{:S(2)}, u32[]{:S(2)}) %collective-permute-start.6) | collective-permute-done | bytes 307232 | tf_op jit(solution)/shard_map/ppermute | solution.py:46
  78.8 6.7 %collective-permute-done.7.refs_7_ = bf16[200,768]{1,0:T(8,128)(2,1)} collective-permute-done((bf16[200,768]{1,0:T(8,128)(2,1)}, bf16[200,768]{1,0:T(8,128)(2,1)}, u32[]{:S(2)}, u32[]{:S(2)}) %collective-permute-start.7) | collective-permute-done | bytes 307232 | tf_op jit(solution)/shard_map/ppermute | solution.py:46
  87.4 7.0 %collective-permute-start.13 = (bf16[128,1600]{1,0:T(8,128)(2,1)}, bf16[128,1600]{1,0:T(8,128)(2,1)S(1)}, u32[]{:S(2)}, u32[]{:S(2)}) collective-permute-start(bf16[128,1600]{1,0:T(8,128)(2,1)} %bitcast.51), channel_id=1, source_target_pairs={{0,0},{1,8},{8,1},{9,9},{2,2},{3,10},{10,3},{11,11},{4,4},{5,12},{... | collective-permute-start | bytes 1228808 | tf_op jit(solution)/shard_map/ppermute | solution.py:50
  116.4 15.6 %attend.1 = (bf16[1024,1600]{1,0:T(8,128)(2,1)}, bf16[1024,768]{1,0:T(8,128)(2,1)}, bf16[1024,256]{1,0:T(8,128)(2,1)}, f32[1024,4]{1,0:T(8,128)}, bf16[8,200,768]{2,1,0:T(8,128)(2,1)}) custom-call(s32[8]{0:T(128)} %stack.39.place_ref, bf16[1024,1600]{1,0:T(8,128)(2,1)} %all-gather.15.cloned.1.call-done.tokens_ref, f32[8,1600]{1,0:T(8,128)} %reshape.109.norm_ref, ...), custom_call_target="tpu_custom_call" | custom-call | flops 2516582400 | bytes 13636640 | tf_op jit(solution)/shard_map/attend/pallas_call | solution.py:122
  141.9 6.7 %all-to-all-done.1.slots_ref = bf16[8,128,256]{2,1,0:T(8,128)(2,1)} async-done(((bf16[8,128,256]{2,1,0:T(8,128)(2,1)}), bf16[8,128,256]{2,1,0:T(8,128)(2,1)}, u32[]{:S(2)}, u32[]{:S(2)}) %all-to-all-start.1) | async-done | bytes 524320 | tf_op jit(solution)/shard_map/all_to_all | solution.py:62
  165.2 7.9 %all-to-all-start.2 = ((bf16[8,128,200]{1,2,0:T(8,128)(2,1)}), bf16[8,128,200]{1,2,0:T(8,128)(2,1)S(1)}, u32[]{:S(2)}, u32[]{:S(2)}) async-start(bf16[8,128,200]{1,2,0:T(8,128)(2,1)} %copy.70), calls=%async_computation.2 | async-start | bytes 819200 | tf_op jit(solution)/shard_map/all_to_all | solution.py:62
  173.0 6.9 %fusion.2 = f32[1024,800]{0,1:T(8,128)} fusion(bf16[1024,1600]{1,0:T(8,128)(2,1)} %all-gather.21.cloned.1.call-done.right_ref, bf16[800,1600]{1,0:T(8,128)(2,1)S(1)} %broadcast_select_fusion.rows_ref), kind=kOutput, calls=%fused_computation.15 | convolution fusion | flops 2621440000 | bytes 9113600 | tf_op jit(solution)/shard_map/dot_general | solution.py:111
  192.5 14.8 %hidden.1 = (bf16[1024,800]{1,0:T(8,128)(2,1)}, bf16[1024,800]{1,0:T(8,128)(2,1)}, f32[1,800]{1,0:T(1,128)}, bf16[1024,1600]{1,0:T(8,128)(2,1)}) custom-call(s32[8]{0:T(128)} %stack.39.place_ref, bf16[1024,1600]{1,0:T(8,128)(2,1)} %all-gather.19.cloned.1.call-done.second_ref.left_ref, bf16[1600,800]{1,0:T(8,128)(2,1)} %bitcast.41, ...), custom_call_target="tpu_custom_call" | custom-call | flops 5242880000 | bytes 15673632 | tf_op jit(solution)/shard_map/hidden/pallas_call | solution.py:122
  207.5 9.1 %fc_grad.1 = (bf16[4,4,32,800]{3,2,1,0:T(8,128)(2,1)}, bf16[4,4,32,800]{3,2,1,0:T(8,128)(2,1)}, bf16[4,4,32,800]{3,2,1,0:T(8,128)(2,1)}, bf16[4,4,32,800]{3,2,1,0:T(8,128)(2,1)}) custom-call(s32[8]{0:T(128)} %stack.39.place_ref, bf16[1024,1600]{1,0:T(8,128)(2,1)} %all-gather.19.cloned.1.call-done.second_ref.left_ref, ...), custom_call_target="tpu_custom_call" | custom-call | flops 2621440000 | bytes 8192032 | tf_op jit(solution)/shard_map/fc_grad/pallas_call | solution.py:122
  220.2 7.4 %proj_grad.1 = (bf16[4,56,1600]{2,1,0:T(8,128)(2,1)}, bf16[4,56,1600]{2,1,0:T(8,128)(2,1)}, bf16[4,56,1600]{2,1,0:T(8,128)(2,1)}, bf16[4,56,1600]{2,1,0:T(8,128)(2,1)}) custom-call(s32[8]{0:T(128)} %stack.39.place_ref, bf16[1024,800]{1,0:T(8,128)(2,1)} %get-tuple-element.157.left_ref.active_ref, bf16[1024,1600]{1,0:T(8,128)(2,1)} %all-gather.21.cloned.1.call-done.right_ref), custom_call_target="tpu_custom_call" | custom-call | flops 2621440000 | bytes 7782432 | tf_op jit(solution)/shard_map/proj_grad/pallas_call | solution.py:122
  229.8 8.0 %down.1 = bf16[1024,1600]{1,0:T(8,128)(2,1)} custom-call(bf16[1024,800]{1,0:T(8,128)(2,1)} %get-tuple-element.157.left_ref.active_ref, bf16[800,1600]{1,0:T(8,128)(2,1)} %copy-done), custom_call_target="tpu_custom_call" | custom-call | flops 1 | bytes 1 | tf_op jit(solution)/shard_map/down/pallas_call | solution.py:122
  247.6 15.2 %collective-permute-done.23.refs_3_ = bf16[4,4,32,800]{3,2,1,0:T(8,128)(2,1)S(1)} collective-permute-done((bf16[4,4,32,800]{3,2,1,0:T(8,128)(2,1)}, bf16[4,4,32,800]{3,2,1,0:T(8,128)(2,1)S(1)}, u32[]{:S(2)}, u32[]{:S(2)}) %collective-permute-start.23) | collective-permute-done | bytes 819232 | tf_op jit(solution)/shard_map/ppermute | solution.py:38
  262.7 6.7 %branch_back.1 = (f32[128,1600]{1,0:T(8,128)}, bf16[128,1600]{1,0:T(8,128)(2,1)}, bf16[8,128,256]{2,1,0:T(8,128)(2,1)}, f32[4,1600]{1,0:T(4,128)}) custom-call(s32[8]{0:T(128)} %stack.39.place_ref, bf16[128,1600]{1,0:T(8,128)(2,1)} %reduce-scatter.3.cloned.1.call-done.grad_ref, f32[128,1600]{1,0:T(8,128)} %get-tuple-element.160.middle_ref, ...), custom_call_target="tpu_custom_call" | custom-call | flops 1 | bytes 1 | tf_op jit(solution)/shard_map/branch_back/pallas_call | solution.py:122
  272.2 6.5 %all-to-all-start.3 = ((bf16[8,128,256]{2,1,0:T(8,128)(2,1)}), bf16[8,128,256]{2,1,0:T(8,128)(2,1)S(1)}, u32[]{:S(2)}, u32[]{:S(2)}) async-start(bf16[8,128,256]{2,1,0:T(8,128)(2,1)} %get-tuple-element.161), calls=%async_computation.4 | async-start | bytes 1048576 | tf_op jit(solution)/shard_map/all_to_all | solution.py:62
  300.5 17.6 %attend_back.1 = (bf16[1024,768]{1,0:T(8,128)(2,1)}, bf16[8,2,128,1600]{3,2,1,0:T(8,128)(2,1)}, f32[1,768]{1,0:T(1,128)}) custom-call(s32[8]{0:T(128)} %stack.39.place_ref, bf16[1024,768]{1,0:T(8,128)(2,1)} %get-tuple-element.168.qkv_ref, bf16[1024,256]{1,0:T(8,128)(2,1)} %bitcast.49, bf16[1024,256]{1,0:T(8,128)(2,1)} %get-tuple-element.133.out_ref, ...), custom_call_target="tpu_custom_call" | custom-call | flops 25165824000 | bytes 16501792 | tf_op jit(solution)/shard_map/attend_back/pallas_call | solution.py:122
  330.5 9.3 %last_grads.1 = bf16[16,80,1600]{2,1,0:T(8,128)(2,1)} custom-call(s32[8]{0:T(128)} %stack.39.place_ref, bf16[1024,1600]{1,0:T(8,128)(2,1)} %get-tuple-element.179.first_ref, bf16[1024,768]{1,0:T(8,128)(2,1)} %get-tuple-element.174.mixed_ref, bf16[1024,200]{1,0:T(8,128)(2,1)} %bitcast.42, bf16[1024,1600]{1,0:T(8,128)(2,1)} %all-gather.23.cloned.1.call-done.branch_ref), custom_call_target="tpu_custom_call" | custom-call | flops 3171942400 | bytes 12632096 | tf_op jit(solution)/shard_map/last_grads/pallas_call | solution.py:122
  341.0 56.4 %all_to_all.46.parts_ref = bf16[16,80,1600]{2,1,0:T(8,128)(2,1)} all-to-all(bf16[16,80,1600]{2,1,0:T(8,128)(2,1)} %last_grads.1), channel_id=1, replica_groups=mesh['x'=4,'zl'=2,'c'=2,'y'=4,'zh'=2] {'zl','x','zh'}, dimensions={0} | all-to-all | bytes 8192000 | tf_op jit(solution)/shard_map/all_to_all | solution.py:62
  400.8 7.3 %all_to_all.47 = bf16[4,32,768]{2,1,0:T(8,128)(2,1)} all-to-all(bf16[4,32,768]{2,1,0:T(8,128)(2,1)} %get-tuple-element.189), channel_id=1, replica_groups=mesh['x'=4,'zl'=2,'c'=2,'y'=4,'zh'=2] {'y'}, dimensions={0} | all-to-all | bytes 393216 | tf_op jit(solution)/shard_map/all_to_all | solution.py:62
  435.3 9.8 %all_to_all.48 = f32[8,3,800]{2,1,0:T(4,128)S(1)} all-to-all(f32[8,3,800]{2,1,0:T(4,128)S(1)} %pad_maximum_fusion), channel_id=1, replica_groups=mesh['x'=4,'zl'=2,'c'=2,'y'=4,'zh'=2] {'y','zh'}, dimensions={0} | all-to-all | bytes 153600 | tf_op jit(solution)/shard_map/all_to_all | solution.py:62
  445.1 9.3 %collective-permute-done.38.refs_2_ = bf16[2,4,32,800]{3,2,1,0:T(8,128)(2,1)S(1)} collective-permute-done((bf16[2,4,32,800]{3,2,1,0:T(8,128)(2,1)}, bf16[2,4,32,800]{3,2,1,0:T(8,128)(2,1)S(1)}, u32[]{:S(2)}, u32[]{:S(2)}) %collective-permute-start.38) | collective-permute-done | bytes 409632 | tf_op jit(solution)/shard_map/ppermute | solution.py:38
  454.7 10.3 %all-gather.25.cloned.1.call-done = bf16[32,32,768]{2,1,0:T(8,128)(2,1)} async-done(((bf16[4,32,768]{2,1,0:T(8,128)(2,1)}), bf16[32,32,768]{2,1,0:T(8,128)(2,1)}) %all-gather.25.cloned.1.call-update) | async-done | bytes 1572880 | tf_op jit(solution)/shard_map/all_gather | solution.py:66
  487.3 9.0 %fc_total.1 = f32[200,6400]{1,0:T(8,128)} custom-call(s32[8]{0:T(128)} %stack.39.place_ref, bf16[2,4,32,800]{3,2,1,0:T(8,128)(2,1)} %fc_both.1.refs_0_, bf16[2,4,32,800]{3,2,1,0:T(8,128)(2,1)} %copy-done.20, bf16[2,4,32,800]{3,2,1,0:T(8,128)(2,1)} %copy-done.19, bf16[2,4,32,800]{3,2,1,0:T(8,128)(2,1)} %copy-done.18, ...), custom_call_target="tpu_custom_call" | custom-call | flops 1 | bytes 1 | tf_op jit(solution)/shard_map/fc_total/pallas_call | solution.py:122
  (292 shorter events, 237.8 us)
Async XLA Ops:
  7.3 109.1 %all-gather.15.cloned.1.call-start = ((), (), s32[]{:S(2)}) async-start(), calls=%async_computation.13 | async-start | bytes 3833856 | tf_op jit(solution)/shard_map/all_gather | solution.py:66
  21.4 127.2 %all-gather.17.cloned.1.call-start = ((), (), s32[]{:S(2)}) async-start(), calls=%async_computation.14 | async-start | bytes 5990400 | tf_op jit(solution)/shard_map/all_gather | solution.py:66
  49.2 116.0 %all-gather.21.cloned.1.call-start = ((), (), s32[]{:S(2)}) async-start(), calls=%async_computation.16 | async-start | bytes 3833856 | tf_op jit(solution)/shard_map/all_gather | solution.py:66
  101.2 40.7 %collective-permute-start.11 = (bf16[800,1600]{1,0:T(8,128)(2,1)S(1)}, bf16[800,1600]{1,0:T(8,128)(2,1)}, u32[]{:S(2)}, u32[]{:S(2)}) collective-permute-start(bf16[800,1600]{1,0:T(8,128)(2,1)S(1)} %copy-done.4), channel_id=1, source_target_pairs={{1,8},{8,1},{3,10},{10,3},{5,12},{12,5},{7,14},{14,7},{17,24},{24,... | collective-permute-start | bytes 7680008 | tf_op jit(solution)/shard_map/ppermute | solution.py:590
  112.7 23.6 %collective-permute-start.9 = (bf16[200,800]{1,0:T(8,128)(2,1)}, bf16[200,800]{1,0:T(8,128)(2,1)}, u32[]{:S(2)}, u32[]{:S(2)}) collective-permute-start(bf16[200,800]{1,0:T(8,128)(2,1)} %get-tuple-element.130), channel_id=1, source_target_pairs={{4,0},{6,2},{0,4},{2,6},{5,1},{7,3},{1,5},{3,7},{12,8},{14,10},{8,... | collective-permute-start | bytes 960008 | tf_op jit(solution)/shard_map/ppermute | solution.py:38
  141.5 51.0 %all-gather.19.cloned.1.call-start = ((), (), s32[]{:S(2)}) async-start(), calls=%async_computation.15 | async-start | bytes 3833856 | tf_op jit(solution)/shard_map/all_gather | solution.py:66
  154.4 30.4 %collective-permute-start.14 = (bf16[200,800]{1,0:T(8,128)(2,1)S(1)}, bf16[200,800]{1,0:T(8,128)(2,1)}, u32[]{:S(2)}, u32[]{:S(2)}) collective-permute-start(bf16[200,800]{1,0:T(8,128)(2,1)S(1)} %copy-done.21), channel_id=1, source_target_pairs={{0,1},{1,0},{2,3},{3,2},{4,5},{5,4},{6,7},{7,6},{8,9},{9,8},{10,11... | collective-permute-start | bytes 960008 | tf_op jit(solution)/shard_map/ppermute | solution.py:46
  157.7 27.1 %collective-permute-start.17 = (bf16[200,800]{1,0:T(8,128)(2,1)}, bf16[200,800]{1,0:T(8,128)(2,1)}, u32[]{:S(2)}, u32[]{:S(2)}) collective-permute-start(bf16[200,800]{1,0:T(8,128)(2,1)} %collective-permute-done.10.refs_3_), channel_id=1, source_target_pairs={{0,1},{1,0},{2,3},{3,2},{4,5},{5,4},{6,7},{7,6},{8,9},{9,8},{10,11... | collective-permute-start | bytes 960008 | tf_op jit(solution)/shard_map/ppermute | solution.py:46
  157.7 27.1 %collective-permute-start.16 = (bf16[200,800]{1,0:T(8,128)(2,1)}, bf16[200,800]{1,0:T(8,128)(2,1)}, u32[]{:S(2)}, u32[]{:S(2)}) collective-permute-start(bf16[200,800]{1,0:T(8,128)(2,1)} %collective-permute-done.9.refs_2_), channel_id=1, source_target_pairs={{0,1},{1,0},{2,3},{3,2},{4,5},{5,4},{6,7},{7,6},{8,9},{9,8},{10,11... | collective-permute-start | bytes 960008 | tf_op jit(solution)/shard_map/ppermute | solution.py:46
  160.7 28.3 %collective-permute-start.15 = (bf16[200,800]{1,0:T(8,128)(2,1)}, bf16[200,800]{1,0:T(8,128)(2,1)}, u32[]{:S(2)}, u32[]{:S(2)}) collective-permute-start(bf16[200,800]{1,0:T(8,128)(2,1)} %collective-permute-done.8.refs_1_), channel_id=1, source_target_pairs={{0,1},{1,0},{2,3},{3,2},{4,5},{5,4},{6,7},{7,6},{8,9},{9,8},{10,11... | collective-permute-start | bytes 960008 | tf_op jit(solution)/shard_map/ppermute | solution.py:46
  165.2 27.3 %all-to-all-start.2 = ((bf16[8,128,200]{1,2,0:T(8,128)(2,1)}), bf16[8,128,200]{1,2,0:T(8,128)(2,1)S(1)}, u32[]{:S(2)}, u32[]{:S(2)}) async-start(bf16[8,128,200]{1,2,0:T(8,128)(2,1)} %copy.70), calls=%async_computation.2 | async-start | bytes 819200 | tf_op jit(solution)/shard_map/all_to_all | solution.py:62
  173.0 89.7 %reduce-scatter.3.cloned.1.call-start = ((), (), s32[]{:S(2)}) async-start(), calls=%async_computation.11 | async-start | bytes 3833856 | tf_op jit(solution)/shard_map/reduce_scatter | solution.py:70
  207.3 123.2 %all-gather.23.cloned.1.call-start = ((), (), s32[]{:S(2)}) async-start(), calls=%async_computation.17 | async-start | bytes 3833856 | tf_op jit(solution)/shard_map/all_gather | solution.py:66
  216.6 30.1 %collective-permute-start.21 = (bf16[4,4,32,800]{3,2,1,0:T(8,128)(2,1)}, bf16[4,4,32,800]{3,2,1,0:T(8,128)(2,1)S(1)}, u32[]{:S(2)}, u32[]{:S(2)}) collective-permute-start(bf16[4,4,32,800]{3,2,1,0:T(8,128)(2,1)} %get-tuple-element.153), channel_id=1, source_target_pairs={{32,0},{64,32},{96,64},{0,96},{33,1},{65,33},{97,65},{1,97},{34,2}... | collective-permute-start | bytes 2457608 | tf_op jit(solution)/shard_map/ppermute | solution.py:38
  219.1 27.6 %collective-permute-start.22 = (bf16[4,4,32,800]{3,2,1,0:T(8,128)(2,1)}, bf16[4,4,32,800]{3,2,1,0:T(8,128)(2,1)S(1)}, u32[]{:S(2)}, u32[]{:S(2)}) collective-permute-start(bf16[4,4,32,800]{3,2,1,0:T(8,128)(2,1)} %get-tuple-element.154), channel_id=1, source_target_pairs={{64,0},{96,32},{0,64},{32,96},{65,1},{97,33},{1,65},{33,97},{66,2}... | collective-permute-start | bytes 2457608 | tf_op jit(solution)/shard_map/ppermute | solution.py:38
  219.6 43.1 %collective-permute-start.23 = (bf16[4,4,32,800]{3,2,1,0:T(8,128)(2,1)}, bf16[4,4,32,800]{3,2,1,0:T(8,128)(2,1)S(1)}, u32[]{:S(2)}, u32[]{:S(2)}) collective-permute-start(bf16[4,4,32,800]{3,2,1,0:T(8,128)(2,1)} %get-tuple-element.155), channel_id=1, source_target_pairs={{96,0},{0,32},{32,64},{64,96},{97,1},{1,33},{33,65},{65,97},{98,2}... | collective-permute-start | bytes 2457608 | tf_op jit(solution)/shard_map/ppermute | solution.py:38
  272.2 27.5 %all-to-all-start.3 = ((bf16[8,128,256]{2,1,0:T(8,128)(2,1)}), bf16[8,128,256]{2,1,0:T(8,128)(2,1)S(1)}, u32[]{:S(2)}, u32[]{:S(2)}) async-start(bf16[8,128,256]{2,1,0:T(8,128)(2,1)} %get-tuple-element.161), calls=%async_computation.4 | async-start | bytes 1048576 | tf_op jit(solution)/shard_map/all_to_all | solution.py:62
  278.8 122.0 %reduce-scatter.5.cloned.1.call-start = ((), (), s32[]{:S(2)}) async-start(), calls=%async_computation.12 | async-start | bytes 7667712 | tf_op jit(solution)/shard_map/reduce_scatter | solution.py:70
  318.2 146.8 %all-gather.25.cloned.1.call-start = ((), (), s32[]{:S(2)}) async-start(), calls=%async_computation.18 | async-start | bytes 1769472 | tf_op jit(solution)/shard_map/all_gather | solution.py:66
  408.2 93.5 %all-gather.27.cloned.1.call-start = ((), (), s32[]{:S(2)}) async-start(), calls=%async_computation.19 | async-start | bytes 1863680 | tf_op jit(solution)/shard_map/all_gather | solution.py:66
  424.1 30.3 %collective-permute-start.38 = (bf16[2,4,32,800]{3,2,1,0:T(8,128)(2,1)}, bf16[2,4,32,800]{3,2,1,0:T(8,128)(2,1)S(1)}, u32[]{:S(2)}, u32[]{:S(2)}) collective-permute-start(bf16[2,4,32,800]{3,2,1,0:T(8,128)(2,1)} %fc_both.1.refs_0_), channel_id=1, source_target_pairs={{64,0},{96,32},{0,64},{32,96},{65,1},{97,33},{1,65},{33,97},{66,2}... | collective-permute-start | bytes 1228808 | tf_op jit(solution)/shard_map/ppermute | solution.py:38
  424.9 29.8 %collective-permute-start.37 = (bf16[2,4,32,800]{3,2,1,0:T(8,128)(2,1)}, bf16[2,4,32,800]{3,2,1,0:T(8,128)(2,1)S(1)}, u32[]{:S(2)}, u32[]{:S(2)}) collective-permute-start(bf16[2,4,32,800]{3,2,1,0:T(8,128)(2,1)} %fc_both.1.refs_0_), channel_id=1, source_target_pairs={{32,0},{64,32},{96,64},{0,96},{33,1},{65,33},{97,65},{1,97},{34,2}... | collective-permute-start | bytes 1228808 | tf_op jit(solution)/shard_map/ppermute | solution.py:38
  465.0 31.3 %collective-permute-start.44 = (bf16[8,4,32,768]{3,2,1,0:T(8,128)(2,1)}, bf16[8,4,32,768]{3,2,1,0:T(8,128)(2,1)S(1)}, u32[]{:S(2)}, u32[]{:S(2)}) collective-permute-start(bf16[8,4,32,768]{3,2,1,0:T(8,128)(2,1)} %bitcast.43), channel_id=1, source_target_pairs={{0,8},{8,0},{1,9},{9,1},{2,10},{10,2},{3,11},{11,3},{4,12},{12,4},... | collective-permute-start | bytes 4718600 | tf_op jit(solution)/shard_map/ppermute | solution.py:58
  475.6 28.3 %collective-permute-start.36 = (bf16[2,128,1600]{1,2,0:T(8,128)(2,1)}, bf16[2,128,1600]{1,2,0:T(8,128)(2,1)}, u32[]{:S(2)}, u32[]{:S(2)}) collective-permute-start(bf16[2,128,1600]{1,2,0:T(8,128)(2,1)} %copy.75), channel_id=1, source_target_pairs={{1,8},{8,1},{3,10},{10,3},{5,12},{12,5},{7,14},{14,7},{17,24},{24,... | collective-permute-start | bytes 2457608 | tf_op jit(solution)/shard_map/ppermute | solution.py:54
  (89 other events, 1625.2 us)
Sparse Core Ops, SparseCore 0:
  21.5 29.1 all-gather.14
  53.0 36.9 all-gather.16
  101.4 37.6 all-gather.20
  153.9 34.7 all-gather.18
  207.4 35.0 reduce-scatter.2
  269.6 32.4 all-gather.22
  318.3 44.6 reduce-scatter.4
  408.3 56.6 all-gather.24
  467.2 34.2 all-gather.26
